TPU v7x, 32 devices: a whole 2x2x4 slice. The times are simulated.
32 devices in a mesh: seg: 8 (over z, x), pitch: 4 (over y, core).
Axes of the slice: x: 2, y: 2, z: 4, core: 2. Of those that a mesh axis runs over, the one named last changes fastest.
Arguments:
- state: float32 [128, 8, 5, 49, 128], P('seg', 'pitch'), may hold values from -6 to 6
- advect: float32 [128, 8, 5, 128], P('seg', 'pitch'), may hold values from 0.2 to 1
- viscous: float32 [128, 8, 5, 128], P('seg', 'pitch'), may hold values from 0.1 to 0.5
- inverse: bfloat16 [128, 8, 5, 5, 128], P('seg', 'pitch'), as said below
- lower: float32 [128, 8, 5, 5, 128], P('seg', 'pitch'), as said below
- upper: float32 [128, 8, 5, 5, 128], P('seg', 'pitch'), as said below
- blades: int32 [2], replicated, may hold values from 20 to 90
- harmonic: int32 [24], replicated, may hold values from 1 to 8, as said below
Outputs:
- update: float32 [128, 8, 5, 49, 128], P('seg', 'pitch')
Inputs may be any that keep to these rules, and one draw needn't show every extreme that they name: inverse holds each cell's given block inverse. lower holds each cell's upstream coupling, already multiplied by the block inverse and negated. upper holds each cell's downstream coupling, already multiplied by the block inverse and negated. `harmonic`: the mode multiples are not all equal.
All inputs are finite; a program needn't handle non-finite values.
Results may differ from a plain program's by a relative error of at most 0.0003.
Values sent between devices are 32-bit elements; how exact they have to be, the bound alone decides.
No kernel may reach another device: no remote copies, remote signals or barrier semaphores. Data moves between devices by JAX's collectives and lax.ppermute only.
A program may use at most 128 MiB of HBM per device.

v0:
```python
import functools
import math

import jax
import jax.numpy as jnp
import numpy as np
from jax import lax
from jax.experimental import pallas as pl
from jax.experimental.pallas import tpu as pltpu
from jax.sharding import PartitionSpec as P

F32 = jnp.float32
BF16 = jnp.bfloat16
V = 5
NT = 49
PAD = 56
DEPTH = 64
LANES = 128
LEAD = 4
MB = 1 << 20

CHUNKS = (((0, 24), False), ((24, 40), True), ((40, 48), False))


def rows_of(chunk):
    (first, last), extra = chunk
    return last - first + (8 if extra else 0)


def padded_even(count):
    return (count + 7) // 8 * 8


def kernel_call(body, out_shapes, scratch=(), vmem=40, flops=1_000_000, moved=4_000_000, name=None):
    smem = pl.BlockSpec(memory_space=pltpu.SMEM)
    vmem_spec = pl.BlockSpec(memory_space=pltpu.VMEM)

    def run(flags, *arrays):
        return pl.pallas_call(
            body,
            out_shape=[jax.ShapeDtypeStruct(s, F32) for s in out_shapes],
            in_specs=[smem] + [vmem_spec] * len(arrays),
            out_specs=[vmem_spec] * len(out_shapes),
            scratch_shapes=list(scratch),
            compiler_params=pltpu.CompilerParams(vmem_limit_bytes=vmem * MB),
            cost_estimate=pl.CostEstimate(flops=flops, bytes_accessed=moved, transcendentals=0),
            name=name,
        )(flags, *arrays)

    return run


def coefficient(ref, z, a, b, p):
    return ref[pl.ds(((z * V + a) * V + b) * 2 + p, 1), :]


def split_left(matrix):
    high = matrix.astype(BF16).astype(F32)
    place = lax.broadcasted_iota(jnp.int32, matrix.shape, 1)
    return jnp.where(place < 2 * DEPTH, high, matrix - high).astype(BF16)


def over_instants(left, cells):
    whole = jnp.concatenate(cells, axis=1)
    if whole.shape[0] < DEPTH:
        whole = jnp.concatenate(
            [whole, jnp.zeros((DEPTH - whole.shape[0], whole.shape[1]), F32)], axis=0
        )
    high = whole.astype(BF16)
    low = (whole - high.astype(F32)).astype(BF16)
    product = jnp.dot(
        left, jnp.concatenate([high, low, high], axis=0), preferred_element_type=F32
    )
    return [product[:, i * LANES : (i + 1) * LANES] for i in range(len(cells))]


def prepare(flags, st, phase, xn, xf, *chunks):
    p = flags[0]
    wrap = flags[1]
    cells = xn.shape[0] // V
    left = split_left(phase[...])
    zeros = jnp.zeros((8, LANES), F32)

    def separate(z):
        for v in range(V):
            j = z * V + v
            for out, q in ((xn, 1 - p), (xf, p)):
                out[j, PAD - 8 : PAD, :] = zeros
                out[j, 0:NT, :] = st[pl.ds(j * 2 * NT + q, NT, stride=2), :]

    def lead(z, carry):
        separate(z)
        return carry

    lax.fori_loop(0, LEAD, lead, 0)

    def rest(z, carry):
        separate(z)
        raw = [xf[z * V + v] for v in range(V)]
        lagged = over_instants(left, raw)
        for v in range(V):
            value = jnp.where(wrap == 1, lagged[v], raw[v])
            j = (z - LEAD) * V + v
            for out, ((first, last), extra) in zip(chunks, CHUNKS):
                width = last - first
                out[pl.ds(pl.multiple_of(j * width, 8), width), :] = value[first:last]
                if extra:
                    out[pl.ds((cells - LEAD) * V * width + j, 1), :] = value[NT - 1 : NT]
        return carry

    lax.fori_loop(LEAD, cells, rest, 0)


def sweeps(source, g, fg, spans, p, inverse, lower, upper, cells):
    for first, last in spans:
        nothing = tuple(jnp.zeros((last - first, LANES), F32) for _ in range(V))

        def ahead(z, current, first=first, last=last):
            right = source(z, first, last)
            result = []
            for a in range(V):
                total = coefficient(inverse, z, a, 0, p) * right[0]
                for b in range(1, V):
                    total += coefficient(inverse, z, a, b, p) * right[b]
                for b in range(V):
                    total += coefficient(lower, z, a, b, p) * current[b]
                g[z * V + a, first:last, :] = total
                result.append(total)
            return tuple(result)

        out = lax.fori_loop(0, cells, ahead, nothing)
        for a in range(V):
            fg[a, first:last, :] = out[a]

        def back(i, current, first=first, last=last):
            z = cells - 1 - i
            result = []
            for a in range(V):
                total = g[z * V + a, first:last, :]
                for b in range(V):
                    total += coefficient(upper, z, a, b, p) * current[b]
                g[z * V + a, first:last, :] = total
                result.append(total)
            return tuple(result)

        out = lax.fori_loop(0, cells, back, nothing)
        for a in range(V):
            fg[V + a, first:last, :] = out[a]


def residuals(x, other, halo, edges, advect, viscous, left, p, cells, put):
    def one(z, above, below):
        here = [x[z * V + v] for v in range(V)]
        timing = over_instants(left, here)
        for v in range(V):
            j = z * V + v
            pitch = other[j] - 2.0 * here[v]
            if halo is not None:
                pitch += halo[j]
            put(
                j,
                advect[pl.ds(j * 2 + p, 1), :] * (above(z, v) - below(z, v))
                + viscous[pl.ds(j * 2 + p, 1), :] * pitch
                - timing[v],
            )

    inner_above = lambda z, v: x[(z - 1) * V + v]
    inner_below = lambda z, v: x[(z + 1) * V + v]
    one(0, lambda z, v: edges[v], inner_below)

    def step(z, carry):
        one(z, inner_above, inner_below)
        return carry

    lax.fori_loop(1, cells - 1, step, 0)
    one(cells - 1, inner_above, lambda z, v: edges[V + v])


def take_edges(edges, from_left, from_right, p):
    skip = from_left.shape[0] - V * NT * 2
    for v in range(V):
        edges[v, PAD - 8 : PAD, :] = jnp.zeros((8, LANES), F32)
        edges[v, 0:NT, :] = from_left[pl.ds(skip + v * 2 * NT + p, NT, stride=2), :]
        edges[V + v, PAD - 8 : PAD, :] = jnp.zeros((8, LANES), F32)
        edges[V + v, 0:NT, :] = from_right[pl.ds(v * 2 * NT + p, NT, stride=2), :]


def near_cell(
    flags, xn, xf, halo, from_left, from_right, advect, viscous, inverse, lower, upper, derive,
    g, fg, edges, right,
):
    p = 1 - flags[0]
    cells = xn.shape[0] // V
    take_edges(edges, from_left, from_right, p)

    def put(j, value):
        right[j] = value

    residuals(xn, xf, halo, edges, advect, viscous, split_left(derive[...]), p, cells, put)
    source = lambda z, first, last: [right[z * V + v, first:last, :] for v in range(V)]
    sweeps(source, g, fg, ((0, 32), (32, PAD)), p, inverse, lower, upper, cells)


def far_base(
    flags, xn, xf, from_left, from_right, slab, advect, viscous, derive, phase, base, edges, halo
):
    p = flags[0]
    wrap = flags[1]
    cells = xn.shape[0] // V
    take_edges(edges, from_left, from_right, p)

    def put(j, value):
        base[j] = value

    residuals(xf, xn, None, edges, advect, viscous, split_left(derive[...]), p, cells, put)
    left = split_left(phase[...])
    for z in range(LEAD):
        for v in range(V):
            halo[v, NT - 1 : PAD, :] = jnp.zeros((PAD - NT + 1, LANES), F32)
            halo[v, 0:NT, :] = slab[pl.ds((z * V + v) * NT, NT), :]
        raw = [halo[v] for v in range(V)]
        lagged = over_instants(left, raw)
        for v in range(V):
            j = z * V + v
            value = jnp.where(wrap == 1, lagged[v], raw[v])
            base[j] += viscous[pl.ds(j * 2 + p, 1), :] * value


def far_chunk(chunk, flags, base, halo, viscous, inverse, lower, upper, g, fg):
    (first, last), extra = chunk
    width = last - first
    p = flags[0]
    cells = base.shape[0] // V
    top = lax.broadcasted_iota(jnp.int32, (8, LANES), 0) == 0

    def source(z, start, stop):
        result = []
        for v in range(V):
            j = z * V + v
            value = base[j, first:last, :]
            if extra:
                value = jnp.concatenate([value, base[j, PAD - 8 : PAD, :]], axis=0)
            h = jnp.maximum(z - LEAD, 0) * V + v
            arrived = halo[pl.ds(pl.multiple_of(h * width, 8), width), :]
            if extra:
                row = halo[pl.ds((cells - LEAD) * V * width + h, 1), :]
                arrived = jnp.concatenate([arrived, jnp.where(top, row, 0.0)], axis=0)
            scale = jnp.where(z >= LEAD, viscous[pl.ds(j * 2 + p, 1), :], 0.0)
            result.append(value + scale * arrived)
        return result

    rows = rows_of(chunk)
    sweeps(source, g, fg, ((0, rows),), p, inverse, lower, upper, cells)


def times(matrix, vector):
    result = []
    for a in range(V):
        total = matrix(a, 0) * vector[0]
        for b in range(1, V):
            total += matrix(a, b) * vector[b]
        result.append(total)
    return result


def plus(one, two):
    return [a + b for a, b in zip(one, two)]


def tiles(ref, c, kind):
    return [ref[c, kind * V + a] for a in range(V)]


def rows(ref, c, kind):
    return lambda a, b: ref[c, kind * V + a, b : b + 1, :]


def unit(a):
    place = lax.broadcasted_iota(jnp.int32, (8, LANES), 0)
    return jnp.where(place == a, 1.0, 0.0).astype(F32)


def transfer(flags, lower, upper, blocks, group, forward):
    cells = blocks.shape[1] // V
    for c in range(2):
        p = 1 - flags[0] if c == 0 else flags[0]

        def ahead(z, current):
            result = times(lambda a, b: coefficient(lower, z, a, b, p), current)
            for a in range(V):
                forward[z * V + a] = result[a]
            return tuple(result)

        through = lax.fori_loop(0, cells, ahead, tuple(unit(a) for a in range(V)))

        def back(i, current):
            z = cells - 1 - i
            result = times(lambda a, b: coefficient(upper, z, a, b, p), current)
            for a in range(V):
                result[a] = result[a] + jnp.concatenate(
                    [forward[z * V + a], jnp.zeros((8, LANES), F32)], axis=0
                )
                blocks[c, z * V + a] = result[a]
            return tuple(result)

        start = tuple(
            jnp.concatenate([jnp.zeros((8, LANES), F32), unit(a)], axis=0) for a in range(V)
        )
        ends = lax.fori_loop(0, cells, back, start)
        for a in range(V):
            group[c, a] = ends[a][:8]
            group[c, V + a] = ends[a][8:]
            group[c, 2 * V + a] = through[a]


def merge_matrices(flags, bit, start, *refs):
    if start:
        group, other, mats, merged, share_out = refs
    else:
        group, other, share, mats, merged, share_out = refs
    right = flags[3 + bit] == 1
    for c in range(2):
        for a in range(V):
            for target, kind, own_if in ((0, 2, True), (1, 0, True), (2, 1, False)):
                mine, theirs = group[c, kind * V + a], other[c, kind * V + a]
                pick_own = right if own_if else jnp.logical_not(right)
                mats[c, target * V + a] = jnp.where(pick_own, mine, theirs)
        if start:
            own = [[unit(a) for a in range(V)], [jnp.zeros((8, LANES), F32)] * V, [unit(a) for a in range(V)]]
        else:
            own = [tiles(share, c, kind) for kind in range(3)]
        for a in range(V):
            mats[c, 3 * V + a] = jnp.where(right, own[0][a], 0.0)
            mats[c, 4 * V + a] = jnp.where(right, own[1][a], 0.0)
            mats[c, 5 * V + a] = jnp.where(right, 0.0, own[2][a])
        p_left = [jnp.where(right, other[c, 2 * V + a], group[c, 2 * V + a]) for a in range(V)]
        g_left = [jnp.where(right, other[c, a], group[c, a]) for a in range(V)]
        h_right = [jnp.where(right, group[c, V + a], other[c, V + a]) for a in range(V)]
        turned = times(rows(mats, c, 1), p_left)
        new_p = times(rows(mats, c, 0), p_left)
        new_g = plus(g_left, times(rows(mats, c, 2), turned))
        new_h = times(rows(mats, c, 2), h_right)
        for a in range(V):
            merged[c, a] = new_g[a]
            merged[c, V + a] = new_h[a]
            merged[c, 2 * V + a] = new_p[a]
        s0 = times(rows(mats, c, 3), p_left)
        s1 = times(rows(mats, c, 4), p_left)
        s1b = times(rows(mats, c, 5), turned)
        s2 = times(rows(mats, c, 5), h_right)
        for a in range(V):
            share_out[c, a] = jnp.where(right, s0[a], own[0][a])
            share_out[c, V + a] = jnp.where(right, s1[a], own[1][a] + s1b[a])
            share_out[c, 2 * V + a] = jnp.where(right, own[2][a], s2[a])


def merge_level(right, c, mats, mine, theirs, inflow):
    f_left = [jnp.where(right, theirs[a], mine[a]) for a in range(V)]
    g_right = [jnp.where(right, mine[V + a], theirs[V + a]) for a in range(V)]
    back = plus(g_right, times(rows(mats, c, 1), f_left))
    from_left = times(rows(mats, c, 3), f_left)
    from_right = plus(
        times(rows(mats, c, 4), f_left), times(rows(mats, c, 5), back)
    )
    if inflow is not None:
        from_left = plus(inflow[:V], from_left)
        from_right = plus(inflow[V:], from_right)
    return f_left, back, from_left + from_right


def merge_flows(bit, c, start, flags, mats, flows, other, *refs):
    if start:
        merged, inflow_out = refs
        inflow = None
    else:
        inflow_in, merged, inflow_out = refs
    right = flags[3 + bit] == 1
    count = flows.shape[1] // 8

    def tile(t, carry):
        span = pl.ds(pl.multiple_of(t * 8, 8), 8)
        mine = [flows[i, span, :] for i in range(2 * V)]
        theirs = [other[i, span, :] for i in range(2 * V)]
        known = None if start else [inflow_in[i, span, :] for i in range(2 * V)]
        f_left, back, total = merge_level(right, c, mats, mine, theirs, known)
        f_right = [jnp.where(right, mine[a], theirs[a]) for a in range(V)]
        g_left = [jnp.where(right, theirs[V + a], mine[V + a]) for a in range(V)]
        new_f = plus(f_right, times(rows(mats, c, 0), f_left))
        new_g = plus(g_left, times(rows(mats, c, 2), back))
        for i, value in enumerate(new_f + new_g):
            merged[i, span, :] = value
        for i, value in enumerate(total):
            inflow_out[i, span, :] = value
        return carry

    lax.fori_loop(0, count, tile, 0)


def last_flows(right, c, mats, flows, other, inflow_in, store):
    for t in range(flows.shape[1] // 8):
        span = slice(t * 8, t * 8 + 8)
        mine = [flows[i, span, :] for i in range(2 * V)]
        theirs = [other[i, span, :] for i in range(2 * V)]
        known = None if inflow_in is None else [inflow_in[i, span, :] for i in range(2 * V)]
        _, _, total = merge_level(right, c, mats, mine, theirs, known)
        for i, value in enumerate(total):
            store(i, span, value)


def corrected(c, z, a, first, last, g, blocks, inflow):
    total = g[z * V + a, first:last, :]
    for b in range(V):
        total += blocks[c, z * V + a, b : b + 1, :] * inflow[b]
        total += blocks[c, z * V + a, 8 + b : 9 + b, :] * inflow[V + b]
    return total


def correct(bit, c, flags, mats, flows, other, inflow_in, g, blocks, result, inflow):
    right = flags[3 + bit] == 1

    def store(i, span, value):
        inflow[i, span, :] = value

    last_flows(right, c, mats, flows, other, inflow_in, store)
    cells = g.shape[0] // V
    total = g.shape[1]
    spans = ((0, 32), (32, total)) if total > 32 else ((0, total),)
    for first, last in spans:
        known = tuple(inflow[i, first:last, :] for i in range(2 * V))

        def step(z, known, first=first, last=last):
            for a in range(V):
                result[z * V + a, first:last, :] = corrected(c, z, a, first, last, g, blocks, known)
            return known

        lax.fori_loop(0, cells, step, known)


def finish(bit, flags, mats, flows, other, inflow_in, g, blocks, near, *refs):
    done, out, inflow = refs[:-2], refs[-2], refs[-1]
    right = flags[3 + bit] == 1
    p = flags[0]

    @pl.when(pl.program_id(0) == 0)
    def _():
        def store(i, span, value):
            inflow[i, span, :] = value

        last_flows(right, 1, mats, flows, other, inflow_in, store)

    first_row, last_row = CHUNKS[-1][0]
    width = last_row - first_row
    known = tuple(inflow[i] for i in range(2 * V))

    def step(z, carry):
        for a in range(V):
            j = z * V + a
            row = j * 2 * NT
            out[pl.ds(row + 1 - p, NT, stride=2), :] = near[j, 0:NT, :]
            for ref, ((first, last), extra) in zip(done, CHUNKS):
                out[pl.ds(row + p + 2 * first, last - first, stride=2), :] = ref[j, 0 : last - first, :]
                if extra:
                    out[pl.ds(row + p + 2 * (NT - 1), 1), :] = ref[j, last - first : last - first + 1, :]
            out[pl.ds(row + p + 2 * first_row, width, stride=2), :] = corrected(1, z, a, 0, width, g, blocks, known)
        return carry

    lax.fori_loop(0, g.shape[0] // V, step, 0)


def phase_ahead(blades, harmonic):
    count = harmonic.shape[0]
    angle = 2.0 * math.pi * np.outer(np.arange(1, count + 1), np.arange(NT)) / NT
    cosine, sine = np.cos(angle).astype(np.float32), np.sin(angle).astype(np.float32)
    ratio = blades[1].astype(F32) / blades[0].astype(F32)
    lag = 2.0 * math.pi * harmonic.astype(F32) * ratio
    turn, cross = jnp.cos(lag)[:, None], jnp.sin(lag)[:, None]
    basis = np.concatenate([cosine, sine], axis=0)
    turned = jnp.concatenate([turn * cosine + cross * sine, turn * sine - cross * cosine], axis=0)
    total = jnp.einsum("kn,km->nm", basis, turned, precision=lax.Precision.HIGHEST)
    return (1.0 + 2.0 * total) / NT


def derivative(blades, harmonic):
    gap = np.arange(NT)[:, None] - np.arange(NT)[None, :]
    safe = np.where(gap == 0, 1.0, np.sin(np.pi * gap / NT))
    table = np.where(gap == 0, 0.0, 0.5 * (1.0 - 2.0 * np.mod(gap, 2)) / safe).astype(np.float32)
    ratio = blades[1].astype(F32) / blades[0].astype(F32)
    return ratio / harmonic.shape[0] * table


def thrice(matrix):
    wide = jnp.pad(matrix, ((0, PAD - NT), (0, DEPTH - NT)))
    return jnp.concatenate([wide] * 3, axis=1)


def local(state, advect, viscous, inverse, lower, upper, blades, harmonic):
    cells = state.shape[0]
    segs, slabs = lax.axis_size("seg"), lax.axis_size("pitch")
    levels = segs.bit_length() - 1
    slab, seg = lax.axis_index("pitch"), lax.axis_index("seg")
    side = slab % 2
    wrap = jnp.logical_or(slab == 0, slab == slabs - 1)
    bits = [(seg >> k) & 1 for k in range(levels)]
    flags = jnp.stack([side, wrap.astype(jnp.int32), seg, *bits]).astype(jnp.int32)
    far_pairs = [(i, (i - 1) % slabs if i % 2 == 0 else (i + 1) % slabs) for i in range(slabs)]
    near_pairs = [(i, i ^ 1) for i in range(slabs)]
    to_far = lambda x: lax.ppermute(x, "pitch", far_pairs)
    to_level = lambda x, k: lax.ppermute(x, "seg", [(i, i ^ (1 << k)) for i in range(segs)])

    st = state.transpose(0, 2, 3, 1, 4).reshape(cells * V * NT * 2, LANES)
    lead_rows = LEAD * V * NT
    slab_out = lax.dynamic_index_in_dim(
        st[: 2 * lead_rows].reshape(lead_rows, 2, LANES), side, axis=1, keepdims=False
    )
    slab_in = to_far(slab_out)

    flat = lambda x: x.transpose(0, 2, 3, 1, 4).reshape(cells * V * V * 2, LANES)
    inv, low, upp = flat(inverse.astype(F32)), flat(lower), flat(upper)
    adv = advect.transpose(0, 2, 1, 3).reshape(cells * V * 2, LANES)
    vis = viscous.transpose(0, 2, 1, 3).reshape(cells * V * 2, LANES)

    edge_rows = padded_even(V * NT * 2)
    from_left = lax.ppermute(st[-edge_rows:], "seg", [(i, i + 1) for i in range(segs - 1)])
    from_right = lax.ppermute(st[:edge_rows], "seg", [(i + 1, i) for i in range(segs - 1)])

    ahead = phase_ahead(blades, harmonic)
    sent = jnp.where(slab == 0, ahead, ahead.T)
    send_phase, take_phase = thrice(sent), thrice(sent.T)
    derive = thrice(derivative(blades, harmonic))

    rest = (cells - LEAD) * V
    chunk_shapes = [
        (rest * (last - first) + (padded_even(rest) if extra else 0), LANES)
        for (first, last), extra in CHUNKS
    ]
    x_shape = (cells * V, PAD, LANES)
    xn, xf, *chunks = kernel_call(
        prepare, [x_shape, x_shape, *chunk_shapes], vmem=24, moved=11_000_000, name="prepare"
    )(flags, st, send_phase)
    arrived = [to_far(chunk) for chunk in chunks]
    halo_near = lax.ppermute(xn, "pitch", near_pairs)

    blocks, group = kernel_call(
        transfer,
        [(2, cells * V, 16, LANES), (2, 3 * V, 8, LANES)],
        [pltpu.VMEM((cells * V, 8, LANES), F32)],
        vmem=16, name="transfer",
    )(flags, low, upp)
    mats, share = [], []
    mats_shape, group_shape = (2, 6 * V, 8, LANES), (2, 3 * V, 8, LANES)
    for k in range(levels):
        out = kernel_call(
            lambda flags, *refs, k=k: merge_matrices(flags, k, k == 0, *refs),
            [mats_shape, group_shape, group_shape], vmem=16, moved=500_000, name="merge_matrices",
        )(flags, group, to_level(group, k), *share)
        mats.append(out[0])
        group, share = out[1], [out[2]]

    def exchange(c, fg):
        inflow = []
        for k in range(levels - 1):
            shape = fg.shape
            fg, known = kernel_call(
                functools.partial(merge_flows, k, c, k == 0),
                [shape, shape], vmem=16, moved=500_000, name="merge_flows",
            )(flags, mats[k], fg, to_level(fg, k), *inflow)
            inflow = [known]
        return fg, to_level(fg, levels - 1), inflow[0]

    def settle(c, fg, g):
        flows = exchange(c, fg)
        return kernel_call(
            functools.partial(correct, levels - 1, c),
            [g.shape], [pltpu.VMEM((2 * V, g.shape[1], LANES), F32)], vmem=24, name="correct",
        )(flags, mats[-1], *flows, g, blocks)[0]

    g_near, fg_near = kernel_call(
        near_cell,
        [x_shape, (2 * V, PAD, LANES)],
        [pltpu.VMEM((2 * V, PAD, LANES), F32), pltpu.VMEM(x_shape, F32)],
        vmem=32, moved=12_000_000, name="near_cell",
    )(flags, xn, xf, halo_near, from_left, from_right, adv, vis, inv, low, upp, derive)
    base = kernel_call(
        far_base,
        [x_shape],
        [pltpu.VMEM((2 * V, PAD, LANES), F32), pltpu.VMEM((V, PAD, LANES), F32)],
        vmem=24, moved=8_000_000, name="far_base",
    )(flags, xn, xf, from_left, from_right, slab_in, adv, vis, derive, take_phase)[0]

    near = settle(0, fg_near, g_near)
    solved = []
    for chunk, halo in zip(CHUNKS, arrived):
        height = rows_of(chunk)
        solved.append(
            kernel_call(
                functools.partial(far_chunk, chunk),
                [(cells * V, height, LANES), (2 * V, height, LANES)], vmem=24, name="far_chunk",
            )(flags, base, halo, vis, inv, low, upp)
        )
    done = [settle(1, fg, g) for g, fg in solved[:-1]]
    g_last, fg_last = solved[-1]
    flows = exchange(1, fg_last)

    steps = 4
    part = cells // steps
    whole = lambda x: pl.BlockSpec(x.shape, lambda i: (0,) * x.ndim)
    by_cell = lambda x: pl.BlockSpec((part * V,) + x.shape[1:], lambda i: (i, 0, 0))
    height = rows_of(CHUNKS[-1])
    out = pl.pallas_call(
        functools.partial(finish, levels - 1),
        grid=(steps,),
        out_shape=jax.ShapeDtypeStruct(st.shape, F32),
        in_specs=[pl.BlockSpec(memory_space=pltpu.SMEM)]
        + [whole(x) for x in (mats[-1], *flows)]
        + [
            by_cell(g_last),
            pl.BlockSpec((2, part * V, 16, LANES), lambda i: (0, i, 0, 0)),
            by_cell(near),
        ]
        + [by_cell(x) for x in done],
        out_specs=pl.BlockSpec((part * V * NT * 2, LANES), lambda i: (i, 0)),
        scratch_shapes=[pltpu.VMEM((2 * V, height, LANES), F32)],
        compiler_params=pltpu.CompilerParams(vmem_limit_bytes=24 * MB),
        name="finish",
    )(flags, mats[-1], *flows, g_last, blocks, near, *done)
    return out.reshape(cells, V, NT, 2, LANES).transpose(0, 3, 1, 2, 4)


def solution(mesh):
    cell = P("seg", "pitch", None, None, None)
    return jax.shard_map(
        local,
        mesh=mesh,
        in_specs=(cell, P("seg", "pitch", None, None), P("seg", "pitch", None, None), cell, cell, cell, P(), P()),
        out_specs=cell,
        check_vma=False,
    )
```

profile of v0, /device:TPU:0, one launch (start us, length us, event | category | flops | bytes accessed | tf_op | source)
XLA Modules:
  0.0 116.9 jit_solution(1144902127499472770)
XLA Ops:
  0.0 1.4 %fusion.17 = (s32[1]{0:T(128)}, s32[1]{0:T(128)}) fusion(s32[2]{0:T(128)} %param.18), kind=kLoop, calls=%fused_computation.27 | loop fusion | bytes 16 | tf_op jit(solution)/shard_map/slice | solution.py:474
  2.7 0.7 fusion.15
  3.4 1.1 fusion.6
  4.5 1.1 fusion.2
  5.6 0.1 copy.13
  5.7 0.6 bitcast_select_fusion
  6.6 2.1 %copy-done.4 = f32[16,2,5,49,128]{4,1,3,2,0:T(2,128)S(1)} copy-done((f32[16,2,5,49,128]{4,1,3,2,0:T(2,128)S(1)}, f32[16,2,5,49,128]{4,1,3,2,0:T(2,128)}, u32[]{:S(2)}) %copy-start.4) | copy-done | bytes 4014104
  8.7 3.1 %prepare.1 = (f32[80,56,128]{2,1,0:T(8,128)S(1)}, f32[80,56,128]{2,1,0:T(8,128)S(1)}, f32[1440,128]{1,0:T(8,128)S(1)}, f32[1024,128]{1,0:T(8,128)S(1)}, f32[480,128]{1,0:T(8,128)S(1)}) custom-call(s32[6]{0:T(128)S(1)} %stack.31.flags, f32[7840,128]{1,0:T(8,128)S(1)} %bitcast.53, f32[56,192]{1,0:T(8,128)S(1)} %pad_maximum_fusion.phase), custom_call_target="tpu_custom_call" | custom-call | flops 1000000 | bytes 11000000 | tf_op jit(solution)/shard_map/prepare/pallas_call | solution.py:39
  11.8 1.4 %copy-done.2 = f32[80,56,128]{2,1,0:T(8,128)} copy-done((f32[80,56,128]{2,1,0:T(8,128)}, f32[80,56,128]{2,1,0:T(8,128)S(1)}, u32[]{:S(2)}) %copy-start.2) | copy-done | bytes 2293784
  13.2 0.8 copy-done.8
  14.0 0.5 collective-permute-start.10
  14.5 0.8 fusion.16
  15.3 1.3 %collective-permute-start.4 = (f32[496,128]{1,0:T(8,128)}, f32[496,128]{1,0:T(8,128)S(1)}, u32[]{:S(2)}, u32[]{:S(2)}) collective-permute-start(f32[496,128]{1,0:T(8,128)} %get-tuple-element.81), channel_id=1, source_target_pairs={{4,0},{8,4},{12,8},{16,12},{20,16},{24,20},{28,24},{5,1},{9,5},{13... | collective-permute-start | bytes 761864 | tf_op jit(solution)/shard_map/ppermute | solution.py:524
  16.6 5.8 %collective-permute-start.3 = (f32[496,128]{1,0:T(8,128)}, f32[496,128]{1,0:T(8,128)}, u32[]{:S(2)}, u32[]{:S(2)}) collective-permute-start(f32[496,128]{1,0:T(8,128)} %get-tuple-element.82), channel_id=1, source_target_pairs={{0,4},{4,8},{8,12},{12,16},{16,20},{20,24},{24,28},{1,5},{5,9},{9,... | collective-permute-start | bytes 761864 | tf_op jit(solution)/shard_map/ppermute | solution.py:523
  22.4 2.3 %slice.27 = f32[4,5,49,2,128]{4,3,2,1,0:T(2,128)} slice(f32[16,5,49,2,128]{4,3,2,1,0:T(2,128)} %bitcast.52), slice={[0:4], [0:5], [0:49], [0:2], [0:128]} | slice | bytes 2007040 | tf_op jit(solution)/shard_map/slice | solution.py:513
  24.8 1.8 %constant_dynamic-slice_fusion = f32[980,1,128]{2,1,0:T(1,128)S(1)} fusion(f32[980,2,128]{2,1,0:T(2,128)} %bitcast.62, s32[]{:T(128)S(6)} %select_n.25), kind=kLoop, calls=%fused_computation.25 | loop fusion | bytes 1003524 | tf_op jit(solution)/shard_map/jit(dynamic_index_in_dim)/dynamic_slice | solution.py:512
  26.6 1.6 %collective-permute-start.5 = (f32[980,128]{1,0:T(8,128)S(1)}, f32[980,128]{1,0:T(8,128)S(1)}, u32[]{:S(2)}, u32[]{:S(2)}) collective-permute-start(f32[980,128]{1,0:T(8,128)S(1)} %bitcast.63), channel_id=1, source_target_pairs={{0,3},{1,2},{2,1},{3,0},{4,7},{5,6},{6,5},{7,4},{8,11},{9,10},{10,... | collective-permute-start | bytes 1505288 | tf_op jit(solution)/shard_map/ppermute | solution.py:507
  28.2 0.2 collective-permute-start.14
  28.4 0.8 broadcast_multiply_fusion
  29.2 1.6 %collective-permute-start.18 = (f32[1024,128]{1,0:T(8,128)}, f32[1024,128]{1,0:T(8,128)S(1)}, u32[]{:S(2)}, u32[]{:S(2)}) collective-permute-start(f32[1024,128]{1,0:T(8,128)} %copy-done.8), channel_id=1, source_target_pairs={{0,3},{1,2},{2,1},{3,0},{4,7},{5,6},{6,5},{7,4},{8,11},{9,10},{10,... | collective-permute-start | bytes 1572872 | tf_op jit(solution)/shard_map/ppermute | solution.py:507
  30.8 1.1 reshape.49
  31.9 0.5 collective-permute-done.3.from_left
  32.4 7.4 %near_cell.1 = (f32[80,56,128]{2,1,0:T(8,128)S(1)}, f32[10,56,128]{2,1,0:T(8,128)S(1)}) custom-call(s32[6]{0:T(128)S(1)} %stack.31.flags, f32[80,56,128]{2,1,0:T(8,128)S(1)} %get-tuple-element.51.xn, f32[80,56,128]{2,1,0:T(8,128)S(1)} %copy-done.3, f32[80,56,128]{2,1,0:T(8,128)} %collective-permute-done.10.halo, ...), custom_call_target="tpu_custom_call" | custom-call | flops 1000000 | bytes 12000000 | tf_op jit(solution)/shard_map/near_cell/pallas_call | solution.py:39
  39.9 2.6 %collective-permute-start.11 = (f32[10,56,128]{2,1,0:T(8,128)S(1)}, f32[10,56,128]{2,1,0:T(8,128)S(1)}, u32[]{:S(2)}, u32[]{:S(2)}) collective-permute-start(f32[10,56,128]{2,1,0:T(8,128)S(1)} %get-tuple-element.61.flows), channel_id=1, source_target_pairs={{0,4},{4,0},{8,12},{12,8},{16,20},{20,16},{24,28},{28,24},{1,5},{5... | collective-permute-start | bytes 860168 | tf_op jit(solution)/shard_map/ppermute | solution.py:508
  42.4 1.6 %transfer.1 = (f32[2,80,16,128]{3,2,1,0:T(8,128)S(1)}, f32[2,15,8,128]{3,2,1,0:T(8,128)S(1)}) custom-call(s32[6]{0:T(128)S(1)} %stack.31.flags, f32[800,128]{1,0:T(8,128)S(1)} %bitcast.39, f32[800,128]{1,0:T(8,128)S(1)} %bitcast.44), custom_call_target="tpu_custom_call" | custom-call | flops 1000000 | bytes 4000000 | tf_op jit(solution)/shard_map/transfer/pallas_call | solution.py:39
  44.1 8.0 %collective-permute-done.refs_1_ = f32[2,15,8,128]{3,2,1,0:T(8,128)S(1)} collective-permute-done((f32[2,15,8,128]{3,2,1,0:T(8,128)S(1)}, f32[2,15,8,128]{3,2,1,0:T(8,128)S(1)}, u32[]{:S(2)}, u32[]{:S(2)}) %collective-permute-start) | collective-permute-done | bytes 122912 | tf_op jit(solution)/shard_map/ppermute | solution.py:508
  52.1 0.7 merge_matrices.3
  52.8 0.9 merge_flows.10
  53.7 3.7 %collective-permute-start.12 = (f32[10,56,128]{2,1,0:T(8,128)S(1)}, f32[10,56,128]{2,1,0:T(8,128)S(1)}, u32[]{:S(2)}, u32[]{:S(2)}) collective-permute-start(f32[10,56,128]{2,1,0:T(8,128)S(1)} %get-tuple-element.62.flows), channel_id=1, source_target_pairs={{0,8},{4,12},{8,0},{12,4},{16,24},{20,28},{24,16},{28,20},{1,9},{5... | collective-permute-start | bytes 860168 | tf_op jit(solution)/shard_map/ppermute | solution.py:508
  57.3 0.1 collective-permute-start.1
  57.5 4.2 %far_base.1.base = f32[80,56,128]{2,1,0:T(8,128)S(1)} custom-call(s32[6]{0:T(128)S(1)} %stack.31.flags, f32[80,56,128]{2,1,0:T(8,128)S(1)} %get-tuple-element.51.xn, f32[80,56,128]{2,1,0:T(8,128)S(1)} %copy-done.3, f32[496,128]{1,0:T(8,128)} %collective-permute-done.3.from_left, f32[496,128]{1,0:T(8,128)S(1)} %collective-permute-done.4.from_right, ...), custom_call_target="tpu_custom_call" | custom-call | flops 1000000 | bytes 8000000 | tf_op jit(solution)/shard_map/far_base/pallas_call | solution.py:39
  61.8 5.4 %collective-permute-done.18.halo = f32[1024,128]{1,0:T(8,128)S(1)} collective-permute-done((f32[1024,128]{1,0:T(8,128)}, f32[1024,128]{1,0:T(8,128)S(1)}, u32[]{:S(2)}, u32[]{:S(2)}) %collective-permute-start.18) | collective-permute-done | bytes 524320 | tf_op jit(solution)/shard_map/ppermute | solution.py:507
  67.1 1.9 %far_chunk.5 = (f32[80,24,128]{2,1,0:T(8,128)S(1)}, f32[10,24,128]{2,1,0:T(8,128)S(1)}) custom-call(s32[6]{0:T(128)S(1)} %stack.31.flags, f32[80,56,128]{2,1,0:T(8,128)S(1)} %far_base.1.base, f32[1024,128]{1,0:T(8,128)S(1)} %collective-permute-done.18.halo, f32[160,128]{1,0:T(8,128)S(1)} %bitcast.57, f32[800,128]{1,0:T(8,128)S(1)} %bitcast.49, ...), custom_call_target="tpu_custom_call" | custom-call | flops 1000000 | bytes 4000000 | tf_op jit(solution)/shard_map/far_chunk/pallas_call | solution.py:39
  69.1 2.6 %collective-permute-start.19 = (f32[10,24,128]{2,1,0:T(8,128)S(1)}, f32[10,24,128]{2,1,0:T(8,128)S(1)}, u32[]{:S(2)}, u32[]{:S(2)}) collective-permute-start(f32[10,24,128]{2,1,0:T(8,128)S(1)} %get-tuple-element.75.flows), channel_id=1, source_target_pairs={{0,4},{4,0},{8,12},{12,8},{16,20},{20,16},{24,28},{28,24},{1,5},{5... | collective-permute-start | bytes 368648 | tf_op jit(solution)/shard_map/ppermute | solution.py:508
  71.6 1.0 collective-permute-start.6
  72.6 1.9 %far_chunk.4 = (f32[80,24,128]{2,1,0:T(8,128)S(1)}, f32[10,24,128]{2,1,0:T(8,128)S(1)}) custom-call(s32[6]{0:T(128)S(1)} %stack.31.flags, f32[80,56,128]{2,1,0:T(8,128)S(1)} %far_base.1.base, f32[1440,128]{1,0:T(8,128)S(1)} %collective-permute-done.14.halo, f32[160,128]{1,0:T(8,128)S(1)} %bitcast.58, f32[800,128]{1,0:T(8,128)S(1)} %bitcast.50, ...), custom_call_target="tpu_custom_call" | custom-call | flops 1000000 | bytes 4000000 | tf_op jit(solution)/shard_map/far_chunk/pallas_call | solution.py:39
  74.5 0.4 collective-permute-start.15
  75.0 0.7 merge_matrices.4
  75.7 0.9 merge_flows.11
  76.6 2.7 %collective-permute-start.13 = (f32[10,56,128]{2,1,0:T(8,128)S(1)}, f32[10,56,128]{2,1,0:T(8,128)S(1)}, u32[]{:S(2)}, u32[]{:S(2)}) collective-permute-start(f32[10,56,128]{2,1,0:T(8,128)S(1)} %get-tuple-element.64.flows), channel_id=1, source_target_pairs={{0,16},{4,20},{8,24},{12,28},{16,0},{20,4},{24,8},{28,12},{1,17},{... | collective-permute-start | bytes 860168 | tf_op jit(solution)/shard_map/ppermute | solution.py:508
  79.2 0.7 merge_flows.14
  79.9 0.9 collective-permute-start.20
  80.9 0.7 merge_flows.12
  81.5 1.3 %collective-permute-start.16 = (f32[10,24,128]{2,1,0:T(8,128)S(1)}, f32[10,24,128]{2,1,0:T(8,128)S(1)}, u32[]{:S(2)}, u32[]{:S(2)}) collective-permute-start(f32[10,24,128]{2,1,0:T(8,128)S(1)} %get-tuple-element.69.flows), channel_id=1, source_target_pairs={{0,8},{4,12},{8,0},{12,4},{16,24},{20,28},{24,16},{28,20},{1,9},{5... | collective-permute-start | bytes 368648 | tf_op jit(solution)/shard_map/ppermute | solution.py:508
  82.8 1.1 collective-permute-start.2
  83.9 1.2 %far_chunk.3 = (f32[80,8,128]{2,1,0:T(8,128)S(1)}, f32[10,8,128]{2,1,0:T(8,128)S(1)}) custom-call(s32[6]{0:T(128)S(1)} %stack.31.flags, f32[80,56,128]{2,1,0:T(8,128)S(1)} %far_base.1.base, f32[480,128]{1,0:T(8,128)S(1)} %collective-permute-done.6.halo, f32[160,128]{1,0:T(8,128)S(1)} %bitcast.59, f32[800,128]{1,0:T(8,128)S(1)} %bitcast.51, ...), custom_call_target="tpu_custom_call" | custom-call | flops 1000000 | bytes 4000000 | tf_op jit(solution)/shard_map/far_chunk/pallas_call | solution.py:39
  85.1 3.9 %collective-permute-done.20.other = f32[10,24,128]{2,1,0:T(8,128)S(1)} collective-permute-done((f32[10,24,128]{2,1,0:T(8,128)S(1)}, f32[10,24,128]{2,1,0:T(8,128)S(1)}, u32[]{:S(2)}, u32[]{:S(2)}) %collective-permute-start.20) | collective-permute-done | bytes 122912 | tf_op jit(solution)/shard_map/ppermute | solution.py:508
  89.1 0.7 merge_flows.15
  89.8 2.4 %collective-permute-start.21 = (f32[10,24,128]{2,1,0:T(8,128)S(1)}, f32[10,24,128]{2,1,0:T(8,128)S(1)}, u32[]{:S(2)}, u32[]{:S(2)}) collective-permute-start(f32[10,24,128]{2,1,0:T(8,128)S(1)} %get-tuple-element.78.flows), channel_id=1, source_target_pairs={{0,16},{4,20},{8,24},{12,28},{16,0},{20,4},{24,8},{28,12},{1,17},{... | collective-permute-start | bytes 368648 | tf_op jit(solution)/shard_map/ppermute | solution.py:508
  92.2 0.4 collective-permute-done.16.other
  92.6 0.7 merge_flows.13
  93.3 1.5 %collective-permute-start.17 = (f32[10,24,128]{2,1,0:T(8,128)S(1)}, f32[10,24,128]{2,1,0:T(8,128)S(1)}, u32[]{:S(2)}, u32[]{:S(2)}) collective-permute-start(f32[10,24,128]{2,1,0:T(8,128)S(1)} %get-tuple-element.71.flows), channel_id=1, source_target_pairs={{0,16},{4,20},{8,24},{12,28},{16,0},{20,4},{24,8},{28,12},{1,17},{... | collective-permute-start | bytes 368648 | tf_op jit(solution)/shard_map/ppermute | solution.py:508
  94.8 1.6 %collective-permute-start.7 = (f32[10,8,128]{2,1,0:T(8,128)S(1)}, f32[10,8,128]{2,1,0:T(8,128)S(1)}, u32[]{:S(2)}, u32[]{:S(2)}) collective-permute-start(f32[10,8,128]{2,1,0:T(8,128)S(1)} %get-tuple-element.54.flows), channel_id=1, source_target_pairs={{0,4},{4,0},{8,12},{12,8},{16,20},{20,16},{24,28},{28,24},{1,5},{5... | collective-permute-start | bytes 122888 | tf_op jit(solution)/shard_map/ppermute | solution.py:508
  96.5 2.4 %collective-permute-done.7.other = f32[10,8,128]{2,1,0:T(8,128)S(1)} collective-permute-done((f32[10,8,128]{2,1,0:T(8,128)S(1)}, f32[10,8,128]{2,1,0:T(8,128)S(1)}, u32[]{:S(2)}, u32[]{:S(2)}) %collective-permute-start.7) | collective-permute-done | bytes 40992 | tf_op jit(solution)/shard_map/ppermute | solution.py:508
  98.8 0.6 merge_flows.8
  99.4 1.2 %collective-permute-start.8 = (f32[10,8,128]{2,1,0:T(8,128)S(1)}, f32[10,8,128]{2,1,0:T(8,128)S(1)}, u32[]{:S(2)}, u32[]{:S(2)}) collective-permute-start(f32[10,8,128]{2,1,0:T(8,128)S(1)} %get-tuple-element.55.flows), channel_id=1, source_target_pairs={{0,8},{4,12},{8,0},{12,4},{16,24},{20,28},{24,16},{28,20},{1,9},{5... | collective-permute-start | bytes 122888 | tf_op jit(solution)/shard_map/ppermute | solution.py:508
  100.7 5.1 %collective-permute-done.8.other = f32[10,8,128]{2,1,0:T(8,128)S(1)} collective-permute-done((f32[10,8,128]{2,1,0:T(8,128)S(1)}, f32[10,8,128]{2,1,0:T(8,128)S(1)}, u32[]{:S(2)}, u32[]{:S(2)}) %collective-permute-start.8) | collective-permute-done | bytes 40992 | tf_op jit(solution)/shard_map/ppermute | solution.py:508
  105.8 0.6 merge_flows.9
  106.4 1.3 %merge_matrices.5 = (f32[2,30,8,128]{3,2,1,0:T(8,128)S(1)}, f32[2,15,8,128]{3,2,1,0:T(8,128)}, f32[2,15,8,128]{3,2,1,0:T(8,128)}) custom-call(s32[6]{0:T(128)S(1)} %stack.31.flags, f32[2,15,8,128]{3,2,1,0:T(8,128)S(1)} %get-tuple-element.46.refs_0_, f32[2,15,8,128]{3,2,1,0:T(8,128)S(1)} %collective-permute-done.2.refs_1_, ...), custom_call_target="tpu_custom_call" | custom-call | flops 1000000 | bytes 500000 | tf_op jit(solution)/shard_map/merge_matrices/pallas_call | solution.py:39
  107.8 1.4 %correct.5.refs_1_ = f32[80,24,128]{2,1,0:T(8,128)S(1)} custom-call(s32[6]{0:T(128)S(1)} %stack.31.flags, f32[2,30,8,128]{3,2,1,0:T(8,128)S(1)} %get-tuple-element.48.mats, f32[10,24,128]{2,1,0:T(8,128)S(1)} %get-tuple-element.78.flows, f32[10,24,128]{2,1,0:T(8,128)S(1)} %collective-permute-done.21.other, f32[10,24,128]{2,1,0:T(8,128)S(1)} %get-tuple-element.79.inflow_in, ...), custom_call_target="tpu_custom_call" | custom-call | flops 1000000 | bytes 4000000 | tf_op jit(solution)/shard_map/correct/pallas_call | solution.py:39
  109.2 0.3 collective-permute-done.17.other
  109.5 1.4 %correct.4.refs_0_ = f32[80,24,128]{2,1,0:T(8,128)S(1)} custom-call(s32[6]{0:T(128)S(1)} %stack.31.flags, f32[2,30,8,128]{3,2,1,0:T(8,128)S(1)} %get-tuple-element.48.mats, f32[10,24,128]{2,1,0:T(8,128)S(1)} %get-tuple-element.71.flows, f32[10,24,128]{2,1,0:T(8,128)S(1)} %collective-permute-done.17.other, f32[10,24,128]{2,1,0:T(8,128)S(1)} %get-tuple-element.72.inflow_in, ...), custom_call_target="tpu_custom_call" | custom-call | flops 1000000 | bytes 4000000 | tf_op jit(solution)/shard_map/correct/pallas_call | solution.py:39
  111.0 2.6 %correct.3.near = f32[80,56,128]{2,1,0:T(8,128)S(1)} custom-call(s32[6]{0:T(128)S(1)} %stack.31.flags, f32[2,30,8,128]{3,2,1,0:T(8,128)S(1)} %get-tuple-element.48.mats, f32[10,56,128]{2,1,0:T(8,128)S(1)} %get-tuple-element.64.flows, f32[10,56,128]{2,1,0:T(8,128)S(1)} %collective-permute-done.13.other, f32[10,56,128]{2,1,0:T(8,128)S(1)} %get-tuple-element.65.inflow_in, ...), custom_call_target="tpu_custom_call" | custom-call | flops 1000000 | bytes 4000000 | tf_op jit(solution)/shard_map/correct/pallas_call | solution.py:39
  113.6 3.3 %finish.1 = f32[7840,128]{1,0:T(8,128)} custom-call(s32[6]{0:T(128)S(1)} %stack.31.flags, f32[2,30,8,128]{3,2,1,0:T(8,128)S(1)} %get-tuple-element.48.mats, f32[10,8,128]{2,1,0:T(8,128)S(1)} %get-tuple-element.57.flows, f32[10,8,128]{2,1,0:T(8,128)S(1)} %collective-permute-done.9.other, f32[10,8,128]{2,1,0:T(8,128)S(1)} %get-tuple-element.58.inflow_in, ...), custom_call_target="tpu_custom_call" | custom-call | tf_op jit(solution)/shard_map/finish/pallas_call | solution.py:609
  (45 shorter events, 0.6 us)
Async XLA Ops:
  6.6 2.1 %copy-start.4 = (f32[16,2,5,49,128]{4,1,3,2,0:T(2,128)S(1)}, f32[16,2,5,49,128]{4,1,3,2,0:T(2,128)}, u32[]{:S(2)}) copy-start(f32[16,2,5,49,128]{4,1,3,2,0:T(2,128)} %param.12) | copy-start | bytes 12042244
  11.8 1.4 %copy-start.2 = (f32[80,56,128]{2,1,0:T(8,128)}, f32[80,56,128]{2,1,0:T(8,128)S(1)}, u32[]{:S(2)}) copy-start(f32[80,56,128]{2,1,0:T(8,128)S(1)} %get-tuple-element.52.xf) | copy-start | bytes 6881284
  13.2 0.8 copy-start.8
  14.0 1.3 %copy-start.9 = (f32[480,128]{1,0:T(8,128)}, f32[480,128]{1,0:T(8,128)S(1)}, u32[]{:S(2)}) copy-start(f32[480,128]{1,0:T(8,128)S(1)} %get-tuple-element.53) | copy-start | bytes 737284
  14.0 8.4 %copy-start.7 = (f32[1440,128]{1,0:T(8,128)}, f32[1440,128]{1,0:T(8,128)S(1)}, u32[]{:S(2)}) copy-start(f32[1440,128]{1,0:T(8,128)S(1)} %get-tuple-element.67) | copy-start | bytes 2211844
  14.0 18.4 %collective-permute-start.10 = (f32[80,56,128]{2,1,0:T(8,128)S(1)}, f32[80,56,128]{2,1,0:T(8,128)}, u32[]{:S(2)}, u32[]{:S(2)}) collective-permute-start(f32[80,56,128]{2,1,0:T(8,128)S(1)} %get-tuple-element.51.xn), channel_id=1, source_target_pairs={{0,1},{1,0},{2,3},{3,2},{4,5},{5,4},{6,7},{7,6},{8,9},{9,8},{10,11... | collective-permute-start | bytes 6881288 | tf_op jit(solution)/shard_map/ppermute | solution.py:541
  15.3 13.9 %collective-permute-start.4 = (f32[496,128]{1,0:T(8,128)}, f32[496,128]{1,0:T(8,128)S(1)}, u32[]{:S(2)}, u32[]{:S(2)}) collective-permute-start(f32[496,128]{1,0:T(8,128)} %get-tuple-element.81), channel_id=1, source_target_pairs={{4,0},{8,4},{12,8},{16,12},{20,16},{24,20},{28,24},{5,1},{9,5},{13... | collective-permute-start | bytes 761864 | tf_op jit(solution)/shard_map/ppermute | solution.py:524
  16.6 15.8 %collective-permute-start.3 = (f32[496,128]{1,0:T(8,128)}, f32[496,128]{1,0:T(8,128)}, u32[]{:S(2)}, u32[]{:S(2)}) collective-permute-start(f32[496,128]{1,0:T(8,128)} %get-tuple-element.82), channel_id=1, source_target_pairs={{0,4},{4,8},{8,12},{12,16},{16,20},{20,24},{24,28},{1,5},{5,9},{9,... | collective-permute-start | bytes 761864 | tf_op jit(solution)/shard_map/ppermute | solution.py:523
  22.4 10.0 %copy-start = (f32[16,2,5,5,128]{4,1,3,2,0:T(2,128)S(1)}, f32[16,2,5,5,128]{4,1,3,2,0:T(2,128)}, u32[]{:S(2)}) copy-start(f32[16,2,5,5,128]{4,1,3,2,0:T(2,128)} %param.16) | copy-start | bytes 1228804
  22.4 10.0 %copy-start.1 = (f32[16,2,5,5,128]{4,1,3,2,0:T(2,128)S(1)}, f32[16,2,5,5,128]{4,1,3,2,0:T(2,128)}, u32[]{:S(2)}) copy-start(f32[16,2,5,5,128]{4,1,3,2,0:T(2,128)} %param.17) | copy-start | bytes 1228804
  22.4 10.0 %copy-start.5 = (f32[16,2,5,128]{3,1,2,0:T(2,128)S(1)}, f32[16,2,5,128]{3,1,2,0:T(2,128)}, u32[]{:S(2)}) copy-start(f32[16,2,5,128]{3,1,2,0:T(2,128)} %param.14) | copy-start | bytes 245764
  22.4 10.0 %copy-start.6 = (f32[16,2,5,128]{3,1,2,0:T(2,128)S(1)}, f32[16,2,5,128]{3,1,2,0:T(2,128)}, u32[]{:S(2)}) copy-start(f32[16,2,5,128]{3,1,2,0:T(2,128)} %param.13) | copy-start | bytes 245764
  24.7 7.7 %copy-start.3 = (f32[80,56,128]{2,1,0:T(8,128)S(1)}, f32[80,56,128]{2,1,0:T(8,128)}, u32[]{:S(2)}) copy-start(f32[80,56,128]{2,1,0:T(8,128)} %copy-done.2) | copy-start | bytes 6881284
  26.6 30.9 %collective-permute-start.5 = (f32[980,128]{1,0:T(8,128)S(1)}, f32[980,128]{1,0:T(8,128)S(1)}, u32[]{:S(2)}, u32[]{:S(2)}) collective-permute-start(f32[980,128]{1,0:T(8,128)S(1)} %bitcast.63), channel_id=1, source_target_pairs={{0,3},{1,2},{2,1},{3,0},{4,7},{5,6},{6,5},{7,4},{8,11},{9,10},{10,... | collective-permute-start | bytes 1505288 | tf_op jit(solution)/shard_map/ppermute | solution.py:507
  28.2 44.4 %collective-permute-start.14 = (f32[1440,128]{1,0:T(8,128)}, f32[1440,128]{1,0:T(8,128)S(1)}, u32[]{:S(2)}, u32[]{:S(2)}) collective-permute-start(f32[1440,128]{1,0:T(8,128)} %copy-done.7), channel_id=1, source_target_pairs={{0,3},{1,2},{2,1},{3,0},{4,7},{5,6},{6,5},{7,4},{8,11},{9,10},{10,... | collective-permute-start | bytes 2211848 | tf_op jit(solution)/shard_map/ppermute | solution.py:507
  29.2 38.0 %collective-permute-start.18 = (f32[1024,128]{1,0:T(8,128)}, f32[1024,128]{1,0:T(8,128)S(1)}, u32[]{:S(2)}, u32[]{:S(2)}) collective-permute-start(f32[1024,128]{1,0:T(8,128)} %copy-done.8), channel_id=1, source_target_pairs={{0,3},{1,2},{2,1},{3,0},{4,7},{5,6},{6,5},{7,4},{8,11},{9,10},{10,... | collective-permute-start | bytes 1572872 | tf_op jit(solution)/shard_map/ppermute | solution.py:507
  32.4 24.9 %copy-start.11 = (f32[49,49]{1,0:T(8,128)S(1)}, f32[49,49]{1,0:T(8,128)}, u32[]{:S(2)}) copy-start(f32[49,49]{1,0:T(8,128)} %get-tuple-element.83) | copy-start | bytes 28816
  39.9 12.9 %collective-permute-start.11 = (f32[10,56,128]{2,1,0:T(8,128)S(1)}, f32[10,56,128]{2,1,0:T(8,128)S(1)}, u32[]{:S(2)}, u32[]{:S(2)}) collective-permute-start(f32[10,56,128]{2,1,0:T(8,128)S(1)} %get-tuple-element.61.flows), channel_id=1, source_target_pairs={{0,4},{4,0},{8,12},{12,8},{16,20},{20,16},{24,28},{28,24},{1,5},{5... | collective-permute-start | bytes 860168 | tf_op jit(solution)/shard_map/ppermute | solution.py:508
  44.0 8.1 %collective-permute-start = (f32[2,15,8,128]{3,2,1,0:T(8,128)S(1)}, f32[2,15,8,128]{3,2,1,0:T(8,128)S(1)}, u32[]{:S(2)}, u32[]{:S(2)}) collective-permute-start(f32[2,15,8,128]{3,2,1,0:T(8,128)S(1)} %get-tuple-element.43.refs_0_), channel_id=1, source_target_pairs={{0,4},{4,0},{8,12},{12,8},{16,20},{20,16},{24,28},{28,24},{1,5},{5... | collective-permute-start | bytes 368648 | tf_op jit(solution)/shard_map/ppermute | solution.py:508
  53.7 22.0 %collective-permute-start.12 = (f32[10,56,128]{2,1,0:T(8,128)S(1)}, f32[10,56,128]{2,1,0:T(8,128)S(1)}, u32[]{:S(2)}, u32[]{:S(2)}) collective-permute-start(f32[10,56,128]{2,1,0:T(8,128)S(1)} %get-tuple-element.62.flows), channel_id=1, source_target_pairs={{0,8},{4,12},{8,0},{12,4},{16,24},{20,28},{24,16},{28,20},{1,9},{5... | collective-permute-start | bytes 860168 | tf_op jit(solution)/shard_map/ppermute | solution.py:508
  57.3 17.6 %collective-permute-start.1 = (f32[2,15,8,128]{3,2,1,0:T(8,128)S(1)}, f32[2,15,8,128]{3,2,1,0:T(8,128)S(1)}, u32[]{:S(2)}, u32[]{:S(2)}) collective-permute-start(f32[2,15,8,128]{3,2,1,0:T(8,128)S(1)} %get-tuple-element.44.refs_0_), channel_id=1, source_target_pairs={{0,8},{4,12},{8,0},{12,4},{16,24},{20,28},{24,16},{28,20},{1,9},{5... | collective-permute-start | bytes 368648 | tf_op jit(solution)/shard_map/ppermute | solution.py:508
  61.7 9.9 %copy-start.10 = (f32[480,128]{1,0:T(8,128)S(1)}, f32[480,128]{1,0:T(8,128)}, u32[]{:S(2)}) copy-start(f32[480,128]{1,0:T(8,128)} %copy-done.9) | copy-start | bytes 737284
  69.1 10.2 %collective-permute-start.19 = (f32[10,24,128]{2,1,0:T(8,128)S(1)}, f32[10,24,128]{2,1,0:T(8,128)S(1)}, u32[]{:S(2)}, u32[]{:S(2)}) collective-permute-start(f32[10,24,128]{2,1,0:T(8,128)S(1)} %get-tuple-element.75.flows), channel_id=1, source_target_pairs={{0,4},{4,0},{8,12},{12,8},{16,20},{20,16},{24,28},{28,24},{1,5},{5... | collective-permute-start | bytes 368648 | tf_op jit(solution)/shard_map/ppermute | solution.py:508
  71.6 12.3 %collective-permute-start.6 = (f32[480,128]{1,0:T(8,128)S(1)}, f32[480,128]{1,0:T(8,128)S(1)}, u32[]{:S(2)}, u32[]{:S(2)}) collective-permute-start(f32[480,128]{1,0:T(8,128)S(1)} %copy-done.10), channel_id=1, source_target_pairs={{0,3},{1,2},{2,1},{3,0},{4,7},{5,6},{6,5},{7,4},{8,11},{9,10},{10,... | collective-permute-start | bytes 737288 | tf_op jit(solution)/shard_map/ppermute | solution.py:507
  74.5 6.3 %collective-permute-start.15 = (f32[10,24,128]{2,1,0:T(8,128)S(1)}, f32[10,24,128]{2,1,0:T(8,128)S(1)}, u32[]{:S(2)}, u32[]{:S(2)}) collective-permute-start(f32[10,24,128]{2,1,0:T(8,128)S(1)} %get-tuple-element.68.flows), channel_id=1, source_target_pairs={{0,4},{4,0},{8,12},{12,8},{16,20},{20,16},{24,28},{28,24},{1,5},{5... | collective-permute-start | bytes 368648 | tf_op jit(solution)/shard_map/ppermute | solution.py:508
  76.6 34.4 %collective-permute-start.13 = (f32[10,56,128]{2,1,0:T(8,128)S(1)}, f32[10,56,128]{2,1,0:T(8,128)S(1)}, u32[]{:S(2)}, u32[]{:S(2)}) collective-permute-start(f32[10,56,128]{2,1,0:T(8,128)S(1)} %get-tuple-element.64.flows), channel_id=1, source_target_pairs={{0,16},{4,20},{8,24},{12,28},{16,0},{20,4},{24,8},{28,12},{1,17},{... | collective-permute-start | bytes 860168 | tf_op jit(solution)/shard_map/ppermute | solution.py:508
  79.9 9.1 %collective-permute-start.20 = (f32[10,24,128]{2,1,0:T(8,128)S(1)}, f32[10,24,128]{2,1,0:T(8,128)S(1)}, u32[]{:S(2)}, u32[]{:S(2)}) collective-permute-start(f32[10,24,128]{2,1,0:T(8,128)S(1)} %get-tuple-element.76.flows), channel_id=1, source_target_pairs={{0,8},{4,12},{8,0},{12,4},{16,24},{20,28},{24,16},{28,20},{1,9},{5... | collective-permute-start | bytes 368648 | tf_op jit(solution)/shard_map/ppermute | solution.py:508
  81.5 11.1 %collective-permute-start.16 = (f32[10,24,128]{2,1,0:T(8,128)S(1)}, f32[10,24,128]{2,1,0:T(8,128)S(1)}, u32[]{:S(2)}, u32[]{:S(2)}) collective-permute-start(f32[10,24,128]{2,1,0:T(8,128)S(1)} %get-tuple-element.69.flows), channel_id=1, source_target_pairs={{0,8},{4,12},{8,0},{12,4},{16,24},{20,28},{24,16},{28,20},{1,9},{5... | collective-permute-start | bytes 368648 | tf_op jit(solution)/shard_map/ppermute | solution.py:508
  82.8 23.6 %collective-permute-start.2 = (f32[2,15,8,128]{3,2,1,0:T(8,128)S(1)}, f32[2,15,8,128]{3,2,1,0:T(8,128)S(1)}, u32[]{:S(2)}, u32[]{:S(2)}) collective-permute-start(f32[2,15,8,128]{3,2,1,0:T(8,128)S(1)} %get-tuple-element.46.refs_0_), channel_id=1, source_target_pairs={{0,16},{4,20},{8,24},{12,28},{16,0},{20,4},{24,8},{28,12},{1,17},{... | collective-permute-start | bytes 368648 | tf_op jit(solution)/shard_map/ppermute | solution.py:508
  89.8 18.0 %collective-permute-start.21 = (f32[10,24,128]{2,1,0:T(8,128)S(1)}, f32[10,24,128]{2,1,0:T(8,128)S(1)}, u32[]{:S(2)}, u32[]{:S(2)}) collective-permute-start(f32[10,24,128]{2,1,0:T(8,128)S(1)} %get-tuple-element.78.flows), channel_id=1, source_target_pairs={{0,16},{4,20},{8,24},{12,28},{16,0},{20,4},{24,8},{28,12},{1,17},{... | collective-permute-start | bytes 368648 | tf_op jit(solution)/shard_map/ppermute | solution.py:508
  93.3 16.2 %collective-permute-start.17 = (f32[10,24,128]{2,1,0:T(8,128)S(1)}, f32[10,24,128]{2,1,0:T(8,128)S(1)}, u32[]{:S(2)}, u32[]{:S(2)}) collective-permute-start(f32[10,24,128]{2,1,0:T(8,128)S(1)} %get-tuple-element.71.flows), channel_id=1, source_target_pairs={{0,16},{4,20},{8,24},{12,28},{16,0},{20,4},{24,8},{28,12},{1,17},{... | collective-permute-start | bytes 368648 | tf_op jit(solution)/shard_map/ppermute | solution.py:508
  94.8 4.0 %collective-permute-start.7 = (f32[10,8,128]{2,1,0:T(8,128)S(1)}, f32[10,8,128]{2,1,0:T(8,128)S(1)}, u32[]{:S(2)}, u32[]{:S(2)}) collective-permute-start(f32[10,8,128]{2,1,0:T(8,128)S(1)} %get-tuple-element.54.flows), channel_id=1, source_target_pairs={{0,4},{4,0},{8,12},{12,8},{16,20},{20,16},{24,28},{28,24},{1,5},{5... | collective-permute-start | bytes 122888 | tf_op jit(solution)/shard_map/ppermute | solution.py:508
  99.4 6.3 %collective-permute-start.8 = (f32[10,8,128]{2,1,0:T(8,128)S(1)}, f32[10,8,128]{2,1,0:T(8,128)S(1)}, u32[]{:S(2)}, u32[]{:S(2)}) collective-permute-start(f32[10,8,128]{2,1,0:T(8,128)S(1)} %get-tuple-element.55.flows), channel_id=1, source_target_pairs={{0,8},{4,12},{8,0},{12,4},{16,24},{20,28},{24,16},{28,20},{1,9},{5... | collective-permute-start | bytes 122888 | tf_op jit(solution)/shard_map/ppermute | solution.py:508
  106.4 7.3 %collective-permute-start.9 = (f32[10,8,128]{2,1,0:T(8,128)S(1)}, f32[10,8,128]{2,1,0:T(8,128)S(1)}, u32[]{:S(2)}, u32[]{:S(2)}) collective-permute-start(f32[10,8,128]{2,1,0:T(8,128)S(1)} %get-tuple-element.57.flows), channel_id=1, source_target_pairs={{0,16},{4,20},{8,24},{12,28},{16,0},{20,4},{24,8},{28,12},{1,17},{... | collective-permute-start | bytes 122888 | tf_op jit(solution)/shard_map/ppermute | solution.py:508
where the time goes:
time: 117 us
  Pallas kernels  38.6 us (33%)
  starting transfers between devices  34.2 us (29%)
  waiting for transfers between devices  26 us (22%)
  local copies, waits for them, and re-layouts  10.9 us (9%)
  other arithmetic  3.39 us (3%)
  matrix products  2.19 us (2%)
  between operations  1.67 us (1%)
    pallas_call x21, Pallas kernels, run(): pl.pallas_call(body, out_shape=[jax.ShapeDtypeStruct(s, F32) for s in out...  35.3 us
    ppermute x15, starting transfers between devices, local(): lax.ppermute(x, 'seg', [(i, i ^ 1 << k) for i in range(segs)])  22.2 us
    ppermute x15, waiting for transfers between devices, local(): lax.ppermute(x, 'seg', [(i, i ^ 1 << k) for i in range(segs)])  20.1 us
    ppermute x1, starting transfers between devices, local(): lax.ppermute(st[-edge_rows:], 'seg', [(i, i + 1) for i in range(segs - 1)])  5.81 us
    ppermute x4, waiting for transfers between devices, local(): to_far = lambda x: lax.ppermute(x, 'pitch', far_pairs)  5.39 us
    unnamed x25, local copies, waits for them, and re-layouts  4.38 us
    ppermute x4, starting transfers between devices, local(): to_far = lambda x: lax.ppermute(x, 'pitch', far_pairs)  4.37 us
    pallas_call x1, Pallas kernels, local(): pl.pallas_call(functools.partial(finish, levels - 1), grid=(steps,), out_...  3.25 us
  transfers between devices with their start and end apart: 22, of which 8 were waited for; matrix products, arithmetic and copies ran while one was open for 6% of the time, Pallas kernels for 28%

commit v1 on v0

v1 whole, which is shorter than its diff:
```python
import functools
import math

import jax
import jax.numpy as jnp
import numpy as np
from jax import lax
from jax.experimental import pallas as pl
from jax.experimental.pallas import tpu as pltpu
from jax.sharding import PartitionSpec as P

F32 = jnp.float32
BF16 = jnp.bfloat16
V = 5
NT = 49
PAD = 56
DEPTH = 64
LANES = 128
LEAD = 4
MB = 1 << 20

CHUNKS = (((0, 24), False), ((24, 40), True), ((40, 48), False))


def rows_of(chunk):
    (first, last), extra = chunk
    return last - first + (8 if extra else 0)


def padded_even(count):
    return (count + 7) // 8 * 8


class Chain:
    def __init__(self, flags):
        self.flags = flags

    def after(self, array):
        self.flags, array = lax.optimization_barrier((self.flags, array))
        return array

    def __call__(self, body, out_shapes, arrays, scratch=(), vmem=24, name=None, grid=None, in_specs=None, out_specs=None):
        smem = pl.BlockSpec(memory_space=pltpu.SMEM)
        held = pl.BlockSpec(memory_space=pltpu.VMEM)
        extra = {} if grid is None else {"grid": grid}
        out = pl.pallas_call(
            body,
            out_shape=[jax.ShapeDtypeStruct(s, F32) for s in out_shapes],
            in_specs=[smem] + (in_specs or [held] * len(arrays)),
            out_specs=out_specs or [held] * len(out_shapes),
            scratch_shapes=list(scratch),
            compiler_params=pltpu.CompilerParams(vmem_limit_bytes=vmem * MB),
            cost_estimate=pl.CostEstimate(flops=1000, bytes_accessed=1000, transcendentals=0),
            name=name,
            **extra,
        )(self.flags, *arrays)
        out = list(out)
        out[0] = self.after(out[0])
        return out


def coefficient(ref, z, a, b, p):
    return ref[pl.ds(((z * V + a) * V + b) * 2 + p, 1), :]


def split_left(matrix):
    high = matrix.astype(BF16).astype(F32)
    place = lax.broadcasted_iota(jnp.int32, matrix.shape, 1)
    return jnp.where(place < 2 * DEPTH, high, matrix - high).astype(BF16)


def lag_matrix(basis, turned, trig, sign):
    half = turned.shape[0] // 2
    count = (half - 4) // 8 * 8
    cosine, sine = turned[:half], turned[half:]
    turn, cross = trig[:count, :1], trig[count : 2 * count, :1] * sign
    right = jnp.concatenate(
        [
            turn * cosine[:count] + cross * sine[:count],
            turn * sine[:count] - cross * cosine[:count],
            cosine[count:],
        ],
        axis=0,
    )
    return jnp.dot(basis, right, preferred_element_type=F32, precision=lax.Precision.HIGHEST)


def over_instants(left, cells):
    whole = jnp.concatenate(cells, axis=1)
    if whole.shape[0] < DEPTH:
        whole = jnp.concatenate(
            [whole, jnp.zeros((DEPTH - whole.shape[0], whole.shape[1]), F32)], axis=0
        )
    high = whole.astype(BF16)
    low = (whole - high.astype(F32)).astype(BF16)
    product = jnp.dot(
        left, jnp.concatenate([high, low, high], axis=0), preferred_element_type=F32
    )
    return [product[:, i * LANES : (i + 1) * LANES] for i in range(len(cells))]


def lead_cells(flags, st, slab):
    p = flags[0]
    width = 4 * NT

    def step(i, carry):
        slab[pl.ds(i * width, width), :] = st[pl.ds(i * 2 * width + p, width, stride=2), :]
        return carry

    lax.fori_loop(0, LEAD * V // 4, step, 0)


def prepare(flags, st, trig, basis, turned, xn, xf, first_cell, last_cell, *chunks):
    p = flags[0]
    wrap = flags[1]
    cells = xn.shape[0] // V
    sign = jnp.where(flags[2] == 1, 1.0, -1.0)
    left = split_left(lag_matrix(basis[...], turned[...], trig[...], sign))
    zeros = jnp.zeros((8, LANES), F32)

    def separate(z):
        for v in range(V):
            j = z * V + v
            for out, q in ((xn, 1 - p), (xf, p)):
                out[j, PAD - 8 : PAD, :] = zeros
                out[j, 0:NT, :] = st[pl.ds(j * 2 * NT + q, NT, stride=2), :]

    def lead(z, carry):
        separate(z)
        return carry

    lax.fori_loop(0, LEAD, lead, 0)

    def rest(z, carry):
        separate(z)
        raw = [xf[z * V + v] for v in range(V)]
        lagged = over_instants(left, raw)
        for v in range(V):
            value = jnp.where(wrap == 1, lagged[v], raw[v])
            j = (z - LEAD) * V + v
            for out, ((first, last), extra) in zip(chunks, CHUNKS):
                width = last - first
                out[pl.ds(pl.multiple_of(j * width, 8), width), :] = value[first:last]
                if extra:
                    out[pl.ds((cells - LEAD) * V * width + j, 1), :] = value[NT - 1 : NT]
        return carry

    lax.fori_loop(LEAD, cells, rest, 0)
    for v in range(V):
        first_cell[v] = xn[v]
        first_cell[V + v] = xf[v]
        last_cell[v] = xn[(cells - 1) * V + v]
        last_cell[V + v] = xf[(cells - 1) * V + v]


def keep_tiles(ref, kind, values, first, last, height):
    for a in range(V):
        for t in range(first // 8, last // 8):
            ref[(kind + a) * height + t] = values[a][t * 8 - first : t * 8 - first + 8]


def sweeps(source, g, fg, spans, p, inverse, lower, upper, cells):
    height = g.shape[1] // 8
    for first, last in spans:
        nothing = tuple(jnp.zeros((last - first, LANES), F32) for _ in range(V))

        def ahead(z, current, first=first, last=last):
            right = source(z, first, last)
            result = []
            for a in range(V):
                total = coefficient(inverse, z, a, 0, p) * right[0]
                for b in range(1, V):
                    total += coefficient(inverse, z, a, b, p) * right[b]
                for b in range(V):
                    total += coefficient(lower, z, a, b, p) * current[b]
                g[z * V + a, first:last, :] = total
                result.append(total)
            return tuple(result)

        out = lax.fori_loop(0, cells, ahead, nothing)
        keep_tiles(fg, 0, out, first, last, height)

        def back(i, current, first=first, last=last):
            z = cells - 1 - i
            result = []
            for a in range(V):
                total = g[z * V + a, first:last, :]
                for b in range(V):
                    total += coefficient(upper, z, a, b, p) * current[b]
                g[z * V + a, first:last, :] = total
                result.append(total)
            return tuple(result)

        out = lax.fori_loop(0, cells, back, nothing)
        keep_tiles(fg, V, out, first, last, height)


def residuals(x, other, halo, from_left, from_right, edge, advect, viscous, left, p, cells, put):
    def one(z, above, below):
        here = [x[z * V + v] for v in range(V)]
        timing = over_instants(left, here)
        for v in range(V):
            j = z * V + v
            pitch = other[j] - 2.0 * here[v]
            if halo is not None:
                pitch += halo[j]
            put(
                j,
                advect[pl.ds(j * 2 + p, 1), :] * (above(z, v) - below(z, v))
                + viscous[pl.ds(j * 2 + p, 1), :] * pitch
                - timing[v],
            )

    inner_above = lambda z, v: x[(z - 1) * V + v]
    inner_below = lambda z, v: x[(z + 1) * V + v]
    one(0, lambda z, v: from_left[edge + v], inner_below)

    def step(z, carry):
        one(z, inner_above, inner_below)
        return carry

    lax.fori_loop(1, cells - 1, step, 0)
    one(cells - 1, inner_above, lambda z, v: from_right[edge + v])


def timing_matrix(table, trig):
    return split_left(table[...] * trig[trig.shape[0] - 8 : trig.shape[0] - 7, :1])


def near_cell(
    flags, xn, xf, halo, from_left, from_right, advect, viscous, inverse, lower, upper, trig, table,
    group, g, flows, right,
):
    p = 1 - flags[0]
    cells = xn.shape[0] // V

    def put(j, value):
        right[j] = value

    residuals(xn, xf, halo, from_left, from_right, 0, advect, viscous, timing_matrix(table, trig), p, cells, put)
    source = lambda z, first, last: [right[z * V + v, first:last, :] for v in range(V)]
    sweeps(source, g, flows, ((0, 32), (32, PAD)), p, inverse, lower, upper, cells)
    for c in range(2):
        for i in range(3 * V):
            flows[NEAR_TILES + c * 3 * V + i] = group[c, i]


def far_base(
    flags, xn, xf, from_left, from_right, slab, advect, viscous, trig, table, basis, turned, base, halo
):
    p = flags[0]
    wrap = flags[1]
    cells = xn.shape[0] // V

    def put(j, value):
        base[j] = value

    residuals(xf, xn, None, from_left, from_right, V, advect, viscous, timing_matrix(table, trig), p, cells, put)
    sign = jnp.where(flags[2] == 1, -1.0, 1.0)
    left = split_left(lag_matrix(basis[...], turned[...], trig[...], sign))
    for z in range(LEAD):
        for v in range(V):
            halo[v, PAD - 8 : PAD, :] = jnp.zeros((8, LANES), F32)
            halo[v, 0:NT, :] = slab[pl.ds((z * V + v) * NT, NT), :]
        raw = [halo[v] for v in range(V)]
        lagged = over_instants(left, raw)
        for v in range(V):
            j = z * V + v
            value = jnp.where(wrap == 1, lagged[v], raw[v])
            base[j] += viscous[pl.ds(j * 2 + p, 1), :] * value


def far_chunk(chunk, flags, base, halo, viscous, inverse, lower, upper, g, fg):
    (first, last), extra = chunk
    width = last - first
    p = flags[0]
    cells = base.shape[0] // V
    top = lax.broadcasted_iota(jnp.int32, (8, LANES), 0) == 0

    def source(z, start, stop):
        result = []
        for v in range(V):
            j = z * V + v
            value = base[j, first:last, :]
            if extra:
                value = jnp.concatenate([value, base[j, PAD - 8 : PAD, :]], axis=0)
            h = jnp.maximum(z - LEAD, 0) * V + v
            arrived = halo[pl.ds(pl.multiple_of(h * width, 8), width), :]
            if extra:
                row = halo[pl.ds((cells - LEAD) * V * width + h, 1), :]
                arrived = jnp.concatenate([arrived, jnp.where(top, row, 0.0)], axis=0)
            scale = jnp.where(z >= LEAD, viscous[pl.ds(j * 2 + p, 1), :], 0.0)
            result.append(value + scale * arrived)
        return result

    rows = rows_of(chunk)
    sweeps(source, g, fg, ((0, rows),), p, inverse, lower, upper, cells)


def times(matrix, vector):
    result = []
    for a in range(V):
        total = matrix(a, 0) * vector[0]
        for b in range(1, V):
            total += matrix(a, b) * vector[b]
        result.append(total)
    return result


def plus(one, two):
    return [a + b for a, b in zip(one, two)]


def tiles(ref, c, kind):
    return [ref[c, kind * V + a] for a in range(V)]


def rows(ref, c, kind):
    return lambda a, b: ref[c, kind * V + a, b : b + 1, :]


def unit(a):
    place = lax.broadcasted_iota(jnp.int32, (8, LANES), 0)
    return jnp.where(place == a, 1.0, 0.0).astype(F32)


def transfer(flags, lower, upper, blocks, group, forward):
    cells = blocks.shape[1] // V
    for c in range(2):
        p = 1 - flags[0] if c == 0 else flags[0]

        def ahead(z, current):
            result = times(lambda a, b: coefficient(lower, z, a, b, p), current)
            for a in range(V):
                forward[z * V + a] = result[a]
            return tuple(result)

        through = lax.fori_loop(0, cells, ahead, tuple(unit(a) for a in range(V)))

        def back(i, current):
            z = cells - 1 - i
            result = times(lambda a, b: coefficient(upper, z, a, b, p), current)
            for a in range(V):
                result[a] = result[a] + jnp.concatenate(
                    [forward[z * V + a], jnp.zeros((8, LANES), F32)], axis=0
                )
                blocks[c, z * V + a] = result[a]
            return tuple(result)

        start = tuple(
            jnp.concatenate([jnp.zeros((8, LANES), F32), unit(a)], axis=0) for a in range(V)
        )
        ends = lax.fori_loop(0, cells, back, start)
        for a in range(V):
            group[c, a] = ends[a][:8]
            group[c, V + a] = ends[a][8:]
            group[c, 2 * V + a] = through[a]


def own_share(share, c):
    if share is None:
        nothing = [jnp.zeros((8, LANES), F32)] * V
        return [[unit(a) for a in range(V)], nothing, [unit(a) for a in range(V)]]
    return [tiles(share, c, kind) for kind in range(3)]


def merge_matrices(right, last_right, mine, other, share, mats, merged, share_out, last):
    for c in range(2):
        group = lambda ref, kind: [ref[NEAR_TILES + (c * 3 + kind) * V + a] for a in range(V)]
        pick = lambda kind, own: [jnp.where(own, m, t) for m, t in zip(group(mine, kind), group(other, kind))]
        left = jnp.logical_not(right)
        own = own_share(share, c)
        nothing = jnp.zeros((8, LANES), F32)
        for kind, values in (
            (0, pick(2, right)),
            (1, pick(0, right)),
            (2, pick(1, left)),
            (3, [jnp.where(right, x, nothing) for x in own[0]]),
            (4, [jnp.where(right, x, nothing) for x in own[1]]),
            (5, [jnp.where(right, nothing, x) for x in own[2]]),
        ):
            for a in range(V):
                mats[c, kind * V + a] = values[a]
        p_left, g_left, h_right = pick(2, left), pick(0, left), pick(1, right)
        turned = times(rows(mats, c, 1), p_left)
        new_g = plus(g_left, times(rows(mats, c, 2), turned))
        if last:
            for a in range(V):
                merged[NEAR_TILES // 2 + c * V + a] = new_g[a]
        else:
            new_h = times(rows(mats, c, 2), h_right)
            new_p = times(rows(mats, c, 0), p_left)
            for a in range(V):
                merged[NEAR_TILES + c * 3 * V + a] = new_g[a]
                merged[NEAR_TILES + (c * 3 + 1) * V + a] = new_h[a]
                merged[NEAR_TILES + (c * 3 + 2) * V + a] = new_p[a]
        s0 = times(rows(mats, c, 3), p_left)
        s1 = times(rows(mats, c, 4), p_left)
        s1b = times(rows(mats, c, 5), turned)
        s2 = times(rows(mats, c, 5), h_right)
        for a in range(V):
            share_out[c, a] = jnp.where(right, s0[a], own[0][a])
            share_out[c, V + a] = jnp.where(right, s1[a], own[1][a] + s1b[a])
            share_out[c, 2 * V + a] = jnp.where(right, own[2][a], s2[a])


def last_matrices(right, mine, other, share, mats):
    nothing = jnp.zeros((8, LANES), F32)
    for c in range(2):
        for a in range(V):
            i = NEAR_TILES // 2 + c * V + a
            mats[c, V + a] = jnp.where(right, mine[i], other[i])
            mats[c, 3 * V + a] = jnp.where(right, share[c, a], nothing)
            mats[c, 4 * V + a] = jnp.where(right, share[c, V + a], nothing)
            mats[c, 5 * V + a] = jnp.where(right, nothing, share[c, 2 * V + a])


def inflow_of(c, mats, f_left, g_right, known):
    back = plus(g_right, times(rows(mats, c, 1), f_left))
    from_left = times(rows(mats, c, 3), f_left)
    from_right = plus(times(rows(mats, c, 4), f_left), times(rows(mats, c, 5), back))
    total = from_left + from_right
    return back, total if known is None else plus(known, total)


def merge_flows(right, last_right, c, mats, flows, other, known, merged, inflow, height, last):
    def tile(t, carry):
        mine = [flows[i * height + t] for i in range(2 * V)]
        theirs = [other[i * height + t] for i in range(2 * V)]
        f_left = [jnp.where(right, y, x) for x, y in zip(mine[:V], theirs[:V])]
        f_right = [jnp.where(right, x, y) for x, y in zip(mine[:V], theirs[:V])]
        g_left = [jnp.where(right, y, x) for x, y in zip(mine[V:], theirs[V:])]
        g_right = [jnp.where(right, x, y) for x, y in zip(mine[V:], theirs[V:])]
        before = None if known is None else [known[i * height + t] for i in range(2 * V)]
        back, total = inflow_of(c, mats, f_left, g_right, before)
        new_f = plus(f_right, times(rows(mats, c, 0), f_left))
        new_g = plus(g_left, times(rows(mats, c, 2), back))
        if last:
            ends = [jnp.where(last_right, y, x) for x, y in zip(new_f, new_g)]
        else:
            ends = new_f + new_g
        for i, value in enumerate(ends):
            merged[i * height + t] = value
        for i, value in enumerate(total):
            inflow[i * height + t] = value
        return carry

    lax.fori_loop(0, height, tile, 0)


def merge_near(bit, levels, flags, *refs):
    start, last = bit == 0, bit == levels - 2
    if start:
        flows, other, mats, merged, share_out, inflow = refs
        share = known = None
    else:
        flows, other, share, known, mats, merged, share_out, inflow = refs
    right, last_right = flags[3 + bit] == 1, flags[2 + levels] == 1
    merge_matrices(right, last_right, flows, other, share, mats, merged, share_out, last)
    merge_flows(right, last_right, 0, mats, flows, other, known, merged, inflow, PAD // 8, last)


def merge_far(bit, levels, flags, mats, flows, other, *refs):
    known, merged, inflow = (None, *refs) if bit == 0 else refs
    right, last_right = flags[3 + bit] == 1, flags[2 + levels] == 1
    last = bit == levels - 2
    height = flows.shape[0] // (2 * V)
    merge_flows(right, last_right, 1, mats, flows, other, known, merged, inflow, height, last)


def last_inflow(right, c, mats, ends, other, known, height, store):
    for t in range(height):
        mine = [ends[a * height + t] for a in range(V)]
        theirs = [other[a * height + t] for a in range(V)]
        f_left = [jnp.where(right, y, x) for x, y in zip(mine, theirs)]
        g_right = [jnp.where(right, x, y) for x, y in zip(mine, theirs)]
        before = [known[i * height + t] for i in range(2 * V)]
        _, total = inflow_of(c, mats, f_left, g_right, before)
        for i, value in enumerate(total):
            store(i, t, value)


def corrected(c, z, a, first, last, g, blocks, inflow):
    total = g[z * V + a, first:last, :]
    for b in range(V):
        total += blocks[c, z * V + a, b : b + 1, :] * inflow[b]
        total += blocks[c, z * V + a, 8 + b : 9 + b, :] * inflow[V + b]
    return total


def correct(c, right, mats, ends, other, known, g, blocks, result, inflow):
    def store(i, t, value):
        inflow[i, t * 8 : t * 8 + 8, :] = value

    height = g.shape[1]
    last_inflow(right, c, mats, ends, other, known, height // 8, store)
    cells = g.shape[0] // V
    for first, last in ((0, 32), (32, height)) if height > 32 else ((0, height),):
        flow = tuple(inflow[i, first:last, :] for i in range(2 * V))

        def step(z, flow, first=first, last=last):
            for a in range(V):
                result[z * V + a, first:last, :] = corrected(c, z, a, first, last, g, blocks, flow)
            return flow

        lax.fori_loop(0, cells, step, flow)


def correct_near(levels, flags, ends, other, share, known, g, blocks, result, mats, inflow):
    right = flags[2 + levels] == 1
    last_matrices(right, ends, other, share, mats)
    correct(0, right, mats, ends, other, known, g, blocks, result, inflow)


def correct_far(levels, flags, mats, ends, other, known, g, blocks, result, inflow):
    correct(1, flags[2 + levels] == 1, mats, ends, other, known, g, blocks, result, inflow)


def finish(levels, flags, mats, ends, other, known, g, blocks, near, *refs):
    done, out, inflow = refs[:-2], refs[-2], refs[-1]
    right = flags[2 + levels] == 1
    p = flags[0]
    first_row, last_row = CHUNKS[-1][0]
    width = last_row - first_row

    @pl.when(pl.program_id(0) == 0)
    def _():
        def store(i, t, value):
            inflow[i, t * 8 : t * 8 + 8, :] = value

        last_inflow(right, 1, mats, ends, other, known, width // 8, store)

    flow = tuple(inflow[i] for i in range(2 * V))

    def step(z, carry):
        for a in range(V):
            j = z * V + a
            row = j * 2 * NT
            out[pl.ds(row + 1 - p, NT, stride=2), :] = near[j, 0:NT, :]
            for ref, ((first, last), extra) in zip(done, CHUNKS):
                out[pl.ds(row + p + 2 * first, last - first, stride=2), :] = ref[j, 0 : last - first, :]
                if extra:
                    out[pl.ds(row + p + 2 * (NT - 1), 1), :] = ref[j, last - first : last - first + 1, :]
            out[pl.ds(row + p + 2 * first_row, width, stride=2), :] = corrected(1, z, a, 0, width, g, blocks, flow)
        return carry

    lax.fori_loop(0, g.shape[0] // V, step, 0)


def phase_tables(count):
    angle = 2.0 * math.pi * np.outer(np.arange(1, count + 1), np.arange(NT)) / NT
    cosine, sine = np.cos(angle), np.sin(angle)
    basis = np.zeros((PAD, 2 * count + 8), np.float32)
    basis[:NT, :count], basis[:NT, count : 2 * count], basis[:NT, 2 * count] = cosine.T, sine.T, 0.5
    turned = np.zeros((2, count + 8, 3, DEPTH), np.float32)
    turned[0, :count, :, :NT], turned[1, :count, :, :NT] = cosine[:, None], sine[:, None]
    turned[0, count, :, :NT] = 1.0
    return (2.0 / NT * basis).astype(np.float32), turned.reshape(2 * (count + 8), 3 * DEPTH)


def derivative_table():
    gap = np.arange(NT)[:, None] - np.arange(NT)[None, :]
    safe = np.where(gap == 0, 1.0, np.sin(np.pi * gap / NT))
    table = np.where(gap == 0, 0.0, 0.5 * (1.0 - 2.0 * np.mod(gap, 2)) / safe)
    wide = np.zeros((PAD, 3, DEPTH), np.float32)
    wide[:NT, :, :NT] = table[:, None]
    return wide.reshape(PAD, 3 * DEPTH)


NEAR_TILES = 2 * V * (PAD // 8)


def local(state, advect, viscous, inverse, lower, upper, blades, harmonic):
    cells = state.shape[0]
    count = harmonic.shape[0]
    segs, slabs = lax.axis_size("seg"), lax.axis_size("pitch")
    levels = segs.bit_length() - 1
    slab, seg = lax.axis_index("pitch"), lax.axis_index("seg")
    side = slab % 2
    wrap = jnp.logical_or(slab == 0, slab == slabs - 1)
    bits = [(seg >> k) & 1 for k in range(levels)]
    run = Chain(
        jnp.stack(
            [side, wrap.astype(jnp.int32), (slab == 0).astype(jnp.int32), *bits]
        ).astype(jnp.int32)
    )
    far_pairs = [(i, (i - 1) % slabs if i % 2 == 0 else (i + 1) % slabs) for i in range(slabs)]
    near_pairs = [(i, i ^ 1) for i in range(slabs)]
    to_far = lambda x: lax.ppermute(x, "pitch", far_pairs)
    to_level = lambda x, k: lax.ppermute(x, "seg", [(i, i ^ (1 << k)) for i in range(segs)])
    x_shape = (cells * V, PAD, LANES)

    st = state.transpose(0, 2, 3, 1, 4).reshape(cells * V * NT * 2, LANES)
    lead_rows = LEAD * V * NT
    slab_in = to_far(
        run(
            lead_cells, [(lead_rows, LANES)], [st], grid=(1,), name="lead_cells",
            in_specs=[pl.BlockSpec((2 * lead_rows, LANES), lambda i: (0, 0))],
            out_specs=[pl.BlockSpec((lead_rows, LANES), lambda i: (0, 0))],
        )[0]
    )

    ratio = blades[1].astype(F32) / blades[0].astype(F32)
    lag = 2.0 * math.pi * harmonic.astype(F32) * ratio
    trig = jnp.concatenate([jnp.cos(lag), jnp.sin(lag), jnp.full((8,), ratio / count)])
    trig = jnp.broadcast_to(trig[:, None], (2 * count + 8, LANES))
    basis, turned = phase_tables(count)
    table = derivative_table()

    rest = (cells - LEAD) * V
    chunk_shapes = [
        (rest * (last - first) + (padded_even(rest) if extra else 0), LANES)
        for (first, last), extra in CHUNKS
    ]
    edge_shape = (2 * V, PAD, LANES)
    xn, xf, first_cell, last_cell, *chunks = run(
        prepare, [x_shape, x_shape, edge_shape, edge_shape, *chunk_shapes], [st, trig, basis, turned],
        name="prepare",
    )
    halo_near = lax.ppermute(xn, "pitch", near_pairs)
    from_left = lax.ppermute(last_cell, "seg", [(i, i + 1) for i in range(segs - 1)])
    from_right = lax.ppermute(first_cell, "seg", [(i + 1, i) for i in range(segs - 1)])
    arrived, before = [], slab_in
    for chunk in chunks:
        if arrived:
            chunk, before = lax.optimization_barrier((chunk, before))
            if len(arrived) == 1:
                slab_in = before
            else:
                arrived[-2] = before
            before = arrived[-1]
        arrived.append(to_far(chunk))

    flat = lambda x: x.transpose(0, 2, 3, 1, 4).reshape(cells * V * V * 2, LANES)
    inv, low, upp = flat(inverse.astype(F32)), flat(lower), flat(upper)
    adv = advect.transpose(0, 2, 1, 3).reshape(cells * V * 2, LANES)
    vis = viscous.transpose(0, 2, 1, 3).reshape(cells * V * 2, LANES)

    blocks, group = run(
        transfer, [(2, cells * V, 16, LANES), (2, 3 * V, 8, LANES)], [low, upp],
        scratch=[pltpu.VMEM((cells * V, 8, LANES), F32)], name="transfer",
    )
    g_near, flows_near = run(
        near_cell, [x_shape, (NEAR_TILES + 6 * V, 8, LANES)],
        [xn, xf, halo_near, from_left, from_right, adv, vis, inv, low, upp, trig, table, group],
        scratch=[pltpu.VMEM(x_shape, F32)], name="near_cell",
    )
    base = run(
        far_base, [x_shape],
        [xn, xf, from_left, from_right, slab_in, adv, vis, trig, table, basis, turned],
        scratch=[pltpu.VMEM((V, PAD, LANES), F32)], name="far_base",
    )[0]

    mats, near_state = [], []
    mats_shape, share_shape = (2, 6 * V, 8, LANES), (2, 3 * V, 8, LANES)

    def near_level(k):
        nonlocal flows_near, near_state
        shape = (NEAR_TILES + 6 * V if k < levels - 2 else NEAR_TILES // 2 + 2 * V, 8, LANES)
        out = run(
            functools.partial(merge_near, k, levels),
            [mats_shape, shape, share_shape, (NEAR_TILES, 8, LANES)],
            [flows_near, to_level(flows_near, k), *near_state], name="merge_near",
        )
        mats.append(out[0])
        flows_near, near_state = out[1], out[2:]

    def far_solve(i):
        height = rows_of(CHUNKS[i])
        g, flows = run(
            functools.partial(far_chunk, CHUNKS[i]),
            [(cells * V, height, LANES), (2 * V * height // 8, 8, LANES)],
            [base, arrived[i], vis, inv, low, upp], name="far_chunk",
        )
        return [g, flows, None]

    def far_level(k, item):
        g, flows, known = item
        count = flows.shape[0]
        out = run(
            functools.partial(merge_far, k, levels),
            [(count if k < levels - 2 else count // 2, 8, LANES), (count, 8, LANES)],
            [mats[k], flows, to_level(flows, k)] + ([] if known is None else [known]), name="merge_far",
        )
        return [g, out[0], out[1]]

    def settle_far(item):
        g, ends, known = item
        return run(
            functools.partial(correct_far, levels), [g.shape],
            [mats[-1], ends, to_level(ends, levels - 1), known, g, blocks],
            scratch=[pltpu.VMEM((2 * V, g.shape[1], LANES), F32)], name="correct_far",
        )[0]

    near_level(0)
    one = far_solve(0)
    for k in range(1, levels - 1):
        near_level(k)
    for k in range(levels - 1):
        one = far_level(k, one)
    near, last = run(
        functools.partial(correct_near, levels), [x_shape, mats_shape],
        [flows_near, to_level(flows_near, levels - 1), *near_state, g_near, blocks],
        scratch=[pltpu.VMEM((2 * V, PAD, LANES), F32)], name="correct_near",
    )
    mats.append(last)
    two = far_solve(1)
    two = far_level(0, two)
    done = [settle_far(one)]
    three = far_solve(2)
    for k in range(1, levels - 1):
        two = far_level(k, two)
    three = far_level(0, three)
    done.append(settle_far(two))
    for k in range(1, levels - 1):
        three = far_level(k, three)
    g_last, ends, known = three

    steps = 4
    part = cells // steps
    whole = lambda x: pl.BlockSpec(x.shape, lambda i: (0,) * x.ndim)
    by_cell = lambda x: pl.BlockSpec((part * V,) + x.shape[1:], lambda i: (i, 0, 0))
    small = [mats[-1], ends, to_level(ends, levels - 1), known]
    out = run(
        functools.partial(finish, levels), [st.shape], [*small, g_last, blocks, near, *done],
        grid=(steps,),
        in_specs=[whole(x) for x in small]
        + [by_cell(g_last), pl.BlockSpec((2, part * V, 16, LANES), lambda i: (0, i, 0, 0))]
        + [by_cell(x) for x in (near, *done)],
        out_specs=[pl.BlockSpec((part * V * NT * 2, LANES), lambda i: (i, 0))],
        scratch=[pltpu.VMEM((2 * V, rows_of(CHUNKS[-1]), LANES), F32)], name="finish",
    )[0]
    return out.reshape(cells, V, NT, 2, LANES).transpose(0, 3, 1, 2, 4)


def solution(mesh):
    cell = P("seg", "pitch", None, None, None)
    return jax.shard_map(
        local,
        mesh=mesh,
        in_specs=(cell, P("seg", "pitch", None, None), P("seg", "pitch", None, None), cell, cell, cell, P(), P()),
        out_specs=cell,
        check_vma=False,
    )
```

time: 117 us -> 110 us (0.940)
  waiting for transfers between devices: 26 us -> 35.5 us
  local copies, waits for them, and re-layouts: 10.9 us -> 3.73 us
  other arithmetic: 3.39 us -> 0.27 us
  Pallas kernels: 38.6 us -> 35.6 us
  matrix products: 2.19 us -> 0 us
  starting transfers between devices: 34.2 us -> 33 us
    ppermute x2, waiting for transfers between devices: 0.46 us -> 8.42 us  [the longest x1 8.42 us: local(): lax.ppermute(last_cell, 'seg', [(i, i + 1) for i in range(segs - 1)])]
    slice x3 -> x1, local copies, waits for them, and re-layouts: 4.54 us -> 1.38 us  [local(): ratio = blades[1].astype(F32) / blades[0].astype(F32)]
    pallas_call x22 -> x20, Pallas kernels: 38.6 us -> 35.6 us  [__call__(): pl.pallas_call(body, out_shape=[jax.ShapeDtypeStruct(s, F32) for s in out...]
    ppermute x15 -> x12, starting transfers between devices: 22.2 us -> 24.8 us  [local(): lax.ppermute(x, 'seg', [(i, i ^ 1 << k) for i in range(segs)])]
    ppermute x4, starting transfers between devices: 4.37 us -> 1.98 us  [local(): to_far = lambda x: lax.ppermute(x, 'pitch', far_pairs)]
    unnamed x25 -> x20, local copies, waits for them, and re-layouts: 4.38 us -> 2.19 us
    dot_general x2 -> x0, matrix products: 2.19 us -> none  [phase_ahead(): jnp.einsum('kn,km->nm', basis, turned, precision=lax.Precision.HIGHEST)]
    dynamic_slice x1 -> x0, local copies, waits for them, and re-layouts: 1.79 us -> none  [local(): lax.dynamic_index_in_dim(st[:2 * lead_rows].reshape(lead_rows, 2, LANES),...]
  transfers between devices with their start and end apart: 22 -> 19, of which waited for: 8 -> 11; matrix products, arithmetic and copies ran while one was open for 6% -> 0% of each run, Pallas kernels for 28% -> 25%
where the time goes in v1:
time: 110 us
  Pallas kernels  35.6 us (32%)
  waiting for transfers between devices  35.5 us (32%)
  starting transfers between devices  33 us (30%)
  local copies, waits for them, and re-layouts  3.73 us (3%)
  between operations  1.6 us (1%)
    pallas_call x20, Pallas kernels, __call__(): pl.pallas_call(body, out_shape=[jax.ShapeDtypeStruct(s, F32) for s in out...  35.6 us
    ppermute x12, starting transfers between devices, local(): lax.ppermute(x, 'seg', [(i, i ^ 1 << k) for i in range(segs)])  24.8 us
    ppermute x12, waiting for transfers between devices, local(): lax.ppermute(x, 'seg', [(i, i ^ 1 << k) for i in range(segs)])  21.9 us
    ppermute x1, waiting for transfers between devices, local(): lax.ppermute(last_cell, 'seg', [(i, i + 1) for i in range(segs - 1)])  8.42 us
    ppermute x4, waiting for transfers between devices, local(): to_far = lambda x: lax.ppermute(x, 'pitch', far_pairs)  5.21 us
    ppermute x1, starting transfers between devices, local(): lax.ppermute(last_cell, 'seg', [(i, i + 1) for i in range(segs - 1)])  4.42 us
  transfers between devices with their start and end apart: 19, of which 11 were waited for; matrix products, arithmetic and copies ran while one was open for 0% of the time, Pallas kernels for 25%

profile of v1, /device:TPU:0, one launch (start us, length us, event | category | flops | bytes accessed | tf_op | source)
XLA Modules:
  0.0 109.7 jit_solution(3729728724724121896)
XLA Ops:
  0.0 1.4 %fusion.2 = (s32[1]{0:T(128)}, s32[1]{0:T(128)}) fusion(s32[2]{0:T(128)} %param.17), kind=kLoop, calls=%fused_computation.4 | loop fusion | bytes 16 | tf_op jit(solution)/shard_map/slice | solution.py:603
  2.0 0.0 copy-start.7
  2.7 0.1 stack.35.flags
  2.8 2.1 %copy-done = f32[16,2,5,49,128]{4,1,3,2,0:T(2,128)S(1)} copy-done((f32[16,2,5,49,128]{4,1,3,2,0:T(2,128)S(1)}, f32[16,2,5,49,128]{4,1,3,2,0:T(2,128)}, u32[]{:S(2)}) %copy-start) | copy-done | bytes 4014104
  5.0 0.6 lead_cells.1
  5.6 0.0 copy-start.1
  5.6 0.0 copy-start.2
  5.7 0.1 pad_maximum_fusion
  5.7 0.1 broadcast_in_dim.10.trig
  5.8 0.0 copy-start.8
  5.8 0.0 copy-start.3
  5.8 0.0 copy-start.4
  5.9 0.0 copy-start.6
  5.9 3.4 %prepare.1 = (f32[80,56,128]{2,1,0:T(8,128)S(1)}, f32[80,56,128]{2,1,0:T(8,128)S(1)}, f32[10,56,128]{2,1,0:T(8,128)S(1)}, f32[10,56,128]{2,1,0:T(8,128)S(1)}, f3...) custom-call(s32[6]{0:T(128)S(1)} %stack.35.flags, f32[7840,128]{1,0:T(8,128)S(1)} %bitcast.30, ...), custom_call_target="tpu_custom_call" | custom-call | flops 1000 | bytes 1000 | tf_op jit(solution)/shard_map/prepare/pallas_call | solution.py:46
  9.3 0.5 collective-permute-start
  9.8 4.4 %collective-permute-start.1 = (f32[10,56,128]{2,1,0:T(8,128)S(1)}, f32[10,56,128]{2,1,0:T(8,128)S(1)}, u32[]{:S(2)}, u32[]{:S(2)}) collective-permute-start(f32[10,56,128]{2,1,0:T(8,128)S(1)} %get-tuple-element.94), channel_id=1, source_target_pairs={{0,4},{4,8},{8,12},{12,16},{16,20},{20,24},{24,28},{1,5},{5,9},{9,... | collective-permute-start | bytes 860168 | tf_op jit(solution)/shard_map/ppermute | solution.py:621
  14.2 1.3 %collective-permute-start.2 = (f32[10,56,128]{2,1,0:T(8,128)S(1)}, f32[10,56,128]{2,1,0:T(8,128)S(1)}, u32[]{:S(2)}, u32[]{:S(2)}) collective-permute-start(f32[10,56,128]{2,1,0:T(8,128)S(1)} %get-tuple-element.95), channel_id=1, source_target_pairs={{4,0},{8,4},{12,8},{16,12},{20,16},{24,20},{28,24},{5,1},{9,5},{13... | collective-permute-start | bytes 860168 | tf_op jit(solution)/shard_map/ppermute | solution.py:622
  15.5 1.4 %collective-permute-start.3 = (f32[980,128]{1,0:T(8,128)S(1)}, f32[980,128]{1,0:T(8,128)S(1)}, u32[]{:S(2)}, u32[]{:S(2)}) collective-permute-start(f32[980,128]{1,0:T(8,128)S(1)} %lead_cells.1), channel_id=1, source_target_pairs={{0,3},{1,2},{2,1},{3,0},{4,7},{5,6},{6,5},{7,4},{8,11},{9,10},{10,... | collective-permute-start | bytes 1505288 | tf_op jit(solution)/shard_map/ppermute | solution.py:589
  16.9 1.6 %transfer.1 = (f32[2,80,16,128]{3,2,1,0:T(8,128)S(1)}, f32[2,15,8,128]{3,2,1,0:T(8,128)S(1)}) custom-call(s32[6]{0:T(128)S(1)} %stack.35.flags, f32[800,128]{1,0:T(8,128)S(1)} %bitcast.35, f32[800,128]{1,0:T(8,128)S(1)} %bitcast.40), custom_call_target="tpu_custom_call" | custom-call | flops 1000 | bytes 1000 | tf_op jit(solution)/shard_map/transfer/pallas_call | solution.py:46
  18.5 0.1 reshape.43
  18.7 8.4 %collective-permute-done.1.from_left = f32[10,56,128]{2,1,0:T(8,128)S(1)} collective-permute-done((f32[10,56,128]{2,1,0:T(8,128)S(1)}, f32[10,56,128]{2,1,0:T(8,128)S(1)}, u32[]{:S(2)}, u32[]{:S(2)}) %collective-permute-start.1) | collective-permute-done | bytes 286752 | tf_op jit(solution)/shard_map/ppermute | solution.py:621
  27.1 0.0 collective-permute-done.2.from_right
  27.1 6.3 %near_cell.1 = (f32[80,56,128]{2,1,0:T(8,128)S(1)}, f32[100,8,128]{2,1,0:T(8,128)S(1)}) custom-call(s32[6]{0:T(128)S(1)} %stack.35.flags, f32[80,56,128]{2,1,0:T(8,128)S(1)} %get-tuple-element.92.xn, f32[80,56,128]{2,1,0:T(8,128)S(1)} %get-tuple-element.93.xf, f32[80,56,128]{2,1,0:T(8,128)S(1)} %collective-permute-done.halo, ...), custom_call_target="tpu_custom_call" | custom-call | flops 1000 | bytes 1000 | tf_op jit(solution)/shard_map/near_cell/pallas_call | solution.py:46
  33.4 2.5 %collective-permute-start.4 = (f32[100,8,128]{2,1,0:T(8,128)S(1)}, f32[100,8,128]{2,1,0:T(8,128)S(1)}, u32[]{:S(2)}, u32[]{:S(2)}) collective-permute-start(f32[100,8,128]{2,1,0:T(8,128)S(1)} %get-tuple-element.103.refs_0_), channel_id=1, source_target_pairs={{0,4},{4,0},{8,12},{12,8},{16,20},{20,16},{24,28},{28,24},{1,5},{5... | collective-permute-start | bytes 1228808 | tf_op jit(solution)/shard_map/ppermute | solution.py:590
  36.0 0.5 collective-permute-start.5
  36.5 4.0 %far_base.1.base = f32[80,56,128]{2,1,0:T(8,128)S(1)} custom-call(s32[6]{0:T(128)S(1)} %stack.35.flags, f32[80,56,128]{2,1,0:T(8,128)S(1)} %get-tuple-element.92.xn, f32[80,56,128]{2,1,0:T(8,128)S(1)} %get-tuple-element.93.xf, f32[10,56,128]{2,1,0:T(8,128)S(1)} %collective-permute-done.1.from_left, f32[10,56,128]{2,1,0:T(8,128)S(1)} %collective-permute-done.2.from_right, ...), custom_call_target="tpu_custom_call" | custom-call | flops 1000 | bytes 1000 | tf_op jit(solution)/shard_map/far_base/pallas_call | solution.py:46
  40.5 4.8 %collective-permute-done.4.refs_1_ = f32[100,8,128]{2,1,0:T(8,128)S(1)} collective-permute-done((f32[100,8,128]{2,1,0:T(8,128)S(1)}, f32[100,8,128]{2,1,0:T(8,128)S(1)}, u32[]{:S(2)}, u32[]{:S(2)}) %collective-permute-start.4) | collective-permute-done | bytes 409632 | tf_op jit(solution)/shard_map/ppermute | solution.py:590
  45.3 1.0 merge_near.2
  46.3 3.1 %collective-permute-start.6 = (f32[100,8,128]{2,1,0:T(8,128)S(1)}, f32[100,8,128]{2,1,0:T(8,128)S(1)}, u32[]{:S(2)}, u32[]{:S(2)}) collective-permute-start(f32[100,8,128]{2,1,0:T(8,128)S(1)} %get-tuple-element.112.refs_0_), channel_id=1, source_target_pairs={{0,8},{4,12},{8,0},{12,4},{16,24},{20,28},{24,16},{28,20},{1,9},{5... | collective-permute-start | bytes 1228808 | tf_op jit(solution)/shard_map/ppermute | solution.py:590
  49.4 0.0 collective-permute-start.10
  49.5 5.2 %collective-permute-done.5.halo = f32[1440,128]{1,0:T(8,128)S(1)} collective-permute-done((f32[1440,128]{1,0:T(8,128)S(1)}, f32[1440,128]{1,0:T(8,128)S(1)}, u32[]{:S(2)}, u32[]{:S(2)}) %collective-permute-start.5) | collective-permute-done | bytes 737312 | tf_op jit(solution)/shard_map/ppermute | solution.py:589
  54.7 1.9 %far_chunk.3 = (f32[80,24,128]{2,1,0:T(8,128)S(1)}, f32[30,8,128]{2,1,0:T(8,128)S(1)}) custom-call(s32[6]{0:T(128)S(1)} %stack.35.flags, f32[80,56,128]{2,1,0:T(8,128)S(1)} %far_base.1.base, f32[1440,128]{1,0:T(8,128)S(1)} %collective-permute-done.5.halo, f32[160,128]{1,0:T(8,128)S(1)} %bitcast.47, f32[800,128]{1,0:T(8,128)S(1)} %bitcast.32, ...), custom_call_target="tpu_custom_call" | custom-call | flops 1000 | bytes 1000 | tf_op jit(solution)/shard_map/far_chunk/pallas_call | solution.py:46
  56.6 0.1 collective-permute-start.7
  56.7 1.5 %collective-permute-done.6.refs_1_ = f32[100,8,128]{2,1,0:T(8,128)S(1)} collective-permute-done((f32[100,8,128]{2,1,0:T(8,128)S(1)}, f32[100,8,128]{2,1,0:T(8,128)S(1)}, u32[]{:S(2)}, u32[]{:S(2)}) %collective-permute-start.6) | collective-permute-done | bytes 409632 | tf_op jit(solution)/shard_map/ppermute | solution.py:590
  58.3 1.0 merge_near.3
  59.3 2.8 %collective-permute-start.9 = (f32[45,8,128]{2,1,0:T(8,128)S(1)}, f32[45,8,128]{2,1,0:T(8,128)S(1)}, u32[]{:S(2)}, u32[]{:S(2)}) collective-permute-start(f32[45,8,128]{2,1,0:T(8,128)S(1)} %get-tuple-element.126.ends), channel_id=1, source_target_pairs={{0,16},{4,20},{8,24},{12,28},{16,0},{20,4},{24,8},{28,12},{1,17},{... | collective-permute-start | bytes 552968 | tf_op jit(solution)/shard_map/ppermute | solution.py:590
  62.1 0.0 collective-permute-done.7.other
  62.1 0.7 merge_far.6
  62.8 1.6 %collective-permute-start.8 = (f32[30,8,128]{2,1,0:T(8,128)S(1)}, f32[30,8,128]{2,1,0:T(8,128)S(1)}, u32[]{:S(2)}, u32[]{:S(2)}) collective-permute-start(f32[30,8,128]{2,1,0:T(8,128)S(1)} %get-tuple-element.122.flows), channel_id=1, source_target_pairs={{0,8},{4,12},{8,0},{12,4},{16,24},{20,28},{24,16},{28,20},{1,9},{5... | collective-permute-start | bytes 368648 | tf_op jit(solution)/shard_map/ppermute | solution.py:590
  64.5 4.0 %collective-permute-done.8.other = f32[30,8,128]{2,1,0:T(8,128)S(1)} collective-permute-done((f32[30,8,128]{2,1,0:T(8,128)S(1)}, f32[30,8,128]{2,1,0:T(8,128)S(1)}, u32[]{:S(2)}, u32[]{:S(2)}) %collective-permute-start.8) | collective-permute-done | bytes 122912 | tf_op jit(solution)/shard_map/ppermute | solution.py:590
  68.5 0.7 merge_far.7
  69.2 1.4 %collective-permute-done.9.other = f32[45,8,128]{2,1,0:T(8,128)S(1)} collective-permute-done((f32[45,8,128]{2,1,0:T(8,128)S(1)}, f32[45,8,128]{2,1,0:T(8,128)S(1)}, u32[]{:S(2)}, u32[]{:S(2)}) %collective-permute-start.9) | collective-permute-done | bytes 184352 | tf_op jit(solution)/shard_map/ppermute | solution.py:590
  70.6 2.6 %correct_near.1 = (f32[80,56,128]{2,1,0:T(8,128)S(1)}, f32[2,30,8,128]{3,2,1,0:T(8,128)S(1)}) custom-call(s32[6]{0:T(128)S(1)} %stack.35.flags, f32[45,8,128]{2,1,0:T(8,128)S(1)} %get-tuple-element.126.ends, f32[45,8,128]{2,1,0:T(8,128)S(1)} %collective-permute-done.9.other, f32[2,15,8,128]{3,2,1,0:T(8,128)S(1)} %get-tuple-element.127.share, ...), custom_call_target="tpu_custom_call" | custom-call | flops 1000 | bytes 1000 | tf_op jit(solution)/shard_map/correct_near/pallas_call | solution.py:46
  73.2 1.9 %far_chunk.4 = (f32[80,24,128]{2,1,0:T(8,128)S(1)}, f32[30,8,128]{2,1,0:T(8,128)S(1)}) custom-call(s32[6]{0:T(128)S(1)} %stack.35.flags, f32[80,56,128]{2,1,0:T(8,128)S(1)} %far_base.1.base, f32[1024,128]{1,0:T(8,128)S(1)} %collective-permute-done.10.halo, f32[160,128]{1,0:T(8,128)S(1)} %bitcast.48, f32[800,128]{1,0:T(8,128)S(1)} %bitcast.33, ...), custom_call_target="tpu_custom_call" | custom-call | flops 1000 | bytes 1000 | tf_op jit(solution)/shard_map/far_chunk/pallas_call | solution.py:46
  75.1 1.9 %collective-permute-start.11 = (f32[30,8,128]{2,1,0:T(8,128)S(1)}, f32[30,8,128]{2,1,0:T(8,128)S(1)}, u32[]{:S(2)}, u32[]{:S(2)}) collective-permute-start(f32[30,8,128]{2,1,0:T(8,128)S(1)} %get-tuple-element.136.flows), channel_id=1, source_target_pairs={{0,4},{4,0},{8,12},{12,8},{16,20},{20,16},{24,28},{28,24},{1,5},{5... | collective-permute-start | bytes 368648 | tf_op jit(solution)/shard_map/ppermute | solution.py:590
  77.0 3.1 %collective-permute-done.11.other = f32[30,8,128]{2,1,0:T(8,128)S(1)} collective-permute-done((f32[30,8,128]{2,1,0:T(8,128)S(1)}, f32[30,8,128]{2,1,0:T(8,128)S(1)}, u32[]{:S(2)}, u32[]{:S(2)}) %collective-permute-start.11) | collective-permute-done | bytes 122912 | tf_op jit(solution)/shard_map/ppermute | solution.py:590
  80.1 0.7 merge_far.8
  80.8 1.2 %collective-permute-start.14 = (f32[30,8,128]{2,1,0:T(8,128)S(1)}, f32[30,8,128]{2,1,0:T(8,128)S(1)}, u32[]{:S(2)}, u32[]{:S(2)}) collective-permute-start(f32[30,8,128]{2,1,0:T(8,128)S(1)} %get-tuple-element.147.flows), channel_id=1, source_target_pairs={{0,8},{4,12},{8,0},{12,4},{16,24},{20,28},{24,16},{28,20},{1,9},{5... | collective-permute-start | bytes 368648 | tf_op jit(solution)/shard_map/ppermute | solution.py:590
  82.0 4.6 %collective-permute-start.12 = (f32[15,8,128]{2,1,0:T(8,128)S(1)}, f32[15,8,128]{2,1,0:T(8,128)S(1)}, u32[]{:S(2)}, u32[]{:S(2)}) collective-permute-start(f32[15,8,128]{2,1,0:T(8,128)S(1)} %get-tuple-element.140.ends), channel_id=1, source_target_pairs={{0,16},{4,20},{8,24},{12,28},{16,0},{20,4},{24,8},{28,12},{1,17},{... | collective-permute-start | bytes 184328 | tf_op jit(solution)/shard_map/ppermute | solution.py:590
  86.6 2.2 %collective-permute-done.12.other = f32[15,8,128]{2,1,0:T(8,128)S(1)} collective-permute-done((f32[15,8,128]{2,1,0:T(8,128)S(1)}, f32[15,8,128]{2,1,0:T(8,128)S(1)}, u32[]{:S(2)}, u32[]{:S(2)}) %collective-permute-start.12) | collective-permute-done | bytes 61472 | tf_op jit(solution)/shard_map/ppermute | solution.py:590
  88.8 1.4 %correct_far.2.refs_0_ = f32[80,24,128]{2,1,0:T(8,128)S(1)} custom-call(s32[6]{0:T(128)S(1)} %stack.35.flags, f32[2,30,8,128]{3,2,1,0:T(8,128)S(1)} %get-tuple-element.139.mats, f32[15,8,128]{2,1,0:T(8,128)S(1)} %get-tuple-element.140.ends, f32[15,8,128]{2,1,0:T(8,128)S(1)} %collective-permute-done.12.other, f32[30,8,128]{2,1,0:T(8,128)S(1)} %get-tuple-element.141.known, ...), custom_call_target="tpu_custom_call" | custom-call | flops 1000 | bytes 1000 | tf_op jit(solution)/shard_map/correct_far/pallas_call | solution.py:46
  90.2 1.2 %far_chunk.5 = (f32[80,8,128]{2,1,0:T(8,128)S(1)}, f32[10,8,128]{2,1,0:T(8,128)S(1)}) custom-call(s32[6]{0:T(128)S(1)} %stack.35.flags, f32[80,56,128]{2,1,0:T(8,128)S(1)} %far_base.1.base, f32[480,128]{1,0:T(8,128)S(1)} %collective-permute-done.13.halo, f32[160,128]{1,0:T(8,128)S(1)} %bitcast.49, f32[800,128]{1,0:T(8,128)S(1)} %bitcast.34, ...), custom_call_target="tpu_custom_call" | custom-call | flops 1000 | bytes 1000 | tf_op jit(solution)/shard_map/far_chunk/pallas_call | solution.py:46
  91.4 1.3 %collective-permute-start.15 = (f32[10,8,128]{2,1,0:T(8,128)S(1)}, f32[10,8,128]{2,1,0:T(8,128)S(1)}, u32[]{:S(2)}, u32[]{:S(2)}) collective-permute-start(f32[10,8,128]{2,1,0:T(8,128)S(1)} %get-tuple-element.151.flows), channel_id=1, source_target_pairs={{0,4},{4,0},{8,12},{12,8},{16,20},{20,16},{24,28},{28,24},{1,5},{5... | collective-permute-start | bytes 122888 | tf_op jit(solution)/shard_map/ppermute | solution.py:590
  92.7 0.7 merge_far.9
  93.4 3.0 %collective-permute-start.16 = (f32[15,8,128]{2,1,0:T(8,128)S(1)}, f32[15,8,128]{2,1,0:T(8,128)S(1)}, u32[]{:S(2)}, u32[]{:S(2)}) collective-permute-start(f32[15,8,128]{2,1,0:T(8,128)S(1)} %get-tuple-element.154.ends), channel_id=1, source_target_pairs={{0,16},{4,20},{8,24},{12,28},{16,0},{20,4},{24,8},{28,12},{1,17},{... | collective-permute-start | bytes 184328 | tf_op jit(solution)/shard_map/ppermute | solution.py:590
  96.4 0.6 merge_far.10
  97.0 0.5 collective-permute-start.17
  97.5 1.1 %collective-permute-done.16.other = f32[15,8,128]{2,1,0:T(8,128)S(1)} collective-permute-done((f32[15,8,128]{2,1,0:T(8,128)S(1)}, f32[15,8,128]{2,1,0:T(8,128)S(1)}, u32[]{:S(2)}, u32[]{:S(2)}) %collective-permute-start.16) | collective-permute-done | bytes 61472 | tf_op jit(solution)/shard_map/ppermute | solution.py:590
  98.6 1.4 %correct_far.3.refs_1_ = f32[80,24,128]{2,1,0:T(8,128)S(1)} custom-call(s32[6]{0:T(128)S(1)} %stack.35.flags, f32[2,30,8,128]{3,2,1,0:T(8,128)S(1)} %get-tuple-element.139.mats, f32[15,8,128]{2,1,0:T(8,128)S(1)} %get-tuple-element.154.ends, f32[15,8,128]{2,1,0:T(8,128)S(1)} %collective-permute-done.16.other, f32[30,8,128]{2,1,0:T(8,128)S(1)} %get-tuple-element.155.known, ...), custom_call_target="tpu_custom_call" | custom-call | flops 1000 | bytes 1000 | tf_op jit(solution)/shard_map/correct_far/pallas_call | solution.py:46
  100.0 1.1 collective-permute-done.17.other
  101.1 0.6 merge_far.11
  101.7 2.1 %collective-permute-start.18 = (f32[5,8,128]{2,1,0:T(8,128)S(1)}, f32[5,8,128]{2,1,0:T(8,128)S(1)}, u32[]{:S(2)}, u32[]{:S(2)}) collective-permute-start(f32[5,8,128]{2,1,0:T(8,128)S(1)} %get-tuple-element.162.ends), channel_id=1, source_target_pairs={{0,16},{4,20},{8,24},{12,28},{16,0},{20,4},{24,8},{28,12},{1,17},{... | collective-permute-start | bytes 61448 | tf_op jit(solution)/shard_map/ppermute | solution.py:590
  103.7 2.7 %collective-permute-done.18.other = f32[5,8,128]{2,1,0:T(8,128)S(1)} collective-permute-done((f32[5,8,128]{2,1,0:T(8,128)S(1)}, f32[5,8,128]{2,1,0:T(8,128)S(1)}, u32[]{:S(2)}, u32[]{:S(2)}) %collective-permute-start.18) | collective-permute-done | bytes 20512 | tf_op jit(solution)/shard_map/ppermute | solution.py:590
  106.5 3.2 %finish.1 = f32[7840,128]{1,0:T(8,128)} custom-call(s32[6]{0:T(128)S(1)} %stack.35.flags, f32[2,30,8,128]{3,2,1,0:T(8,128)S(1)} %get-tuple-element.139.mats, f32[5,8,128]{2,1,0:T(8,128)S(1)} %get-tuple-element.162.ends, f32[5,8,128]{2,1,0:T(8,128)S(1)} %collective-permute-done.18.other, f32[10,8,128]{2,1,0:T(8,128)S(1)} %get-tuple-element.163.known, ...), custom_call_target="tpu_custom_call" | custom-call | flops 1000 | bytes 1000 | tf_op jit(solution)/shard_map/finish/pallas_call | solution.py:46
  (21 shorter events, 0.1 us)
Async XLA Ops:
  0.0 5.6 %copy-start.9 = (s32[24]{0:T(128)S(1)}, s32[24]{0:T(128)}, u32[]{:S(2)}) copy-start(s32[24]{0:T(128)} %param.18) | copy-start | bytes 292
  2.0 3.8 %copy-start.7 = (f32[56,56]{1,0:T(8,128)S(1)}, f32[56,56]{1,0:T(8,128)}, u32[]{:S(2)}) copy-start(f32[56,56]{1,0:T(8,128)} %constant.39.clone.basis) | copy-start | bytes 37636
  2.8 2.1 %copy-start = (f32[16,2,5,49,128]{4,1,3,2,0:T(2,128)S(1)}, f32[16,2,5,49,128]{4,1,3,2,0:T(2,128)}, u32[]{:S(2)}) copy-start(f32[16,2,5,49,128]{4,1,3,2,0:T(2,128)} %param.11) | copy-start | bytes 12042244
  5.0 0.9 copy-start.5
  5.6 11.4 %copy-start.1 = (f32[16,2,5,5,128]{4,1,3,2,0:T(2,128)S(1)}, f32[16,2,5,5,128]{4,1,3,2,0:T(2,128)}, u32[]{:S(2)}) copy-start(f32[16,2,5,5,128]{4,1,3,2,0:T(2,128)} %param.15) | copy-start | bytes 1228804
  5.6 11.3 %copy-start.2 = (f32[16,2,5,5,128]{4,1,3,2,0:T(2,128)S(1)}, f32[16,2,5,5,128]{4,1,3,2,0:T(2,128)}, u32[]{:S(2)}) copy-start(f32[16,2,5,5,128]{4,1,3,2,0:T(2,128)} %param.16) | copy-start | bytes 1228804
  5.8 12.7 %copy-start.8 = (bf16[16,2,5,5,128]{4,1,3,2,0:T(2,128)(2,1)S(1)}, bf16[16,2,5,5,128]{4,1,3,2,0:T(2,128)(2,1)}, u32[]{:S(2)}) copy-start(bf16[16,2,5,5,128]{4,1,3,2,0:T(2,128)(2,1)} %param.14) | copy-start | bytes 614404
  5.8 21.3 %copy-start.3 = (f32[16,2,5,128]{3,1,2,0:T(2,128)S(1)}, f32[16,2,5,128]{3,1,2,0:T(2,128)}, u32[]{:S(2)}) copy-start(f32[16,2,5,128]{3,1,2,0:T(2,128)} %param.13) | copy-start | bytes 245764
  5.8 21.2 %copy-start.4 = (f32[16,2,5,128]{3,1,2,0:T(2,128)S(1)}, f32[16,2,5,128]{3,1,2,0:T(2,128)}, u32[]{:S(2)}) copy-start(f32[16,2,5,128]{3,1,2,0:T(2,128)} %param.12) | copy-start | bytes 245764
  5.9 21.2 %copy-start.6 = (f32[56,192]{1,0:T(8,128)S(1)}, f32[56,192]{1,0:T(8,128)}, u32[]{:S(2)}) copy-start(f32[56,192]{1,0:T(8,128)} %constant.41.clone.table) | copy-start | bytes 129028
  9.3 17.8 %collective-permute-start = (f32[80,56,128]{2,1,0:T(8,128)S(1)}, f32[80,56,128]{2,1,0:T(8,128)S(1)}, u32[]{:S(2)}, u32[]{:S(2)}) collective-permute-start(f32[80,56,128]{2,1,0:T(8,128)S(1)} %get-tuple-element.92.xn), channel_id=1, source_target_pairs={{0,1},{1,0},{2,3},{3,2},{4,5},{5,4},{6,7},{7,6},{8,9},{9,8},{10,11... | collective-permute-start | bytes 6881288 | tf_op jit(solution)/shard_map/ppermute | solution.py:620
  9.8 17.3 %collective-permute-start.1 = (f32[10,56,128]{2,1,0:T(8,128)S(1)}, f32[10,56,128]{2,1,0:T(8,128)S(1)}, u32[]{:S(2)}, u32[]{:S(2)}) collective-permute-start(f32[10,56,128]{2,1,0:T(8,128)S(1)} %get-tuple-element.94), channel_id=1, source_target_pairs={{0,4},{4,8},{8,12},{12,16},{16,20},{20,24},{24,28},{1,5},{5,9},{9,... | collective-permute-start | bytes 860168 | tf_op jit(solution)/shard_map/ppermute | solution.py:621
  14.2 12.9 %collective-permute-start.2 = (f32[10,56,128]{2,1,0:T(8,128)S(1)}, f32[10,56,128]{2,1,0:T(8,128)S(1)}, u32[]{:S(2)}, u32[]{:S(2)}) collective-permute-start(f32[10,56,128]{2,1,0:T(8,128)S(1)} %get-tuple-element.95), channel_id=1, source_target_pairs={{4,0},{8,4},{12,8},{16,12},{20,16},{24,20},{28,24},{5,1},{9,5},{13... | collective-permute-start | bytes 860168 | tf_op jit(solution)/shard_map/ppermute | solution.py:622
  15.5 21.0 %collective-permute-start.3 = (f32[980,128]{1,0:T(8,128)S(1)}, f32[980,128]{1,0:T(8,128)S(1)}, u32[]{:S(2)}, u32[]{:S(2)}) collective-permute-start(f32[980,128]{1,0:T(8,128)S(1)} %lead_cells.1), channel_id=1, source_target_pairs={{0,3},{1,2},{2,1},{3,0},{4,7},{5,6},{6,5},{7,4},{8,11},{9,10},{10,... | collective-permute-start | bytes 1505288 | tf_op jit(solution)/shard_map/ppermute | solution.py:589
  33.4 11.9 %collective-permute-start.4 = (f32[100,8,128]{2,1,0:T(8,128)S(1)}, f32[100,8,128]{2,1,0:T(8,128)S(1)}, u32[]{:S(2)}, u32[]{:S(2)}) collective-permute-start(f32[100,8,128]{2,1,0:T(8,128)S(1)} %get-tuple-element.103.refs_0_), channel_id=1, source_target_pairs={{0,4},{4,0},{8,12},{12,8},{16,20},{20,16},{24,28},{28,24},{1,5},{5... | collective-permute-start | bytes 1228808 | tf_op jit(solution)/shard_map/ppermute | solution.py:590
  36.0 18.7 %collective-permute-start.5 = (f32[1440,128]{1,0:T(8,128)S(1)}, f32[1440,128]{1,0:T(8,128)S(1)}, u32[]{:S(2)}, u32[]{:S(2)}) collective-permute-start(f32[1440,128]{1,0:T(8,128)S(1)} %get-tuple-element.108), channel_id=1, source_target_pairs={{0,3},{1,2},{2,1},{3,0},{4,7},{5,6},{6,5},{7,4},{8,11},{9,10},{10,... | collective-permute-start | bytes 2211848 | tf_op jit(solution)/shard_map/ppermute | solution.py:589
  46.3 12.0 %collective-permute-start.6 = (f32[100,8,128]{2,1,0:T(8,128)S(1)}, f32[100,8,128]{2,1,0:T(8,128)S(1)}, u32[]{:S(2)}, u32[]{:S(2)}) collective-permute-start(f32[100,8,128]{2,1,0:T(8,128)S(1)} %get-tuple-element.112.refs_0_), channel_id=1, source_target_pairs={{0,8},{4,12},{8,0},{12,4},{16,24},{20,28},{24,16},{28,20},{1,9},{5... | collective-permute-start | bytes 1228808 | tf_op jit(solution)/shard_map/ppermute | solution.py:590
  49.4 23.7 %collective-permute-start.10 = (f32[1024,128]{1,0:T(8,128)S(1)}, f32[1024,128]{1,0:T(8,128)S(1)}, u32[]{:S(2)}, u32[]{:S(2)}) collective-permute-start(f32[1024,128]{1,0:T(8,128)S(1)} %get-tuple-element.133), channel_id=1, source_target_pairs={{0,3},{1,2},{2,1},{3,0},{4,7},{5,6},{6,5},{7,4},{8,11},{9,10},{10,... | collective-permute-start | bytes 1572872 | tf_op jit(solution)/shard_map/ppermute | solution.py:589
  56.6 5.5 %collective-permute-start.7 = (f32[30,8,128]{2,1,0:T(8,128)S(1)}, f32[30,8,128]{2,1,0:T(8,128)S(1)}, u32[]{:S(2)}, u32[]{:S(2)}) collective-permute-start(f32[30,8,128]{2,1,0:T(8,128)S(1)} %get-tuple-element.118.flows), channel_id=1, source_target_pairs={{0,4},{4,0},{8,12},{12,8},{16,20},{20,16},{24,28},{28,24},{1,5},{5... | collective-permute-start | bytes 368648 | tf_op jit(solution)/shard_map/ppermute | solution.py:590
  59.3 11.3 %collective-permute-start.9 = (f32[45,8,128]{2,1,0:T(8,128)S(1)}, f32[45,8,128]{2,1,0:T(8,128)S(1)}, u32[]{:S(2)}, u32[]{:S(2)}) collective-permute-start(f32[45,8,128]{2,1,0:T(8,128)S(1)} %get-tuple-element.126.ends), channel_id=1, source_target_pairs={{0,16},{4,20},{8,24},{12,28},{16,0},{20,4},{24,8},{28,12},{1,17},{... | collective-permute-start | bytes 552968 | tf_op jit(solution)/shard_map/ppermute | solution.py:590
  62.8 5.7 %collective-permute-start.8 = (f32[30,8,128]{2,1,0:T(8,128)S(1)}, f32[30,8,128]{2,1,0:T(8,128)S(1)}, u32[]{:S(2)}, u32[]{:S(2)}) collective-permute-start(f32[30,8,128]{2,1,0:T(8,128)S(1)} %get-tuple-element.122.flows), channel_id=1, source_target_pairs={{0,8},{4,12},{8,0},{12,4},{16,24},{20,28},{24,16},{28,20},{1,9},{5... | collective-permute-start | bytes 368648 | tf_op jit(solution)/shard_map/ppermute | solution.py:590
  64.5 25.7 %collective-permute-start.13 = (f32[480,128]{1,0:T(8,128)S(1)}, f32[480,128]{1,0:T(8,128)S(1)}, u32[]{:S(2)}, u32[]{:S(2)}) collective-permute-start(f32[480,128]{1,0:T(8,128)S(1)} %get-tuple-element.144), channel_id=1, source_target_pairs={{0,3},{1,2},{2,1},{3,0},{4,7},{5,6},{6,5},{7,4},{8,11},{9,10},{10,... | collective-permute-start | bytes 737288 | tf_op jit(solution)/shard_map/ppermute | solution.py:589
  75.1 4.9 %collective-permute-start.11 = (f32[30,8,128]{2,1,0:T(8,128)S(1)}, f32[30,8,128]{2,1,0:T(8,128)S(1)}, u32[]{:S(2)}, u32[]{:S(2)}) collective-permute-start(f32[30,8,128]{2,1,0:T(8,128)S(1)} %get-tuple-element.136.flows), channel_id=1, source_target_pairs={{0,4},{4,0},{8,12},{12,8},{16,20},{20,16},{24,28},{28,24},{1,5},{5... | collective-permute-start | bytes 368648 | tf_op jit(solution)/shard_map/ppermute | solution.py:590
  80.8 11.9 %collective-permute-start.14 = (f32[30,8,128]{2,1,0:T(8,128)S(1)}, f32[30,8,128]{2,1,0:T(8,128)S(1)}, u32[]{:S(2)}, u32[]{:S(2)}) collective-permute-start(f32[30,8,128]{2,1,0:T(8,128)S(1)} %get-tuple-element.147.flows), channel_id=1, source_target_pairs={{0,8},{4,12},{8,0},{12,4},{16,24},{20,28},{24,16},{28,20},{1,9},{5... | collective-permute-start | bytes 368648 | tf_op jit(solution)/shard_map/ppermute | solution.py:590
  82.0 6.8 %collective-permute-start.12 = (f32[15,8,128]{2,1,0:T(8,128)S(1)}, f32[15,8,128]{2,1,0:T(8,128)S(1)}, u32[]{:S(2)}, u32[]{:S(2)}) collective-permute-start(f32[15,8,128]{2,1,0:T(8,128)S(1)} %get-tuple-element.140.ends), channel_id=1, source_target_pairs={{0,16},{4,20},{8,24},{12,28},{16,0},{20,4},{24,8},{28,12},{1,17},{... | collective-permute-start | bytes 184328 | tf_op jit(solution)/shard_map/ppermute | solution.py:590
  91.4 5.0 %collective-permute-start.15 = (f32[10,8,128]{2,1,0:T(8,128)S(1)}, f32[10,8,128]{2,1,0:T(8,128)S(1)}, u32[]{:S(2)}, u32[]{:S(2)}) collective-permute-start(f32[10,8,128]{2,1,0:T(8,128)S(1)} %get-tuple-element.151.flows), channel_id=1, source_target_pairs={{0,4},{4,0},{8,12},{12,8},{16,20},{20,16},{24,28},{28,24},{1,5},{5... | collective-permute-start | bytes 122888 | tf_op jit(solution)/shard_map/ppermute | solution.py:590
  93.4 5.2 %collective-permute-start.16 = (f32[15,8,128]{2,1,0:T(8,128)S(1)}, f32[15,8,128]{2,1,0:T(8,128)S(1)}, u32[]{:S(2)}, u32[]{:S(2)}) collective-permute-start(f32[15,8,128]{2,1,0:T(8,128)S(1)} %get-tuple-element.154.ends), channel_id=1, source_target_pairs={{0,16},{4,20},{8,24},{12,28},{16,0},{20,4},{24,8},{28,12},{1,17},{... | collective-permute-start | bytes 184328 | tf_op jit(solution)/shard_map/ppermute | solution.py:590
  97.0 4.1 %collective-permute-start.17 = (f32[10,8,128]{2,1,0:T(8,128)S(1)}, f32[10,8,128]{2,1,0:T(8,128)S(1)}, u32[]{:S(2)}, u32[]{:S(2)}) collective-permute-start(f32[10,8,128]{2,1,0:T(8,128)S(1)} %get-tuple-element.158.flows), channel_id=1, source_target_pairs={{0,8},{4,12},{8,0},{12,4},{16,24},{20,28},{24,16},{28,20},{1,9},{5... | collective-permute-start | bytes 122888 | tf_op jit(solution)/shard_map/ppermute | solution.py:590
  101.7 4.8 %collective-permute-start.18 = (f32[5,8,128]{2,1,0:T(8,128)S(1)}, f32[5,8,128]{2,1,0:T(8,128)S(1)}, u32[]{:S(2)}, u32[]{:S(2)}) collective-permute-start(f32[5,8,128]{2,1,0:T(8,128)S(1)} %get-tuple-element.162.ends), channel_id=1, source_target_pairs={{0,16},{4,20},{8,24},{12,28},{16,0},{20,4},{24,8},{28,12},{1,17},{... | collective-permute-start | bytes 61448 | tf_op jit(solution)/shard_map/ppermute | solution.py:590

commit v2 on v1

v2 whole, which is shorter than its diff:
```python
import functools
import math

import jax
import jax.numpy as jnp
import numpy as np
from jax import lax
from jax.experimental import pallas as pl
from jax.experimental.pallas import tpu as pltpu
from jax.sharding import PartitionSpec as P

F32 = jnp.float32
BF16 = jnp.bfloat16
V = 5
NT = 49
PAD = 56
DEPTH = 64
LANES = 128
LEAD = 4
MB = 1 << 20

CHUNKS = (((0, 8), False), ((8, 24), False), ((24, 40), True), ((40, 48), False))


def rows_of(chunk):
    (first, last), extra = chunk
    return last - first + (8 if extra else 0)


def padded_even(count):
    return (count + 7) // 8 * 8


class Chain:
    def __init__(self, flags):
        self.flags = flags

    def after(self, array):
        self.flags, array = lax.optimization_barrier((self.flags, array))
        return array

    def __call__(self, body, out_shapes, arrays, scratch=(), vmem=24, name=None, grid=None, in_specs=None, out_specs=None, scalars=()):
        smem = pl.BlockSpec(memory_space=pltpu.SMEM)
        held = pl.BlockSpec(memory_space=pltpu.VMEM)
        extra = {} if grid is None else {"grid": grid}
        out = pl.pallas_call(
            body,
            out_shape=[jax.ShapeDtypeStruct(s, F32) for s in out_shapes],
            in_specs=[smem] * (1 + len(scalars)) + (in_specs or [held] * len(arrays)),
            out_specs=out_specs or [held] * len(out_shapes),
            scratch_shapes=list(scratch),
            compiler_params=pltpu.CompilerParams(vmem_limit_bytes=vmem * MB),
            cost_estimate=pl.CostEstimate(flops=1000, bytes_accessed=1000, transcendentals=0),
            name=name,
            **extra,
        )(self.flags, *scalars, *arrays)
        out = list(out)
        out[0] = self.after(out[0])
        return out


def coefficient(ref, z, a, b, p):
    return ref[pl.ds(((z * V + a) * V + b) * 2 + p, 1), :]


def split_left(matrix):
    high = matrix.astype(BF16).astype(F32)
    place = lax.broadcasted_iota(jnp.int32, matrix.shape, 1)
    return jnp.where(place < 2 * DEPTH, high, matrix - high).astype(BF16)


def lag_matrix(basis, turned, trig, sign):
    half = turned.shape[0] // 2
    count = (half - 4) // 8 * 8
    cosine, sine = turned[:half], turned[half:]
    turn, cross = trig[:count, :1], trig[count : 2 * count, :1] * sign
    right = jnp.concatenate(
        [
            turn * cosine[:count] + cross * sine[:count],
            turn * sine[:count] - cross * cosine[:count],
            cosine[count:],
        ],
        axis=0,
    )
    return jnp.dot(basis, right, preferred_element_type=F32, precision=lax.Precision.HIGHEST)


def over_instants(left, cells):
    whole = jnp.concatenate(cells, axis=1)
    if whole.shape[0] < DEPTH:
        whole = jnp.concatenate(
            [whole, jnp.zeros((DEPTH - whole.shape[0], whole.shape[1]), F32)], axis=0
        )
    high = whole.astype(BF16)
    low = (whole - high.astype(F32)).astype(BF16)
    product = jnp.dot(
        left, jnp.concatenate([high, low, high], axis=0), preferred_element_type=F32
    )
    return [product[:, i * LANES : (i + 1) * LANES] for i in range(len(cells))]


def split_cells(st, slab, first_cell, last_cell, xn, xf):
    p = lax.axis_index("pitch") % 2
    edge = first_cell.shape[0]
    zeros = jnp.zeros((8, LANES), F32)
    width = 4 * NT

    def step(i, carry):
        slab[pl.ds(i * width, width), :] = st[pl.ds(i * 2 * width + p, width, stride=2), :]
        return carry

    lax.fori_loop(0, LEAD * V // 4, step, 0)
    first_cell[...] = st[0:edge, :]
    last_cell[...] = st[st.shape[0] - edge :, :]

    def separate(z, carry):
        for v in range(V):
            j = z * V + v
            for out, q in ((xn, 1 - p), (xf, p)):
                out[j, PAD - 8 : PAD, :] = zeros
                out[j, 0:NT, :] = st[pl.ds(j * 2 * NT + q, NT, stride=2), :]
        return carry

    lax.fori_loop(0, xn.shape[0] // V, separate, 0)


def lags(blades, harmonic, trig):
    count = harmonic.shape[0]
    rotor = jnp.full(harmonic.shape, blades[0]).astype(F32)
    stator = jnp.full(harmonic.shape, blades[1]).astype(F32)
    turns = harmonic[...] * stator
    lag = (turns - rotor * jnp.floor(turns / rotor)) / rotor * (2.0 * math.pi)
    trig[0:count, :] = jnp.cos(lag)
    trig[count : 2 * count, :] = jnp.sin(lag)
    trig[2 * count : 2 * count + 8, :] = (stator / rotor / count)[:8]


def prepare(flags, blades, xf, harmonic, basis, turned, trig, *chunks):
    lags(blades, harmonic, trig)
    wrap = flags[1]
    cells = xf.shape[0] // V
    sign = jnp.where(flags[2] == 1, 1.0, -1.0)
    left = split_left(lag_matrix(basis[...], turned[...], trig[...], sign))

    def step(z, carry):
        raw = [xf[z * V + v] for v in range(V)]
        lagged = over_instants(left, raw)
        for v in range(V):
            value = jnp.where(wrap == 1, lagged[v], raw[v])
            j = (z - LEAD) * V + v
            for out, ((first, last), extra) in zip(chunks, CHUNKS):
                width = last - first
                out[pl.ds(pl.multiple_of(j * width, 8), width), :] = value[first:last]
                if extra:
                    out[pl.ds((cells - LEAD) * V * width + j, 1), :] = value[NT - 1 : NT]
        return carry

    lax.fori_loop(LEAD, cells, step, 0)


def keep_tiles(ref, offset, values, first, last, height):
    for a in range(V):
        for t in range(first // 8, last // 8):
            ref[offset + a * height + t] = values[a][t * 8 - first : t * 8 - first + 8]


def sweeps(source, g, fg, offset, spans, p, inverse, lower, upper, cells):
    height = g.shape[1] // 8
    for first, last in spans:
        nothing = tuple(jnp.zeros((last - first, LANES), F32) for _ in range(V))

        def ahead(z, current, first=first, last=last):
            right = source(z, first, last)
            result = []
            for a in range(V):
                total = coefficient(inverse, z, a, 0, p) * right[0]
                for b in range(1, V):
                    total += coefficient(inverse, z, a, b, p) * right[b]
                for b in range(V):
                    total += coefficient(lower, z, a, b, p) * current[b]
                g[z * V + a, first:last, :] = total
                result.append(total)
            return tuple(result)

        out = lax.fori_loop(0, cells, ahead, nothing)
        keep_tiles(fg, offset, out, first, last, height)

        def back(i, current, first=first, last=last):
            z = cells - 1 - i
            result = []
            for a in range(V):
                total = g[z * V + a, first:last, :]
                for b in range(V):
                    total += coefficient(upper, z, a, b, p) * current[b]
                g[z * V + a, first:last, :] = total
                result.append(total)
            return tuple(result)

        out = lax.fori_loop(0, cells, back, nothing)
        keep_tiles(fg, offset + V * height, out, first, last, height)


def take_edges(edges, from_left, from_right, p):
    skip = from_left.shape[0] - V * NT * 2
    for v in range(V):
        edges[v, PAD - 8 : PAD, :] = jnp.zeros((8, LANES), F32)
        edges[v, 0:NT, :] = from_left[pl.ds(skip + v * 2 * NT + p, NT, stride=2), :]
        edges[V + v, PAD - 8 : PAD, :] = jnp.zeros((8, LANES), F32)
        edges[V + v, 0:NT, :] = from_right[pl.ds(v * 2 * NT + p, NT, stride=2), :]


def residuals(x, other, halo, edges, advect, viscous, left, p, cells, put):
    def one(z, above, below):
        here = [x[z * V + v] for v in range(V)]
        timing = over_instants(left, here)
        for v in range(V):
            j = z * V + v
            pitch = other[j] - 2.0 * here[v]
            if halo is not None:
                pitch += halo[j]
            put(
                j,
                advect[pl.ds(j * 2 + p, 1), :] * (above(z, v) - below(z, v))
                + viscous[pl.ds(j * 2 + p, 1), :] * pitch
                - timing[v],
            )

    inner_above = lambda z, v: x[(z - 1) * V + v]
    inner_below = lambda z, v: x[(z + 1) * V + v]
    one(0, lambda z, v: edges[v], inner_below)

    def step(z, carry):
        one(z, inner_above, inner_below)
        return carry

    lax.fori_loop(1, cells - 1, step, 0)
    one(cells - 1, inner_above, lambda z, v: edges[V + v])


def timing_matrix(table, trig):
    return split_left(table[...] * trig[trig.shape[0] - 8 : trig.shape[0] - 7, :1])


def near_cell(
    flags, xn, xf, halo, from_left, from_right, advect, viscous, inverse, lower, upper, trig, table,
    g, flows, right, edges,
):
    p = 1 - flags[0]
    cells = xn.shape[0] // V
    take_edges(edges, from_left, from_right, p)

    def put(j, value):
        right[j] = value

    residuals(xn, xf, halo, edges, advect, viscous, timing_matrix(table, trig), p, cells, put)
    source = lambda z, first, last: [right[z * V + v, first:last, :] for v in range(V)]
    sweeps(source, g, flows, 0, ((0, 32), (32, PAD)), p, inverse, lower, upper, cells)


def far_base(flags, xn, xf, from_left, from_right, advect, viscous, trig, table, base, edges):
    p = flags[0]
    cells = xn.shape[0] // V
    take_edges(edges, from_left, from_right, p)

    def put(j, value):
        base[j] = value

    residuals(xf, xn, None, edges, advect, viscous, timing_matrix(table, trig), p, cells, put)


def far_lead(flags, slab, trig, basis, turned, lead, halo):
    wrap = flags[1]
    sign = jnp.where(flags[2] == 1, -1.0, 1.0)
    left = split_left(lag_matrix(basis[...], turned[...], trig[...], sign))
    for z in range(LEAD):
        for v in range(V):
            halo[v, PAD - 8 : PAD, :] = jnp.zeros((8, LANES), F32)
            halo[v, 0:NT, :] = slab[pl.ds((z * V + v) * NT, NT), :]
        raw = [halo[v] for v in range(V)]
        lagged = over_instants(left, raw)
        for v in range(V):
            lead[z * V + v] = jnp.where(wrap == 1, lagged[v], raw[v])


def far_chunk(chunk, flags, base, lead, halo, viscous, inverse, lower, upper, *refs):
    others, (g, fg) = refs[:-2], refs[-2:]
    (first, last), extra = chunk
    width = last - first
    p = flags[0]
    cells = base.shape[0] // V
    top = lax.broadcasted_iota(jnp.int32, (8, LANES), 0) == 0
    offset = 0
    for other in others:
        fg[0 : other.shape[0]] = other[...]
        offset = other.shape[0]

    def pieces(ref, j, rows):
        value = ref[j, first:last, :]
        return jnp.concatenate([value, ref[j, PAD - 8 : PAD, :]], axis=0) if extra else value

    def source(z, start, stop):
        result = []
        for v in range(V):
            j = z * V + v
            h = jnp.maximum(z - LEAD, 0) * V + v
            arrived = halo[pl.ds(pl.multiple_of(h * width, 8), width), :]
            if extra:
                row = halo[pl.ds((cells - LEAD) * V * width + h, 1), :]
                arrived = jnp.concatenate([arrived, jnp.where(top, row, 0.0)], axis=0)
            early = pieces(lead, jnp.minimum(z, LEAD - 1) * V + v, rows)
            arrived = jnp.where(z >= LEAD, arrived, early)
            result.append(pieces(base, j, rows) + viscous[pl.ds(j * 2 + p, 1), :] * arrived)
        return result

    height = rows_of(chunk)
    sweeps(source, g, fg, offset, ((0, height),), p, inverse, lower, upper, cells)


def times(matrix, vector):
    result = []
    for a in range(V):
        total = matrix(a, 0) * vector[0]
        for b in range(1, V):
            total += matrix(a, b) * vector[b]
        result.append(total)
    return result


def plus(one, two):
    return [a + b for a, b in zip(one, two)]


def tiles(ref, c, kind):
    return [ref[c, kind * V + a] for a in range(V)]


def rows(ref, c, kind):
    return lambda a, b: ref[c, kind * V + a, b : b + 1, :]


def unit(a):
    place = lax.broadcasted_iota(jnp.int32, (8, LANES), 0)
    return jnp.where(place == a, 1.0, 0.0).astype(F32)


def transfer(flags, lower, upper, blocks, group, forward):
    cells = blocks.shape[1] // V
    for c in range(2):
        p = 1 - flags[0] if c == 0 else flags[0]

        def ahead(z, current):
            result = times(lambda a, b: coefficient(lower, z, a, b, p), current)
            for a in range(V):
                forward[z * V + a] = result[a]
            return tuple(result)

        through = lax.fori_loop(0, cells, ahead, tuple(unit(a) for a in range(V)))

        def back(i, current):
            z = cells - 1 - i
            result = times(lambda a, b: coefficient(upper, z, a, b, p), current)
            for a in range(V):
                result[a] = result[a] + jnp.concatenate(
                    [forward[z * V + a], jnp.zeros((8, LANES), F32)], axis=0
                )
                blocks[c, z * V + a] = result[a]
            return tuple(result)

        start = tuple(
            jnp.concatenate([jnp.zeros((8, LANES), F32), unit(a)], axis=0) for a in range(V)
        )
        ends = lax.fori_loop(0, cells, back, start)
        for a in range(V):
            group[c, a] = ends[a][:8]
            group[c, V + a] = ends[a][8:]
            group[c, 2 * V + a] = through[a]


def merge_matrices(bit, levels, flags, *refs):
    start, last = bit == 0, bit == levels - 1
    refs = list(refs)
    mine, other = refs.pop(0), refs.pop(0)
    share = None if start else refs.pop(0)
    mats = refs.pop(0)
    merged, share_out = (None, None) if last else refs
    right = flags[3 + bit] == 1
    left = jnp.logical_not(right)
    nothing = jnp.zeros((8, LANES), F32)
    for c in range(2):
        pick = lambda kind, own: [jnp.where(own, m, t) for m, t in zip(tiles(mine, c, kind), tiles(other, c, kind))]
        if start:
            own = [[unit(a) for a in range(V)], [nothing] * V, [unit(a) for a in range(V)]]
        else:
            own = [tiles(share, c, kind) for kind in range(3)]
        found = [
            (1, pick(0, right)),
            (3, [jnp.where(right, x, nothing) for x in own[0]]),
            (4, [jnp.where(right, x, nothing) for x in own[1]]),
            (5, [jnp.where(right, nothing, x) for x in own[2]]),
        ]
        if not last:
            found += [(0, pick(2, right)), (2, pick(1, left))]
        for kind, values in found:
            for a in range(V):
                mats[c, kind * V + a] = values[a]
        if last:
            continue
        p_left, g_left, h_right = pick(2, left), pick(0, left), pick(1, right)
        turned = times(rows(mats, c, 1), p_left)
        new = [plus(g_left, times(rows(mats, c, 2), turned))]
        if bit < levels - 2:
            new += [times(rows(mats, c, 2), h_right), times(rows(mats, c, 0), p_left)]
        for kind, values in enumerate(new):
            for a in range(V):
                merged[c, kind * V + a] = values[a]
        s0 = times(rows(mats, c, 3), p_left)
        s1 = times(rows(mats, c, 4), p_left)
        s1b = times(rows(mats, c, 5), turned)
        s2 = times(rows(mats, c, 5), h_right)
        for a in range(V):
            share_out[c, a] = jnp.where(right, s0[a], own[0][a])
            share_out[c, V + a] = jnp.where(right, s1[a], own[1][a] + s1b[a])
            share_out[c, 2 * V + a] = jnp.where(right, own[2][a], s2[a])


def inflow_of(c, mats, f_left, g_right, known):
    back = plus(g_right, times(rows(mats, c, 1), f_left))
    from_left = times(rows(mats, c, 3), f_left)
    from_right = plus(times(rows(mats, c, 4), f_left), times(rows(mats, c, 5), back))
    total = from_left + from_right
    return back, total if known is None else plus(known, total)


def merge_flows(parts, bit, levels, flags, mats, flows, other, *refs):
    known, merged, inflow = (None, *refs) if bit == 0 else refs
    right, last_right = flags[3 + bit] == 1, flags[2 + levels] == 1
    last = bit == levels - 2
    start = 0
    for c, height in parts:

        def tile(t, carry, c=c, height=height, start=start):
            at = lambda i: start * 2 * V + i * height + t
            mine = [flows[at(i)] for i in range(2 * V)]
            theirs = [other[at(i)] for i in range(2 * V)]
            f_left = [jnp.where(right, y, x) for x, y in zip(mine[:V], theirs[:V])]
            f_right = [jnp.where(right, x, y) for x, y in zip(mine[:V], theirs[:V])]
            g_left = [jnp.where(right, y, x) for x, y in zip(mine[V:], theirs[V:])]
            g_right = [jnp.where(right, x, y) for x, y in zip(mine[V:], theirs[V:])]
            before = None if known is None else [known[at(i)] for i in range(2 * V)]
            back, total = inflow_of(c, mats, f_left, g_right, before)
            new_f = plus(f_right, times(rows(mats, c, 0), f_left))
            new_g = plus(g_left, times(rows(mats, c, 2), back))
            if last:
                for i in range(V):
                    end = jnp.where(last_right, new_g[i], new_f[i])
                    merged[start * V + i * height + t] = end
            else:
                for i, value in enumerate(new_f + new_g):
                    merged[at(i)] = value
            for i, value in enumerate(total):
                inflow[at(i)] = value
            return carry

        lax.fori_loop(0, height, tile, 0)
        start += height


def last_inflow(right, c, mats, ends, other, known, start, height, inflow):
    for t in range(height):
        mine = [ends[start * V + a * height + t] for a in range(V)]
        theirs = [other[start * V + a * height + t] for a in range(V)]
        f_left = [jnp.where(right, y, x) for x, y in zip(mine, theirs)]
        g_right = [jnp.where(right, x, y) for x, y in zip(mine, theirs)]
        before = [known[start * 2 * V + i * height + t] for i in range(2 * V)]
        _, total = inflow_of(c, mats, f_left, g_right, before)
        for i, value in enumerate(total):
            inflow[i, t * 8 : t * 8 + 8, :] = value


def corrected(c, z, a, first, last, g, blocks, inflow):
    total = g[z * V + a, first:last, :]
    for b in range(V):
        total += blocks[c, z * V + a, b : b + 1, :] * inflow[b]
        total += blocks[c, z * V + a, 8 + b : 9 + b, :] * inflow[V + b]
    return total


def correct(parts, levels, flags, mats, ends, other, known, blocks, *refs):
    solved, results, inflow = refs[: len(parts)], refs[len(parts) : -1], refs[-1]
    right = flags[2 + levels] == 1
    start = 0
    for (c, tall), g, result in zip(parts, solved, results):
        last_inflow(right, c, mats, ends, other, known, start, tall, inflow)
        start += tall
        height = tall * 8
        for first, last in ((0, 32), (32, height)) if height > 32 else ((0, height),):
            flow = tuple(inflow[i, first:last, :] for i in range(2 * V))

            def step(z, flow, c=c, first=first, last=last, g=g, result=result):
                for a in range(V):
                    result[z * V + a, first:last, :] = corrected(c, z, a, first, last, g, blocks, flow)
                return flow

            lax.fori_loop(0, g.shape[0] // V, step, flow)


def finish(levels, flags, mats, ends, other, known, g, blocks, near, *refs):
    done, out, inflow = refs[:-2], refs[-2], refs[-1]
    right = flags[2 + levels] == 1
    p = flags[0]
    first_row, last_row = CHUNKS[-1][0]
    width = last_row - first_row

    @pl.when(pl.program_id(0) == 0)
    def _():
        last_inflow(right, 1, mats, ends, other, known, 0, width // 8, inflow)

    flow = tuple(inflow[i] for i in range(2 * V))

    def step(z, carry):
        for a in range(V):
            j = z * V + a
            row = j * 2 * NT
            out[pl.ds(row + 1 - p, NT, stride=2), :] = near[j, 0:NT, :]
            for ref, ((first, last), extra) in zip(done, CHUNKS):
                out[pl.ds(row + p + 2 * first, last - first, stride=2), :] = ref[j, 0 : last - first, :]
                if extra:
                    out[pl.ds(row + p + 2 * (NT - 1), 1), :] = ref[j, last - first : last - first + 1, :]
            out[pl.ds(row + p + 2 * first_row, width, stride=2), :] = corrected(1, z, a, 0, width, g, blocks, flow)
        return carry

    lax.fori_loop(0, g.shape[0] // V, step, 0)


def phase_tables(count):
    angle = 2.0 * math.pi * np.outer(np.arange(1, count + 1), np.arange(NT)) / NT
    cosine, sine = np.cos(angle), np.sin(angle)
    basis = np.zeros((PAD, 2 * count + 8), np.float32)
    basis[:NT, :count], basis[:NT, count : 2 * count], basis[:NT, 2 * count] = cosine.T, sine.T, 0.5
    turned = np.zeros((2, count + 8, 3, DEPTH), np.float32)
    turned[0, :count, :, :NT], turned[1, :count, :, :NT] = cosine[:, None], sine[:, None]
    turned[0, count, :, :NT] = 1.0
    return (2.0 / NT * basis).astype(np.float32), turned.reshape(2 * (count + 8), 3 * DEPTH)


def derivative_table():
    gap = np.arange(NT)[:, None] - np.arange(NT)[None, :]
    safe = np.where(gap == 0, 1.0, np.sin(np.pi * gap / NT))
    table = np.where(gap == 0, 0.0, 0.5 * (1.0 - 2.0 * np.mod(gap, 2)) / safe)
    wide = np.zeros((PAD, 3, DEPTH), np.float32)
    wide[:NT, :, :NT] = table[:, None]
    return wide.reshape(PAD, 3 * DEPTH)


def local(state, advect, viscous, inverse, lower, upper, blades, harmonic):
    cells = state.shape[0]
    count = harmonic.shape[0]
    segs, slabs = lax.axis_size("seg"), lax.axis_size("pitch")
    levels = segs.bit_length() - 1
    far_pairs = [(i, (i - 1) % slabs if i % 2 == 0 else (i + 1) % slabs) for i in range(slabs)]
    near_pairs = [(i, i ^ 1) for i in range(slabs)]
    to_far = lambda x: lax.ppermute(x, "pitch", far_pairs)
    to_level = lambda x, k: lax.ppermute(x, "seg", [(i, i ^ (1 << k)) for i in range(segs)])
    x_shape = (cells * V, PAD, LANES)

    st = state.transpose(0, 2, 3, 1, 4).reshape(cells * V * NT * 2, LANES)
    lead_rows, edge_rows = LEAD * V * NT, padded_even(V * NT * 2)
    held = pl.BlockSpec(memory_space=pltpu.VMEM)
    shapes = [(lead_rows, LANES), (edge_rows, LANES), (edge_rows, LANES), x_shape, x_shape]
    slab_out, first_cell, last_cell, xn, xf = pl.pallas_call(
        split_cells,
        out_shape=[jax.ShapeDtypeStruct(x, F32) for x in shapes],
        in_specs=[held],
        out_specs=[held] * 5,
        compiler_params=pltpu.CompilerParams(vmem_limit_bytes=16 * MB),
        name="split_cells",
    )(st)
    halo_near = lax.ppermute(xn, "pitch", near_pairs)
    slab_in = to_far(slab_out)
    from_left = lax.ppermute(last_cell, "seg", [(i, i + 1) for i in range(segs - 1)])
    from_right = lax.ppermute(first_cell, "seg", [(i + 1, i) for i in range(segs - 1)])

    slab, seg = lax.axis_index("pitch"), lax.axis_index("seg")
    side = slab % 2
    wrap = jnp.logical_or(slab == 0, slab == slabs - 1)
    bits = [(seg >> k) & 1 for k in range(levels)]
    run = Chain(
        jnp.stack(
            [side, wrap.astype(jnp.int32), (slab == 0).astype(jnp.int32), *bits]
        ).astype(jnp.int32)
    )
    run.after(slab_out)
    basis, turned = phase_tables(count)
    table = derivative_table()
    wide_harmonic = jnp.broadcast_to(harmonic.astype(F32)[:, None], (count, LANES))

    rest = (cells - LEAD) * V
    chunk_shapes = [
        (rest * (last - first) + (padded_even(rest) if extra else 0), LANES)
        for (first, last), extra in CHUNKS
    ]
    trig, *chunks = run(
        prepare, [(2 * count + 8, LANES), *chunk_shapes], [xf, wide_harmonic, basis, turned],
        scalars=[blades], name="prepare",
    )
    chunks[0], halo_near = lax.optimization_barrier((chunks[0], halo_near))
    arrived = [slab_in]
    for chunk in chunks:
        if len(arrived) >= 2:
            chunk, arrived[-2] = lax.optimization_barrier((chunk, arrived[-2]))
        arrived.append(to_far(chunk))
    slab_in, *arrived = arrived

    flat = lambda x: x.transpose(0, 2, 3, 1, 4).reshape(cells * V * V * 2, LANES)
    inv, low, upp = flat(inverse.astype(F32)), flat(lower), flat(upper)
    adv = advect.transpose(0, 2, 1, 3).reshape(cells * V * 2, LANES)
    vis = viscous.transpose(0, 2, 1, 3).reshape(cells * V * 2, LANES)
    edges = pltpu.VMEM((2 * V, PAD, LANES), F32)

    mats, group, share = [], None, []
    mats_shape = (2, 6 * V, 8, LANES)

    def merge_group(k):
        nonlocal group, share
        shapes = [mats_shape]
        if k < levels - 1:
            shapes += [(2, 3 * V if k < levels - 2 else V, 8, LANES), (2, 3 * V, 8, LANES)]
        out = run(
            functools.partial(merge_matrices, k, levels), shapes,
            [group, to_level(group, k), *share], name="merge_matrices",
        )
        mats.append(out[0])
        if k < levels - 1:
            group, share = out[1], [out[2]]

    def solve_chunk(i, others=()):
        height = rows_of(CHUNKS[i])
        tall = 2 * V * height // 8 + sum(x.shape[0] for x in others)
        g, flows = run(
            functools.partial(far_chunk, CHUNKS[i]), [(cells * V, height, LANES), (tall, 8, LANES)],
            [base, lead, arrived[i], vis, inv, low, upp, *others], name="far_chunk",
        )
        return g, flows

    class Exchange:
        def __init__(self, parts, flows, solved):
            self.parts = [(c, g.shape[1] // 8) for c, g in zip(parts, solved)]
            self.flows, self.known, self.solved, self.level = flows, [], solved, 0

        def step(self):
            tall = sum(h for _, h in self.parts)
            k = self.level
            out = run(
                functools.partial(merge_flows, self.parts, k, levels),
                [((2 if k < levels - 2 else 1) * V * tall, 8, LANES), (2 * V * tall, 8, LANES)],
                [mats[k], self.flows, to_level(self.flows, k), *self.known], name="merge_flows",
            )
            self.flows, self.known, self.level = out[0], [out[1]], k + 1

        def last(self):
            return [mats[-1], self.flows, to_level(self.flows, levels - 1), *self.known]

        def correct(self):
            tall = max(h for _, h in self.parts)
            return run(
                functools.partial(correct, self.parts, levels), [g.shape for g in self.solved],
                [*self.last(), blocks, *self.solved],
                scratch=[pltpu.VMEM((2 * V, tall * 8, LANES), F32)], name="correct",
            )

    blocks, group = run(
        transfer, [(2, cells * V, 16, LANES), (2, 3 * V, 8, LANES)], [low, upp],
        scratch=[pltpu.VMEM((cells * V, 8, LANES), F32)], name="transfer",
    )
    base = run(
        far_base, [x_shape], [xn, xf, from_left, from_right, adv, vis, trig, table],
        scratch=[edges], name="far_base",
    )[0]
    lead = run(
        far_lead, [(LEAD * V, PAD, LANES)], [slab_in, trig, basis, turned],
        scratch=[pltpu.VMEM((V, PAD, LANES), F32)], name="far_lead",
    )[0]
    g_near, flows_near = run(
        near_cell, [x_shape, (2 * V * PAD // 8, 8, LANES)],
        [xn, xf, halo_near, from_left, from_right, adv, vis, inv, low, upp, trig, table],
        scratch=[pltpu.VMEM(x_shape, F32), edges], name="near_cell",
    )
    g_first, flows = solve_chunk(0, [flows_near])
    first = Exchange([0, 1], flows, [g_near, g_first])
    for k in range(levels):
        merge_group(k)
    first.step()
    g, flows = solve_chunk(1)
    second = Exchange([1], flows, [g])
    first.step()
    second.step()
    g, flows = solve_chunk(2)
    third = Exchange([1], flows, [g])
    second.step()
    g, flows = solve_chunk(3)
    fourth = Exchange([1], flows, [g])
    third.step()
    for k in range(levels - 3):
        first.step()
        second.step()
    done_first = first.correct()
    fourth.step()
    done_second = second.correct()
    third.step()
    fourth.step()
    done_third = third.correct()
    for k in range(levels - 3):
        third.step()
        fourth.step()
    near, *done = [*done_first, *done_second, *done_third]
    g_last = fourth.solved[0]

    steps = 4
    part = cells // steps
    whole = lambda x: pl.BlockSpec(x.shape, lambda i: (0,) * x.ndim)
    by_cell = lambda x: pl.BlockSpec((part * V,) + x.shape[1:], lambda i: (i, 0, 0))
    small = fourth.last()
    out = run(
        functools.partial(finish, levels), [st.shape], [*small, g_last, blocks, near, *done],
        grid=(steps,),
        in_specs=[whole(x) for x in small]
        + [by_cell(g_last), pl.BlockSpec((2, part * V, 16, LANES), lambda i: (0, i, 0, 0))]
        + [by_cell(x) for x in (near, *done)],
        out_specs=[pl.BlockSpec((part * V * NT * 2, LANES), lambda i: (i, 0))],
        scratch=[pltpu.VMEM((2 * V, rows_of(CHUNKS[-1]), LANES), F32)], name="finish",
    )[0]
    return out.reshape(cells, V, NT, 2, LANES).transpose(0, 3, 1, 2, 4)


def solution(mesh):
    cell = P("seg", "pitch", None, None, None)
    return jax.shard_map(
        local,
        mesh=mesh,
        in_specs=(cell, P("seg", "pitch", None, None), P("seg", "pitch", None, None), cell, cell, cell, P(), P()),
        out_specs=cell,
        check_vma=False,
    )
```

time: 110 us -> 108 us (0.982)
  waiting for transfers between devices: 35.5 us -> 24.6 us
  Pallas kernels: 35.6 us -> 43.9 us
  starting transfers between devices: 33 us -> 34.8 us
  between operations: 1.6 us -> 0.28 us
    pallas_call x20 -> x24, Pallas kernels: 35.6 us -> 41.7 us  [__call__(): pl.pallas_call(body, out_shape=[jax.ShapeDtypeStruct(s, F32) for s in out...]
    ppermute x4 -> x5, waiting for transfers between devices: 5.21 us -> 0.01 us  [local(): to_far = lambda x: lax.ppermute(x, 'pitch', far_pairs)]
    ppermute x1, waiting for transfers between devices: 8.42 us -> 3.33 us  [local(): lax.ppermute(last_cell, 'seg', [(i, i + 1) for i in range(segs - 1)])]
    ppermute x4 -> x5, starting transfers between devices: 1.98 us -> 4.45 us  [local(): to_far = lambda x: lax.ppermute(x, 'pitch', far_pairs)]
    pallas_call x0 -> x1, Pallas kernels: none -> 2.2 us  [local(): pl.pallas_call(split_cells, out_shape=[jax.ShapeDtypeStruct(x, F32) for x...]
    unnamed x20 -> x22, local copies, waits for them, and re-layouts: 2.19 us -> 3.78 us
    slice x1 -> x0, local copies, waits for them, and re-layouts: 1.38 us -> none  [local(): ratio = blades[1].astype(F32) / blades[0].astype(F32)]
    ppermute x12 -> x15, waiting for transfers between devices: 21.9 us -> 21.3 us  [local(): lax.ppermute(x, 'seg', [(i, i ^ 1 << k) for i in range(segs)])]
  transfers between devices with their start and end apart: 19 -> 23, of which waited for: 11 -> 10; matrix products, arithmetic and copies ran while one was open for 0% -> 0% of each run, Pallas kernels for 25% -> 35%
where the time goes in v2:
time: 108 us
  Pallas kernels  43.9 us (41%)
  starting transfers between devices  34.8 us (32%)
  waiting for transfers between devices  24.6 us (23%)
  local copies, waits for them, and re-layouts  3.94 us (4%)
    pallas_call x24, Pallas kernels, __call__(): pl.pallas_call(body, out_shape=[jax.ShapeDtypeStruct(s, F32) for s in out...  41.7 us
    ppermute x15, starting transfers between devices, local(): lax.ppermute(x, 'seg', [(i, i ^ 1 << k) for i in range(segs)])  25.2 us
    ppermute x15, waiting for transfers between devices, local(): lax.ppermute(x, 'seg', [(i, i ^ 1 << k) for i in range(segs)])  21.3 us
    ppermute x5, starting transfers between devices, local(): to_far = lambda x: lax.ppermute(x, 'pitch', far_pairs)  4.45 us
    unnamed x22, local copies, waits for them, and re-layouts  3.78 us
    ppermute x1, starting transfers between devices, local(): lax.ppermute(last_cell, 'seg', [(i, i + 1) for i in range(segs - 1)])  3.4 us
    ppermute x1, waiting for transfers between devices, local(): lax.ppermute(last_cell, 'seg', [(i, i + 1) for i in range(segs - 1)])  3.33 us
    pallas_call x1, Pallas kernels, local(): pl.pallas_call(split_cells, out_shape=[jax.ShapeDtypeStruct(x, F32) for x...  2.2 us
  transfers between devices with their start and end apart: 23, of which 10 were waited for; matrix products, arithmetic and copies ran while one was open for 0% of the time, Pallas kernels for 35%

profile of v2, /device:TPU:0, one launch (start us, length us, event | category | flops | bytes accessed | tf_op | source)
XLA Modules:
  0.0 107.6 jit_solution(6583037191527418499)
XLA Ops:
  0.0 2.2 %copy-done.2 = f32[16,2,5,49,128]{4,1,3,2,0:T(2,128)S(1)} copy-done((f32[16,2,5,49,128]{4,1,3,2,0:T(2,128)S(1)}, f32[16,2,5,49,128]{4,1,3,2,0:T(2,128)}, u32[]{:S(2)}) %copy-start.2) | copy-done | bytes 4014104
  2.2 2.2 %split_cells.1 = (f32[980,128]{1,0:T(8,128)}, f32[496,128]{1,0:T(8,128)}, f32[496,128]{1,0:T(8,128)}, f32[80,56,128]{2,1,0:T(8,128)}, f32[80,56,128]{2,1,0:T(8,128)S(1)}) custom-call(f32[7840,128]{1,0:T(8,128)S(1)} %bitcast.44), custom_call_target="tpu_custom_call" | custom-call | tf_op jit(solution)/shard_map/split_cells/pallas_call | solution.py:570
  4.4 0.5 collective-permute-start.3
  4.8 2.6 %collective-permute-start.2 = (f32[980,128]{1,0:T(8,128)}, f32[980,128]{1,0:T(8,128)}, u32[]{:S(2)}, u32[]{:S(2)}) collective-permute-start(f32[980,128]{1,0:T(8,128)} %get-tuple-element.107), channel_id=1, source_target_pairs={{0,3},{1,2},{2,1},{3,0},{4,7},{5,6},{6,5},{7,4},{8,11},{9,10},{10,... | collective-permute-start | bytes 1505288 | tf_op jit(solution)/shard_map/ppermute | solution.py:562
  7.5 3.4 %collective-permute-start = (f32[496,128]{1,0:T(8,128)}, f32[496,128]{1,0:T(8,128)S(1)}, u32[]{:S(2)}, u32[]{:S(2)}) collective-permute-start(f32[496,128]{1,0:T(8,128)} %get-tuple-element.115), channel_id=1, source_target_pairs={{0,4},{4,8},{8,12},{12,16},{16,20},{20,24},{24,28},{1,5},{5,9},{9,... | collective-permute-start | bytes 761864 | tf_op jit(solution)/shard_map/ppermute | solution.py:580
  10.9 1.3 %collective-permute-start.1 = (f32[496,128]{1,0:T(8,128)}, f32[496,128]{1,0:T(8,128)}, u32[]{:S(2)}, u32[]{:S(2)}) collective-permute-start(f32[496,128]{1,0:T(8,128)} %get-tuple-element.116), channel_id=1, source_target_pairs={{4,0},{8,4},{12,8},{16,12},{20,16},{24,20},{28,24},{5,1},{9,5},{13... | collective-permute-start | bytes 761864 | tf_op jit(solution)/shard_map/ppermute | solution.py:581
  12.2 0.1 stack.35.flags
  12.3 0.1 broadcast_in_dim.2.harmonic
  12.4 0.8 copy-done.5
  13.2 0.7 copy-done.7
  14.0 3.1 %prepare.1 = (f32[56,128]{1,0:T(8,128)S(1)}, f32[480,128]{1,0:T(8,128)S(1)}, f32[960,128]{1,0:T(8,128)S(1)}, f32[1024,128]{1,0:T(8,128)S(1)}, f32[480,128]{1,0:T(8,128)S(1)}) custom-call(s32[6]{0:T(128)S(1)} %stack.35.flags, s32[2]{0:T(128)S(1)} %copy-done.8, f32[80,56,128]{2,1,0:T(8,128)S(1)} %get-tuple-element.109.xf, ...), custom_call_target="tpu_custom_call" | custom-call | flops 1000 | bytes 1000 | tf_op jit(solution)/shard_map/prepare/pallas_call | solution.py:46
  17.0 0.0 collective-permute-done.3.halo
  17.1 0.1 collective-permute-start.4
  17.2 1.6 %transfer.1 = (f32[2,80,16,128]{3,2,1,0:T(8,128)S(1)}, f32[2,15,8,128]{3,2,1,0:T(8,128)S(1)}) custom-call(s32[6]{0:T(128)S(1)} %stack.35.flags, f32[800,128]{1,0:T(8,128)S(1)} %bitcast.27, f32[800,128]{1,0:T(8,128)S(1)} %bitcast.33), custom_call_target="tpu_custom_call" | custom-call | flops 1000 | bytes 1000 | tf_op jit(solution)/shard_map/transfer/pallas_call | solution.py:46
  18.7 0.1 reshape.36
  18.9 3.3 %collective-permute-done.from_left = f32[496,128]{1,0:T(8,128)S(1)} collective-permute-done((f32[496,128]{1,0:T(8,128)}, f32[496,128]{1,0:T(8,128)S(1)}, u32[]{:S(2)}, u32[]{:S(2)}) %collective-permute-start) | collective-permute-done | bytes 253984 | tf_op jit(solution)/shard_map/ppermute | solution.py:580
  22.2 4.6 %far_base.1.base = f32[80,56,128]{2,1,0:T(8,128)S(1)} custom-call(s32[6]{0:T(128)S(1)} %stack.35.flags, f32[80,56,128]{2,1,0:T(8,128)} %get-tuple-element.114.xn, f32[80,56,128]{2,1,0:T(8,128)S(1)} %get-tuple-element.109.xf, f32[496,128]{1,0:T(8,128)S(1)} %collective-permute-done.from_left, f32[496,128]{1,0:T(8,128)} %collective-permute-done.1.from_right, ...), custom_call_target="tpu_custom_call" | custom-call | flops 1000 | bytes 1000 | tf_op jit(solution)/shard_map/far_base/pallas_call | solution.py:46
  26.9 1.7 %far_lead.1.lead = f32[20,56,128]{2,1,0:T(8,128)S(1)} custom-call(s32[6]{0:T(128)S(1)} %stack.35.flags, f32[980,128]{1,0:T(8,128)} %collective-permute-done.2.slab, f32[56,128]{1,0:T(8,128)S(1)} %get-tuple-element.117.trig, f32[56,56]{1,0:T(8,128)S(1)} %copy-done.7, f32[64,192]{1,0:T(8,128)S(1)} %copy-done.5), custom_call_target="tpu_custom_call" | custom-call | flops 1000 | bytes 1000 | tf_op jit(solution)/shard_map/far_lead/pallas_call | solution.py:46
  28.6 8.1 %near_cell.1 = (f32[80,56,128]{2,1,0:T(8,128)S(1)}, f32[70,8,128]{2,1,0:T(8,128)S(1)}) custom-call(s32[6]{0:T(128)S(1)} %stack.35.flags, f32[80,56,128]{2,1,0:T(8,128)} %get-tuple-element.114.xn, f32[80,56,128]{2,1,0:T(8,128)S(1)} %get-tuple-element.109.xf, f32[80,56,128]{2,1,0:T(8,128)} %collective-permute-done.3.halo, ...), custom_call_target="tpu_custom_call" | custom-call | flops 1000 | bytes 1000 | tf_op jit(solution)/shard_map/near_cell/pallas_call | solution.py:46
  36.7 0.0 collective-permute-done.4.halo
  36.7 1.3 %far_chunk.4 = (f32[80,8,128]{2,1,0:T(8,128)S(1)}, f32[80,8,128]{2,1,0:T(8,128)S(1)}) custom-call(s32[6]{0:T(128)S(1)} %stack.35.flags, f32[80,56,128]{2,1,0:T(8,128)S(1)} %far_base.1.base, f32[20,56,128]{2,1,0:T(8,128)S(1)} %far_lead.1.lead, f32[480,128]{1,0:T(8,128)S(1)} %collective-permute-done.4.halo, f32[160,128]{1,0:T(8,128)S(1)} %bitcast.47, ...), custom_call_target="tpu_custom_call" | custom-call | flops 1000 | bytes 1000 | tf_op jit(solution)/shard_map/far_chunk/pallas_call | solution.py:46
  38.0 2.4 %collective-permute-start.8 = (f32[80,8,128]{2,1,0:T(8,128)S(1)}, f32[80,8,128]{2,1,0:T(8,128)S(1)}, u32[]{:S(2)}, u32[]{:S(2)}) collective-permute-start(f32[80,8,128]{2,1,0:T(8,128)S(1)} %get-tuple-element.145.flows), channel_id=1, source_target_pairs={{0,4},{4,0},{8,12},{12,8},{16,20},{20,16},{24,28},{28,24},{1,5},{5... | collective-permute-start | bytes 983048 | tf_op jit(solution)/shard_map/ppermute | solution.py:563
  40.4 0.1 collective-permute-start.5
  40.5 1.7 %collective-permute-start.12 = (f32[1024,128]{1,0:T(8,128)S(1)}, f32[1024,128]{1,0:T(8,128)S(1)}, u32[]{:S(2)}, u32[]{:S(2)}) collective-permute-start(f32[1024,128]{1,0:T(8,128)S(1)} %get-tuple-element.161), channel_id=1, source_target_pairs={{0,3},{1,2},{2,1},{3,0},{4,7},{5,6},{6,5},{7,4},{8,11},{9,10},{10,... | collective-permute-start | bytes 1572872 | tf_op jit(solution)/shard_map/ppermute | solution.py:562
  42.2 7.9 %collective-permute-done.5.refs_1_ = f32[2,15,8,128]{3,2,1,0:T(8,128)S(1)} collective-permute-done((f32[2,15,8,128]{3,2,1,0:T(8,128)S(1)}, f32[2,15,8,128]{3,2,1,0:T(8,128)S(1)}, u32[]{:S(2)}, u32[]{:S(2)}) %collective-permute-start.5) | collective-permute-done | bytes 122912 | tf_op jit(solution)/shard_map/ppermute | solution.py:563
  50.2 0.7 merge_matrices.3
  50.8 3.7 %collective-permute-start.6 = (f32[2,15,8,128]{3,2,1,0:T(8,128)S(1)}, f32[2,15,8,128]{3,2,1,0:T(8,128)S(1)}, u32[]{:S(2)}, u32[]{:S(2)}) collective-permute-start(f32[2,15,8,128]{3,2,1,0:T(8,128)S(1)} %get-tuple-element.137.refs_0_), channel_id=1, source_target_pairs={{0,8},{4,12},{8,0},{12,4},{16,24},{20,28},{24,16},{28,20},{1,9},{5... | collective-permute-start | bytes 368648 | tf_op jit(solution)/shard_map/ppermute | solution.py:563
  54.5 2.9 %collective-permute-done.6.refs_1_ = f32[2,15,8,128]{3,2,1,0:T(8,128)S(1)} collective-permute-done((f32[2,15,8,128]{3,2,1,0:T(8,128)S(1)}, f32[2,15,8,128]{3,2,1,0:T(8,128)S(1)}, u32[]{:S(2)}, u32[]{:S(2)}) %collective-permute-start.6) | collective-permute-done | bytes 122912 | tf_op jit(solution)/shard_map/ppermute | solution.py:563
  57.4 0.7 merge_matrices.4
  58.0 3.1 %collective-permute-start.7 = (f32[2,5,8,128]{3,2,1,0:T(8,128)S(1)}, f32[2,5,8,128]{3,2,1,0:T(8,128)S(1)}, u32[]{:S(2)}, u32[]{:S(2)}) collective-permute-start(f32[2,5,8,128]{3,2,1,0:T(8,128)S(1)} %get-tuple-element.141.refs_0_), channel_id=1, source_target_pairs={{0,16},{4,20},{8,24},{12,28},{16,0},{20,4},{24,8},{28,12},{1,17},{... | collective-permute-start | bytes 122888 | tf_op jit(solution)/shard_map/ppermute | solution.py:563
  61.1 2.0 %collective-permute-done.7.refs_1_ = f32[2,5,8,128]{3,2,1,0:T(8,128)S(1)} collective-permute-done((f32[2,5,8,128]{3,2,1,0:T(8,128)S(1)}, f32[2,5,8,128]{3,2,1,0:T(8,128)S(1)}, u32[]{:S(2)}, u32[]{:S(2)}) %collective-permute-start.7) | collective-permute-done | bytes 40992 | tf_op jit(solution)/shard_map/ppermute | solution.py:563
  63.1 0.6 merge_matrices.5.mats
  63.7 0.9 merge_flows.8
  64.6 2.0 %collective-permute-start.10 = (f32[80,8,128]{2,1,0:T(8,128)S(1)}, f32[80,8,128]{2,1,0:T(8,128)S(1)}, u32[]{:S(2)}, u32[]{:S(2)}) collective-permute-start(f32[80,8,128]{2,1,0:T(8,128)S(1)} %get-tuple-element.154.flows), channel_id=1, source_target_pairs={{0,8},{4,12},{8,0},{12,4},{16,24},{20,28},{24,16},{28,20},{1,9},{5... | collective-permute-start | bytes 983048 | tf_op jit(solution)/shard_map/ppermute | solution.py:563
  66.6 1.5 %far_chunk.5 = (f32[80,16,128]{2,1,0:T(8,128)S(1)}, f32[20,8,128]{2,1,0:T(8,128)S(1)}) custom-call(s32[6]{0:T(128)S(1)} %stack.35.flags, f32[80,56,128]{2,1,0:T(8,128)S(1)} %far_base.1.base, f32[20,56,128]{2,1,0:T(8,128)S(1)} %far_lead.1.lead, f32[960,128]{1,0:T(8,128)S(1)} %collective-permute-done.9.halo, f32[160,128]{1,0:T(8,128)S(1)} %bitcast.48, ...), custom_call_target="tpu_custom_call" | custom-call | flops 1000 | bytes 1000 | tf_op jit(solution)/shard_map/far_chunk/pallas_call | solution.py:46
  68.2 0.4 collective-permute-start.11
  68.5 3.3 %collective-permute-done.10.other = f32[80,8,128]{2,1,0:T(8,128)S(1)} collective-permute-done((f32[80,8,128]{2,1,0:T(8,128)S(1)}, f32[80,8,128]{2,1,0:T(8,128)S(1)}, u32[]{:S(2)}, u32[]{:S(2)}) %collective-permute-start.10) | collective-permute-done | bytes 327712 | tf_op jit(solution)/shard_map/ppermute | solution.py:563
  71.8 1.0 merge_flows.9
  72.7 0.4 collective-permute-done.11.other
  73.2 0.6 merge_flows.10
  73.8 2.0 %far_chunk.6 = (f32[80,24,128]{2,1,0:T(8,128)S(1)}, f32[30,8,128]{2,1,0:T(8,128)S(1)}) custom-call(s32[6]{0:T(128)S(1)} %stack.35.flags, f32[80,56,128]{2,1,0:T(8,128)S(1)} %far_base.1.base, f32[20,56,128]{2,1,0:T(8,128)S(1)} %far_lead.1.lead, f32[1024,128]{1,0:T(8,128)S(1)} %collective-permute-done.12.halo, f32[160,128]{1,0:T(8,128)S(1)} %bitcast.49, ...), custom_call_target="tpu_custom_call" | custom-call | flops 1000 | bytes 1000 | tf_op jit(solution)/shard_map/far_chunk/pallas_call | solution.py:46
  75.8 0.4 collective-permute-start.15
  76.2 1.5 %collective-permute-start.13 = (f32[20,8,128]{2,1,0:T(8,128)S(1)}, f32[20,8,128]{2,1,0:T(8,128)S(1)}, u32[]{:S(2)}, u32[]{:S(2)}) collective-permute-start(f32[20,8,128]{2,1,0:T(8,128)S(1)} %get-tuple-element.164.flows), channel_id=1, source_target_pairs={{0,8},{4,12},{8,0},{12,4},{16,24},{20,28},{24,16},{28,20},{1,9},{5... | collective-permute-start | bytes 245768 | tf_op jit(solution)/shard_map/ppermute | solution.py:563
  77.7 2.9 %collective-permute-start.16 = (f32[40,8,128]{2,1,0:T(8,128)S(1)}, f32[40,8,128]{2,1,0:T(8,128)S(1)}, u32[]{:S(2)}, u32[]{:S(2)}) collective-permute-start(f32[40,8,128]{2,1,0:T(8,128)S(1)} %get-tuple-element.175.ends), channel_id=1, source_target_pairs={{0,16},{4,20},{8,24},{12,28},{16,0},{20,4},{24,8},{28,12},{1,17},{... | collective-permute-start | bytes 491528 | tf_op jit(solution)/shard_map/ppermute | solution.py:563
  80.6 1.9 %collective-permute-done.13.other = f32[20,8,128]{2,1,0:T(8,128)S(1)} collective-permute-done((f32[20,8,128]{2,1,0:T(8,128)S(1)}, f32[20,8,128]{2,1,0:T(8,128)S(1)}, u32[]{:S(2)}, u32[]{:S(2)}) %collective-permute-start.13) | collective-permute-done | bytes 81952 | tf_op jit(solution)/shard_map/ppermute | solution.py:563
  82.5 0.7 merge_flows.11
  83.2 1.3 %far_chunk.7 = (f32[80,8,128]{2,1,0:T(8,128)S(1)}, f32[10,8,128]{2,1,0:T(8,128)S(1)}) custom-call(s32[6]{0:T(128)S(1)} %stack.35.flags, f32[80,56,128]{2,1,0:T(8,128)S(1)} %far_base.1.base, f32[20,56,128]{2,1,0:T(8,128)S(1)} %far_lead.1.lead, f32[480,128]{1,0:T(8,128)S(1)} %collective-permute-done.14.halo, f32[160,128]{1,0:T(8,128)S(1)} %bitcast.50, ...), custom_call_target="tpu_custom_call" | custom-call | flops 1000 | bytes 1000 | tf_op jit(solution)/shard_map/far_chunk/pallas_call | solution.py:46
  84.4 0.7 merge_flows.12
  85.1 0.4 collective-permute-start.19
  85.5 1.9 %collective-permute-start.17 = (f32[10,8,128]{2,1,0:T(8,128)S(1)}, f32[10,8,128]{2,1,0:T(8,128)S(1)}, u32[]{:S(2)}, u32[]{:S(2)}) collective-permute-start(f32[10,8,128]{2,1,0:T(8,128)S(1)} %get-tuple-element.182.flows), channel_id=1, source_target_pairs={{0,4},{4,0},{8,12},{12,8},{16,20},{20,16},{24,28},{28,24},{1,5},{5... | collective-permute-start | bytes 122888 | tf_op jit(solution)/shard_map/ppermute | solution.py:563
  87.4 2.8 %collective-permute-start.18 = (f32[10,8,128]{2,1,0:T(8,128)S(1)}, f32[10,8,128]{2,1,0:T(8,128)S(1)}, u32[]{:S(2)}, u32[]{:S(2)}) collective-permute-start(f32[10,8,128]{2,1,0:T(8,128)S(1)} %get-tuple-element.185.ends), channel_id=1, source_target_pairs={{0,16},{4,20},{8,24},{12,28},{16,0},{20,4},{24,8},{28,12},{1,17},{... | collective-permute-start | bytes 122888 | tf_op jit(solution)/shard_map/ppermute | solution.py:563
  90.1 3.0 %correct.3 = (f32[80,56,128]{2,1,0:T(8,128)S(1)}, f32[80,8,128]{2,1,0:T(8,128)S(1)}) custom-call(s32[6]{0:T(128)S(1)} %stack.35.flags, f32[2,30,8,128]{3,2,1,0:T(8,128)S(1)} %merge_matrices.5.mats, f32[40,8,128]{2,1,0:T(8,128)S(1)} %get-tuple-element.175.ends, f32[40,8,128]{2,1,0:T(8,128)S(1)} %collective-permute-done.16.other, ...), custom_call_target="tpu_custom_call" | custom-call | flops 1000 | bytes 1000 | tf_op jit(solution)/shard_map/correct/pallas_call | solution.py:46
  93.1 0.6 merge_flows.13
  93.7 1.2 %correct.4.refs_1_ = f32[80,16,128]{2,1,0:T(8,128)S(1)} custom-call(s32[6]{0:T(128)S(1)} %stack.35.flags, f32[2,30,8,128]{3,2,1,0:T(8,128)S(1)} %merge_matrices.5.mats, f32[10,8,128]{2,1,0:T(8,128)S(1)} %get-tuple-element.185.ends, f32[10,8,128]{2,1,0:T(8,128)S(1)} %collective-permute-done.18.other, f32[20,8,128]{2,1,0:T(8,128)S(1)} %get-tuple-element.186.known, ...), custom_call_target="tpu_custom_call" | custom-call | flops 1000 | bytes 1000 | tf_op jit(solution)/shard_map/correct/pallas_call | solution.py:46
  94.9 0.9 collective-permute-start.20
  95.8 0.7 merge_flows.14
  96.5 1.4 %collective-permute-start.21 = (f32[15,8,128]{2,1,0:T(8,128)S(1)}, f32[15,8,128]{2,1,0:T(8,128)S(1)}, u32[]{:S(2)}, u32[]{:S(2)}) collective-permute-start(f32[15,8,128]{2,1,0:T(8,128)S(1)} %get-tuple-element.197.ends), channel_id=1, source_target_pairs={{0,16},{4,20},{8,24},{12,28},{16,0},{20,4},{24,8},{28,12},{1,17},{... | collective-permute-start | bytes 184328 | tf_op jit(solution)/shard_map/ppermute | solution.py:563
  97.9 1.1 %collective-permute-done.20.other = f32[10,8,128]{2,1,0:T(8,128)S(1)} collective-permute-done((f32[10,8,128]{2,1,0:T(8,128)S(1)}, f32[10,8,128]{2,1,0:T(8,128)S(1)}, u32[]{:S(2)}, u32[]{:S(2)}) %collective-permute-start.20) | collective-permute-done | bytes 40992 | tf_op jit(solution)/shard_map/ppermute | solution.py:563
  99.0 0.6 merge_flows.15
  99.6 1.6 %collective-permute-start.22 = (f32[5,8,128]{2,1,0:T(8,128)S(1)}, f32[5,8,128]{2,1,0:T(8,128)S(1)}, u32[]{:S(2)}, u32[]{:S(2)}) collective-permute-start(f32[5,8,128]{2,1,0:T(8,128)S(1)} %get-tuple-element.201.ends), channel_id=1, source_target_pairs={{0,16},{4,20},{8,24},{12,28},{16,0},{20,4},{24,8},{28,12},{1,17},{... | collective-permute-start | bytes 61448 | tf_op jit(solution)/shard_map/ppermute | solution.py:563
  101.2 0.5 collective-permute-done.21.other
  101.7 1.4 %correct.5.refs_2_ = f32[80,24,128]{2,1,0:T(8,128)S(1)} custom-call(s32[6]{0:T(128)S(1)} %stack.35.flags, f32[2,30,8,128]{3,2,1,0:T(8,128)S(1)} %merge_matrices.5.mats, f32[15,8,128]{2,1,0:T(8,128)S(1)} %get-tuple-element.197.ends, f32[15,8,128]{2,1,0:T(8,128)S(1)} %collective-permute-done.21.other, f32[30,8,128]{2,1,0:T(8,128)S(1)} %get-tuple-element.198.known, ...), custom_call_target="tpu_custom_call" | custom-call | flops 1000 | bytes 1000 | tf_op jit(solution)/shard_map/correct/pallas_call | solution.py:46
  103.1 1.2 %collective-permute-done.22.other = f32[5,8,128]{2,1,0:T(8,128)S(1)} collective-permute-done((f32[5,8,128]{2,1,0:T(8,128)S(1)}, f32[5,8,128]{2,1,0:T(8,128)S(1)}, u32[]{:S(2)}, u32[]{:S(2)}) %collective-permute-start.22) | collective-permute-done | bytes 20512 | tf_op jit(solution)/shard_map/ppermute | solution.py:563
  104.4 3.2 %finish.1 = f32[7840,128]{1,0:T(8,128)} custom-call(s32[6]{0:T(128)S(1)} %stack.35.flags, f32[2,30,8,128]{3,2,1,0:T(8,128)S(1)} %merge_matrices.5.mats, f32[5,8,128]{2,1,0:T(8,128)S(1)} %get-tuple-element.201.ends, f32[5,8,128]{2,1,0:T(8,128)S(1)} %collective-permute-done.22.other, f32[10,8,128]{2,1,0:T(8,128)S(1)} %get-tuple-element.202.known, ...), custom_call_target="tpu_custom_call" | custom-call | flops 1000 | bytes 1000 | tf_op jit(solution)/shard_map/finish/pallas_call | solution.py:46
  (33 shorter events, 0.1 us)
Async XLA Ops:
  0.0 12.3 %copy-start.10 = (s32[24]{0:T(128)S(1)}, s32[24]{0:T(128)}, u32[]{:S(2)}) copy-start(s32[24]{0:T(128)} %param.18) | copy-start | bytes 292
  0.0 12.4 %copy-start.8 = (s32[2]{0:T(128)S(1)}, s32[2]{0:T(128)}, u32[]{:S(2)}) copy-start(s32[2]{0:T(128)} %blades.1) | copy-start | bytes 28
  0.0 2.2 %copy-start.2 = (f32[16,2,5,49,128]{4,1,3,2,0:T(2,128)S(1)}, f32[16,2,5,49,128]{4,1,3,2,0:T(2,128)}, u32[]{:S(2)}) copy-start(f32[16,2,5,49,128]{4,1,3,2,0:T(2,128)} %param.11) | copy-start | bytes 12042244
  2.2 15.0 %copy-start = (f32[16,2,5,5,128]{4,1,3,2,0:T(2,128)S(1)}, f32[16,2,5,5,128]{4,1,3,2,0:T(2,128)}, u32[]{:S(2)}) copy-start(f32[16,2,5,5,128]{4,1,3,2,0:T(2,128)} %param.15) | copy-start | bytes 1228804
  2.2 15.0 %copy-start.1 = (f32[16,2,5,5,128]{4,1,3,2,0:T(2,128)S(1)}, f32[16,2,5,5,128]{4,1,3,2,0:T(2,128)}, u32[]{:S(2)}) copy-start(f32[16,2,5,5,128]{4,1,3,2,0:T(2,128)} %param.16) | copy-start | bytes 1228804
  4.4 17.8 %copy-start.3 = (f32[16,2,5,128]{3,1,2,0:T(2,128)S(1)}, f32[16,2,5,128]{3,1,2,0:T(2,128)}, u32[]{:S(2)}) copy-start(f32[16,2,5,128]{3,1,2,0:T(2,128)} %param.13) | copy-start | bytes 245764
  4.4 17.8 %copy-start.4 = (f32[16,2,5,128]{3,1,2,0:T(2,128)S(1)}, f32[16,2,5,128]{3,1,2,0:T(2,128)}, u32[]{:S(2)}) copy-start(f32[16,2,5,128]{3,1,2,0:T(2,128)} %param.12) | copy-start | bytes 245764
  4.4 12.7 %collective-permute-start.3 = (f32[80,56,128]{2,1,0:T(8,128)}, f32[80,56,128]{2,1,0:T(8,128)}, u32[]{:S(2)}, u32[]{:S(2)}) collective-permute-start(f32[80,56,128]{2,1,0:T(8,128)} %get-tuple-element.114.xn), channel_id=1, source_target_pairs={{0,1},{1,0},{2,3},{3,2},{4,5},{5,4},{6,7},{7,6},{8,9},{9,8},{10,11... | collective-permute-start | bytes 6881288 | tf_op jit(solution)/shard_map/ppermute | solution.py:578
  4.8 22.0 %collective-permute-start.2 = (f32[980,128]{1,0:T(8,128)}, f32[980,128]{1,0:T(8,128)}, u32[]{:S(2)}, u32[]{:S(2)}) collective-permute-start(f32[980,128]{1,0:T(8,128)} %get-tuple-element.107), channel_id=1, source_target_pairs={{0,3},{1,2},{2,1},{3,0},{4,7},{5,6},{6,5},{7,4},{8,11},{9,10},{10,... | collective-permute-start | bytes 1505288 | tf_op jit(solution)/shard_map/ppermute | solution.py:562
  7.5 14.8 %collective-permute-start = (f32[496,128]{1,0:T(8,128)}, f32[496,128]{1,0:T(8,128)S(1)}, u32[]{:S(2)}, u32[]{:S(2)}) collective-permute-start(f32[496,128]{1,0:T(8,128)} %get-tuple-element.115), channel_id=1, source_target_pairs={{0,4},{4,8},{8,12},{12,16},{16,20},{20,24},{24,28},{1,5},{5,9},{9,... | collective-permute-start | bytes 761864 | tf_op jit(solution)/shard_map/ppermute | solution.py:580
  10.9 11.4 %collective-permute-start.1 = (f32[496,128]{1,0:T(8,128)}, f32[496,128]{1,0:T(8,128)}, u32[]{:S(2)}, u32[]{:S(2)}) collective-permute-start(f32[496,128]{1,0:T(8,128)} %get-tuple-element.116), channel_id=1, source_target_pairs={{4,0},{8,4},{12,8},{16,12},{20,16},{24,20},{28,24},{5,1},{9,5},{13... | collective-permute-start | bytes 761864 | tf_op jit(solution)/shard_map/ppermute | solution.py:581
  12.4 0.8 copy-start.5
  13.2 0.7 copy-start.7
  14.0 4.8 %copy-start.9 = (bf16[16,2,5,5,128]{4,1,3,2,0:T(2,128)(2,1)S(1)}, bf16[16,2,5,5,128]{4,1,3,2,0:T(2,128)(2,1)}, u32[]{:S(2)}) copy-start(bf16[16,2,5,5,128]{4,1,3,2,0:T(2,128)(2,1)} %param.14) | copy-start | bytes 614404
  14.0 8.3 %copy-start.6 = (f32[56,192]{1,0:T(8,128)S(1)}, f32[56,192]{1,0:T(8,128)}, u32[]{:S(2)}) copy-start(f32[56,192]{1,0:T(8,128)} %constant.34.clone.table) | copy-start | bytes 129028
  17.1 19.6 %collective-permute-start.4 = (f32[480,128]{1,0:T(8,128)S(1)}, f32[480,128]{1,0:T(8,128)S(1)}, u32[]{:S(2)}, u32[]{:S(2)}) collective-permute-start(f32[480,128]{1,0:T(8,128)S(1)} %get-tuple-element.129), channel_id=1, source_target_pairs={{0,3},{1,2},{2,1},{3,0},{4,7},{5,6},{6,5},{7,4},{8,11},{9,10},{10,... | collective-permute-start | bytes 737288 | tf_op jit(solution)/shard_map/ppermute | solution.py:562
  38.0 25.7 %collective-permute-start.8 = (f32[80,8,128]{2,1,0:T(8,128)S(1)}, f32[80,8,128]{2,1,0:T(8,128)S(1)}, u32[]{:S(2)}, u32[]{:S(2)}) collective-permute-start(f32[80,8,128]{2,1,0:T(8,128)S(1)} %get-tuple-element.145.flows), channel_id=1, source_target_pairs={{0,4},{4,0},{8,12},{12,8},{16,20},{20,16},{24,28},{28,24},{1,5},{5... | collective-permute-start | bytes 983048 | tf_op jit(solution)/shard_map/ppermute | solution.py:563
  40.4 9.7 %collective-permute-start.5 = (f32[2,15,8,128]{3,2,1,0:T(8,128)S(1)}, f32[2,15,8,128]{3,2,1,0:T(8,128)S(1)}, u32[]{:S(2)}, u32[]{:S(2)}) collective-permute-start(f32[2,15,8,128]{3,2,1,0:T(8,128)S(1)} %get-tuple-element.134.refs_0_), channel_id=1, source_target_pairs={{0,4},{4,0},{8,12},{12,8},{16,20},{20,16},{24,28},{28,24},{1,5},{5... | collective-permute-start | bytes 368648 | tf_op jit(solution)/shard_map/ppermute | solution.py:563
  40.5 26.1 %collective-permute-start.9 = (f32[960,128]{1,0:T(8,128)S(1)}, f32[960,128]{1,0:T(8,128)S(1)}, u32[]{:S(2)}, u32[]{:S(2)}) collective-permute-start(f32[960,128]{1,0:T(8,128)S(1)} %get-tuple-element.149), channel_id=1, source_target_pairs={{0,3},{1,2},{2,1},{3,0},{4,7},{5,6},{6,5},{7,4},{8,11},{9,10},{10,... | collective-permute-start | bytes 1474568 | tf_op jit(solution)/shard_map/ppermute | solution.py:562
  40.5 33.3 %collective-permute-start.12 = (f32[1024,128]{1,0:T(8,128)S(1)}, f32[1024,128]{1,0:T(8,128)S(1)}, u32[]{:S(2)}, u32[]{:S(2)}) collective-permute-start(f32[1024,128]{1,0:T(8,128)S(1)} %get-tuple-element.161), channel_id=1, source_target_pairs={{0,3},{1,2},{2,1},{3,0},{4,7},{5,6},{6,5},{7,4},{8,11},{9,10},{10,... | collective-permute-start | bytes 1572872 | tf_op jit(solution)/shard_map/ppermute | solution.py:562
  50.8 6.5 %collective-permute-start.6 = (f32[2,15,8,128]{3,2,1,0:T(8,128)S(1)}, f32[2,15,8,128]{3,2,1,0:T(8,128)S(1)}, u32[]{:S(2)}, u32[]{:S(2)}) collective-permute-start(f32[2,15,8,128]{3,2,1,0:T(8,128)S(1)} %get-tuple-element.137.refs_0_), channel_id=1, source_target_pairs={{0,8},{4,12},{8,0},{12,4},{16,24},{20,28},{24,16},{28,20},{1,9},{5... | collective-permute-start | bytes 368648 | tf_op jit(solution)/shard_map/ppermute | solution.py:563
  58.0 5.1 %collective-permute-start.7 = (f32[2,5,8,128]{3,2,1,0:T(8,128)S(1)}, f32[2,5,8,128]{3,2,1,0:T(8,128)S(1)}, u32[]{:S(2)}, u32[]{:S(2)}) collective-permute-start(f32[2,5,8,128]{3,2,1,0:T(8,128)S(1)} %get-tuple-element.141.refs_0_), channel_id=1, source_target_pairs={{0,16},{4,20},{8,24},{12,28},{16,0},{20,4},{24,8},{28,12},{1,17},{... | collective-permute-start | bytes 122888 | tf_op jit(solution)/shard_map/ppermute | solution.py:563
  64.6 7.1 %collective-permute-start.10 = (f32[80,8,128]{2,1,0:T(8,128)S(1)}, f32[80,8,128]{2,1,0:T(8,128)S(1)}, u32[]{:S(2)}, u32[]{:S(2)}) collective-permute-start(f32[80,8,128]{2,1,0:T(8,128)S(1)} %get-tuple-element.154.flows), channel_id=1, source_target_pairs={{0,8},{4,12},{8,0},{12,4},{16,24},{20,28},{24,16},{28,20},{1,9},{5... | collective-permute-start | bytes 983048 | tf_op jit(solution)/shard_map/ppermute | solution.py:563
  66.6 16.5 %collective-permute-start.14 = (f32[480,128]{1,0:T(8,128)S(1)}, f32[480,128]{1,0:T(8,128)S(1)}, u32[]{:S(2)}, u32[]{:S(2)}) collective-permute-start(f32[480,128]{1,0:T(8,128)S(1)} %get-tuple-element.168), channel_id=1, source_target_pairs={{0,3},{1,2},{2,1},{3,0},{4,7},{5,6},{6,5},{7,4},{8,11},{9,10},{10,... | collective-permute-start | bytes 737288 | tf_op jit(solution)/shard_map/ppermute | solution.py:562
  68.2 5.0 %collective-permute-start.11 = (f32[20,8,128]{2,1,0:T(8,128)S(1)}, f32[20,8,128]{2,1,0:T(8,128)S(1)}, u32[]{:S(2)}, u32[]{:S(2)}) collective-permute-start(f32[20,8,128]{2,1,0:T(8,128)S(1)} %get-tuple-element.158.flows), channel_id=1, source_target_pairs={{0,4},{4,0},{8,12},{12,8},{16,20},{20,16},{24,28},{28,24},{1,5},{5... | collective-permute-start | bytes 245768 | tf_op jit(solution)/shard_map/ppermute | solution.py:563
  75.8 8.6 %collective-permute-start.15 = (f32[30,8,128]{2,1,0:T(8,128)S(1)}, f32[30,8,128]{2,1,0:T(8,128)S(1)}, u32[]{:S(2)}, u32[]{:S(2)}) collective-permute-start(f32[30,8,128]{2,1,0:T(8,128)S(1)} %get-tuple-element.171.flows), channel_id=1, source_target_pairs={{0,4},{4,0},{8,12},{12,8},{16,20},{20,16},{24,28},{28,24},{1,5},{5... | collective-permute-start | bytes 368648 | tf_op jit(solution)/shard_map/ppermute | solution.py:563
  76.2 6.3 %collective-permute-start.13 = (f32[20,8,128]{2,1,0:T(8,128)S(1)}, f32[20,8,128]{2,1,0:T(8,128)S(1)}, u32[]{:S(2)}, u32[]{:S(2)}) collective-permute-start(f32[20,8,128]{2,1,0:T(8,128)S(1)} %get-tuple-element.164.flows), channel_id=1, source_target_pairs={{0,8},{4,12},{8,0},{12,4},{16,24},{20,28},{24,16},{28,20},{1,9},{5... | collective-permute-start | bytes 245768 | tf_op jit(solution)/shard_map/ppermute | solution.py:563
  77.7 12.5 %collective-permute-start.16 = (f32[40,8,128]{2,1,0:T(8,128)S(1)}, f32[40,8,128]{2,1,0:T(8,128)S(1)}, u32[]{:S(2)}, u32[]{:S(2)}) collective-permute-start(f32[40,8,128]{2,1,0:T(8,128)S(1)} %get-tuple-element.175.ends), channel_id=1, source_target_pairs={{0,16},{4,20},{8,24},{12,28},{16,0},{20,4},{24,8},{28,12},{1,17},{... | collective-permute-start | bytes 491528 | tf_op jit(solution)/shard_map/ppermute | solution.py:563
  85.1 10.7 %collective-permute-start.19 = (f32[30,8,128]{2,1,0:T(8,128)S(1)}, f32[30,8,128]{2,1,0:T(8,128)S(1)}, u32[]{:S(2)}, u32[]{:S(2)}) collective-permute-start(f32[30,8,128]{2,1,0:T(8,128)S(1)} %get-tuple-element.189.flows), channel_id=1, source_target_pairs={{0,8},{4,12},{8,0},{12,4},{16,24},{20,28},{24,16},{28,20},{1,9},{5... | collective-permute-start | bytes 368648 | tf_op jit(solution)/shard_map/ppermute | solution.py:563
  85.5 7.6 %collective-permute-start.17 = (f32[10,8,128]{2,1,0:T(8,128)S(1)}, f32[10,8,128]{2,1,0:T(8,128)S(1)}, u32[]{:S(2)}, u32[]{:S(2)}) collective-permute-start(f32[10,8,128]{2,1,0:T(8,128)S(1)} %get-tuple-element.182.flows), channel_id=1, source_target_pairs={{0,4},{4,0},{8,12},{12,8},{16,20},{20,16},{24,28},{28,24},{1,5},{5... | collective-permute-start | bytes 122888 | tf_op jit(solution)/shard_map/ppermute | solution.py:563
  87.4 6.4 %collective-permute-start.18 = (f32[10,8,128]{2,1,0:T(8,128)S(1)}, f32[10,8,128]{2,1,0:T(8,128)S(1)}, u32[]{:S(2)}, u32[]{:S(2)}) collective-permute-start(f32[10,8,128]{2,1,0:T(8,128)S(1)} %get-tuple-element.185.ends), channel_id=1, source_target_pairs={{0,16},{4,20},{8,24},{12,28},{16,0},{20,4},{24,8},{28,12},{1,17},{... | collective-permute-start | bytes 122888 | tf_op jit(solution)/shard_map/ppermute | solution.py:563
  94.9 4.1 %collective-permute-start.20 = (f32[10,8,128]{2,1,0:T(8,128)S(1)}, f32[10,8,128]{2,1,0:T(8,128)S(1)}, u32[]{:S(2)}, u32[]{:S(2)}) collective-permute-start(f32[10,8,128]{2,1,0:T(8,128)S(1)} %get-tuple-element.193.flows), channel_id=1, source_target_pairs={{0,8},{4,12},{8,0},{12,4},{16,24},{20,28},{24,16},{28,20},{1,9},{5... | collective-permute-start | bytes 122888 | tf_op jit(solution)/shard_map/ppermute | solution.py:563
  96.5 5.2 %collective-permute-start.21 = (f32[15,8,128]{2,1,0:T(8,128)S(1)}, f32[15,8,128]{2,1,0:T(8,128)S(1)}, u32[]{:S(2)}, u32[]{:S(2)}) collective-permute-start(f32[15,8,128]{2,1,0:T(8,128)S(1)} %get-tuple-element.197.ends), channel_id=1, source_target_pairs={{0,16},{4,20},{8,24},{12,28},{16,0},{20,4},{24,8},{28,12},{1,17},{... | collective-permute-start | bytes 184328 | tf_op jit(solution)/shard_map/ppermute | solution.py:563
  99.6 4.7 %collective-permute-start.22 = (f32[5,8,128]{2,1,0:T(8,128)S(1)}, f32[5,8,128]{2,1,0:T(8,128)S(1)}, u32[]{:S(2)}, u32[]{:S(2)}) collective-permute-start(f32[5,8,128]{2,1,0:T(8,128)S(1)} %get-tuple-element.201.ends), channel_id=1, source_target_pairs={{0,16},{4,20},{8,24},{12,28},{16,0},{20,4},{24,8},{28,12},{1,17},{... | collective-permute-start | bytes 61448 | tf_op jit(solution)/shard_map/ppermute | solution.py:563

commit v3 on v2

--- a/solution.py
+++ b/solution.py
@@ -19,7 +19,7 @@
 LEAD = 4
 MB = 1 << 20
 
-CHUNKS = (((0, 8), False), ((8, 24), False), ((24, 40), True), ((40, 48), False))
+CHUNKS = (((0, 32), False), ((32, 48), True))
 
 
 def rows_of(chunk):
@@ -39,7 +39,7 @@
         self.flags, array = lax.optimization_barrier((self.flags, array))
         return array
 
-    def __call__(self, body, out_shapes, arrays, scratch=(), vmem=24, name=None, grid=None, in_specs=None, out_specs=None, scalars=()):
+    def __call__(self, body, out_shapes, arrays, scratch=(), vmem=24, name=None, grid=None, in_specs=None, out_specs=None, scalars=(), flops=1000):
         smem = pl.BlockSpec(memory_space=pltpu.SMEM)
         held = pl.BlockSpec(memory_space=pltpu.VMEM)
         extra = {} if grid is None else {"grid": grid}
@@ -50,7 +50,7 @@
             out_specs=out_specs or [held] * len(out_shapes),
             scratch_shapes=list(scratch),
             compiler_params=pltpu.CompilerParams(vmem_limit_bytes=vmem * MB),
-            cost_estimate=pl.CostEstimate(flops=1000, bytes_accessed=1000, transcendentals=0),
+            cost_estimate=pl.CostEstimate(flops=flops, bytes_accessed=1000, transcendentals=0),
             name=name,
             **extra,
         )(self.flags, *scalars, *arrays)
@@ -243,7 +243,7 @@
 
 def near_cell(
     flags, xn, xf, halo, from_left, from_right, advect, viscous, inverse, lower, upper, trig, table,
-    g, flows, right, edges,
+    group, g, flows, right, edges,
 ):
     p = 1 - flags[0]
     cells = xn.shape[0] // V
@@ -255,6 +255,9 @@
     residuals(xn, xf, halo, edges, advect, viscous, timing_matrix(table, trig), p, cells, put)
     source = lambda z, first, last: [right[z * V + v, first:last, :] for v in range(V)]
     sweeps(source, g, flows, 0, ((0, 32), (32, PAD)), p, inverse, lower, upper, cells)
+    for c in range(2):
+        for i in range(3 * V):
+            flows[2 * V * PAD // 8 + c * 3 * V + i] = group[c, i]
 
 
 def far_base(flags, xn, xf, from_left, from_right, advect, viscous, trig, table, base, edges):
@@ -282,17 +285,12 @@
             lead[z * V + v] = jnp.where(wrap == 1, lagged[v], raw[v])
 
 
-def far_chunk(chunk, flags, base, lead, halo, viscous, inverse, lower, upper, *refs):
-    others, (g, fg) = refs[:-2], refs[-2:]
+def far_chunk(chunk, flags, base, lead, halo, viscous, inverse, lower, upper, g, fg):
     (first, last), extra = chunk
     width = last - first
     p = flags[0]
     cells = base.shape[0] // V
     top = lax.broadcasted_iota(jnp.int32, (8, LANES), 0) == 0
-    offset = 0
-    for other in others:
-        fg[0 : other.shape[0]] = other[...]
-        offset = other.shape[0]
 
     def pieces(ref, j, rows):
         value = ref[j, first:last, :]
@@ -313,7 +311,7 @@
         return result
 
     height = rows_of(chunk)
-    sweeps(source, g, fg, offset, ((0, height),), p, inverse, lower, upper, cells)
+    sweeps(source, g, fg, 0, ((0, height),), p, inverse, lower, upper, cells)
 
 
 def times(matrix, vector):
@@ -376,18 +374,15 @@
             group[c, 2 * V + a] = through[a]
 
 
-def merge_matrices(bit, levels, flags, *refs):
+def merge_matrices(bit, levels, flags, mine, other, share, mats, merged, share_out, offset, new_offset):
     start, last = bit == 0, bit == levels - 1
-    refs = list(refs)
-    mine, other = refs.pop(0), refs.pop(0)
-    share = None if start else refs.pop(0)
-    mats = refs.pop(0)
-    merged, share_out = (None, None) if last else refs
     right = flags[3 + bit] == 1
     left = jnp.logical_not(right)
     nothing = jnp.zeros((8, LANES), F32)
     for c in range(2):
-        pick = lambda kind, own: [jnp.where(own, m, t) for m, t in zip(tiles(mine, c, kind), tiles(other, c, kind))]
+        kinds = 1 if last else 3
+        at = lambda ref, kind: [ref[offset + (c * kinds + kind) * V + a] for a in range(V)]
+        pick = lambda kind, own: [jnp.where(own, m, t) for m, t in zip(at(mine, kind), at(other, kind))]
         if start:
             own = [[unit(a) for a in range(V)], [nothing] * V, [unit(a) for a in range(V)]]
         else:
@@ -412,7 +407,7 @@
             new += [times(rows(mats, c, 2), h_right), times(rows(mats, c, 0), p_left)]
         for kind, values in enumerate(new):
             for a in range(V):
-                merged[c, kind * V + a] = values[a]
+                merged[new_offset + (c * len(new) + kind) * V + a] = values[a]
         s0 = times(rows(mats, c, 3), p_left)
         s1 = times(rows(mats, c, 4), p_left)
         s1b = times(rows(mats, c, 5), turned)
@@ -429,6 +424,14 @@
     from_right = plus(times(rows(mats, c, 4), f_left), times(rows(mats, c, 5), back))
     total = from_left + from_right
     return back, total if known is None else plus(known, total)
+
+
+def merge_all(parts, bit, levels, flags, flows, other, *refs):
+    share, known, mats, merged, share_out, inflow = (None, None, *refs) if bit == 0 else refs
+    tall = sum(height for _, height in parts) * V
+    new_offset = tall * (1 if bit == levels - 2 else 2)
+    merge_matrices(bit, levels, flags, flows, other, share, mats, merged, share_out, 2 * tall, new_offset)
+    merge_flows(parts, bit, levels, flags, mats, flows, other, *([] if known is None else [known]), merged, inflow)
 
 
 def merge_flows(parts, bit, levels, flags, mats, flows, other, *refs):
@@ -504,16 +507,24 @@
             lax.fori_loop(0, g.shape[0] // V, step, flow)
 
 
+def correct_all(parts, levels, flags, ends, other, share, known, blocks, *refs):
+    count = len(parts)
+    solved, results, mats, inflow = refs[:count], refs[count : 2 * count], refs[-2], refs[-1]
+    tall = sum(height for _, height in parts) * V
+    merge_matrices(levels - 1, levels, flags, ends, other, share, mats, None, None, tall, 0)
+    correct(parts, levels, flags, mats, ends, other, known, blocks, *solved, *results, inflow)
+
+
 def finish(levels, flags, mats, ends, other, known, g, blocks, near, *refs):
     done, out, inflow = refs[:-2], refs[-2], refs[-1]
     right = flags[2 + levels] == 1
     p = flags[0]
-    first_row, last_row = CHUNKS[-1][0]
-    width = last_row - first_row
+    (first_row, last_row), last_extra = CHUNKS[-1]
+    width, height = last_row - first_row, rows_of(CHUNKS[-1])
 
     @pl.when(pl.program_id(0) == 0)
     def _():
-        last_inflow(right, 1, mats, ends, other, known, 0, width // 8, inflow)
+        last_inflow(right, 1, mats, ends, other, known, 0, height // 8, inflow)
 
     flow = tuple(inflow[i] for i in range(2 * V))
 
@@ -526,7 +537,10 @@
                 out[pl.ds(row + p + 2 * first, last - first, stride=2), :] = ref[j, 0 : last - first, :]
                 if extra:
                     out[pl.ds(row + p + 2 * (NT - 1), 1), :] = ref[j, last - first : last - first + 1, :]
-            out[pl.ds(row + p + 2 * first_row, width, stride=2), :] = corrected(1, z, a, 0, width, g, blocks, flow)
+            value = corrected(1, z, a, 0, height, g, blocks, flow)
+            out[pl.ds(row + p + 2 * first_row, width, stride=2), :] = value[:width]
+            if last_extra:
+                out[pl.ds(row + p + 2 * (NT - 1), 1), :] = value[width : width + 1]
         return carry
 
     lax.fori_loop(0, g.shape[0] // V, step, 0)
@@ -603,7 +617,6 @@
         prepare, [(2 * count + 8, LANES), *chunk_shapes], [xf, wide_harmonic, basis, turned],
         scalars=[blades], name="prepare",
     )
-    chunks[0], halo_near = lax.optimization_barrier((chunks[0], halo_near))
     arrived = [slab_in]
     for chunk in chunks:
         if len(arrived) >= 2:
@@ -617,56 +630,60 @@
     vis = viscous.transpose(0, 2, 1, 3).reshape(cells * V * 2, LANES)
     edges = pltpu.VMEM((2 * V, PAD, LANES), F32)
 
-    mats, group, share = [], None, []
+    mats = []
     mats_shape = (2, 6 * V, 8, LANES)
 
-    def merge_group(k):
-        nonlocal group, share
-        shapes = [mats_shape]
-        if k < levels - 1:
-            shapes += [(2, 3 * V if k < levels - 2 else V, 8, LANES), (2, 3 * V, 8, LANES)]
-        out = run(
-            functools.partial(merge_matrices, k, levels), shapes,
-            [group, to_level(group, k), *share], name="merge_matrices",
+    def solve_chunk(i):
+        height = rows_of(CHUNKS[i])
+        return run(
+            functools.partial(far_chunk, CHUNKS[i]),
+            [(cells * V, height, LANES), (2 * V * height // 8, 8, LANES)],
+            [base, lead, arrived[i], vis, inv, low, upp], name="far_chunk",
         )
-        mats.append(out[0])
-        if k < levels - 1:
-            group, share = out[1], [out[2]]
-
-    def solve_chunk(i, others=()):
-        height = rows_of(CHUNKS[i])
-        tall = 2 * V * height // 8 + sum(x.shape[0] for x in others)
-        g, flows = run(
-            functools.partial(far_chunk, CHUNKS[i]), [(cells * V, height, LANES), (tall, 8, LANES)],
-            [base, lead, arrived[i], vis, inv, low, upp, *others], name="far_chunk",
-        )
-        return g, flows
 
     class Exchange:
-        def __init__(self, parts, flows, solved):
-            self.parts = [(c, g.shape[1] // 8) for c, g in zip(parts, solved)]
-            self.flows, self.known, self.solved, self.level = flows, [], solved, 0
+        def __init__(self, c, g, flows, leads=False):
+            self.parts, self.leads = [(c, g.shape[1] // 8)], leads
+            self.flows, self.known, self.solved, self.level = flows, [], g, 0
+            self.scratch = [pltpu.VMEM((2 * V, g.shape[1], LANES), F32)]
 
         def step(self):
-            tall = sum(h for _, h in self.parts)
-            k = self.level
-            out = run(
-                functools.partial(merge_flows, self.parts, k, levels),
-                [((2 if k < levels - 2 else 1) * V * tall, 8, LANES), (2 * V * tall, 8, LANES)],
-                [mats[k], self.flows, to_level(self.flows, k), *self.known], name="merge_flows",
-            )
-            self.flows, self.known, self.level = out[0], [out[1]], k + 1
+            tall, k = self.parts[0][1], self.level
+            shape = ((2 if k < levels - 2 else 1) * V * tall, 8, LANES)
+            inflow = (2 * V * tall, 8, LANES)
+            other = to_level(self.flows, k)
+            if self.leads:
+                shape = (shape[0] + (6 * V if k < levels - 2 else 2 * V),) + shape[1:]
+                out = run(
+                    functools.partial(merge_all, self.parts, k, levels),
+                    [mats_shape, shape, (2, 3 * V, 8, LANES), inflow],
+                    [self.flows, other, *self.known], name="merge_all",
+                )
+                mats.append(out[0])
+                self.flows, self.known = out[1], out[2:]
+            else:
+                out = run(
+                    functools.partial(merge_flows, self.parts, k, levels), [shape, inflow],
+                    [mats[k], self.flows, other, *self.known], name="merge_flows",
+                )
+                self.flows, self.known = out[0], out[1:]
+            self.level = k + 1
 
         def last(self):
-            return [mats[-1], self.flows, to_level(self.flows, levels - 1), *self.known]
+            return [self.flows, to_level(self.flows, levels - 1), *self.known]
 
         def correct(self):
-            tall = max(h for _, h in self.parts)
+            if self.leads:
+                result, last = run(
+                    functools.partial(correct_all, self.parts, levels), [self.solved.shape, mats_shape],
+                    [*self.last(), blocks, self.solved], scratch=self.scratch, name="correct_all",
+                )
+                mats.append(last)
+                return result
             return run(
-                functools.partial(correct, self.parts, levels), [g.shape for g in self.solved],
-                [*self.last(), blocks, *self.solved],
-                scratch=[pltpu.VMEM((2 * V, tall * 8, LANES), F32)], name="correct",
-            )
+                functools.partial(correct, self.parts, levels), [self.solved.shape],
+                [mats[-1], *self.last(), blocks, self.solved], scratch=self.scratch, name="correct",
+            )[0]
 
     blocks, group = run(
         transfer, [(2, cells * V, 16, LANES), (2, 3 * V, 8, LANES)], [low, upp],
@@ -681,45 +698,31 @@
         scratch=[pltpu.VMEM((V, PAD, LANES), F32)], name="far_lead",
     )[0]
     g_near, flows_near = run(
-        near_cell, [x_shape, (2 * V * PAD // 8, 8, LANES)],
-        [xn, xf, halo_near, from_left, from_right, adv, vis, inv, low, upp, trig, table],
-        scratch=[pltpu.VMEM(x_shape, F32), edges], name="near_cell",
+        near_cell, [x_shape, (2 * V * PAD // 8 + 6 * V, 8, LANES)],
+        [xn, xf, halo_near, from_left, from_right, adv, vis, inv, low, upp, trig, table, group],
+        scratch=[pltpu.VMEM(x_shape, F32), edges], name="near_cell", flops=6_000_000_000,
     )
-    g_first, flows = solve_chunk(0, [flows_near])
-    first = Exchange([0, 1], flows, [g_near, g_first])
-    for k in range(levels):
-        merge_group(k)
-    first.step()
-    g, flows = solve_chunk(1)
-    second = Exchange([1], flows, [g])
+    first = Exchange(0, g_near, flows_near, leads=True)
+    second = Exchange(1, *solve_chunk(0))
     first.step()
     second.step()
-    g, flows = solve_chunk(2)
-    third = Exchange([1], flows, [g])
-    second.step()
-    g, flows = solve_chunk(3)
-    fourth = Exchange([1], flows, [g])
+    for k in range(1, levels - 1):
+        first.step()
+    third = Exchange(1, *solve_chunk(1))
+    for k in range(1, levels - 1):
+        second.step()
     third.step()
-    for k in range(levels - 3):
-        first.step()
-        second.step()
-    done_first = first.correct()
-    fourth.step()
-    done_second = second.correct()
-    third.step()
-    fourth.step()
-    done_third = third.correct()
-    for k in range(levels - 3):
+    near = first.correct()
+    for k in range(1, levels - 1):
         third.step()
-        fourth.step()
-    near, *done = [*done_first, *done_second, *done_third]
-    g_last = fourth.solved[0]
+    done = [second.correct()]
+    g_last = third.solved
+    small = [mats[-1], *third.last()]
 
     steps = 4
     part = cells // steps
     whole = lambda x: pl.BlockSpec(x.shape, lambda i: (0,) * x.ndim)
     by_cell = lambda x: pl.BlockSpec((part * V,) + x.shape[1:], lambda i: (i, 0, 0))
-    small = fourth.last()
     out = run(
         functools.partial(finish, levels), [st.shape], [*small, g_last, blocks, near, *done],
         grid=(steps,),

time: 108 us -> 89 us (0.82)
  starting transfers between devices: 34.8 us -> 23.4 us
  Pallas kernels: 43.9 us -> 38.5 us
  local copies, waits for them, and re-layouts: 3.94 us -> 2.36 us
    ppermute x15 -> x9, starting transfers between devices: 25.2 us -> 15.6 us  [local(): lax.ppermute(x, 'seg', [(i, i ^ 1 << k) for i in range(segs)])]
    pallas_call x24 -> x16, Pallas kernels: 41.7 us -> 36.3 us  [__call__(): pl.pallas_call(body, out_shape=[jax.ShapeDtypeStruct(s, F32) for s in out...]
    ppermute x15 -> x9, waiting for transfers between devices: 21.3 us -> 17.8 us  [local(): lax.ppermute(x, 'seg', [(i, i ^ 1 << k) for i in range(segs)])]
    ppermute x5 -> x3, starting transfers between devices: 4.45 us -> 2.7 us  [local(): to_far = lambda x: lax.ppermute(x, 'pitch', far_pairs)]
    unnamed x22, local copies, waits for them, and re-layouts: 3.78 us -> 2.2 us
    ppermute x1, waiting for transfers between devices: 3.33 us -> 4.83 us  [local(): lax.ppermute(last_cell, 'seg', [(i, i + 1) for i in range(segs - 1)])]
    ppermute x5 -> x3, waiting for transfers between devices: 0.01 us -> 1.51 us  [local(): to_far = lambda x: lax.ppermute(x, 'pitch', far_pairs)]
  transfers between devices with their start and end apart: 23 -> 15, of which waited for: 10 -> 9; matrix products, arithmetic and copies ran while one was open for 0% -> 0% of each run, Pallas kernels for 35% -> 37%
where the time goes in v3:
time: 89 us; the launch traced here: 88.8 us
  Pallas kernels  38.5 us (43%)
  waiting for transfers between devices  24.1 us (27%)
  starting transfers between devices  23.4 us (26%)
  local copies, waits for them, and re-layouts  2.36 us (3%)
    pallas_call x16, Pallas kernels, __call__(): pl.pallas_call(body, out_shape=[jax.ShapeDtypeStruct(s, F32) for s in out...  36.3 us
    ppermute x9, waiting for transfers between devices, local(): lax.ppermute(x, 'seg', [(i, i ^ 1 << k) for i in range(segs)])  17.8 us
    ppermute x9, starting transfers between devices, local(): lax.ppermute(x, 'seg', [(i, i ^ 1 << k) for i in range(segs)])  15.6 us
    ppermute x1, waiting for transfers between devices, local(): lax.ppermute(last_cell, 'seg', [(i, i + 1) for i in range(segs - 1)])  4.83 us
    ppermute x1, starting transfers between devices, local(): lax.ppermute(last_cell, 'seg', [(i, i + 1) for i in range(segs - 1)])  3.4 us
    ppermute x3, starting transfers between devices, local(): to_far = lambda x: lax.ppermute(x, 'pitch', far_pairs)  2.7 us
    pallas_call x1, Pallas kernels, local(): pl.pallas_call(split_cells, out_shape=[jax.ShapeDtypeStruct(x, F32) for x...  2.22 us
    unnamed x22, local copies, waits for them, and re-layouts  2.2 us
  transfers between devices with their start and end apart: 15, of which 9 were waited for; matrix products, arithmetic and copies ran while one was open for 0% of the time, Pallas kernels for 37%

profile of v3, /device:TPU:0, one launch (start us, length us, event | category | flops | bytes accessed | tf_op | source)
XLA Modules:
  0.0 88.8 jit_solution(13999527994825955456)
XLA Ops:
  0.0 0.0 copy-start.10
  0.0 0.0 copy-start.8
  0.0 0.0 copy-start
  0.0 2.2 %copy-done = f32[16,2,5,49,128]{4,1,3,2,0:T(2,128)S(1)} copy-done((f32[16,2,5,49,128]{4,1,3,2,0:T(2,128)S(1)}, f32[16,2,5,49,128]{4,1,3,2,0:T(2,128)}, u32[]{:S(2)}) %copy-start) | copy-done | bytes 4014104
  2.2 2.2 %split_cells.1 = (f32[980,128]{1,0:T(8,128)}, f32[496,128]{1,0:T(8,128)}, f32[496,128]{1,0:T(8,128)}, f32[80,56,128]{2,1,0:T(8,128)}, f32[80,56,128]{2,1,0:T(8,128)S(1)}) custom-call(f32[7840,128]{1,0:T(8,128)S(1)} %bitcast.27), custom_call_target="tpu_custom_call" | custom-call | tf_op jit(solution)/shard_map/split_cells/pallas_call | solution.py:584
  4.4 0.5 collective-permute-start.3
  4.9 2.6 %collective-permute-start.2 = (f32[980,128]{1,0:T(8,128)}, f32[980,128]{1,0:T(8,128)}, u32[]{:S(2)}, u32[]{:S(2)}) collective-permute-start(f32[980,128]{1,0:T(8,128)} %get-tuple-element.73), channel_id=1, source_target_pairs={{0,3},{1,2},{2,1},{3,0},{4,7},{5,6},{6,5},{7,4},{8,11},{9,10},{10,... | collective-permute-start | bytes 1505288 | tf_op jit(solution)/shard_map/ppermute | solution.py:576
  7.5 3.4 %collective-permute-start = (f32[496,128]{1,0:T(8,128)}, f32[496,128]{1,0:T(8,128)S(1)}, u32[]{:S(2)}, u32[]{:S(2)}) collective-permute-start(f32[496,128]{1,0:T(8,128)} %get-tuple-element.81), channel_id=1, source_target_pairs={{0,4},{4,8},{8,12},{12,16},{16,20},{20,24},{24,28},{1,5},{5,9},{9,... | collective-permute-start | bytes 761864 | tf_op jit(solution)/shard_map/ppermute | solution.py:594
  10.9 1.3 %collective-permute-start.1 = (f32[496,128]{1,0:T(8,128)}, f32[496,128]{1,0:T(8,128)}, u32[]{:S(2)}, u32[]{:S(2)}) collective-permute-start(f32[496,128]{1,0:T(8,128)} %get-tuple-element.82), channel_id=1, source_target_pairs={{4,0},{8,4},{12,8},{16,12},{20,16},{24,20},{28,24},{5,1},{9,5},{13... | collective-permute-start | bytes 761864 | tf_op jit(solution)/shard_map/ppermute | solution.py:595
  12.2 0.0 copy-done.10
  12.2 0.1 stack.35.flags
  12.3 0.1 broadcast_in_dim.2.harmonic
  12.4 0.0 copy-done.8
  12.4 0.0 copy-done.4
  12.4 0.0 copy-done.5
  12.4 3.1 %prepare.1 = (f32[56,128]{1,0:T(8,128)S(1)}, f32[1920,128]{1,0:T(8,128)S(1)}, f32[1024,128]{1,0:T(8,128)S(1)}) custom-call(s32[6]{0:T(128)S(1)} %stack.35.flags, s32[2]{0:T(128)S(1)} %copy-done.8, f32[80,56,128]{2,1,0:T(8,128)S(1)} %get-tuple-element.75.xf, f32[24,128]{1,0:T(8,128)S(1)} %broadcast_in_dim.2.harmonic, f32[56,56]{1,0:T(8,128)S(1)} %copy-done.5, ...), custom_call_target="tpu_custom_call" | custom-call | flops 1000 | bytes 1000 | tf_op jit(solution)/shard_map/prepare/pallas_call | solution.py:46
  15.5 0.1 collective-permute-start.4
  15.6 0.0 copy-done.1
  15.6 0.0 copy-done.2
  15.6 1.6 %transfer.1 = (f32[2,80,16,128]{3,2,1,0:T(8,128)S(1)}, f32[2,15,8,128]{3,2,1,0:T(8,128)S(1)}) custom-call(s32[6]{0:T(128)S(1)} %stack.35.flags, f32[800,128]{1,0:T(8,128)S(1)} %bitcast.28, f32[800,128]{1,0:T(8,128)S(1)} %bitcast.32), custom_call_target="tpu_custom_call" | custom-call | flops 1000 | bytes 1000 | tf_op jit(solution)/shard_map/transfer/pallas_call | solution.py:46
  17.2 0.0 copy-done.9
  17.2 0.1 reshape.36
  17.4 4.8 %collective-permute-done.from_left = f32[496,128]{1,0:T(8,128)S(1)} collective-permute-done((f32[496,128]{1,0:T(8,128)}, f32[496,128]{1,0:T(8,128)S(1)}, u32[]{:S(2)}, u32[]{:S(2)}) %collective-permute-start) | collective-permute-done | bytes 253984 | tf_op jit(solution)/shard_map/ppermute | solution.py:594
  22.2 0.0 collective-permute-done.1.from_right
  22.2 0.0 copy-done.3
  22.2 0.0 copy-done.6
  22.2 0.0 copy-done.7
  22.2 4.6 %far_base.1.base = f32[80,56,128]{2,1,0:T(8,128)S(1)} custom-call(s32[6]{0:T(128)S(1)} %stack.35.flags, f32[80,56,128]{2,1,0:T(8,128)} %get-tuple-element.80.xn, f32[80,56,128]{2,1,0:T(8,128)S(1)} %get-tuple-element.75.xf, f32[496,128]{1,0:T(8,128)S(1)} %collective-permute-done.from_left, f32[496,128]{1,0:T(8,128)} %collective-permute-done.1.from_right, ...), custom_call_target="tpu_custom_call" | custom-call | flops 1000 | bytes 1000 | tf_op jit(solution)/shard_map/far_base/pallas_call | solution.py:46
  26.8 0.0 collective-permute-done.2.slab
  26.8 1.7 %far_lead.1.lead = f32[20,56,128]{2,1,0:T(8,128)S(1)} custom-call(s32[6]{0:T(128)S(1)} %stack.35.flags, f32[980,128]{1,0:T(8,128)} %collective-permute-done.2.slab, f32[56,128]{1,0:T(8,128)S(1)} %get-tuple-element.83.trig, f32[56,56]{1,0:T(8,128)S(1)} %copy-done.5, f32[64,192]{1,0:T(8,128)S(1)} %copy-done.4), custom_call_target="tpu_custom_call" | custom-call | flops 1000 | bytes 1000 | tf_op jit(solution)/shard_map/far_lead/pallas_call | solution.py:46
  28.5 0.0 collective-permute-done.3.halo
  28.5 8.1 %near_cell.1 = (f32[80,56,128]{2,1,0:T(8,128)S(1)}, f32[100,8,128]{2,1,0:T(8,128)S(1)}) custom-call(s32[6]{0:T(128)S(1)} %stack.35.flags, f32[80,56,128]{2,1,0:T(8,128)} %get-tuple-element.80.xn, f32[80,56,128]{2,1,0:T(8,128)S(1)} %get-tuple-element.75.xf, f32[80,56,128]{2,1,0:T(8,128)} %collective-permute-done.3.halo, ...), custom_call_target="tpu_custom_call" | custom-call | flops 6000000000 | bytes 1000 | tf_op jit(solution)/shard_map/near_cell/pallas_call | solution.py:46
  36.7 2.4 %collective-permute-start.5 = (f32[100,8,128]{2,1,0:T(8,128)S(1)}, f32[100,8,128]{2,1,0:T(8,128)S(1)}, u32[]{:S(2)}, u32[]{:S(2)}) collective-permute-start(f32[100,8,128]{2,1,0:T(8,128)S(1)} %get-tuple-element.96.flows), channel_id=1, source_target_pairs={{0,4},{4,0},{8,12},{12,8},{16,20},{20,16},{24,28},{28,24},{1,5},{5... | collective-permute-start | bytes 1228808 | tf_op jit(solution)/shard_map/ppermute | solution.py:577
  39.1 0.0 collective-permute-start.8
  39.1 1.5 %collective-permute-done.4.halo = f32[1920,128]{1,0:T(8,128)S(1)} collective-permute-done((f32[1920,128]{1,0:T(8,128)S(1)}, f32[1920,128]{1,0:T(8,128)S(1)}, u32[]{:S(2)}, u32[]{:S(2)}) %collective-permute-start.4) | collective-permute-done | bytes 983072 | tf_op jit(solution)/shard_map/ppermute | solution.py:576
  40.6 2.4 %far_chunk.2 = (f32[80,32,128]{2,1,0:T(8,128)S(1)}, f32[40,8,128]{2,1,0:T(8,128)S(1)}) custom-call(s32[6]{0:T(128)S(1)} %stack.35.flags, f32[80,56,128]{2,1,0:T(8,128)S(1)} %far_base.1.base, f32[20,56,128]{2,1,0:T(8,128)S(1)} %far_lead.1.lead, f32[1920,128]{1,0:T(8,128)S(1)} %collective-permute-done.4.halo, f32[160,128]{1,0:T(8,128)S(1)} %bitcast.41, ...), custom_call_target="tpu_custom_call" | custom-call | flops 1000 | bytes 1000 | tf_op jit(solution)/shard_map/far_chunk/pallas_call | solution.py:46
  43.0 4.9 %collective-permute-done.5.other = f32[100,8,128]{2,1,0:T(8,128)S(1)} collective-permute-done((f32[100,8,128]{2,1,0:T(8,128)S(1)}, f32[100,8,128]{2,1,0:T(8,128)S(1)}, u32[]{:S(2)}, u32[]{:S(2)}) %collective-permute-start.5) | collective-permute-done | bytes 409632 | tf_op jit(solution)/shard_map/ppermute | solution.py:577
  47.9 1.0 %merge_all.2 = (f32[2,30,8,128]{3,2,1,0:T(8,128)S(1)}, f32[100,8,128]{2,1,0:T(8,128)S(1)}, f32[2,15,8,128]{3,2,1,0:T(8,128)S(1)}, f32[70,8,128]{2,1,0:T(8,128)S(1)}) custom-call(s32[6]{0:T(128)S(1)} %stack.35.flags, f32[100,8,128]{2,1,0:T(8,128)S(1)} %get-tuple-element.96.flows, f32[100,8,128]{2,1,0:T(8,128)S(1)} %collective-permute-done.5.other), custom_call_target="tpu_custom_call" | custom-call | flops 1000 | bytes 1000 | tf_op jit(solution)/shard_map/merge_all/pallas_call | solution.py:46
  48.9 3.7 %collective-permute-start.7 = (f32[100,8,128]{2,1,0:T(8,128)S(1)}, f32[100,8,128]{2,1,0:T(8,128)S(1)}, u32[]{:S(2)}, u32[]{:S(2)}) collective-permute-start(f32[100,8,128]{2,1,0:T(8,128)S(1)} %get-tuple-element.103.flows), channel_id=1, source_target_pairs={{0,8},{4,12},{8,0},{12,4},{16,24},{20,28},{24,16},{28,20},{1,9},{5... | collective-permute-start | bytes 1228808 | tf_op jit(solution)/shard_map/ppermute | solution.py:577
  52.7 0.3 collective-permute-start.6
  53.0 5.0 %collective-permute-done.6.other = f32[40,8,128]{2,1,0:T(8,128)S(1)} collective-permute-done((f32[40,8,128]{2,1,0:T(8,128)S(1)}, f32[40,8,128]{2,1,0:T(8,128)S(1)}, u32[]{:S(2)}, u32[]{:S(2)}) %collective-permute-start.6) | collective-permute-done | bytes 163872 | tf_op jit(solution)/shard_map/ppermute | solution.py:577
  58.0 0.8 merge_flows.4
  58.7 0.1 collective-permute-start.9
  58.9 4.2 %collective-permute-done.7.other = f32[100,8,128]{2,1,0:T(8,128)S(1)} collective-permute-done((f32[100,8,128]{2,1,0:T(8,128)S(1)}, f32[100,8,128]{2,1,0:T(8,128)S(1)}, u32[]{:S(2)}, u32[]{:S(2)}) %collective-permute-start.7) | collective-permute-done | bytes 409632 | tf_op jit(solution)/shard_map/ppermute | solution.py:577
  63.1 1.0 %merge_all.3 = (f32[2,30,8,128]{3,2,1,0:T(8,128)S(1)}, f32[45,8,128]{2,1,0:T(8,128)S(1)}, f32[2,15,8,128]{3,2,1,0:T(8,128)S(1)}, f32[70,8,128]{2,1,0:T(8,128)S(1)}) custom-call(s32[6]{0:T(128)S(1)} %stack.35.flags, f32[100,8,128]{2,1,0:T(8,128)S(1)} %get-tuple-element.103.flows, f32[100,8,128]{2,1,0:T(8,128)S(1)} %collective-permute-done.7.other, ...), custom_call_target="tpu_custom_call" | custom-call | flops 1000 | bytes 1000 | tf_op jit(solution)/shard_map/merge_all/pallas_call | solution.py:46
  64.1 0.0 collective-permute-done.8.halo
  64.1 2.0 %far_chunk.3 = (f32[80,24,128]{2,1,0:T(8,128)S(1)}, f32[30,8,128]{2,1,0:T(8,128)S(1)}) custom-call(s32[6]{0:T(128)S(1)} %stack.35.flags, f32[80,56,128]{2,1,0:T(8,128)S(1)} %far_base.1.base, f32[20,56,128]{2,1,0:T(8,128)S(1)} %far_lead.1.lead, f32[1024,128]{1,0:T(8,128)S(1)} %collective-permute-done.8.halo, f32[160,128]{1,0:T(8,128)S(1)} %bitcast.42, ...), custom_call_target="tpu_custom_call" | custom-call | flops 1000 | bytes 1000 | tf_op jit(solution)/shard_map/far_chunk/pallas_call | solution.py:46
  66.1 0.3 collective-permute-start.10
  66.3 3.1 %collective-permute-start.11 = (f32[45,8,128]{2,1,0:T(8,128)S(1)}, f32[45,8,128]{2,1,0:T(8,128)S(1)}, u32[]{:S(2)}, u32[]{:S(2)}) collective-permute-start(f32[45,8,128]{2,1,0:T(8,128)S(1)} %get-tuple-element.119.ends), channel_id=1, source_target_pairs={{0,16},{4,20},{8,24},{12,28},{16,0},{20,4},{24,8},{28,12},{1,17},{... | collective-permute-start | bytes 552968 | tf_op jit(solution)/shard_map/ppermute | solution.py:577
  69.5 0.0 collective-permute-done.9.other
  69.5 0.8 merge_flows.5
  70.3 0.8 collective-permute-done.10.other
  71.0 0.7 merge_flows.6
  71.7 2.0 %collective-permute-start.12 = (f32[30,8,128]{2,1,0:T(8,128)S(1)}, f32[30,8,128]{2,1,0:T(8,128)S(1)}, u32[]{:S(2)}, u32[]{:S(2)}) collective-permute-start(f32[30,8,128]{2,1,0:T(8,128)S(1)} %get-tuple-element.126.flows), channel_id=1, source_target_pairs={{0,8},{4,12},{8,0},{12,4},{16,24},{20,28},{24,16},{28,20},{1,9},{5... | collective-permute-start | bytes 368648 | tf_op jit(solution)/shard_map/ppermute | solution.py:577
  73.7 2.6 %collective-permute-start.13 = (f32[20,8,128]{2,1,0:T(8,128)S(1)}, f32[20,8,128]{2,1,0:T(8,128)S(1)}, u32[]{:S(2)}, u32[]{:S(2)}) collective-permute-start(f32[20,8,128]{2,1,0:T(8,128)S(1)} %get-tuple-element.131.ends), channel_id=1, source_target_pairs={{0,16},{4,20},{8,24},{12,28},{16,0},{20,4},{24,8},{28,12},{1,17},{... | collective-permute-start | bytes 245768 | tf_op jit(solution)/shard_map/ppermute | solution.py:577
  76.3 0.5 collective-permute-done.11.other
  76.8 2.6 %correct_all.1 = (f32[80,56,128]{2,1,0:T(8,128)S(1)}, f32[2,30,8,128]{3,2,1,0:T(8,128)S(1)}) custom-call(s32[6]{0:T(128)S(1)} %stack.35.flags, f32[45,8,128]{2,1,0:T(8,128)S(1)} %get-tuple-element.119.ends, f32[45,8,128]{2,1,0:T(8,128)S(1)} %collective-permute-done.11.other, f32[2,15,8,128]{3,2,1,0:T(8,128)S(1)} %get-tuple-element.120.share, ...), custom_call_target="tpu_custom_call" | custom-call | flops 1000 | bytes 1000 | tf_op jit(solution)/shard_map/correct_all/pallas_call | solution.py:46
  79.4 0.0 collective-permute-done.12.other
  79.4 0.7 merge_flows.7
  80.1 1.0 %collective-permute-start.14 = (f32[15,8,128]{2,1,0:T(8,128)S(1)}, f32[15,8,128]{2,1,0:T(8,128)S(1)}, u32[]{:S(2)}, u32[]{:S(2)}) collective-permute-start(f32[15,8,128]{2,1,0:T(8,128)S(1)} %get-tuple-element.135.ends), channel_id=1, source_target_pairs={{0,16},{4,20},{8,24},{12,28},{16,0},{20,4},{24,8},{28,12},{1,17},{... | collective-permute-start | bytes 184328 | tf_op jit(solution)/shard_map/ppermute | solution.py:577
  81.1 0.2 collective-permute-done.13.other
  81.2 1.7 %correct.1.refs_0_ = f32[80,32,128]{2,1,0:T(8,128)S(1)} custom-call(s32[6]{0:T(128)S(1)} %stack.35.flags, f32[2,30,8,128]{3,2,1,0:T(8,128)S(1)} %get-tuple-element.130.mats, f32[20,8,128]{2,1,0:T(8,128)S(1)} %get-tuple-element.131.ends, f32[20,8,128]{2,1,0:T(8,128)S(1)} %collective-permute-done.13.other, f32[40,8,128]{2,1,0:T(8,128)S(1)} %get-tuple-element.132.known, ...), custom_call_target="tpu_custom_call" | custom-call | flops 1000 | bytes 1000 | tf_op jit(solution)/shard_map/correct/pallas_call | solution.py:46
  83.0 2.3 %collective-permute-done.14.other = f32[15,8,128]{2,1,0:T(8,128)S(1)} collective-permute-done((f32[15,8,128]{2,1,0:T(8,128)S(1)}, f32[15,8,128]{2,1,0:T(8,128)S(1)}, u32[]{:S(2)}, u32[]{:S(2)}) %collective-permute-start.14) | collective-permute-done | bytes 61472 | tf_op jit(solution)/shard_map/ppermute | solution.py:577
  85.3 3.5 %finish.1 = f32[7840,128]{1,0:T(8,128)} custom-call(s32[6]{0:T(128)S(1)} %stack.35.flags, f32[2,30,8,128]{3,2,1,0:T(8,128)S(1)} %get-tuple-element.130.mats, f32[15,8,128]{2,1,0:T(8,128)S(1)} %get-tuple-element.135.ends, f32[15,8,128]{2,1,0:T(8,128)S(1)} %collective-permute-done.14.other, f32[30,8,128]{2,1,0:T(8,128)S(1)} %get-tuple-element.136.known, ...), custom_call_target="tpu_custom_call" | custom-call | flops 1000 | bytes 1000 | tf_op jit(solution)/shard_map/finish/pallas_call | solution.py:46
  (9 shorter events, 0.0 us)
Async XLA Ops:
  0.0 12.2 %copy-start.10 = (s32[24]{0:T(128)S(1)}, s32[24]{0:T(128)}, u32[]{:S(2)}) copy-start(s32[24]{0:T(128)} %param.18) | copy-start | bytes 292
  0.0 12.4 %copy-start.8 = (s32[2]{0:T(128)S(1)}, s32[2]{0:T(128)}, u32[]{:S(2)}) copy-start(s32[2]{0:T(128)} %blades.1) | copy-start | bytes 28
  0.0 2.2 %copy-start = (f32[16,2,5,49,128]{4,1,3,2,0:T(2,128)S(1)}, f32[16,2,5,49,128]{4,1,3,2,0:T(2,128)}, u32[]{:S(2)}) copy-start(f32[16,2,5,49,128]{4,1,3,2,0:T(2,128)} %param.11) | copy-start | bytes 12042244
  2.2 10.2 %copy-start.4 = (f32[64,192]{1,0:T(8,128)S(1)}, f32[64,192]{1,0:T(8,128)}, u32[]{:S(2)}) copy-start(f32[64,192]{1,0:T(8,128)} %constant.33.clone.turned) | copy-start | bytes 147460
  2.2 10.2 %copy-start.5 = (f32[56,56]{1,0:T(8,128)S(1)}, f32[56,56]{1,0:T(8,128)}, u32[]{:S(2)}) copy-start(f32[56,56]{1,0:T(8,128)} %constant.32.clone.basis) | copy-start | bytes 37636
  2.2 13.4 %copy-start.1 = (f32[16,2,5,5,128]{4,1,3,2,0:T(2,128)S(1)}, f32[16,2,5,5,128]{4,1,3,2,0:T(2,128)}, u32[]{:S(2)}) copy-start(f32[16,2,5,5,128]{4,1,3,2,0:T(2,128)} %param.15) | copy-start | bytes 1228804
  2.2 13.4 %copy-start.2 = (f32[16,2,5,5,128]{4,1,3,2,0:T(2,128)S(1)}, f32[16,2,5,5,128]{4,1,3,2,0:T(2,128)}, u32[]{:S(2)}) copy-start(f32[16,2,5,5,128]{4,1,3,2,0:T(2,128)} %param.16) | copy-start | bytes 1228804
  4.4 17.8 %copy-start.3 = (f32[16,2,5,128]{3,1,2,0:T(2,128)S(1)}, f32[16,2,5,128]{3,1,2,0:T(2,128)}, u32[]{:S(2)}) copy-start(f32[16,2,5,128]{3,1,2,0:T(2,128)} %param.13) | copy-start | bytes 245764
  4.4 24.1 %collective-permute-start.3 = (f32[80,56,128]{2,1,0:T(8,128)}, f32[80,56,128]{2,1,0:T(8,128)}, u32[]{:S(2)}, u32[]{:S(2)}) collective-permute-start(f32[80,56,128]{2,1,0:T(8,128)} %get-tuple-element.80.xn), channel_id=1, source_target_pairs={{0,1},{1,0},{2,3},{3,2},{4,5},{5,4},{6,7},{7,6},{8,9},{9,8},{10,11... | collective-permute-start | bytes 6881288 | tf_op jit(solution)/shard_map/ppermute | solution.py:592
  4.9 22.0 %collective-permute-start.2 = (f32[980,128]{1,0:T(8,128)}, f32[980,128]{1,0:T(8,128)}, u32[]{:S(2)}, u32[]{:S(2)}) collective-permute-start(f32[980,128]{1,0:T(8,128)} %get-tuple-element.73), channel_id=1, source_target_pairs={{0,3},{1,2},{2,1},{3,0},{4,7},{5,6},{6,5},{7,4},{8,11},{9,10},{10,... | collective-permute-start | bytes 1505288 | tf_op jit(solution)/shard_map/ppermute | solution.py:576
  7.5 14.7 %collective-permute-start = (f32[496,128]{1,0:T(8,128)}, f32[496,128]{1,0:T(8,128)S(1)}, u32[]{:S(2)}, u32[]{:S(2)}) collective-permute-start(f32[496,128]{1,0:T(8,128)} %get-tuple-element.81), channel_id=1, source_target_pairs={{0,4},{4,8},{8,12},{12,16},{16,20},{20,24},{24,28},{1,5},{5,9},{9,... | collective-permute-start | bytes 761864 | tf_op jit(solution)/shard_map/ppermute | solution.py:594
  10.9 11.3 %collective-permute-start.1 = (f32[496,128]{1,0:T(8,128)}, f32[496,128]{1,0:T(8,128)}, u32[]{:S(2)}, u32[]{:S(2)}) collective-permute-start(f32[496,128]{1,0:T(8,128)} %get-tuple-element.82), channel_id=1, source_target_pairs={{4,0},{8,4},{12,8},{16,12},{20,16},{24,20},{28,24},{5,1},{9,5},{13... | collective-permute-start | bytes 761864 | tf_op jit(solution)/shard_map/ppermute | solution.py:595
  12.3 4.9 %copy-start.9 = (bf16[16,2,5,5,128]{4,1,3,2,0:T(2,128)(2,1)S(1)}, bf16[16,2,5,5,128]{4,1,3,2,0:T(2,128)(2,1)}, u32[]{:S(2)}) copy-start(bf16[16,2,5,5,128]{4,1,3,2,0:T(2,128)(2,1)} %param.14) | copy-start | bytes 614404
  12.3 9.9 %copy-start.6 = (f32[16,2,5,128]{3,1,2,0:T(2,128)S(1)}, f32[16,2,5,128]{3,1,2,0:T(2,128)}, u32[]{:S(2)}) copy-start(f32[16,2,5,128]{3,1,2,0:T(2,128)} %param.12) | copy-start | bytes 245764
  12.3 9.9 %copy-start.7 = (f32[56,192]{1,0:T(8,128)S(1)}, f32[56,192]{1,0:T(8,128)}, u32[]{:S(2)}) copy-start(f32[56,192]{1,0:T(8,128)} %constant.34.clone.table) | copy-start | bytes 129028
  15.5 25.1 %collective-permute-start.4 = (f32[1920,128]{1,0:T(8,128)S(1)}, f32[1920,128]{1,0:T(8,128)S(1)}, u32[]{:S(2)}, u32[]{:S(2)}) collective-permute-start(f32[1920,128]{1,0:T(8,128)S(1)} %get-tuple-element.93), channel_id=1, source_target_pairs={{0,3},{1,2},{2,1},{3,0},{4,7},{5,6},{6,5},{7,4},{8,11},{9,10},{10,... | collective-permute-start | bytes 2949128 | tf_op jit(solution)/shard_map/ppermute | solution.py:576
  36.7 11.2 %collective-permute-start.5 = (f32[100,8,128]{2,1,0:T(8,128)S(1)}, f32[100,8,128]{2,1,0:T(8,128)S(1)}, u32[]{:S(2)}, u32[]{:S(2)}) collective-permute-start(f32[100,8,128]{2,1,0:T(8,128)S(1)} %get-tuple-element.96.flows), channel_id=1, source_target_pairs={{0,4},{4,0},{8,12},{12,8},{16,20},{20,16},{24,28},{28,24},{1,5},{5... | collective-permute-start | bytes 1228808 | tf_op jit(solution)/shard_map/ppermute | solution.py:577
  39.1 25.0 %collective-permute-start.8 = (f32[1024,128]{1,0:T(8,128)S(1)}, f32[1024,128]{1,0:T(8,128)S(1)}, u32[]{:S(2)}, u32[]{:S(2)}) collective-permute-start(f32[1024,128]{1,0:T(8,128)S(1)} %get-tuple-element.108), channel_id=1, source_target_pairs={{0,3},{1,2},{2,1},{3,0},{4,7},{5,6},{6,5},{7,4},{8,11},{9,10},{10,... | collective-permute-start | bytes 1572872 | tf_op jit(solution)/shard_map/ppermute | solution.py:576
  48.9 14.1 %collective-permute-start.7 = (f32[100,8,128]{2,1,0:T(8,128)S(1)}, f32[100,8,128]{2,1,0:T(8,128)S(1)}, u32[]{:S(2)}, u32[]{:S(2)}) collective-permute-start(f32[100,8,128]{2,1,0:T(8,128)S(1)} %get-tuple-element.103.flows), channel_id=1, source_target_pairs={{0,8},{4,12},{8,0},{12,4},{16,24},{20,28},{24,16},{28,20},{1,9},{5... | collective-permute-start | bytes 1228808 | tf_op jit(solution)/shard_map/ppermute | solution.py:577
  52.7 5.3 %collective-permute-start.6 = (f32[40,8,128]{2,1,0:T(8,128)S(1)}, f32[40,8,128]{2,1,0:T(8,128)S(1)}, u32[]{:S(2)}, u32[]{:S(2)}) collective-permute-start(f32[40,8,128]{2,1,0:T(8,128)S(1)} %get-tuple-element.100.flows), channel_id=1, source_target_pairs={{0,4},{4,0},{8,12},{12,8},{16,20},{20,16},{24,28},{28,24},{1,5},{5... | collective-permute-start | bytes 491528 | tf_op jit(solution)/shard_map/ppermute | solution.py:577
  58.7 10.7 %collective-permute-start.9 = (f32[40,8,128]{2,1,0:T(8,128)S(1)}, f32[40,8,128]{2,1,0:T(8,128)S(1)}, u32[]{:S(2)}, u32[]{:S(2)}) collective-permute-start(f32[40,8,128]{2,1,0:T(8,128)S(1)} %get-tuple-element.112.flows), channel_id=1, source_target_pairs={{0,8},{4,12},{8,0},{12,4},{16,24},{20,28},{24,16},{28,20},{1,9},{5... | collective-permute-start | bytes 491528 | tf_op jit(solution)/shard_map/ppermute | solution.py:577
  66.1 4.9 %collective-permute-start.10 = (f32[30,8,128]{2,1,0:T(8,128)S(1)}, f32[30,8,128]{2,1,0:T(8,128)S(1)}, u32[]{:S(2)}, u32[]{:S(2)}) collective-permute-start(f32[30,8,128]{2,1,0:T(8,128)S(1)} %get-tuple-element.116.flows), channel_id=1, source_target_pairs={{0,4},{4,0},{8,12},{12,8},{16,20},{20,16},{24,28},{28,24},{1,5},{5... | collective-permute-start | bytes 368648 | tf_op jit(solution)/shard_map/ppermute | solution.py:577
  66.3 10.4 %collective-permute-start.11 = (f32[45,8,128]{2,1,0:T(8,128)S(1)}, f32[45,8,128]{2,1,0:T(8,128)S(1)}, u32[]{:S(2)}, u32[]{:S(2)}) collective-permute-start(f32[45,8,128]{2,1,0:T(8,128)S(1)} %get-tuple-element.119.ends), channel_id=1, source_target_pairs={{0,16},{4,20},{8,24},{12,28},{16,0},{20,4},{24,8},{28,12},{1,17},{... | collective-permute-start | bytes 552968 | tf_op jit(solution)/shard_map/ppermute | solution.py:577
  71.7 7.6 %collective-permute-start.12 = (f32[30,8,128]{2,1,0:T(8,128)S(1)}, f32[30,8,128]{2,1,0:T(8,128)S(1)}, u32[]{:S(2)}, u32[]{:S(2)}) collective-permute-start(f32[30,8,128]{2,1,0:T(8,128)S(1)} %get-tuple-element.126.flows), channel_id=1, source_target_pairs={{0,8},{4,12},{8,0},{12,4},{16,24},{20,28},{24,16},{28,20},{1,9},{5... | collective-permute-start | bytes 368648 | tf_op jit(solution)/shard_map/ppermute | solution.py:577
  73.7 7.5 %collective-permute-start.13 = (f32[20,8,128]{2,1,0:T(8,128)S(1)}, f32[20,8,128]{2,1,0:T(8,128)S(1)}, u32[]{:S(2)}, u32[]{:S(2)}) collective-permute-start(f32[20,8,128]{2,1,0:T(8,128)S(1)} %get-tuple-element.131.ends), channel_id=1, source_target_pairs={{0,16},{4,20},{8,24},{12,28},{16,0},{20,4},{24,8},{28,12},{1,17},{... | collective-permute-start | bytes 245768 | tf_op jit(solution)/shard_map/ppermute | solution.py:577
  80.1 5.2 %collective-permute-start.14 = (f32[15,8,128]{2,1,0:T(8,128)S(1)}, f32[15,8,128]{2,1,0:T(8,128)S(1)}, u32[]{:S(2)}, u32[]{:S(2)}) collective-permute-start(f32[15,8,128]{2,1,0:T(8,128)S(1)} %get-tuple-element.135.ends), channel_id=1, source_target_pairs={{0,16},{4,20},{8,24},{12,28},{16,0},{20,4},{24,8},{28,12},{1,17},{... | collective-permute-start | bytes 184328 | tf_op jit(solution)/shard_map/ppermute | solution.py:577

commit v4 on v3

--- a/solution.py
+++ b/solution.py
@@ -19,7 +19,7 @@
 LEAD = 4
 MB = 1 << 20
 
-CHUNKS = (((0, 32), False), ((32, 48), True))
+CHUNKS = (((0, 24), False), ((24, 40), True), ((40, 48), False))
 
 
 def rows_of(chunk):
@@ -85,7 +85,7 @@
     return jnp.dot(basis, right, preferred_element_type=F32, precision=lax.Precision.HIGHEST)
 
 
-def over_instants(left, cells):
+def over_instants(lefts, cells):
     whole = jnp.concatenate(cells, axis=1)
     if whole.shape[0] < DEPTH:
         whole = jnp.concatenate(
@@ -93,10 +93,9 @@
         )
     high = whole.astype(BF16)
     low = (whole - high.astype(F32)).astype(BF16)
-    product = jnp.dot(
-        left, jnp.concatenate([high, low, high], axis=0), preferred_element_type=F32
-    )
-    return [product[:, i * LANES : (i + 1) * LANES] for i in range(len(cells))]
+    right = jnp.concatenate([high, low, high], axis=0)
+    products = [jnp.dot(left, right, preferred_element_type=F32) for left in lefts]
+    return [[x[:, i * LANES : (i + 1) * LANES] for i in range(len(cells))] for x in products]
 
 
 def split_cells(st, slab, first_cell, last_cell, xn, xf):
@@ -135,27 +134,75 @@
     trig[2 * count : 2 * count + 8, :] = (stator / rotor / count)[:8]
 
 
-def prepare(flags, blades, xf, harmonic, basis, turned, trig, *chunks):
+def own_terms(z, x, other, advect, viscous, p, timing, above, below, base):
+    for v in range(V):
+        j = z * V + v
+        total = viscous[pl.ds(j * 2 + p, 1), :] * (other[j] - 2.0 * x[j]) - timing[v]
+        rate = advect[pl.ds(j * 2 + p, 1), :]
+        if above and below:
+            total += rate * (x[j - V] - x[j + V])
+        else:
+            total += rate * (x[j - V] if above else -x[j + V])
+        base[j] = total
+
+
+def timing_matrix(table, trig):
+    return split_left(table[...] * trig[trig.shape[0] - 8 : trig.shape[0] - 7, :1])
+
+
+def prepare(flags, blades, xn, xf, harmonic, basis, turned, advect, viscous, table, trig, base, *chunks):
     lags(blades, harmonic, trig)
-    wrap = flags[1]
+    p, wrap = flags[0], flags[1]
     cells = xf.shape[0] // V
     sign = jnp.where(flags[2] == 1, 1.0, -1.0)
-    left = split_left(lag_matrix(basis[...], turned[...], trig[...], sign))
-
-    def step(z, carry):
+    lag = split_left(lag_matrix(basis[...], turned[...], trig[...], sign))
+    derive = timing_matrix(table, trig)
+
+    def one(z, above=True, below=True, sends=True):
         raw = [xf[z * V + v] for v in range(V)]
-        lagged = over_instants(left, raw)
+        timing, *lagged = over_instants([derive, lag] if sends else [derive], raw)
+        own_terms(z, xf, xn, advect, viscous, p, timing, above, below, base)
+        if not sends:
+            return
         for v in range(V):
-            value = jnp.where(wrap == 1, lagged[v], raw[v])
+            value = jnp.where(wrap == 1, lagged[0][v], raw[v])
             j = (z - LEAD) * V + v
             for out, ((first, last), extra) in zip(chunks, CHUNKS):
                 width = last - first
                 out[pl.ds(pl.multiple_of(j * width, 8), width), :] = value[first:last]
                 if extra:
                     out[pl.ds((cells - LEAD) * V * width + j, 1), :] = value[NT - 1 : NT]
+
+    def early(z, carry):
+        one(z, sends=False)
         return carry
 
-    lax.fori_loop(LEAD, cells, step, 0)
+    def late(z, carry):
+        one(z)
+        return carry
+
+    one(0, above=False, sends=False)
+    lax.fori_loop(1, LEAD, early, 0)
+    lax.fori_loop(LEAD, cells - 1, late, 0)
+    one(cells - 1, below=False)
+
+
+def near_base(flags, xn, xf, advect, viscous, table, trig, base):
+    p = 1 - flags[0]
+    cells = xn.shape[0] // V
+    derive = timing_matrix(table, trig)
+
+    def one(z, above=True, below=True):
+        (timing,) = over_instants([derive], [xn[z * V + v] for v in range(V)])
+        own_terms(z, xn, xf, advect, viscous, p, timing, above, below, base)
+
+    def inner(z, carry):
+        one(z)
+        return carry
+
+    one(0, above=False)
+    lax.fori_loop(1, cells - 1, inner, 0)
+    one(cells - 1, below=False)
 
 
 def keep_tiles(ref, offset, values, first, last, height):
@@ -182,7 +229,8 @@
                 result.append(total)
             return tuple(result)
 
-        out = lax.fori_loop(0, cells, ahead, nothing)
+        out = lax.fori_loop(1, cells - 1, ahead, ahead(0, nothing))
+        out = ahead(cells - 1, out)
         keep_tiles(fg, offset, out, first, last, height)
 
         def back(i, current, first=first, last=last):
@@ -209,66 +257,33 @@
         edges[V + v, 0:NT, :] = from_right[pl.ds(v * 2 * NT + p, NT, stride=2), :]
 
 
-def residuals(x, other, halo, edges, advect, viscous, left, p, cells, put):
-    def one(z, above, below):
-        here = [x[z * V + v] for v in range(V)]
-        timing = over_instants(left, here)
+def edge_terms(z, cells, values, edges, advect, p, first, last):
+    if not isinstance(z, int):
+        return values
+    return [
+        value
+        + (1.0 if z == 0 else -1.0)
+        * advect[pl.ds((z * V + v) * 2 + p, 1), :]
+        * edges[v if z == 0 else V + v, first:last, :]
+        for v, value in enumerate(values)
+    ]
+
+
+def near_cell(
+    flags, base, halo, from_left, from_right, advect, viscous, inverse, lower, upper, g, flows, edges
+):
+    p = 1 - flags[0]
+    cells = base.shape[0] // V
+    take_edges(edges, from_left, from_right, p)
+
+    def source(z, first, last):
+        values = []
         for v in range(V):
             j = z * V + v
-            pitch = other[j] - 2.0 * here[v]
-            if halo is not None:
-                pitch += halo[j]
-            put(
-                j,
-                advect[pl.ds(j * 2 + p, 1), :] * (above(z, v) - below(z, v))
-                + viscous[pl.ds(j * 2 + p, 1), :] * pitch
-                - timing[v],
-            )
-
-    inner_above = lambda z, v: x[(z - 1) * V + v]
-    inner_below = lambda z, v: x[(z + 1) * V + v]
-    one(0, lambda z, v: edges[v], inner_below)
-
-    def step(z, carry):
-        one(z, inner_above, inner_below)
-        return carry
-
-    lax.fori_loop(1, cells - 1, step, 0)
-    one(cells - 1, inner_above, lambda z, v: edges[V + v])
-
-
-def timing_matrix(table, trig):
-    return split_left(table[...] * trig[trig.shape[0] - 8 : trig.shape[0] - 7, :1])
-
-
-def near_cell(
-    flags, xn, xf, halo, from_left, from_right, advect, viscous, inverse, lower, upper, trig, table,
-    group, g, flows, right, edges,
-):
-    p = 1 - flags[0]
-    cells = xn.shape[0] // V
-    take_edges(edges, from_left, from_right, p)
-
-    def put(j, value):
-        right[j] = value
-
-    residuals(xn, xf, halo, edges, advect, viscous, timing_matrix(table, trig), p, cells, put)
-    source = lambda z, first, last: [right[z * V + v, first:last, :] for v in range(V)]
+            values.append(base[j, first:last, :] + viscous[pl.ds(j * 2 + p, 1), :] * halo[j, first:last, :])
+        return edge_terms(z, cells, values, edges, advect, p, first, last)
+
     sweeps(source, g, flows, 0, ((0, 32), (32, PAD)), p, inverse, lower, upper, cells)
-    for c in range(2):
-        for i in range(3 * V):
-            flows[2 * V * PAD // 8 + c * 3 * V + i] = group[c, i]
-
-
-def far_base(flags, xn, xf, from_left, from_right, advect, viscous, trig, table, base, edges):
-    p = flags[0]
-    cells = xn.shape[0] // V
-    take_edges(edges, from_left, from_right, p)
-
-    def put(j, value):
-        base[j] = value
-
-    residuals(xf, xn, None, edges, advect, viscous, timing_matrix(table, trig), p, cells, put)
 
 
 def far_lead(flags, slab, trig, basis, turned, lead, halo):
@@ -280,19 +295,20 @@
             halo[v, PAD - 8 : PAD, :] = jnp.zeros((8, LANES), F32)
             halo[v, 0:NT, :] = slab[pl.ds((z * V + v) * NT, NT), :]
         raw = [halo[v] for v in range(V)]
-        lagged = over_instants(left, raw)
+        (lagged,) = over_instants([left], raw)
         for v in range(V):
             lead[z * V + v] = jnp.where(wrap == 1, lagged[v], raw[v])
 
 
-def far_chunk(chunk, flags, base, lead, halo, viscous, inverse, lower, upper, g, fg):
+def far_chunk(chunk, flags, base, lead, halo, from_left, from_right, advect, viscous, inverse, lower, upper, g, fg, edges):
     (first, last), extra = chunk
     width = last - first
     p = flags[0]
     cells = base.shape[0] // V
     top = lax.broadcasted_iota(jnp.int32, (8, LANES), 0) == 0
-
-    def pieces(ref, j, rows):
+    take_edges(edges, from_left, from_right, p)
+
+    def pieces(ref, j):
         value = ref[j, first:last, :]
         return jnp.concatenate([value, ref[j, PAD - 8 : PAD, :]], axis=0) if extra else value
 
@@ -305,9 +321,14 @@
             if extra:
                 row = halo[pl.ds((cells - LEAD) * V * width + h, 1), :]
                 arrived = jnp.concatenate([arrived, jnp.where(top, row, 0.0)], axis=0)
-            early = pieces(lead, jnp.minimum(z, LEAD - 1) * V + v, rows)
+            early = pieces(lead, jnp.minimum(z, LEAD - 1) * V + v)
             arrived = jnp.where(z >= LEAD, arrived, early)
-            result.append(pieces(base, j, rows) + viscous[pl.ds(j * 2 + p, 1), :] * arrived)
+            value = pieces(base, j) + viscous[pl.ds(j * 2 + p, 1), :] * arrived
+            if isinstance(z, int):
+                rate = advect[pl.ds(j * 2 + p, 1), :]
+                edge = pieces(edges, v if z == 0 else V + v)
+                value += rate * edge if z == 0 else -rate * edge
+            result.append(value)
         return result
 
     height = rows_of(chunk)
@@ -369,19 +390,21 @@
         )
         ends = lax.fori_loop(0, cells, back, start)
         for a in range(V):
-            group[c, a] = ends[a][:8]
-            group[c, V + a] = ends[a][8:]
-            group[c, 2 * V + a] = through[a]
-
-
-def merge_matrices(bit, levels, flags, mine, other, share, mats, merged, share_out, offset, new_offset):
+            group[c * 3 * V + a] = ends[a][:8]
+            group[(c * 3 + 1) * V + a] = ends[a][8:]
+            group[(c * 3 + 2) * V + a] = through[a]
+
+
+def merge_matrices(bit, levels, flags, mine, other, *refs):
     start, last = bit == 0, bit == levels - 1
+    share, refs = (None, refs) if start else (refs[0], refs[1:])
+    mats, merged, share_out = (refs[0], None, None) if last else refs
     right = flags[3 + bit] == 1
     left = jnp.logical_not(right)
     nothing = jnp.zeros((8, LANES), F32)
     for c in range(2):
         kinds = 1 if last else 3
-        at = lambda ref, kind: [ref[offset + (c * kinds + kind) * V + a] for a in range(V)]
+        at = lambda ref, kind: [ref[(c * kinds + kind) * V + a] for a in range(V)]
         pick = lambda kind, own: [jnp.where(own, m, t) for m, t in zip(at(mine, kind), at(other, kind))]
         if start:
             own = [[unit(a) for a in range(V)], [nothing] * V, [unit(a) for a in range(V)]]
@@ -407,7 +430,7 @@
             new += [times(rows(mats, c, 2), h_right), times(rows(mats, c, 0), p_left)]
         for kind, values in enumerate(new):
             for a in range(V):
-                merged[new_offset + (c * len(new) + kind) * V + a] = values[a]
+                merged[(c * len(new) + kind) * V + a] = values[a]
         s0 = times(rows(mats, c, 3), p_left)
         s1 = times(rows(mats, c, 4), p_left)
         s1b = times(rows(mats, c, 5), turned)
@@ -424,14 +447,6 @@
     from_right = plus(times(rows(mats, c, 4), f_left), times(rows(mats, c, 5), back))
     total = from_left + from_right
     return back, total if known is None else plus(known, total)
-
-
-def merge_all(parts, bit, levels, flags, flows, other, *refs):
-    share, known, mats, merged, share_out, inflow = (None, None, *refs) if bit == 0 else refs
-    tall = sum(height for _, height in parts) * V
-    new_offset = tall * (1 if bit == levels - 2 else 2)
-    merge_matrices(bit, levels, flags, flows, other, share, mats, merged, share_out, 2 * tall, new_offset)
-    merge_flows(parts, bit, levels, flags, mats, flows, other, *([] if known is None else [known]), merged, inflow)
 
 
 def merge_flows(parts, bit, levels, flags, mats, flows, other, *refs):
@@ -507,14 +522,6 @@
             lax.fori_loop(0, g.shape[0] // V, step, flow)
 
 
-def correct_all(parts, levels, flags, ends, other, share, known, blocks, *refs):
-    count = len(parts)
-    solved, results, mats, inflow = refs[:count], refs[count : 2 * count], refs[-2], refs[-1]
-    tall = sum(height for _, height in parts) * V
-    merge_matrices(levels - 1, levels, flags, ends, other, share, mats, None, None, tall, 0)
-    correct(parts, levels, flags, mats, ends, other, known, blocks, *solved, *results, inflow)
-
-
 def finish(levels, flags, mats, ends, other, known, g, blocks, near, *refs):
     done, out, inflow = refs[:-2], refs[-2], refs[-1]
     right = flags[2 + levels] == 1
@@ -564,6 +571,9 @@
     wide = np.zeros((PAD, 3, DEPTH), np.float32)
     wide[:NT, :, :NT] = table[:, None]
     return wide.reshape(PAD, 3 * DEPTH)
+
+
+COSTS = (0, 0, 6_000_000_000, 0)
 
 
 def local(state, advect, viscous, inverse, lower, upper, blades, harmonic):
@@ -613,9 +623,11 @@
         (rest * (last - first) + (padded_even(rest) if extra else 0), LANES)
         for (first, last), extra in CHUNKS
     ]
-    trig, *chunks = run(
-        prepare, [(2 * count + 8, LANES), *chunk_shapes], [xf, wide_harmonic, basis, turned],
-        scalars=[blades], name="prepare",
+    adv = advect.transpose(0, 2, 1, 3).reshape(cells * V * 2, LANES)
+    vis = viscous.transpose(0, 2, 1, 3).reshape(cells * V * 2, LANES)
+    trig, base, *chunks = run(
+        prepare, [(2 * count + 8, LANES), x_shape, *chunk_shapes],
+        [xn, xf, wide_harmonic, basis, turned, adv, vis, table], scalars=[blades], name="prepare",
     )
     arrived = [slab_in]
     for chunk in chunks:
@@ -626,98 +638,98 @@
 
     flat = lambda x: x.transpose(0, 2, 3, 1, 4).reshape(cells * V * V * 2, LANES)
     inv, low, upp = flat(inverse.astype(F32)), flat(lower), flat(upper)
-    adv = advect.transpose(0, 2, 1, 3).reshape(cells * V * 2, LANES)
-    vis = viscous.transpose(0, 2, 1, 3).reshape(cells * V * 2, LANES)
     edges = pltpu.VMEM((2 * V, PAD, LANES), F32)
 
-    mats = []
-    mats_shape = (2, 6 * V, 8, LANES)
+    mats, group, share = [], None, []
+
+    def merge_group(k):
+        nonlocal group, share
+        shapes = [(2, 6 * V, 8, LANES)]
+        if k < levels - 1:
+            shapes += [((6 if k < levels - 2 else 2) * V, 8, LANES), (2, 3 * V, 8, LANES)]
+        out = run(
+            functools.partial(merge_matrices, k, levels), shapes,
+            [group, to_level(group, k), *share], name="merge_matrices",
+        )
+        mats.append(out[0])
+        if k < levels - 1:
+            group, share = out[1], [out[2]]
 
     def solve_chunk(i):
         height = rows_of(CHUNKS[i])
         return run(
             functools.partial(far_chunk, CHUNKS[i]),
             [(cells * V, height, LANES), (2 * V * height // 8, 8, LANES)],
-            [base, lead, arrived[i], vis, inv, low, upp], name="far_chunk",
+            [base, lead, arrived[i], from_left, from_right, adv, vis, inv, low, upp],
+            scratch=[edges], name="far_chunk",
         )
 
     class Exchange:
-        def __init__(self, c, g, flows, leads=False):
-            self.parts, self.leads = [(c, g.shape[1] // 8)], leads
+        def __init__(self, c, g, flows):
+            self.parts = [(c, g.shape[1] // 8)]
             self.flows, self.known, self.solved, self.level = flows, [], g, 0
-            self.scratch = [pltpu.VMEM((2 * V, g.shape[1], LANES), F32)]
 
         def step(self):
             tall, k = self.parts[0][1], self.level
             shape = ((2 if k < levels - 2 else 1) * V * tall, 8, LANES)
-            inflow = (2 * V * tall, 8, LANES)
-            other = to_level(self.flows, k)
-            if self.leads:
-                shape = (shape[0] + (6 * V if k < levels - 2 else 2 * V),) + shape[1:]
-                out = run(
-                    functools.partial(merge_all, self.parts, k, levels),
-                    [mats_shape, shape, (2, 3 * V, 8, LANES), inflow],
-                    [self.flows, other, *self.known], name="merge_all",
-                )
-                mats.append(out[0])
-                self.flows, self.known = out[1], out[2:]
-            else:
-                out = run(
-                    functools.partial(merge_flows, self.parts, k, levels), [shape, inflow],
-                    [mats[k], self.flows, other, *self.known], name="merge_flows",
-                )
-                self.flows, self.known = out[0], out[1:]
-            self.level = k + 1
+            out = run(
+                functools.partial(merge_flows, self.parts, k, levels),
+                [shape, (2 * V * tall, 8, LANES)],
+                [mats[k], self.flows, to_level(self.flows, k), *self.known], name="merge_flows",
+            )
+            self.flows, self.known, self.level = out[0], out[1:], k + 1
 
         def last(self):
-            return [self.flows, to_level(self.flows, levels - 1), *self.known]
+            return [mats[-1], self.flows, to_level(self.flows, levels - 1), *self.known]
 
         def correct(self):
-            if self.leads:
-                result, last = run(
-                    functools.partial(correct_all, self.parts, levels), [self.solved.shape, mats_shape],
-                    [*self.last(), blocks, self.solved], scratch=self.scratch, name="correct_all",
-                )
-                mats.append(last)
-                return result
             return run(
                 functools.partial(correct, self.parts, levels), [self.solved.shape],
-                [mats[-1], *self.last(), blocks, self.solved], scratch=self.scratch, name="correct",
+                [*self.last(), blocks, self.solved],
+                scratch=[pltpu.VMEM((2 * V, self.solved.shape[1], LANES), F32)], name="correct",
             )[0]
 
+    base_near = run(
+        near_base, [x_shape], [xn, xf, adv, vis, table, trig], name="near_base", flops=COSTS[0]
+    )[0]
     blocks, group = run(
-        transfer, [(2, cells * V, 16, LANES), (2, 3 * V, 8, LANES)], [low, upp],
-        scratch=[pltpu.VMEM((cells * V, 8, LANES), F32)], name="transfer",
+        transfer, [(2, cells * V, 16, LANES), (6 * V, 8, LANES)], [low, upp],
+        scratch=[pltpu.VMEM((cells * V, 8, LANES), F32)], name="transfer", flops=COSTS[1],
     )
-    base = run(
-        far_base, [x_shape], [xn, xf, from_left, from_right, adv, vis, trig, table],
-        scratch=[edges], name="far_base",
-    )[0]
+    first = Exchange(
+        0,
+        *run(
+            near_cell, [x_shape, (2 * V * PAD // 8, 8, LANES)],
+            [base_near, halo_near, from_left, from_right, adv, vis, inv, low, upp],
+            scratch=[edges], name="near_cell", flops=COSTS[2],
+        )
+    )
     lead = run(
         far_lead, [(LEAD * V, PAD, LANES)], [slab_in, trig, basis, turned],
-        scratch=[pltpu.VMEM((V, PAD, LANES), F32)], name="far_lead",
+        scratch=[pltpu.VMEM((V, PAD, LANES), F32)], name="far_lead", flops=COSTS[3],
     )[0]
-    g_near, flows_near = run(
-        near_cell, [x_shape, (2 * V * PAD // 8 + 6 * V, 8, LANES)],
-        [xn, xf, halo_near, from_left, from_right, adv, vis, inv, low, upp, trig, table, group],
-        scratch=[pltpu.VMEM(x_shape, F32), edges], name="near_cell", flops=6_000_000_000,
-    )
-    first = Exchange(0, g_near, flows_near, leads=True)
     second = Exchange(1, *solve_chunk(0))
+    merge_group(0)
     first.step()
     second.step()
-    for k in range(1, levels - 1):
-        first.step()
+    for k in range(1, levels):
+        merge_group(k)
     third = Exchange(1, *solve_chunk(1))
     for k in range(1, levels - 1):
         second.step()
+        first.step()
+    fourth = Exchange(1, *solve_chunk(2))
     third.step()
+    done = [second.correct()]
+    fourth.step()
+    for k in range(1, levels - 1):
+        third.step()
     near = first.correct()
     for k in range(1, levels - 1):
-        third.step()
-    done = [second.correct()]
-    g_last = third.solved
-    small = [mats[-1], *third.last()]
+        fourth.step()
+    done.append(third.correct())
+    g_last = fourth.solved
+    small = fourth.last()
 
     steps = 4
     part = cells // steps

time: 89 us -> 95.1 us (1.069)
  starting transfers between devices: 23.4 us -> 32.8 us
  waiting for transfers between devices: 24.1 us -> 16.3 us
  local copies, waits for them, and re-layouts: 2.36 us -> 6.96 us
    ppermute x9 -> x15, starting transfers between devices: 15.6 us -> 23.2 us  [local(): lax.ppermute(x, 'seg', [(i, i ^ 1 << k) for i in range(segs)])]
    ppermute x9 -> x15, waiting for transfers between devices: 17.8 us -> 12.2 us  [local(): lax.ppermute(x, 'seg', [(i, i ^ 1 << k) for i in range(segs)])]
    ppermute x1, waiting for transfers between devices: 4.83 us -> 0.01 us  [local(): lax.ppermute(last_cell, 'seg', [(i, i + 1) for i in range(segs - 1)])]
    unnamed x22 -> x30, local copies, waits for them, and re-layouts: 2.2 us -> 6.8 us
    ppermute x3 -> x4, waiting for transfers between devices: 1.51 us -> 4.02 us  [local(): to_far = lambda x: lax.ppermute(x, 'pitch', far_pairs)]
    ppermute x3 -> x4, starting transfers between devices: 2.7 us -> 4.47 us  [local(): to_far = lambda x: lax.ppermute(x, 'pitch', far_pairs)]
    pallas_call x16 -> x23, Pallas kernels: 36.3 us -> 36.9 us  [__call__(): pl.pallas_call(body, out_shape=[jax.ShapeDtypeStruct(s, F32) for s in out...]
  transfers between devices with their start and end apart: 15 -> 22, of which waited for: 9 -> 8; matrix products, arithmetic and copies ran while one was open for 0% -> 0% of each run, Pallas kernels for 37% -> 35%
where the time goes in v4:
time: 95.1 us; the launch traced here: 94.8 us
  Pallas kernels  38.3 us (40%)
  starting transfers between devices  32.8 us (34%)
  waiting for transfers between devices  16.3 us (17%)
  local copies, waits for them, and re-layouts  6.96 us (7%)
    pallas_call x23, Pallas kernels, __call__(): pl.pallas_call(body, out_shape=[jax.ShapeDtypeStruct(s, F32) for s in out...  36.9 us
    ppermute x15, starting transfers between devices, local(): lax.ppermute(x, 'seg', [(i, i ^ 1 << k) for i in range(segs)])  23.2 us
    ppermute x15, waiting for transfers between devices, local(): lax.ppermute(x, 'seg', [(i, i ^ 1 << k) for i in range(segs)])  12.2 us
    unnamed x30, local copies, waits for them, and re-layouts  6.8 us
    ppermute x4, starting transfers between devices, local(): to_far = lambda x: lax.ppermute(x, 'pitch', far_pairs)  4.47 us
    ppermute x4, waiting for transfers between devices, local(): to_far = lambda x: lax.ppermute(x, 'pitch', far_pairs)  4.02 us
    ppermute x1, starting transfers between devices, local(): lax.ppermute(last_cell, 'seg', [(i, i + 1) for i in range(segs - 1)])  3.4 us
  transfers between devices with their start and end apart: 22, of which 8 were waited for; matrix products, arithmetic and copies ran while one was open for 0% of the time, Pallas kernels for 35%

profile of v4, /device:TPU:0, one launch (start us, length us, event | category | flops | bytes accessed | tf_op | source)
XLA Modules:
  0.0 94.8 jit_solution(17264506041921093850)
XLA Ops:
  0.0 2.2 %copy-done.5 = f32[16,2,5,49,128]{4,1,3,2,0:T(2,128)S(1)} copy-done((f32[16,2,5,49,128]{4,1,3,2,0:T(2,128)S(1)}, f32[16,2,5,49,128]{4,1,3,2,0:T(2,128)}, u32[]{:S(2)}) %copy-start.5) | copy-done | bytes 4014104
  2.2 1.4 %split_cells.1 = (f32[980,128]{1,0:T(8,128)}, f32[496,128]{1,0:T(8,128)}, f32[496,128]{1,0:T(8,128)}, f32[80,56,128]{2,1,0:T(8,128)S(1)}, f32[80,56,128]{2,1,0:T(8,128)S(1)}) custom-call(f32[7840,128]{1,0:T(8,128)S(1)} %bitcast.41), custom_call_target="tpu_custom_call" | custom-call | tf_op jit(solution)/shard_map/split_cells/pallas_call | solution.py:594
  3.6 1.4 %copy-done = f32[80,56,128]{2,1,0:T(8,128)} copy-done((f32[80,56,128]{2,1,0:T(8,128)}, f32[80,56,128]{2,1,0:T(8,128)S(1)}, u32[]{:S(2)}) %copy-start) | copy-done | bytes 2293784
  5.0 0.5 collective-permute-start
  5.4 2.6 %collective-permute-start.3 = (f32[980,128]{1,0:T(8,128)}, f32[980,128]{1,0:T(8,128)S(1)}, u32[]{:S(2)}, u32[]{:S(2)}) collective-permute-start(f32[980,128]{1,0:T(8,128)} %get-tuple-element.97), channel_id=1, source_target_pairs={{0,3},{1,2},{2,1},{3,0},{4,7},{5,6},{6,5},{7,4},{8,11},{9,10},{10,... | collective-permute-start | bytes 1505288 | tf_op jit(solution)/shard_map/ppermute | solution.py:586
  8.1 3.4 %collective-permute-start.1 = (f32[496,128]{1,0:T(8,128)}, f32[496,128]{1,0:T(8,128)S(1)}, u32[]{:S(2)}, u32[]{:S(2)}) collective-permute-start(f32[496,128]{1,0:T(8,128)} %get-tuple-element.108), channel_id=1, source_target_pairs={{0,4},{4,8},{8,12},{12,16},{16,20},{20,24},{24,28},{1,5},{5,9},{9,... | collective-permute-start | bytes 761864 | tf_op jit(solution)/shard_map/ppermute | solution.py:604
  11.5 1.3 %collective-permute-start.2 = (f32[496,128]{1,0:T(8,128)}, f32[496,128]{1,0:T(8,128)S(1)}, u32[]{:S(2)}, u32[]{:S(2)}) collective-permute-start(f32[496,128]{1,0:T(8,128)} %get-tuple-element.109), channel_id=1, source_target_pairs={{4,0},{8,4},{12,8},{16,12},{20,16},{24,20},{28,24},{5,1},{9,5},{13... | collective-permute-start | bytes 761864 | tf_op jit(solution)/shard_map/ppermute | solution.py:605
  12.8 0.1 stack.35.flags
  12.9 0.1 broadcast_in_dim.2.harmonic
  13.0 0.0 copy-start.1
  13.0 1.6 %copy-done.1 = f32[80,56,128]{2,1,0:T(8,128)S(1)} copy-done((f32[80,56,128]{2,1,0:T(8,128)S(1)}, f32[80,56,128]{2,1,0:T(8,128)}, u32[]{:S(2)}) %copy-start.1) | copy-done | bytes 2293784
  14.6 0.8 copy-done.9
  15.5 0.7 copy-done.10
  16.2 4.2 %prepare.1 = (f32[56,128]{1,0:T(8,128)S(1)}, f32[80,56,128]{2,1,0:T(8,128)S(1)}, f32[1440,128]{1,0:T(8,128)S(1)}, f32[1024,128]{1,0:T(8,128)S(1)}, f32[480,128]{1,0:T(8,128)S(1)}) custom-call(s32[6]{0:T(128)S(1)} %stack.35.flags, s32[2]{0:T(128)S(1)} %copy-done.12, f32[80,56,128]{2,1,0:T(8,128)S(1)} %get-tuple-element.99.xn, f32[80,56,128]{2,1,0:T(8,128)S(1)} %copy-done.1, ...), custom_call_target="tpu_custom_call" | custom-call | flops 1000 | bytes 1000 | tf_op jit(solution)/shard_map/prepare/pallas_call | solution.py:46
  20.4 0.1 collective-permute-start.4
  20.6 0.0 copy-start.13
  20.6 3.6 %near_base.1.base = f32[80,56,128]{2,1,0:T(8,128)S(1)} custom-call(s32[6]{0:T(128)S(1)} %stack.35.flags, f32[80,56,128]{2,1,0:T(8,128)S(1)} %get-tuple-element.99.xn, f32[80,56,128]{2,1,0:T(8,128)S(1)} %copy-done.2, f32[160,128]{1,0:T(8,128)S(1)} %bitcast.43, f32[160,128]{1,0:T(8,128)S(1)} %bitcast.49, f32[56,192]{1,0:T(8,128)S(1)} %copy-done.9, ...), custom_call_target="tpu_custom_call" | custom-call | bytes 1000 | tf_op jit(solution)/shard_map/near_base/pallas_call | solution.py:46
  24.1 1.6 %transfer.1 = (f32[2,80,16,128]{3,2,1,0:T(8,128)S(1)}, f32[30,8,128]{2,1,0:T(8,128)S(1)}) custom-call(s32[6]{0:T(128)S(1)} %stack.35.flags, f32[800,128]{1,0:T(8,128)S(1)} %bitcast.27, f32[800,128]{1,0:T(8,128)S(1)} %bitcast.32), custom_call_target="tpu_custom_call" | custom-call | bytes 1000 | tf_op jit(solution)/shard_map/transfer/pallas_call | solution.py:46
  25.7 0.1 reshape.36
  25.9 1.8 %collective-permute-start.10 = (f32[1024,128]{1,0:T(8,128)S(1)}, f32[1024,128]{1,0:T(8,128)S(1)}, u32[]{:S(2)}, u32[]{:S(2)}) collective-permute-start(f32[1024,128]{1,0:T(8,128)S(1)} %get-tuple-element.139), channel_id=1, source_target_pairs={{0,3},{1,2},{2,1},{3,0},{4,7},{5,6},{6,5},{7,4},{8,11},{9,10},{10,... | collective-permute-start | bytes 1572872 | tf_op jit(solution)/shard_map/ppermute | solution.py:586
  27.7 0.0 copy-start.11
  27.7 4.8 %near_cell.1 = (f32[80,56,128]{2,1,0:T(8,128)S(1)}, f32[70,8,128]{2,1,0:T(8,128)S(1)}) custom-call(s32[6]{0:T(128)S(1)} %stack.35.flags, f32[80,56,128]{2,1,0:T(8,128)S(1)} %near_base.1.base, f32[80,56,128]{2,1,0:T(8,128)} %collective-permute-done.halo, f32[496,128]{1,0:T(8,128)S(1)} %collective-permute-done.1.from_left, ...), custom_call_target="tpu_custom_call" | custom-call | flops 6000000000 | bytes 1000 | tf_op jit(solution)/shard_map/near_cell/pallas_call | solution.py:46
  32.5 2.7 %collective-permute-start.6 = (f32[70,8,128]{2,1,0:T(8,128)S(1)}, f32[70,8,128]{2,1,0:T(8,128)S(1)}, u32[]{:S(2)}, u32[]{:S(2)}) collective-permute-start(f32[70,8,128]{2,1,0:T(8,128)S(1)} %get-tuple-element.126.flows), channel_id=1, source_target_pairs={{0,4},{4,0},{8,12},{12,8},{16,20},{20,16},{24,28},{28,24},{1,5},{5... | collective-permute-start | bytes 860168 | tf_op jit(solution)/shard_map/ppermute | solution.py:587
  35.2 0.1 collective-permute-start.5
  35.3 4.0 %collective-permute-done.4.halo = f32[1440,128]{1,0:T(8,128)S(1)} collective-permute-done((f32[1440,128]{1,0:T(8,128)S(1)}, f32[1440,128]{1,0:T(8,128)S(1)}, u32[]{:S(2)}, u32[]{:S(2)}) %collective-permute-start.4) | collective-permute-done | bytes 737312 | tf_op jit(solution)/shard_map/ppermute | solution.py:586
  39.3 1.2 %far_lead.1.lead = f32[20,56,128]{2,1,0:T(8,128)S(1)} custom-call(s32[6]{0:T(128)S(1)} %stack.35.flags, f32[980,128]{1,0:T(8,128)S(1)} %collective-permute-done.3.slab, f32[56,128]{1,0:T(8,128)S(1)} %get-tuple-element.103.trig, f32[56,56]{1,0:T(8,128)S(1)} %copy-done.11, f32[64,192]{1,0:T(8,128)S(1)} %copy-done.8), custom_call_target="tpu_custom_call" | custom-call | bytes 1000 | tf_op jit(solution)/shard_map/far_lead/pallas_call | solution.py:46
  40.5 1.9 %far_chunk.3 = (f32[80,24,128]{2,1,0:T(8,128)S(1)}, f32[30,8,128]{2,1,0:T(8,128)S(1)}) custom-call(s32[6]{0:T(128)S(1)} %stack.35.flags, f32[80,56,128]{2,1,0:T(8,128)S(1)} %get-tuple-element.115.base, f32[20,56,128]{2,1,0:T(8,128)S(1)} %far_lead.1.lead, f32[1440,128]{1,0:T(8,128)S(1)} %collective-permute-done.4.halo, ...), custom_call_target="tpu_custom_call" | custom-call | flops 1000 | bytes 1000 | tf_op jit(solution)/shard_map/far_chunk/pallas_call | solution.py:46
  42.4 1.9 %collective-permute-done.5.other = f32[30,8,128]{2,1,0:T(8,128)S(1)} collective-permute-done((f32[30,8,128]{2,1,0:T(8,128)S(1)}, f32[30,8,128]{2,1,0:T(8,128)S(1)}, u32[]{:S(2)}, u32[]{:S(2)}) %collective-permute-start.5) | collective-permute-done | bytes 122912 | tf_op jit(solution)/shard_map/ppermute | solution.py:587
  44.3 0.7 merge_matrices.3
  44.9 1.8 %collective-permute-start.7 = (f32[30,8,128]{2,1,0:T(8,128)S(1)}, f32[30,8,128]{2,1,0:T(8,128)S(1)}, u32[]{:S(2)}, u32[]{:S(2)}) collective-permute-start(f32[30,8,128]{2,1,0:T(8,128)S(1)} %get-tuple-element.129.flows), channel_id=1, source_target_pairs={{0,4},{4,0},{8,12},{12,8},{16,20},{20,16},{24,28},{28,24},{1,5},{5... | collective-permute-start | bytes 368648 | tf_op jit(solution)/shard_map/ppermute | solution.py:587
  46.8 1.6 %collective-permute-start.8 = (f32[30,8,128]{2,1,0:T(8,128)S(1)}, f32[30,8,128]{2,1,0:T(8,128)S(1)}, u32[]{:S(2)}, u32[]{:S(2)}) collective-permute-start(f32[30,8,128]{2,1,0:T(8,128)S(1)} %get-tuple-element.132.mine), channel_id=1, source_target_pairs={{0,8},{4,12},{8,0},{12,4},{16,24},{20,28},{24,16},{28,20},{1,9},{5... | collective-permute-start | bytes 368648 | tf_op jit(solution)/shard_map/ppermute | solution.py:587
  48.3 0.9 merge_flows.8
  49.2 0.5 collective-permute-start.12
  49.8 0.1 collective-permute-done.7.other
  49.9 0.7 merge_flows.9
  50.6 2.3 %collective-permute-done.8.other = f32[30,8,128]{2,1,0:T(8,128)S(1)} collective-permute-done((f32[30,8,128]{2,1,0:T(8,128)S(1)}, f32[30,8,128]{2,1,0:T(8,128)S(1)}, u32[]{:S(2)}, u32[]{:S(2)}) %collective-permute-start.8) | collective-permute-done | bytes 122912 | tf_op jit(solution)/shard_map/ppermute | solution.py:587
  52.9 0.7 merge_matrices.4
  53.5 2.6 %collective-permute-start.9 = (f32[10,8,128]{2,1,0:T(8,128)S(1)}, f32[10,8,128]{2,1,0:T(8,128)S(1)}, u32[]{:S(2)}, u32[]{:S(2)}) collective-permute-start(f32[10,8,128]{2,1,0:T(8,128)S(1)} %get-tuple-element.136.mine), channel_id=1, source_target_pairs={{0,16},{4,20},{8,24},{12,28},{16,0},{20,4},{24,8},{28,12},{1,17},{... | collective-permute-start | bytes 122888 | tf_op jit(solution)/shard_map/ppermute | solution.py:587
  56.2 1.7 %collective-permute-start.11 = (f32[30,8,128]{2,1,0:T(8,128)S(1)}, f32[30,8,128]{2,1,0:T(8,128)S(1)}, u32[]{:S(2)}, u32[]{:S(2)}) collective-permute-start(f32[30,8,128]{2,1,0:T(8,128)S(1)} %get-tuple-element.143.flows), channel_id=1, source_target_pairs={{0,8},{4,12},{8,0},{12,4},{16,24},{20,28},{24,16},{28,20},{1,9},{5... | collective-permute-start | bytes 368648 | tf_op jit(solution)/shard_map/ppermute | solution.py:587
  57.9 0.9 collective-permute-done.9.other
  58.8 0.6 merge_matrices.5.mats
  59.4 2.0 %far_chunk.4 = (f32[80,24,128]{2,1,0:T(8,128)S(1)}, f32[30,8,128]{2,1,0:T(8,128)S(1)}) custom-call(s32[6]{0:T(128)S(1)} %stack.35.flags, f32[80,56,128]{2,1,0:T(8,128)S(1)} %get-tuple-element.115.base, f32[20,56,128]{2,1,0:T(8,128)S(1)} %far_lead.1.lead, f32[1024,128]{1,0:T(8,128)S(1)} %collective-permute-done.10.halo, ...), custom_call_target="tpu_custom_call" | custom-call | flops 1000 | bytes 1000 | tf_op jit(solution)/shard_map/far_chunk/pallas_call | solution.py:46
  61.4 1.3 %collective-permute-start.14 = (f32[30,8,128]{2,1,0:T(8,128)S(1)}, f32[30,8,128]{2,1,0:T(8,128)S(1)}, u32[]{:S(2)}, u32[]{:S(2)}) collective-permute-start(f32[30,8,128]{2,1,0:T(8,128)S(1)} %get-tuple-element.154.flows), channel_id=1, source_target_pairs={{0,4},{4,0},{8,12},{12,8},{16,20},{20,16},{24,28},{28,24},{1,5},{5... | collective-permute-start | bytes 368648 | tf_op jit(solution)/shard_map/ppermute | solution.py:587
  62.7 0.7 merge_flows.10
  63.5 0.9 merge_flows.11
  64.4 1.3 %far_chunk.5 = (f32[80,8,128]{2,1,0:T(8,128)S(1)}, f32[10,8,128]{2,1,0:T(8,128)S(1)}) custom-call(s32[6]{0:T(128)S(1)} %stack.35.flags, f32[80,56,128]{2,1,0:T(8,128)S(1)} %get-tuple-element.115.base, f32[20,56,128]{2,1,0:T(8,128)S(1)} %far_lead.1.lead, f32[480,128]{1,0:T(8,128)S(1)} %collective-permute-done.13.halo, ...), custom_call_target="tpu_custom_call" | custom-call | flops 1000 | bytes 1000 | tf_op jit(solution)/shard_map/far_chunk/pallas_call | solution.py:46
  65.7 0.7 collective-permute-done.14.other
  66.4 0.7 merge_flows.12
  67.1 3.3 %collective-permute-start.17 = (f32[30,8,128]{2,1,0:T(8,128)S(1)}, f32[30,8,128]{2,1,0:T(8,128)S(1)}, u32[]{:S(2)}, u32[]{:S(2)}) collective-permute-start(f32[30,8,128]{2,1,0:T(8,128)S(1)} %get-tuple-element.166.flows), channel_id=1, source_target_pairs={{0,8},{4,12},{8,0},{12,4},{16,24},{20,28},{24,16},{28,20},{1,9},{5... | collective-permute-start | bytes 368648 | tf_op jit(solution)/shard_map/ppermute | solution.py:587
  70.4 1.1 %collective-permute-start.18 = (f32[35,8,128]{2,1,0:T(8,128)S(1)}, f32[35,8,128]{2,1,0:T(8,128)S(1)}, u32[]{:S(2)}, u32[]{:S(2)}) collective-permute-start(f32[35,8,128]{2,1,0:T(8,128)S(1)} %get-tuple-element.170.ends), channel_id=1, source_target_pairs={{0,16},{4,20},{8,24},{12,28},{16,0},{20,4},{24,8},{28,12},{1,17},{... | collective-permute-start | bytes 430088 | tf_op jit(solution)/shard_map/ppermute | solution.py:587
  71.5 1.9 %collective-permute-start.15 = (f32[15,8,128]{2,1,0:T(8,128)S(1)}, f32[15,8,128]{2,1,0:T(8,128)S(1)}, u32[]{:S(2)}, u32[]{:S(2)}) collective-permute-start(f32[15,8,128]{2,1,0:T(8,128)S(1)} %get-tuple-element.158.ends), channel_id=1, source_target_pairs={{0,16},{4,20},{8,24},{12,28},{16,0},{20,4},{24,8},{28,12},{1,17},{... | collective-permute-start | bytes 184328 | tf_op jit(solution)/shard_map/ppermute | solution.py:587
  73.3 1.4 %collective-permute-start.16 = (f32[10,8,128]{2,1,0:T(8,128)S(1)}, f32[10,8,128]{2,1,0:T(8,128)S(1)}, u32[]{:S(2)}, u32[]{:S(2)}) collective-permute-start(f32[10,8,128]{2,1,0:T(8,128)S(1)} %get-tuple-element.163.flows), channel_id=1, source_target_pairs={{0,4},{4,0},{8,12},{12,8},{16,20},{20,16},{24,28},{28,24},{1,5},{5... | collective-permute-start | bytes 122888 | tf_op jit(solution)/shard_map/ppermute | solution.py:587
  74.7 4.0 %collective-permute-done.15.other = f32[15,8,128]{2,1,0:T(8,128)S(1)} collective-permute-done((f32[15,8,128]{2,1,0:T(8,128)S(1)}, f32[15,8,128]{2,1,0:T(8,128)S(1)}, u32[]{:S(2)}, u32[]{:S(2)}) %collective-permute-start.15) | collective-permute-done | bytes 61472 | tf_op jit(solution)/shard_map/ppermute | solution.py:587
  78.8 1.4 %correct.3.refs_0_ = f32[80,24,128]{2,1,0:T(8,128)S(1)} custom-call(s32[6]{0:T(128)S(1)} %stack.35.flags, f32[2,30,8,128]{3,2,1,0:T(8,128)S(1)} %merge_matrices.5.mats, f32[15,8,128]{2,1,0:T(8,128)S(1)} %get-tuple-element.158.ends, f32[15,8,128]{2,1,0:T(8,128)S(1)} %collective-permute-done.15.other, f32[30,8,128]{2,1,0:T(8,128)S(1)} %get-tuple-element.159.known, ...), custom_call_target="tpu_custom_call" | custom-call | flops 1000 | bytes 1000 | tf_op jit(solution)/shard_map/correct/pallas_call | solution.py:46
  80.2 0.6 merge_flows.13
  80.8 0.1 collective-permute-start.19
  80.9 0.7 merge_flows.14
  81.6 2.0 %collective-permute-start.20 = (f32[15,8,128]{2,1,0:T(8,128)S(1)}, f32[15,8,128]{2,1,0:T(8,128)S(1)}, u32[]{:S(2)}, u32[]{:S(2)}) collective-permute-start(f32[15,8,128]{2,1,0:T(8,128)S(1)} %get-tuple-element.178.ends), channel_id=1, source_target_pairs={{0,16},{4,20},{8,24},{12,28},{16,0},{20,4},{24,8},{28,12},{1,17},{... | collective-permute-start | bytes 184328 | tf_op jit(solution)/shard_map/ppermute | solution.py:587
  83.6 2.6 %correct.4.near = f32[80,56,128]{2,1,0:T(8,128)S(1)} custom-call(s32[6]{0:T(128)S(1)} %stack.35.flags, f32[2,30,8,128]{3,2,1,0:T(8,128)S(1)} %merge_matrices.5.mats, f32[35,8,128]{2,1,0:T(8,128)S(1)} %get-tuple-element.170.ends, f32[35,8,128]{2,1,0:T(8,128)S(1)} %collective-permute-done.18.other, f32[70,8,128]{2,1,0:T(8,128)S(1)} %get-tuple-element.171.known, ...), custom_call_target="tpu_custom_call" | custom-call | flops 1000 | bytes 1000 | tf_op jit(solution)/shard_map/correct/pallas_call | solution.py:46
  86.2 0.6 merge_flows.15
  86.8 1.1 %collective-permute-start.21 = (f32[5,8,128]{2,1,0:T(8,128)S(1)}, f32[5,8,128]{2,1,0:T(8,128)S(1)}, u32[]{:S(2)}, u32[]{:S(2)}) collective-permute-start(f32[5,8,128]{2,1,0:T(8,128)S(1)} %get-tuple-element.182.ends), channel_id=1, source_target_pairs={{0,16},{4,20},{8,24},{12,28},{16,0},{20,4},{24,8},{28,12},{1,17},{... | collective-permute-start | bytes 61448 | tf_op jit(solution)/shard_map/ppermute | solution.py:587
  87.9 1.4 %correct.5.refs_1_ = f32[80,24,128]{2,1,0:T(8,128)S(1)} custom-call(s32[6]{0:T(128)S(1)} %stack.35.flags, f32[2,30,8,128]{3,2,1,0:T(8,128)S(1)} %merge_matrices.5.mats, f32[15,8,128]{2,1,0:T(8,128)S(1)} %get-tuple-element.178.ends, f32[15,8,128]{2,1,0:T(8,128)S(1)} %collective-permute-done.20.other, f32[30,8,128]{2,1,0:T(8,128)S(1)} %get-tuple-element.179.known, ...), custom_call_target="tpu_custom_call" | custom-call | flops 1000 | bytes 1000 | tf_op jit(solution)/shard_map/correct/pallas_call | solution.py:46
  89.3 2.3 %collective-permute-done.21.other = f32[5,8,128]{2,1,0:T(8,128)S(1)} collective-permute-done((f32[5,8,128]{2,1,0:T(8,128)S(1)}, f32[5,8,128]{2,1,0:T(8,128)S(1)}, u32[]{:S(2)}, u32[]{:S(2)}) %collective-permute-start.21) | collective-permute-done | bytes 20512 | tf_op jit(solution)/shard_map/ppermute | solution.py:587
  91.6 3.2 %finish.1 = f32[7840,128]{1,0:T(8,128)} custom-call(s32[6]{0:T(128)S(1)} %stack.35.flags, f32[2,30,8,128]{3,2,1,0:T(8,128)S(1)} %merge_matrices.5.mats, f32[5,8,128]{2,1,0:T(8,128)S(1)} %get-tuple-element.182.ends, f32[5,8,128]{2,1,0:T(8,128)S(1)} %collective-permute-done.21.other, f32[10,8,128]{2,1,0:T(8,128)S(1)} %get-tuple-element.183.known, ...), custom_call_target="tpu_custom_call" | custom-call | flops 1000 | bytes 1000 | tf_op jit(solution)/shard_map/finish/pallas_call | solution.py:46
  (38 shorter events, 0.1 us)
Async XLA Ops:
  0.0 12.9 %copy-start.14 = (s32[24]{0:T(128)S(1)}, s32[24]{0:T(128)}, u32[]{:S(2)}) copy-start(s32[24]{0:T(128)} %param.18) | copy-start | bytes 292
  0.0 13.0 %copy-start.12 = (s32[2]{0:T(128)S(1)}, s32[2]{0:T(128)}, u32[]{:S(2)}) copy-start(s32[2]{0:T(128)} %blades.1) | copy-start | bytes 28
  0.0 2.2 %copy-start.5 = (f32[16,2,5,49,128]{4,1,3,2,0:T(2,128)S(1)}, f32[16,2,5,49,128]{4,1,3,2,0:T(2,128)}, u32[]{:S(2)}) copy-start(f32[16,2,5,49,128]{4,1,3,2,0:T(2,128)} %param.11) | copy-start | bytes 12042244
  2.2 10.8 %copy-start.6 = (f32[16,2,5,128]{3,1,2,0:T(2,128)S(1)}, f32[16,2,5,128]{3,1,2,0:T(2,128)}, u32[]{:S(2)}) copy-start(f32[16,2,5,128]{3,1,2,0:T(2,128)} %param.12) | copy-start | bytes 245764
  2.2 10.8 %copy-start.7 = (f32[16,2,5,128]{3,1,2,0:T(2,128)S(1)}, f32[16,2,5,128]{3,1,2,0:T(2,128)}, u32[]{:S(2)}) copy-start(f32[16,2,5,128]{3,1,2,0:T(2,128)} %param.13) | copy-start | bytes 245764
  2.2 10.8 %copy-start.8 = (f32[64,192]{1,0:T(8,128)S(1)}, f32[64,192]{1,0:T(8,128)}, u32[]{:S(2)}) copy-start(f32[64,192]{1,0:T(8,128)} %constant.33.clone.turned) | copy-start | bytes 147460
  3.6 1.4 %copy-start = (f32[80,56,128]{2,1,0:T(8,128)}, f32[80,56,128]{2,1,0:T(8,128)S(1)}, u32[]{:S(2)}) copy-start(f32[80,56,128]{2,1,0:T(8,128)S(1)} %get-tuple-element.100.xf) | copy-start | bytes 6881284
  5.0 22.7 %collective-permute-start = (f32[80,56,128]{2,1,0:T(8,128)S(1)}, f32[80,56,128]{2,1,0:T(8,128)}, u32[]{:S(2)}, u32[]{:S(2)}) collective-permute-start(f32[80,56,128]{2,1,0:T(8,128)S(1)} %get-tuple-element.99.xn), channel_id=1, source_target_pairs={{0,1},{1,0},{2,3},{3,2},{4,5},{5,4},{6,7},{7,6},{8,9},{9,8},{10,11... | collective-permute-start | bytes 6881288 | tf_op jit(solution)/shard_map/ppermute | solution.py:602
  5.4 20.4 %collective-permute-start.3 = (f32[980,128]{1,0:T(8,128)}, f32[980,128]{1,0:T(8,128)S(1)}, u32[]{:S(2)}, u32[]{:S(2)}) collective-permute-start(f32[980,128]{1,0:T(8,128)} %get-tuple-element.97), channel_id=1, source_target_pairs={{0,3},{1,2},{2,1},{3,0},{4,7},{5,6},{6,5},{7,4},{8,11},{9,10},{10,... | collective-permute-start | bytes 1505288 | tf_op jit(solution)/shard_map/ppermute | solution.py:586
  8.1 19.6 %collective-permute-start.1 = (f32[496,128]{1,0:T(8,128)}, f32[496,128]{1,0:T(8,128)S(1)}, u32[]{:S(2)}, u32[]{:S(2)}) collective-permute-start(f32[496,128]{1,0:T(8,128)} %get-tuple-element.108), channel_id=1, source_target_pairs={{0,4},{4,8},{8,12},{12,16},{16,20},{20,24},{24,28},{1,5},{5,9},{9,... | collective-permute-start | bytes 761864 | tf_op jit(solution)/shard_map/ppermute | solution.py:604
  11.5 16.2 %collective-permute-start.2 = (f32[496,128]{1,0:T(8,128)}, f32[496,128]{1,0:T(8,128)S(1)}, u32[]{:S(2)}, u32[]{:S(2)}) collective-permute-start(f32[496,128]{1,0:T(8,128)} %get-tuple-element.109), channel_id=1, source_target_pairs={{4,0},{8,4},{12,8},{16,12},{20,16},{24,20},{28,24},{5,1},{9,5},{13... | collective-permute-start | bytes 761864 | tf_op jit(solution)/shard_map/ppermute | solution.py:605
  13.0 1.6 %copy-start.1 = (f32[80,56,128]{2,1,0:T(8,128)S(1)}, f32[80,56,128]{2,1,0:T(8,128)}, u32[]{:S(2)}) copy-start(f32[80,56,128]{2,1,0:T(8,128)} %copy-done) | copy-start | bytes 6881284
  14.6 0.8 copy-start.9
  15.5 0.7 copy-start.10
  16.2 4.3 %copy-start.2 = (f32[80,56,128]{2,1,0:T(8,128)S(1)}, f32[80,56,128]{2,1,0:T(8,128)}, u32[]{:S(2)}) copy-start(f32[80,56,128]{2,1,0:T(8,128)} %copy-done) | copy-start | bytes 6881284
  20.4 18.9 %collective-permute-start.4 = (f32[1440,128]{1,0:T(8,128)S(1)}, f32[1440,128]{1,0:T(8,128)S(1)}, u32[]{:S(2)}, u32[]{:S(2)}) collective-permute-start(f32[1440,128]{1,0:T(8,128)S(1)} %get-tuple-element.118), channel_id=1, source_target_pairs={{0,3},{1,2},{2,1},{3,0},{4,7},{5,6},{6,5},{7,4},{8,11},{9,10},{10,... | collective-permute-start | bytes 2211848 | tf_op jit(solution)/shard_map/ppermute | solution.py:586
  20.5 3.6 %copy-start.3 = (f32[16,2,5,5,128]{4,1,3,2,0:T(2,128)S(1)}, f32[16,2,5,5,128]{4,1,3,2,0:T(2,128)}, u32[]{:S(2)}) copy-start(f32[16,2,5,5,128]{4,1,3,2,0:T(2,128)} %param.15) | copy-start | bytes 1228804
  20.5 3.6 %copy-start.4 = (f32[16,2,5,5,128]{4,1,3,2,0:T(2,128)S(1)}, f32[16,2,5,5,128]{4,1,3,2,0:T(2,128)}, u32[]{:S(2)}) copy-start(f32[16,2,5,5,128]{4,1,3,2,0:T(2,128)} %param.16) | copy-start | bytes 1228804
  20.6 5.2 %copy-start.13 = (bf16[16,2,5,5,128]{4,1,3,2,0:T(2,128)(2,1)S(1)}, bf16[16,2,5,5,128]{4,1,3,2,0:T(2,128)(2,1)}, u32[]{:S(2)}) copy-start(bf16[16,2,5,5,128]{4,1,3,2,0:T(2,128)(2,1)} %param.14) | copy-start | bytes 614404
  25.9 33.5 %collective-permute-start.10 = (f32[1024,128]{1,0:T(8,128)S(1)}, f32[1024,128]{1,0:T(8,128)S(1)}, u32[]{:S(2)}, u32[]{:S(2)}) collective-permute-start(f32[1024,128]{1,0:T(8,128)S(1)} %get-tuple-element.139), channel_id=1, source_target_pairs={{0,3},{1,2},{2,1},{3,0},{4,7},{5,6},{6,5},{7,4},{8,11},{9,10},{10,... | collective-permute-start | bytes 1572872 | tf_op jit(solution)/shard_map/ppermute | solution.py:586
  27.7 11.6 %copy-start.11 = (f32[56,56]{1,0:T(8,128)S(1)}, f32[56,56]{1,0:T(8,128)}, u32[]{:S(2)}) copy-start(f32[56,56]{1,0:T(8,128)} %constant.32.clone.basis) | copy-start | bytes 37636
  32.5 15.8 %collective-permute-start.6 = (f32[70,8,128]{2,1,0:T(8,128)S(1)}, f32[70,8,128]{2,1,0:T(8,128)S(1)}, u32[]{:S(2)}, u32[]{:S(2)}) collective-permute-start(f32[70,8,128]{2,1,0:T(8,128)S(1)} %get-tuple-element.126.flows), channel_id=1, source_target_pairs={{0,4},{4,0},{8,12},{12,8},{16,20},{20,16},{24,28},{28,24},{1,5},{5... | collective-permute-start | bytes 860168 | tf_op jit(solution)/shard_map/ppermute | solution.py:587
  35.2 9.1 %collective-permute-start.5 = (f32[30,8,128]{2,1,0:T(8,128)S(1)}, f32[30,8,128]{2,1,0:T(8,128)S(1)}, u32[]{:S(2)}, u32[]{:S(2)}) collective-permute-start(f32[30,8,128]{2,1,0:T(8,128)S(1)} %get-tuple-element.122.mine), channel_id=1, source_target_pairs={{0,4},{4,0},{8,12},{12,8},{16,20},{20,16},{24,28},{28,24},{1,5},{5... | collective-permute-start | bytes 368648 | tf_op jit(solution)/shard_map/ppermute | solution.py:587
  44.9 4.9 %collective-permute-start.7 = (f32[30,8,128]{2,1,0:T(8,128)S(1)}, f32[30,8,128]{2,1,0:T(8,128)S(1)}, u32[]{:S(2)}, u32[]{:S(2)}) collective-permute-start(f32[30,8,128]{2,1,0:T(8,128)S(1)} %get-tuple-element.129.flows), channel_id=1, source_target_pairs={{0,4},{4,0},{8,12},{12,8},{16,20},{20,16},{24,28},{28,24},{1,5},{5... | collective-permute-start | bytes 368648 | tf_op jit(solution)/shard_map/ppermute | solution.py:587
  46.8 6.1 %collective-permute-start.8 = (f32[30,8,128]{2,1,0:T(8,128)S(1)}, f32[30,8,128]{2,1,0:T(8,128)S(1)}, u32[]{:S(2)}, u32[]{:S(2)}) collective-permute-start(f32[30,8,128]{2,1,0:T(8,128)S(1)} %get-tuple-element.132.mine), channel_id=1, source_target_pairs={{0,8},{4,12},{8,0},{12,4},{16,24},{20,28},{24,16},{28,20},{1,9},{5... | collective-permute-start | bytes 368648 | tf_op jit(solution)/shard_map/ppermute | solution.py:587
  49.2 14.2 %collective-permute-start.12 = (f32[70,8,128]{2,1,0:T(8,128)S(1)}, f32[70,8,128]{2,1,0:T(8,128)S(1)}, u32[]{:S(2)}, u32[]{:S(2)}) collective-permute-start(f32[70,8,128]{2,1,0:T(8,128)S(1)} %get-tuple-element.147.flows), channel_id=1, source_target_pairs={{0,8},{4,12},{8,0},{12,4},{16,24},{20,28},{24,16},{28,20},{1,9},{5... | collective-permute-start | bytes 860168 | tf_op jit(solution)/shard_map/ppermute | solution.py:587
  49.7 14.6 %collective-permute-start.13 = (f32[480,128]{1,0:T(8,128)S(1)}, f32[480,128]{1,0:T(8,128)S(1)}, u32[]{:S(2)}, u32[]{:S(2)}) collective-permute-start(f32[480,128]{1,0:T(8,128)S(1)} %get-tuple-element.151), channel_id=1, source_target_pairs={{0,3},{1,2},{2,1},{3,0},{4,7},{5,6},{6,5},{7,4},{8,11},{9,10},{10,... | collective-permute-start | bytes 737288 | tf_op jit(solution)/shard_map/ppermute | solution.py:586
  53.5 5.3 %collective-permute-start.9 = (f32[10,8,128]{2,1,0:T(8,128)S(1)}, f32[10,8,128]{2,1,0:T(8,128)S(1)}, u32[]{:S(2)}, u32[]{:S(2)}) collective-permute-start(f32[10,8,128]{2,1,0:T(8,128)S(1)} %get-tuple-element.136.mine), channel_id=1, source_target_pairs={{0,16},{4,20},{8,24},{12,28},{16,0},{20,4},{24,8},{28,12},{1,17},{... | collective-permute-start | bytes 122888 | tf_op jit(solution)/shard_map/ppermute | solution.py:587
  56.2 6.6 %collective-permute-start.11 = (f32[30,8,128]{2,1,0:T(8,128)S(1)}, f32[30,8,128]{2,1,0:T(8,128)S(1)}, u32[]{:S(2)}, u32[]{:S(2)}) collective-permute-start(f32[30,8,128]{2,1,0:T(8,128)S(1)} %get-tuple-element.143.flows), channel_id=1, source_target_pairs={{0,8},{4,12},{8,0},{12,4},{16,24},{20,28},{24,16},{28,20},{1,9},{5... | collective-permute-start | bytes 368648 | tf_op jit(solution)/shard_map/ppermute | solution.py:587
  61.4 4.9 %collective-permute-start.14 = (f32[30,8,128]{2,1,0:T(8,128)S(1)}, f32[30,8,128]{2,1,0:T(8,128)S(1)}, u32[]{:S(2)}, u32[]{:S(2)}) collective-permute-start(f32[30,8,128]{2,1,0:T(8,128)S(1)} %get-tuple-element.154.flows), channel_id=1, source_target_pairs={{0,4},{4,0},{8,12},{12,8},{16,20},{20,16},{24,28},{28,24},{1,5},{5... | collective-permute-start | bytes 368648 | tf_op jit(solution)/shard_map/ppermute | solution.py:587
  67.1 13.8 %collective-permute-start.17 = (f32[30,8,128]{2,1,0:T(8,128)S(1)}, f32[30,8,128]{2,1,0:T(8,128)S(1)}, u32[]{:S(2)}, u32[]{:S(2)}) collective-permute-start(f32[30,8,128]{2,1,0:T(8,128)S(1)} %get-tuple-element.166.flows), channel_id=1, source_target_pairs={{0,8},{4,12},{8,0},{12,4},{16,24},{20,28},{24,16},{28,20},{1,9},{5... | collective-permute-start | bytes 368648 | tf_op jit(solution)/shard_map/ppermute | solution.py:587
  70.4 13.2 %collective-permute-start.18 = (f32[35,8,128]{2,1,0:T(8,128)S(1)}, f32[35,8,128]{2,1,0:T(8,128)S(1)}, u32[]{:S(2)}, u32[]{:S(2)}) collective-permute-start(f32[35,8,128]{2,1,0:T(8,128)S(1)} %get-tuple-element.170.ends), channel_id=1, source_target_pairs={{0,16},{4,20},{8,24},{12,28},{16,0},{20,4},{24,8},{28,12},{1,17},{... | collective-permute-start | bytes 430088 | tf_op jit(solution)/shard_map/ppermute | solution.py:587
  71.5 7.3 %collective-permute-start.15 = (f32[15,8,128]{2,1,0:T(8,128)S(1)}, f32[15,8,128]{2,1,0:T(8,128)S(1)}, u32[]{:S(2)}, u32[]{:S(2)}) collective-permute-start(f32[15,8,128]{2,1,0:T(8,128)S(1)} %get-tuple-element.158.ends), channel_id=1, source_target_pairs={{0,16},{4,20},{8,24},{12,28},{16,0},{20,4},{24,8},{28,12},{1,17},{... | collective-permute-start | bytes 184328 | tf_op jit(solution)/shard_map/ppermute | solution.py:587
  73.3 6.9 %collective-permute-start.16 = (f32[10,8,128]{2,1,0:T(8,128)S(1)}, f32[10,8,128]{2,1,0:T(8,128)S(1)}, u32[]{:S(2)}, u32[]{:S(2)}) collective-permute-start(f32[10,8,128]{2,1,0:T(8,128)S(1)} %get-tuple-element.163.flows), channel_id=1, source_target_pairs={{0,4},{4,0},{8,12},{12,8},{16,20},{20,16},{24,28},{28,24},{1,5},{5... | collective-permute-start | bytes 122888 | tf_op jit(solution)/shard_map/ppermute | solution.py:587
  80.8 5.4 %collective-permute-start.19 = (f32[10,8,128]{2,1,0:T(8,128)S(1)}, f32[10,8,128]{2,1,0:T(8,128)S(1)}, u32[]{:S(2)}, u32[]{:S(2)}) collective-permute-start(f32[10,8,128]{2,1,0:T(8,128)S(1)} %get-tuple-element.174.flows), channel_id=1, source_target_pairs={{0,8},{4,12},{8,0},{12,4},{16,24},{20,28},{24,16},{28,20},{1,9},{5... | collective-permute-start | bytes 122888 | tf_op jit(solution)/shard_map/ppermute | solution.py:587
  81.6 6.3 %collective-permute-start.20 = (f32[15,8,128]{2,1,0:T(8,128)S(1)}, f32[15,8,128]{2,1,0:T(8,128)S(1)}, u32[]{:S(2)}, u32[]{:S(2)}) collective-permute-start(f32[15,8,128]{2,1,0:T(8,128)S(1)} %get-tuple-element.178.ends), channel_id=1, source_target_pairs={{0,16},{4,20},{8,24},{12,28},{16,0},{20,4},{24,8},{28,12},{1,17},{... | collective-permute-start | bytes 184328 | tf_op jit(solution)/shard_map/ppermute | solution.py:587
  86.8 4.7 %collective-permute-start.21 = (f32[5,8,128]{2,1,0:T(8,128)S(1)}, f32[5,8,128]{2,1,0:T(8,128)S(1)}, u32[]{:S(2)}, u32[]{:S(2)}) collective-permute-start(f32[5,8,128]{2,1,0:T(8,128)S(1)} %get-tuple-element.182.ends), channel_id=1, source_target_pairs={{0,16},{4,20},{8,24},{12,28},{16,0},{20,4},{24,8},{28,12},{1,17},{... | collective-permute-start | bytes 61448 | tf_op jit(solution)/shard_map/ppermute | solution.py:587

commit v5 on v4

--- a/solution.py
+++ b/solution.py
@@ -19,7 +19,7 @@
 LEAD = 4
 MB = 1 << 20
 
-CHUNKS = (((0, 24), False), ((24, 40), True), ((40, 48), False))
+CHUNKS = (((0, 32), True), ((32, 48), False))
 
 
 def rows_of(chunk):
@@ -35,11 +35,14 @@
     def __init__(self, flags):
         self.flags = flags
 
+    def before(self, array):
+        return lax.optimization_barrier((self.flags, array))[1]
+
     def after(self, array):
         self.flags, array = lax.optimization_barrier((self.flags, array))
         return array
 
-    def __call__(self, body, out_shapes, arrays, scratch=(), vmem=24, name=None, grid=None, in_specs=None, out_specs=None, scalars=(), flops=1000):
+    def __call__(self, body, out_shapes, arrays, scratch=(), vmem=16, name=None, grid=None, in_specs=None, out_specs=None, scalars=(), flops=1000):
         smem = pl.BlockSpec(memory_space=pltpu.SMEM)
         held = pl.BlockSpec(memory_space=pltpu.VMEM)
         extra = {} if grid is None else {"grid": grid}
@@ -587,6 +590,21 @@
     to_level = lambda x, k: lax.ppermute(x, "seg", [(i, i ^ (1 << k)) for i in range(segs)])
     x_shape = (cells * V, PAD, LANES)
 
+    slab, seg = lax.axis_index("pitch"), lax.axis_index("seg")
+    side = slab % 2
+    wrap = jnp.logical_or(slab == 0, slab == slabs - 1)
+    bits = [(seg >> k) & 1 for k in range(levels)]
+    run = Chain(
+        jnp.stack(
+            [side, wrap.astype(jnp.int32), (slab == 0).astype(jnp.int32), *bits]
+        ).astype(jnp.int32)
+    )
+    flat = lambda x: x.transpose(0, 2, 3, 1, 4).reshape(cells * V * V * 2, LANES)
+    inv, low, upp = flat(inverse.astype(F32)), flat(lower), flat(upper)
+    blocks, group = run(
+        transfer, [(2, cells * V, 16, LANES), (6 * V, 8, LANES)], [low, upp],
+        scratch=[pltpu.VMEM((cells * V, 8, LANES), F32)], name="transfer", flops=COSTS[1],
+    )
     st = state.transpose(0, 2, 3, 1, 4).reshape(cells * V * NT * 2, LANES)
     lead_rows, edge_rows = LEAD * V * NT, padded_even(V * NT * 2)
     held = pl.BlockSpec(memory_space=pltpu.VMEM)
@@ -598,22 +616,12 @@
         out_specs=[held] * 5,
         compiler_params=pltpu.CompilerParams(vmem_limit_bytes=16 * MB),
         name="split_cells",
-    )(st)
+    )(run.before(st))
     halo_near = lax.ppermute(xn, "pitch", near_pairs)
     slab_in = to_far(slab_out)
     from_left = lax.ppermute(last_cell, "seg", [(i, i + 1) for i in range(segs - 1)])
     from_right = lax.ppermute(first_cell, "seg", [(i + 1, i) for i in range(segs - 1)])
 
-    slab, seg = lax.axis_index("pitch"), lax.axis_index("seg")
-    side = slab % 2
-    wrap = jnp.logical_or(slab == 0, slab == slabs - 1)
-    bits = [(seg >> k) & 1 for k in range(levels)]
-    run = Chain(
-        jnp.stack(
-            [side, wrap.astype(jnp.int32), (slab == 0).astype(jnp.int32), *bits]
-        ).astype(jnp.int32)
-    )
-    run.after(slab_out)
     basis, turned = phase_tables(count)
     table = derivative_table()
     wide_harmonic = jnp.broadcast_to(harmonic.astype(F32)[:, None], (count, LANES))
@@ -636,11 +644,9 @@
         arrived.append(to_far(chunk))
     slab_in, *arrived = arrived
 
-    flat = lambda x: x.transpose(0, 2, 3, 1, 4).reshape(cells * V * V * 2, LANES)
-    inv, low, upp = flat(inverse.astype(F32)), flat(lower), flat(upper)
     edges = pltpu.VMEM((2 * V, PAD, LANES), F32)
 
-    mats, group, share = [], None, []
+    mats, share = [], []
 
     def merge_group(k):
         nonlocal group, share
@@ -689,13 +695,15 @@
                 scratch=[pltpu.VMEM((2 * V, self.solved.shape[1], LANES), F32)], name="correct",
             )[0]
 
+    group, halo_near = lax.optimization_barrier((group, halo_near))
     base_near = run(
         near_base, [x_shape], [xn, xf, adv, vis, table, trig], name="near_base", flops=COSTS[0]
     )[0]
-    blocks, group = run(
-        transfer, [(2, cells * V, 16, LANES), (6 * V, 8, LANES)], [low, upp],
-        scratch=[pltpu.VMEM((cells * V, 8, LANES), F32)], name="transfer", flops=COSTS[1],
-    )
+    merge_group(0)
+    lead = run(
+        far_lead, [(LEAD * V, PAD, LANES)], [slab_in, trig, basis, turned],
+        scratch=[pltpu.VMEM((V, PAD, LANES), F32)], name="far_lead", flops=COSTS[3],
+    )[0]
     first = Exchange(
         0,
         *run(
@@ -704,32 +712,22 @@
             scratch=[edges], name="near_cell", flops=COSTS[2],
         )
     )
-    lead = run(
-        far_lead, [(LEAD * V, PAD, LANES)], [slab_in, trig, basis, turned],
-        scratch=[pltpu.VMEM((V, PAD, LANES), F32)], name="far_lead", flops=COSTS[3],
-    )[0]
-    second = Exchange(1, *solve_chunk(0))
-    merge_group(0)
-    first.step()
-    second.step()
     for k in range(1, levels):
         merge_group(k)
-    third = Exchange(1, *solve_chunk(1))
+    first.step()
+    second = Exchange(1, *solve_chunk(0))
     for k in range(1, levels - 1):
         second.step()
         first.step()
-    fourth = Exchange(1, *solve_chunk(2))
+    second.step()
+    third = Exchange(1, *solve_chunk(1))
     third.step()
-    done = [second.correct()]
-    fourth.step()
+    near = first.correct()
     for k in range(1, levels - 1):
         third.step()
-    near = first.correct()
-    for k in range(1, levels - 1):
-        fourth.step()
-    done.append(third.correct())
-    g_last = fourth.solved
-    small = fourth.last()
+    done = [second.correct()]
+    g_last = third.solved
+    small = third.last()
 
     steps = 4
     part = cells // steps

time: 95.1 us -> 87.6 us (0.921)
  the two profiles are of different devices: /device:TPU:0 before, /device:TPU:24 now
where the time goes in v5:
time: 87.6 us; the launch traced here: 87.3 us
  waiting for transfers between devices  34 us (39%)
  Pallas kernels  33.7 us (38%)
  starting transfers between devices  14.8 us (17%)
  local copies, waits for them, and re-layouts  4.34 us (5%)
    ppermute x12, waiting for transfers between devices, local(): lax.ppermute(x, 'seg', [(i, i ^ 1 << k) for i in range(segs)])  34 us
    pallas_call x19, Pallas kernels, __call__(): pl.pallas_call(body, out_shape=[jax.ShapeDtypeStruct(s, F32) for s in out...  33.2 us
    ppermute x12, starting transfers between devices, local(): lax.ppermute(x, 'seg', [(i, i ^ 1 << k) for i in range(segs)])  6.27 us
    unnamed x26, local copies, waits for them, and re-layouts  4.18 us
    ppermute x1, starting transfers between devices, local(): lax.ppermute(last_cell, 'seg', [(i, i + 1) for i in range(segs - 1)])  3.39 us
    ppermute x1, starting transfers between devices, local(): lax.ppermute(first_cell, 'seg', [(i + 1, i) for i in range(segs - 1)])  3.34 us
  transfers between devices with their start and end apart: 18, of which 9 were waited for; matrix products, arithmetic and copies ran while one was open for 0% of the time, Pallas kernels for 31%

profile of v5, /device:TPU:24, one launch (start us, length us, event | category | flops | bytes accessed | tf_op | source)
XLA Modules:
  0.0 87.3 jit_solution(12553423627850682368)
XLA Ops:
  0.0 0.1 stack.35.flags
  0.1 1.0 %copy-done.1 = f32[16,2,5,5,128]{4,1,3,2,0:T(2,128)S(1)} copy-done((f32[16,2,5,5,128]{4,1,3,2,0:T(2,128)S(1)}, f32[16,2,5,5,128]{4,1,3,2,0:T(2,128)}, u32[]{:S(2)}) %copy-start.1) | copy-done | bytes 409624
  1.1 1.0 %copy-done.3 = f32[16,2,5,5,128]{4,1,3,2,0:T(2,128)S(1)} copy-done((f32[16,2,5,5,128]{4,1,3,2,0:T(2,128)S(1)}, f32[16,2,5,5,128]{4,1,3,2,0:T(2,128)}, u32[]{:S(2)}) %copy-start.3) | copy-done | bytes 409624
  2.1 0.0 copy-start.8
  2.1 0.0 copy-start.9
  2.1 0.0 copy-start.10
  2.1 1.6 %transfer.1 = (f32[2,80,16,128]{3,2,1,0:T(8,128)S(1)}, f32[30,8,128]{2,1,0:T(8,128)S(1)}) custom-call(s32[6]{0:T(128)S(1)} %stack.35.flags, f32[800,128]{1,0:T(8,128)S(1)} %bitcast.28, f32[800,128]{1,0:T(8,128)S(1)} %bitcast.32), custom_call_target="tpu_custom_call" | custom-call | bytes 1000 | tf_op jit(solution)/shard_map/transfer/pallas_call | solution.py:49
  3.7 0.0 copy-start
  3.7 2.1 %copy-done = f32[16,2,5,49,128]{4,1,3,2,0:T(2,128)S(1)} copy-done((f32[16,2,5,49,128]{4,1,3,2,0:T(2,128)S(1)}, f32[16,2,5,49,128]{4,1,3,2,0:T(2,128)}, u32[]{:S(2)}) %copy-start) | copy-done | bytes 4014104
  5.9 0.5 split_cells.1
  6.3 0.1 collective-permute-start
  6.4 1.6 %collective-permute-start.2 = (f32[980,128]{1,0:T(8,128)S(1)}, f32[980,128]{1,0:T(8,128)S(1)}, u32[]{:S(2)}, u32[]{:S(2)}) collective-permute-start(f32[980,128]{1,0:T(8,128)S(1)} %get-tuple-element.96), channel_id=1, source_target_pairs={{0,3},{1,2},{2,1},{3,0},{4,7},{5,6},{6,5},{7,4},{8,11},{9,10},{10,... | collective-permute-start | bytes 1505288 | tf_op jit(solution)/shard_map/ppermute | solution.py:589
  8.1 3.4 %collective-permute-start.3 = (f32[496,128]{1,0:T(8,128)S(1)}, f32[496,128]{1,0:T(8,128)S(1)}, u32[]{:S(2)}, u32[]{:S(2)}) collective-permute-start(f32[496,128]{1,0:T(8,128)S(1)} %get-tuple-element.101), channel_id=1, source_target_pairs={{0,4},{4,8},{8,12},{12,16},{16,20},{20,24},{24,28},{1,5},{5,9},{9,... | collective-permute-start | bytes 761864 | tf_op jit(solution)/shard_map/ppermute | solution.py:622
  11.5 3.3 %collective-permute-start.4 = (f32[496,128]{1,0:T(8,128)S(1)}, f32[496,128]{1,0:T(8,128)S(1)}, u32[]{:S(2)}, u32[]{:S(2)}) collective-permute-start(f32[496,128]{1,0:T(8,128)S(1)} %get-tuple-element.102), channel_id=1, source_target_pairs={{4,0},{8,4},{12,8},{16,12},{20,16},{24,20},{28,24},{5,1},{9,5},{13... | collective-permute-start | bytes 761864 | tf_op jit(solution)/shard_map/ppermute | solution.py:623
  14.8 0.1 broadcast_in_dim.2.harmonic
  14.9 4.2 %prepare.1 = (f32[56,128]{1,0:T(8,128)S(1)}, f32[80,56,128]{2,1,0:T(8,128)S(1)}, f32[1984,128]{1,0:T(8,128)S(1)}, f32[960,128]{1,0:T(8,128)S(1)}) custom-call(s32[6]{0:T(128)S(1)} %stack.35.flags, s32[2]{0:T(128)S(1)} %copy-done.10, f32[80,56,128]{2,1,0:T(8,128)S(1)} %get-tuple-element.85.xn, f32[80,56,128]{2,1,0:T(8,128)S(1)} %get-tuple-element.86.xf, ...), custom_call_target="tpu_custom_call" | custom-call | flops 1000 | bytes 1000 | tf_op jit(solution)/shard_map/prepare/pallas_call | solution.py:49
  19.2 0.1 collective-permute-start.8
  19.2 0.0 collective-permute-done.halo
  19.3 0.7 collective-permute-start.1
  19.9 3.5 %near_base.1.base = f32[80,56,128]{2,1,0:T(8,128)S(1)} custom-call(s32[6]{0:T(128)S(1)} %stack.35.flags, f32[80,56,128]{2,1,0:T(8,128)S(1)} %get-tuple-element.85.xn, f32[80,56,128]{2,1,0:T(8,128)S(1)} %get-tuple-element.86.xf, f32[160,128]{1,0:T(8,128)S(1)} %bitcast.40, f32[160,128]{1,0:T(8,128)S(1)} %bitcast.45, f32[56,192]{1,0:T(8,128)S(1)} %copy-done.8, ...), custom_call_target="tpu_custom_call" | custom-call | bytes 1000 | tf_op jit(solution)/shard_map/near_base/pallas_call | solution.py:49
  23.5 0.1 reshape.36
  23.6 0.0 collective-permute-done.2.slab
  23.6 3.4 %collective-permute-done.1.other = f32[30,8,128]{2,1,0:T(8,128)S(1)} collective-permute-done((f32[30,8,128]{2,1,0:T(8,128)S(1)}, f32[30,8,128]{2,1,0:T(8,128)S(1)}, u32[]{:S(2)}, u32[]{:S(2)}) %collective-permute-start.1) | collective-permute-done | bytes 122912 | tf_op jit(solution)/shard_map/ppermute | solution.py:590
  27.0 0.7 merge_matrices.3
  27.7 1.2 %far_lead.1.lead = f32[20,56,128]{2,1,0:T(8,128)S(1)} custom-call(s32[6]{0:T(128)S(1)} %stack.35.flags, f32[980,128]{1,0:T(8,128)S(1)} %collective-permute-done.2.slab, f32[56,128]{1,0:T(8,128)S(1)} %get-tuple-element.89.trig, f32[56,56]{1,0:T(8,128)S(1)} %copy-done.9, f32[64,192]{1,0:T(8,128)S(1)} %copy-done.7), custom_call_target="tpu_custom_call" | custom-call | bytes 1000 | tf_op jit(solution)/shard_map/far_lead/pallas_call | solution.py:49
  28.9 0.0 collective-permute-done.3.from_left
  28.9 0.0 collective-permute-done.4.from_right
  28.9 3.7 %near_cell.1 = (f32[80,56,128]{2,1,0:T(8,128)S(1)}, f32[70,8,128]{2,1,0:T(8,128)S(1)}) custom-call(s32[6]{0:T(128)S(1)} %stack.35.flags, f32[80,56,128]{2,1,0:T(8,128)S(1)} %near_base.1.base, f32[80,56,128]{2,1,0:T(8,128)S(1)} %collective-permute-done.halo, f32[496,128]{1,0:T(8,128)S(1)} %collective-permute-done.3.from_left, ...), custom_call_target="tpu_custom_call" | custom-call | flops 6000000000 | bytes 1000 | tf_op jit(solution)/shard_map/near_cell/pallas_call | solution.py:49
  32.7 0.1 collective-permute-start.7
  32.7 1.0 %collective-permute-start.5 = (f32[30,8,128]{2,1,0:T(8,128)S(1)}, f32[30,8,128]{2,1,0:T(8,128)S(1)}, u32[]{:S(2)}, u32[]{:S(2)}) collective-permute-start(f32[30,8,128]{2,1,0:T(8,128)S(1)} %get-tuple-element.105.mine), channel_id=1, source_target_pairs={{0,8},{4,12},{8,0},{12,4},{16,24},{20,28},{24,16},{28,20},{1,9},{5... | collective-permute-start | bytes 368648 | tf_op jit(solution)/shard_map/ppermute | solution.py:590
  33.8 0.0 collective-permute-start.12
  33.8 4.3 %collective-permute-done.5.other = f32[30,8,128]{2,1,0:T(8,128)S(1)} collective-permute-done((f32[30,8,128]{2,1,0:T(8,128)S(1)}, f32[30,8,128]{2,1,0:T(8,128)S(1)}, u32[]{:S(2)}, u32[]{:S(2)}) %collective-permute-start.5) | collective-permute-done | bytes 122912 | tf_op jit(solution)/shard_map/ppermute | solution.py:590
  38.0 0.6 merge_matrices.4
  38.7 0.5 collective-permute-start.6
  39.2 4.9 %collective-permute-done.6.other = f32[10,8,128]{2,1,0:T(8,128)S(1)} collective-permute-done((f32[10,8,128]{2,1,0:T(8,128)S(1)}, f32[10,8,128]{2,1,0:T(8,128)S(1)}, u32[]{:S(2)}, u32[]{:S(2)}) %collective-permute-start.6) | collective-permute-done | bytes 40992 | tf_op jit(solution)/shard_map/ppermute | solution.py:590
  44.1 0.6 merge_matrices.5.mats
  44.7 0.0 collective-permute-done.7.other
  44.7 0.9 %merge_flows.6 = (f32[70,8,128]{2,1,0:T(8,128)S(1)}, f32[70,8,128]{2,1,0:T(8,128)S(1)}) custom-call(s32[6]{0:T(128)S(1)} %stack.35.flags, f32[2,30,8,128]{3,2,1,0:T(8,128)S(1)} %get-tuple-element.112.mats, f32[70,8,128]{2,1,0:T(8,128)S(1)} %get-tuple-element.113.flows, f32[70,8,128]{2,1,0:T(8,128)S(1)} %collective-permute-done.7.other), custom_call_target="tpu_custom_call" | custom-call | flops 1000 | bytes 1000 | tf_op jit(solution)/shard_map/merge_flows/pallas_call | solution.py:49
  45.6 2.8 %far_chunk.2 = (f32[80,40,128]{2,1,0:T(8,128)S(1)}, f32[50,8,128]{2,1,0:T(8,128)S(1)}) custom-call(s32[6]{0:T(128)S(1)} %stack.35.flags, f32[80,56,128]{2,1,0:T(8,128)S(1)} %get-tuple-element.116.base, f32[20,56,128]{2,1,0:T(8,128)S(1)} %far_lead.1.lead, f32[1984,128]{1,0:T(8,128)S(1)} %collective-permute-done.8.halo, ...), custom_call_target="tpu_custom_call" | custom-call | flops 1000 | bytes 1000 | tf_op jit(solution)/shard_map/far_chunk/pallas_call | solution.py:49
  48.4 1.6 %collective-permute-start.9 = (f32[50,8,128]{2,1,0:T(8,128)S(1)}, f32[50,8,128]{2,1,0:T(8,128)S(1)}, u32[]{:S(2)}, u32[]{:S(2)}) collective-permute-start(f32[50,8,128]{2,1,0:T(8,128)S(1)} %get-tuple-element.121.flows), channel_id=1, source_target_pairs={{0,4},{4,0},{8,12},{12,8},{16,20},{20,16},{24,28},{28,24},{1,5},{5... | collective-permute-start | bytes 614408 | tf_op jit(solution)/shard_map/ppermute | solution.py:590
  50.0 0.2 collective-permute-start.10
  50.1 4.0 %collective-permute-done.9.other = f32[50,8,128]{2,1,0:T(8,128)S(1)} collective-permute-done((f32[50,8,128]{2,1,0:T(8,128)S(1)}, f32[50,8,128]{2,1,0:T(8,128)S(1)}, u32[]{:S(2)}, u32[]{:S(2)}) %collective-permute-start.9) | collective-permute-done | bytes 204832 | tf_op jit(solution)/shard_map/ppermute | solution.py:590
  54.2 0.8 merge_flows.7
  55.0 0.3 collective-permute-start.11
  55.3 3.2 %collective-permute-done.10.other = f32[70,8,128]{2,1,0:T(8,128)S(1)} collective-permute-done((f32[70,8,128]{2,1,0:T(8,128)S(1)}, f32[70,8,128]{2,1,0:T(8,128)S(1)}, u32[]{:S(2)}, u32[]{:S(2)}) %collective-permute-start.10) | collective-permute-done | bytes 286752 | tf_op jit(solution)/shard_map/ppermute | solution.py:590
  58.6 0.9 %merge_flows.8 = (f32[35,8,128]{2,1,0:T(8,128)S(1)}, f32[70,8,128]{2,1,0:T(8,128)S(1)}) custom-call(s32[6]{0:T(128)S(1)} %stack.35.flags, f32[2,30,8,128]{3,2,1,0:T(8,128)S(1)} %get-tuple-element.124.mats, f32[70,8,128]{2,1,0:T(8,128)S(1)} %get-tuple-element.125.flows, f32[70,8,128]{2,1,0:T(8,128)S(1)} %collective-permute-done.10.other, ...), custom_call_target="tpu_custom_call" | custom-call | flops 1000 | bytes 1000 | tf_op jit(solution)/shard_map/merge_flows/pallas_call | solution.py:49
  59.5 1.5 %collective-permute-done.11.other = f32[50,8,128]{2,1,0:T(8,128)S(1)} collective-permute-done((f32[50,8,128]{2,1,0:T(8,128)S(1)}, f32[50,8,128]{2,1,0:T(8,128)S(1)}, u32[]{:S(2)}, u32[]{:S(2)}) %collective-permute-start.11) | collective-permute-done | bytes 204832 | tf_op jit(solution)/shard_map/ppermute | solution.py:590
  61.0 0.8 merge_flows.9
  61.8 0.0 collective-permute-done.12.halo
  61.8 1.6 %far_chunk.3 = (f32[80,16,128]{2,1,0:T(8,128)S(1)}, f32[20,8,128]{2,1,0:T(8,128)S(1)}) custom-call(s32[6]{0:T(128)S(1)} %stack.35.flags, f32[80,56,128]{2,1,0:T(8,128)S(1)} %get-tuple-element.116.base, f32[20,56,128]{2,1,0:T(8,128)S(1)} %far_lead.1.lead, f32[960,128]{1,0:T(8,128)S(1)} %collective-permute-done.12.halo, ...), custom_call_target="tpu_custom_call" | custom-call | flops 1000 | bytes 1000 | tf_op jit(solution)/shard_map/far_chunk/pallas_call | solution.py:49
  63.4 1.4 %collective-permute-start.13 = (f32[20,8,128]{2,1,0:T(8,128)S(1)}, f32[20,8,128]{2,1,0:T(8,128)S(1)}, u32[]{:S(2)}, u32[]{:S(2)}) collective-permute-start(f32[20,8,128]{2,1,0:T(8,128)S(1)} %get-tuple-element.136.flows), channel_id=1, source_target_pairs={{0,4},{4,0},{8,12},{12,8},{16,20},{20,16},{24,28},{28,24},{1,5},{5... | collective-permute-start | bytes 245768 | tf_op jit(solution)/shard_map/ppermute | solution.py:590
  64.8 0.0 collective-permute-start.14
  64.8 3.1 %collective-permute-done.13.other = f32[20,8,128]{2,1,0:T(8,128)S(1)} collective-permute-done((f32[20,8,128]{2,1,0:T(8,128)S(1)}, f32[20,8,128]{2,1,0:T(8,128)S(1)}, u32[]{:S(2)}, u32[]{:S(2)}) %collective-permute-start.13) | collective-permute-done | bytes 81952 | tf_op jit(solution)/shard_map/ppermute | solution.py:590
  67.9 0.6 merge_flows.10
  68.6 0.2 collective-permute-start.15
  68.8 0.1 collective-permute-start.16
  68.9 6.9 %collective-permute-done.14.other = f32[35,8,128]{2,1,0:T(8,128)S(1)} collective-permute-done((f32[35,8,128]{2,1,0:T(8,128)S(1)}, f32[35,8,128]{2,1,0:T(8,128)S(1)}, u32[]{:S(2)}, u32[]{:S(2)}) %collective-permute-start.14) | collective-permute-done | bytes 143392 | tf_op jit(solution)/shard_map/ppermute | solution.py:590
  75.8 2.6 %correct.2.near = f32[80,56,128]{2,1,0:T(8,128)S(1)} custom-call(s32[6]{0:T(128)S(1)} %stack.35.flags, f32[2,30,8,128]{3,2,1,0:T(8,128)S(1)} %merge_matrices.5.mats, f32[35,8,128]{2,1,0:T(8,128)S(1)} %get-tuple-element.140.ends, f32[35,8,128]{2,1,0:T(8,128)S(1)} %collective-permute-done.14.other, f32[70,8,128]{2,1,0:T(8,128)S(1)} %get-tuple-element.141.known, ...), custom_call_target="tpu_custom_call" | custom-call | flops 1000 | bytes 1000 | tf_op jit(solution)/shard_map/correct/pallas_call | solution.py:49
  78.4 0.7 merge_flows.11
  79.0 0.1 collective-permute-start.17
  79.1 0.0 collective-permute-done.16.other
  79.1 2.1 %correct.3.refs_0_ = f32[80,40,128]{2,1,0:T(8,128)S(1)} custom-call(s32[6]{0:T(128)S(1)} %stack.35.flags, f32[2,30,8,128]{3,2,1,0:T(8,128)S(1)} %merge_matrices.5.mats, f32[25,8,128]{2,1,0:T(8,128)S(1)} %get-tuple-element.149.ends, f32[25,8,128]{2,1,0:T(8,128)S(1)} %collective-permute-done.16.other, f32[50,8,128]{2,1,0:T(8,128)S(1)} %get-tuple-element.150.known, ...), custom_call_target="tpu_custom_call" | custom-call | flops 1000 | bytes 1000 | tf_op jit(solution)/shard_map/correct/pallas_call | solution.py:49
  81.3 2.7 %collective-permute-done.17.other = f32[10,8,128]{2,1,0:T(8,128)S(1)} collective-permute-done((f32[10,8,128]{2,1,0:T(8,128)S(1)}, f32[10,8,128]{2,1,0:T(8,128)S(1)}, u32[]{:S(2)}, u32[]{:S(2)}) %collective-permute-start.17) | collective-permute-done | bytes 40992 | tf_op jit(solution)/shard_map/ppermute | solution.py:590
  84.0 3.3 %finish.1 = f32[7840,128]{1,0:T(8,128)} custom-call(s32[6]{0:T(128)S(1)} %stack.35.flags, f32[2,30,8,128]{3,2,1,0:T(8,128)S(1)} %merge_matrices.5.mats, f32[10,8,128]{2,1,0:T(8,128)S(1)} %get-tuple-element.153.ends, f32[10,8,128]{2,1,0:T(8,128)S(1)} %collective-permute-done.17.other, f32[20,8,128]{2,1,0:T(8,128)S(1)} %get-tuple-element.154.known, ...), custom_call_target="tpu_custom_call" | custom-call | flops 1000 | bytes 1000 | tf_op jit(solution)/shard_map/finish/pallas_call | solution.py:49
  (22 shorter events, 0.0 us)
Async XLA Ops:
  0.1 1.0 %copy-start.1 = (f32[16,2,5,5,128]{4,1,3,2,0:T(2,128)S(1)}, f32[16,2,5,5,128]{4,1,3,2,0:T(2,128)}, u32[]{:S(2)}) copy-start(f32[16,2,5,5,128]{4,1,3,2,0:T(2,128)} %param.15) | copy-start | bytes 1228804
  1.1 1.0 %copy-start.3 = (f32[16,2,5,5,128]{4,1,3,2,0:T(2,128)S(1)}, f32[16,2,5,5,128]{4,1,3,2,0:T(2,128)}, u32[]{:S(2)}) copy-start(f32[16,2,5,5,128]{4,1,3,2,0:T(2,128)} %param.16) | copy-start | bytes 1228804
  2.1 12.7 %copy-start.12 = (s32[24]{0:T(128)S(1)}, s32[24]{0:T(128)}, u32[]{:S(2)}) copy-start(s32[24]{0:T(128)} %param.18) | copy-start | bytes 292
  2.1 12.8 %copy-start.5 = (f32[16,2,5,128]{3,1,2,0:T(2,128)S(1)}, f32[16,2,5,128]{3,1,2,0:T(2,128)}, u32[]{:S(2)}) copy-start(f32[16,2,5,128]{3,1,2,0:T(2,128)} %param.12) | copy-start | bytes 245764
  2.1 12.8 %copy-start.6 = (f32[16,2,5,128]{3,1,2,0:T(2,128)S(1)}, f32[16,2,5,128]{3,1,2,0:T(2,128)}, u32[]{:S(2)}) copy-start(f32[16,2,5,128]{3,1,2,0:T(2,128)} %param.13) | copy-start | bytes 245764
  2.1 12.8 %copy-start.7 = (f32[64,192]{1,0:T(8,128)S(1)}, f32[64,192]{1,0:T(8,128)}, u32[]{:S(2)}) copy-start(f32[64,192]{1,0:T(8,128)} %constant.33.clone.turned) | copy-start | bytes 147460
  2.1 12.8 %copy-start.8 = (f32[56,192]{1,0:T(8,128)S(1)}, f32[56,192]{1,0:T(8,128)}, u32[]{:S(2)}) copy-start(f32[56,192]{1,0:T(8,128)} %constant.34.clone.table) | copy-start | bytes 129028
  2.1 12.8 %copy-start.9 = (f32[56,56]{1,0:T(8,128)S(1)}, f32[56,56]{1,0:T(8,128)}, u32[]{:S(2)}) copy-start(f32[56,56]{1,0:T(8,128)} %constant.32.clone.basis) | copy-start | bytes 37636
  2.1 12.8 %copy-start.10 = (s32[2]{0:T(128)S(1)}, s32[2]{0:T(128)}, u32[]{:S(2)}) copy-start(s32[2]{0:T(128)} %blades.1) | copy-start | bytes 28
  3.7 2.1 %copy-start = (f32[16,2,5,49,128]{4,1,3,2,0:T(2,128)S(1)}, f32[16,2,5,49,128]{4,1,3,2,0:T(2,128)}, u32[]{:S(2)}) copy-start(f32[16,2,5,49,128]{4,1,3,2,0:T(2,128)} %param.11) | copy-start | bytes 12042244
  6.3 12.9 %collective-permute-start = (f32[80,56,128]{2,1,0:T(8,128)S(1)}, f32[80,56,128]{2,1,0:T(8,128)S(1)}, u32[]{:S(2)}, u32[]{:S(2)}) collective-permute-start(f32[80,56,128]{2,1,0:T(8,128)S(1)} %get-tuple-element.85.xn), channel_id=1, source_target_pairs={{0,1},{1,0},{2,3},{3,2},{4,5},{5,4},{6,7},{7,6},{8,9},{9,8},{10,11... | collective-permute-start | bytes 6881288 | tf_op jit(solution)/shard_map/ppermute | solution.py:620
  6.4 17.2 %collective-permute-start.2 = (f32[980,128]{1,0:T(8,128)S(1)}, f32[980,128]{1,0:T(8,128)S(1)}, u32[]{:S(2)}, u32[]{:S(2)}) collective-permute-start(f32[980,128]{1,0:T(8,128)S(1)} %get-tuple-element.96), channel_id=1, source_target_pairs={{0,3},{1,2},{2,1},{3,0},{4,7},{5,6},{6,5},{7,4},{8,11},{9,10},{10,... | collective-permute-start | bytes 1505288 | tf_op jit(solution)/shard_map/ppermute | solution.py:589
  8.1 20.8 %collective-permute-start.3 = (f32[496,128]{1,0:T(8,128)S(1)}, f32[496,128]{1,0:T(8,128)S(1)}, u32[]{:S(2)}, u32[]{:S(2)}) collective-permute-start(f32[496,128]{1,0:T(8,128)S(1)} %get-tuple-element.101), channel_id=1, source_target_pairs={{0,4},{4,8},{8,12},{12,16},{16,20},{20,24},{24,28},{1,5},{5,9},{9,... | collective-permute-start | bytes 761864 | tf_op jit(solution)/shard_map/ppermute | solution.py:622
  11.5 17.4 %collective-permute-start.4 = (f32[496,128]{1,0:T(8,128)S(1)}, f32[496,128]{1,0:T(8,128)S(1)}, u32[]{:S(2)}, u32[]{:S(2)}) collective-permute-start(f32[496,128]{1,0:T(8,128)S(1)} %get-tuple-element.102), channel_id=1, source_target_pairs={{4,0},{8,4},{12,8},{16,12},{20,16},{24,20},{28,24},{5,1},{9,5},{13... | collective-permute-start | bytes 761864 | tf_op jit(solution)/shard_map/ppermute | solution.py:623
  19.2 26.4 %collective-permute-start.8 = (f32[1984,128]{1,0:T(8,128)S(1)}, f32[1984,128]{1,0:T(8,128)S(1)}, u32[]{:S(2)}, u32[]{:S(2)}) collective-permute-start(f32[1984,128]{1,0:T(8,128)S(1)} %get-tuple-element.118), channel_id=1, source_target_pairs={{0,3},{1,2},{2,1},{3,0},{4,7},{5,6},{6,5},{7,4},{8,11},{9,10},{10,... | collective-permute-start | bytes 3047432 | tf_op jit(solution)/shard_map/ppermute | solution.py:589
  19.3 7.8 %collective-permute-start.1 = (f32[30,8,128]{2,1,0:T(8,128)S(1)}, f32[30,8,128]{2,1,0:T(8,128)S(1)}, u32[]{:S(2)}, u32[]{:S(2)}) collective-permute-start(f32[30,8,128]{2,1,0:T(8,128)S(1)} %get-tuple-element.92.mine), channel_id=1, source_target_pairs={{0,4},{4,0},{8,12},{12,8},{16,20},{20,16},{24,28},{28,24},{1,5},{5... | collective-permute-start | bytes 368648 | tf_op jit(solution)/shard_map/ppermute | solution.py:590
  19.9 3.5 %copy-start.11 = (bf16[16,2,5,5,128]{4,1,3,2,0:T(2,128)(2,1)S(1)}, bf16[16,2,5,5,128]{4,1,3,2,0:T(2,128)(2,1)}, u32[]{:S(2)}) copy-start(bf16[16,2,5,5,128]{4,1,3,2,0:T(2,128)(2,1)} %param.14) | copy-start | bytes 614404
  19.9 9.0 %copy-start.2 = (f32[16,2,5,5,128]{4,1,3,2,0:T(2,128)S(1)}, f32[16,2,5,5,128]{4,1,3,2,0:T(2,128)}, u32[]{:S(2)}) copy-start(f32[16,2,5,5,128]{4,1,3,2,0:T(2,128)} %param.15) | copy-start | bytes 1228804
  19.9 9.0 %copy-start.4 = (f32[16,2,5,5,128]{4,1,3,2,0:T(2,128)S(1)}, f32[16,2,5,5,128]{4,1,3,2,0:T(2,128)}, u32[]{:S(2)}) copy-start(f32[16,2,5,5,128]{4,1,3,2,0:T(2,128)} %param.16) | copy-start | bytes 1228804
  32.7 12.0 %collective-permute-start.7 = (f32[70,8,128]{2,1,0:T(8,128)S(1)}, f32[70,8,128]{2,1,0:T(8,128)S(1)}, u32[]{:S(2)}, u32[]{:S(2)}) collective-permute-start(f32[70,8,128]{2,1,0:T(8,128)S(1)} %get-tuple-element.113.flows), channel_id=1, source_target_pairs={{0,4},{4,0},{8,12},{12,8},{16,20},{20,16},{24,28},{28,24},{1,5},{5... | collective-permute-start | bytes 860168 | tf_op jit(solution)/shard_map/ppermute | solution.py:590
  32.7 5.3 %collective-permute-start.5 = (f32[30,8,128]{2,1,0:T(8,128)S(1)}, f32[30,8,128]{2,1,0:T(8,128)S(1)}, u32[]{:S(2)}, u32[]{:S(2)}) collective-permute-start(f32[30,8,128]{2,1,0:T(8,128)S(1)} %get-tuple-element.105.mine), channel_id=1, source_target_pairs={{0,8},{4,12},{8,0},{12,4},{16,24},{20,28},{24,16},{28,20},{1,9},{5... | collective-permute-start | bytes 368648 | tf_op jit(solution)/shard_map/ppermute | solution.py:590
  33.8 28.1 %collective-permute-start.12 = (f32[960,128]{1,0:T(8,128)S(1)}, f32[960,128]{1,0:T(8,128)S(1)}, u32[]{:S(2)}, u32[]{:S(2)}) collective-permute-start(f32[960,128]{1,0:T(8,128)S(1)} %get-tuple-element.133), channel_id=1, source_target_pairs={{0,3},{1,2},{2,1},{3,0},{4,7},{5,6},{6,5},{7,4},{8,11},{9,10},{10,... | collective-permute-start | bytes 1474568 | tf_op jit(solution)/shard_map/ppermute | solution.py:589
  38.7 5.4 %collective-permute-start.6 = (f32[10,8,128]{2,1,0:T(8,128)S(1)}, f32[10,8,128]{2,1,0:T(8,128)S(1)}, u32[]{:S(2)}, u32[]{:S(2)}) collective-permute-start(f32[10,8,128]{2,1,0:T(8,128)S(1)} %get-tuple-element.109.mine), channel_id=1, source_target_pairs={{0,16},{4,20},{8,24},{12,28},{16,0},{20,4},{24,8},{28,12},{1,17},{... | collective-permute-start | bytes 122888 | tf_op jit(solution)/shard_map/ppermute | solution.py:590
  48.4 5.8 %collective-permute-start.9 = (f32[50,8,128]{2,1,0:T(8,128)S(1)}, f32[50,8,128]{2,1,0:T(8,128)S(1)}, u32[]{:S(2)}, u32[]{:S(2)}) collective-permute-start(f32[50,8,128]{2,1,0:T(8,128)S(1)} %get-tuple-element.121.flows), channel_id=1, source_target_pairs={{0,4},{4,0},{8,12},{12,8},{16,20},{20,16},{24,28},{28,24},{1,5},{5... | collective-permute-start | bytes 614408 | tf_op jit(solution)/shard_map/ppermute | solution.py:590
  50.0 8.6 %collective-permute-start.10 = (f32[70,8,128]{2,1,0:T(8,128)S(1)}, f32[70,8,128]{2,1,0:T(8,128)S(1)}, u32[]{:S(2)}, u32[]{:S(2)}) collective-permute-start(f32[70,8,128]{2,1,0:T(8,128)S(1)} %get-tuple-element.125.flows), channel_id=1, source_target_pairs={{0,8},{4,12},{8,0},{12,4},{16,24},{20,28},{24,16},{28,20},{1,9},{5... | collective-permute-start | bytes 860168 | tf_op jit(solution)/shard_map/ppermute | solution.py:590
  55.0 6.0 %collective-permute-start.11 = (f32[50,8,128]{2,1,0:T(8,128)S(1)}, f32[50,8,128]{2,1,0:T(8,128)S(1)}, u32[]{:S(2)}, u32[]{:S(2)}) collective-permute-start(f32[50,8,128]{2,1,0:T(8,128)S(1)} %get-tuple-element.129.flows), channel_id=1, source_target_pairs={{0,8},{4,12},{8,0},{12,4},{16,24},{20,28},{24,16},{28,20},{1,9},{5... | collective-permute-start | bytes 614408 | tf_op jit(solution)/shard_map/ppermute | solution.py:590
  63.4 4.5 %collective-permute-start.13 = (f32[20,8,128]{2,1,0:T(8,128)S(1)}, f32[20,8,128]{2,1,0:T(8,128)S(1)}, u32[]{:S(2)}, u32[]{:S(2)}) collective-permute-start(f32[20,8,128]{2,1,0:T(8,128)S(1)} %get-tuple-element.136.flows), channel_id=1, source_target_pairs={{0,4},{4,0},{8,12},{12,8},{16,20},{20,16},{24,28},{28,24},{1,5},{5... | collective-permute-start | bytes 245768 | tf_op jit(solution)/shard_map/ppermute | solution.py:590
  64.8 11.0 %collective-permute-start.14 = (f32[35,8,128]{2,1,0:T(8,128)S(1)}, f32[35,8,128]{2,1,0:T(8,128)S(1)}, u32[]{:S(2)}, u32[]{:S(2)}) collective-permute-start(f32[35,8,128]{2,1,0:T(8,128)S(1)} %get-tuple-element.140.ends), channel_id=1, source_target_pairs={{0,16},{4,20},{8,24},{12,28},{16,0},{20,4},{24,8},{28,12},{1,17},{... | collective-permute-start | bytes 430088 | tf_op jit(solution)/shard_map/ppermute | solution.py:590
  68.6 9.8 %collective-permute-start.15 = (f32[20,8,128]{2,1,0:T(8,128)S(1)}, f32[20,8,128]{2,1,0:T(8,128)S(1)}, u32[]{:S(2)}, u32[]{:S(2)}) collective-permute-start(f32[20,8,128]{2,1,0:T(8,128)S(1)} %get-tuple-element.145.flows), channel_id=1, source_target_pairs={{0,8},{4,12},{8,0},{12,4},{16,24},{20,28},{24,16},{28,20},{1,9},{5... | collective-permute-start | bytes 245768 | tf_op jit(solution)/shard_map/ppermute | solution.py:590
  68.8 10.3 %collective-permute-start.16 = (f32[25,8,128]{2,1,0:T(8,128)S(1)}, f32[25,8,128]{2,1,0:T(8,128)S(1)}, u32[]{:S(2)}, u32[]{:S(2)}) collective-permute-start(f32[25,8,128]{2,1,0:T(8,128)S(1)} %get-tuple-element.149.ends), channel_id=1, source_target_pairs={{0,16},{4,20},{8,24},{12,28},{16,0},{20,4},{24,8},{28,12},{1,17},{... | collective-permute-start | bytes 307208 | tf_op jit(solution)/shard_map/ppermute | solution.py:590
  79.0 5.0 %collective-permute-start.17 = (f32[10,8,128]{2,1,0:T(8,128)S(1)}, f32[10,8,128]{2,1,0:T(8,128)S(1)}, u32[]{:S(2)}, u32[]{:S(2)}) collective-permute-start(f32[10,8,128]{2,1,0:T(8,128)S(1)} %get-tuple-element.153.ends), channel_id=1, source_target_pairs={{0,16},{4,20},{8,24},{12,28},{16,0},{20,4},{24,8},{28,12},{1,17},{... | collective-permute-start | bytes 122888 | tf_op jit(solution)/shard_map/ppermute | solution.py:590

commit v6 on v5

--- a/solution.py
+++ b/solution.py
@@ -273,7 +273,8 @@
 
 
 def near_cell(
-    flags, base, halo, from_left, from_right, advect, viscous, inverse, lower, upper, g, flows, edges
+    flags, base, halo, from_left, from_right, advect, viscous, inverse, lower, upper, group,
+    g, flows, edges,
 ):
     p = 1 - flags[0]
     cells = base.shape[0] // V
@@ -287,6 +288,7 @@
         return edge_terms(z, cells, values, edges, advect, p, first, last)
 
     sweeps(source, g, flows, 0, ((0, 32), (32, PAD)), p, inverse, lower, upper, cells)
+    flows[2 * V * PAD // 8 :] = group[...]
 
 
 def far_lead(flags, slab, trig, basis, turned, lead, halo):
@@ -398,16 +400,14 @@
             group[(c * 3 + 2) * V + a] = through[a]
 
 
-def merge_matrices(bit, levels, flags, mine, other, *refs):
+def merge_matrices(bit, levels, flags, mine, other, share, mats, merged, share_out, offset, new_offset):
     start, last = bit == 0, bit == levels - 1
-    share, refs = (None, refs) if start else (refs[0], refs[1:])
-    mats, merged, share_out = (refs[0], None, None) if last else refs
     right = flags[3 + bit] == 1
     left = jnp.logical_not(right)
     nothing = jnp.zeros((8, LANES), F32)
     for c in range(2):
         kinds = 1 if last else 3
-        at = lambda ref, kind: [ref[(c * kinds + kind) * V + a] for a in range(V)]
+        at = lambda ref, kind: [ref[offset + (c * kinds + kind) * V + a] for a in range(V)]
         pick = lambda kind, own: [jnp.where(own, m, t) for m, t in zip(at(mine, kind), at(other, kind))]
         if start:
             own = [[unit(a) for a in range(V)], [nothing] * V, [unit(a) for a in range(V)]]
@@ -433,7 +433,7 @@
             new += [times(rows(mats, c, 2), h_right), times(rows(mats, c, 0), p_left)]
         for kind, values in enumerate(new):
             for a in range(V):
-                merged[(c * len(new) + kind) * V + a] = values[a]
+                merged[new_offset + (c * len(new) + kind) * V + a] = values[a]
         s0 = times(rows(mats, c, 3), p_left)
         s1 = times(rows(mats, c, 4), p_left)
         s1b = times(rows(mats, c, 5), turned)
@@ -450,6 +450,14 @@
     from_right = plus(times(rows(mats, c, 4), f_left), times(rows(mats, c, 5), back))
     total = from_left + from_right
     return back, total if known is None else plus(known, total)
+
+
+def merge_all(parts, bit, levels, flags, flows, other, *refs):
+    share, known, mats, merged, share_out, inflow = (None, None, *refs) if bit == 0 else refs
+    tall = sum(height for _, height in parts) * V
+    new_offset = tall * (1 if bit == levels - 2 else 2)
+    merge_matrices(bit, levels, flags, flows, other, share, mats, merged, share_out, 2 * tall, new_offset)
+    merge_flows(parts, bit, levels, flags, mats, flows, other, *([] if known is None else [known]), merged, inflow)
 
 
 def merge_flows(parts, bit, levels, flags, mats, flows, other, *refs):
@@ -525,35 +533,49 @@
             lax.fori_loop(0, g.shape[0] // V, step, flow)
 
 
+def correct_all(parts, levels, flags, ends, other, share, known, blocks, *refs):
+    count = len(parts)
+    solved, results, mats, inflow = refs[:count], refs[count : 2 * count], refs[-2], refs[-1]
+    tall = sum(height for _, height in parts) * V
+    merge_matrices(levels - 1, levels, flags, ends, other, share, mats, None, None, tall, 0)
+    correct(parts, levels, flags, mats, ends, other, known, blocks, *solved, *results, inflow)
+
+
 def finish(levels, flags, mats, ends, other, known, g, blocks, near, *refs):
-    done, out, inflow = refs[:-2], refs[-2], refs[-1]
+    done, (out, inflow, held, sems) = refs[:-4], refs[-4:]
     right = flags[2 + levels] == 1
     p = flags[0]
     (first_row, last_row), last_extra = CHUNKS[-1]
     width, height = last_row - first_row, rows_of(CHUNKS[-1])
-
-    @pl.when(pl.program_id(0) == 0)
-    def _():
-        last_inflow(right, 1, mats, ends, other, known, 0, height // 8, inflow)
-
+    last_inflow(right, 1, mats, ends, other, known, 0, height // 8, inflow)
     flow = tuple(inflow[i] for i in range(2 * V))
 
     def step(z, carry):
         for a in range(V):
             j = z * V + a
             row = j * 2 * NT
-            out[pl.ds(row + 1 - p, NT, stride=2), :] = near[j, 0:NT, :]
+            held[pl.ds(row + 1 - p, NT, stride=2), :] = near[j, 0:NT, :]
             for ref, ((first, last), extra) in zip(done, CHUNKS):
-                out[pl.ds(row + p + 2 * first, last - first, stride=2), :] = ref[j, 0 : last - first, :]
+                held[pl.ds(row + p + 2 * first, last - first, stride=2), :] = ref[j, 0 : last - first, :]
                 if extra:
-                    out[pl.ds(row + p + 2 * (NT - 1), 1), :] = ref[j, last - first : last - first + 1, :]
+                    held[pl.ds(row + p + 2 * (NT - 1), 1), :] = ref[j, last - first : last - first + 1, :]
             value = corrected(1, z, a, 0, height, g, blocks, flow)
-            out[pl.ds(row + p + 2 * first_row, width, stride=2), :] = value[:width]
+            held[pl.ds(row + p + 2 * first_row, width, stride=2), :] = value[:width]
             if last_extra:
-                out[pl.ds(row + p + 2 * (NT - 1), 1), :] = value[width : width + 1]
+                held[pl.ds(row + p + 2 * (NT - 1), 1), :] = value[width : width + 1]
         return carry
 
-    lax.fori_loop(0, g.shape[0] // V, step, 0)
+    parts = sems.shape[0]
+    cells = g.shape[0] // V // parts
+    size = held.shape[0] // parts
+    copies = []
+    for i in range(parts):
+        lax.fori_loop(i * cells, (i + 1) * cells, step, 0)
+        span = pl.ds(i * size, size)
+        copies.append(pltpu.make_async_copy(held.at[span, :], out.at[span, :], sems.at[i]))
+        copies[-1].start()
+    for copy in copies:
+        copy.wait()
 
 
 def phase_tables(count):
@@ -601,10 +623,6 @@
     )
     flat = lambda x: x.transpose(0, 2, 3, 1, 4).reshape(cells * V * V * 2, LANES)
     inv, low, upp = flat(inverse.astype(F32)), flat(lower), flat(upper)
-    blocks, group = run(
-        transfer, [(2, cells * V, 16, LANES), (6 * V, 8, LANES)], [low, upp],
-        scratch=[pltpu.VMEM((cells * V, 8, LANES), F32)], name="transfer", flops=COSTS[1],
-    )
     st = state.transpose(0, 2, 3, 1, 4).reshape(cells * V * NT * 2, LANES)
     lead_rows, edge_rows = LEAD * V * NT, padded_even(V * NT * 2)
     held = pl.BlockSpec(memory_space=pltpu.VMEM)
@@ -616,7 +634,7 @@
         out_specs=[held] * 5,
         compiler_params=pltpu.CompilerParams(vmem_limit_bytes=16 * MB),
         name="split_cells",
-    )(run.before(st))
+    )(st)
     halo_near = lax.ppermute(xn, "pitch", near_pairs)
     slab_in = to_far(slab_out)
     from_left = lax.ppermute(last_cell, "seg", [(i, i + 1) for i in range(segs - 1)])
@@ -646,20 +664,8 @@
 
     edges = pltpu.VMEM((2 * V, PAD, LANES), F32)
 
-    mats, share = [], []
-
-    def merge_group(k):
-        nonlocal group, share
-        shapes = [(2, 6 * V, 8, LANES)]
-        if k < levels - 1:
-            shapes += [((6 if k < levels - 2 else 2) * V, 8, LANES), (2, 3 * V, 8, LANES)]
-        out = run(
-            functools.partial(merge_matrices, k, levels), shapes,
-            [group, to_level(group, k), *share], name="merge_matrices",
-        )
-        mats.append(out[0])
-        if k < levels - 1:
-            group, share = out[1], [out[2]]
+    mats = []
+    mats_shape = (2, 6 * V, 8, LANES)
 
     def solve_chunk(i):
         height = rows_of(CHUNKS[i])
@@ -671,35 +677,56 @@
         )
 
     class Exchange:
-        def __init__(self, c, g, flows):
-            self.parts = [(c, g.shape[1] // 8)]
+        def __init__(self, c, g, flows, leads=False):
+            self.parts, self.leads = [(c, g.shape[1] // 8)], leads
             self.flows, self.known, self.solved, self.level = flows, [], g, 0
+            self.scratch = [pltpu.VMEM((2 * V, g.shape[1], LANES), F32)]
 
         def step(self):
             tall, k = self.parts[0][1], self.level
             shape = ((2 if k < levels - 2 else 1) * V * tall, 8, LANES)
-            out = run(
-                functools.partial(merge_flows, self.parts, k, levels),
-                [shape, (2 * V * tall, 8, LANES)],
-                [mats[k], self.flows, to_level(self.flows, k), *self.known], name="merge_flows",
-            )
-            self.flows, self.known, self.level = out[0], out[1:], k + 1
+            inflow = (2 * V * tall, 8, LANES)
+            other = to_level(self.flows, k)
+            if self.leads:
+                shape = (shape[0] + (6 * V if k < levels - 2 else 2 * V),) + shape[1:]
+                out = run(
+                    functools.partial(merge_all, self.parts, k, levels),
+                    [mats_shape, shape, (2, 3 * V, 8, LANES), inflow],
+                    [self.flows, other, *self.known], name="merge_all",
+                )
+                mats.append(out[0])
+                self.flows, self.known = out[1], out[2:]
+            else:
+                out = run(
+                    functools.partial(merge_flows, self.parts, k, levels), [shape, inflow],
+                    [mats[k], self.flows, other, *self.known], name="merge_flows",
+                )
+                self.flows, self.known = out[0], out[1:]
+            self.level = k + 1
 
         def last(self):
-            return [mats[-1], self.flows, to_level(self.flows, levels - 1), *self.known]
+            return [self.flows, to_level(self.flows, levels - 1), *self.known]
 
         def correct(self):
+            if self.leads:
+                result, last = run(
+                    functools.partial(correct_all, self.parts, levels), [self.solved.shape, mats_shape],
+                    [*self.last(), blocks, self.solved], scratch=self.scratch, name="correct_all",
+                )
+                mats.append(last)
+                return result
             return run(
                 functools.partial(correct, self.parts, levels), [self.solved.shape],
-                [*self.last(), blocks, self.solved],
-                scratch=[pltpu.VMEM((2 * V, self.solved.shape[1], LANES), F32)], name="correct",
+                [mats[-1], *self.last(), blocks, self.solved], scratch=self.scratch, name="correct",
             )[0]
 
-    group, halo_near = lax.optimization_barrier((group, halo_near))
     base_near = run(
         near_base, [x_shape], [xn, xf, adv, vis, table, trig], name="near_base", flops=COSTS[0]
     )[0]
-    merge_group(0)
+    blocks, group = run(
+        transfer, [(2, cells * V, 16, LANES), (6 * V, 8, LANES)], [low, upp],
+        scratch=[pltpu.VMEM((cells * V, 8, LANES), F32)], name="transfer", flops=COSTS[1],
+    )
     lead = run(
         far_lead, [(LEAD * V, PAD, LANES)], [slab_in, trig, basis, turned],
         scratch=[pltpu.VMEM((V, PAD, LANES), F32)], name="far_lead", flops=COSTS[3],
@@ -707,40 +734,37 @@
     first = Exchange(
         0,
         *run(
-            near_cell, [x_shape, (2 * V * PAD // 8, 8, LANES)],
-            [base_near, halo_near, from_left, from_right, adv, vis, inv, low, upp],
+            near_cell, [x_shape, (2 * V * PAD // 8 + 6 * V, 8, LANES)],
+            [base_near, halo_near, from_left, from_right, adv, vis, inv, low, upp, group],
             scratch=[edges], name="near_cell", flops=COSTS[2],
-        )
+        ),
+        leads=True,
     )
-    for k in range(1, levels):
-        merge_group(k)
     first.step()
     second = Exchange(1, *solve_chunk(0))
+    second.step()
+    for k in range(1, levels - 1):
+        first.step()
+    third = Exchange(1, *solve_chunk(1))
     for k in range(1, levels - 1):
         second.step()
-        first.step()
-    second.step()
-    third = Exchange(1, *solve_chunk(1))
     third.step()
     near = first.correct()
     for k in range(1, levels - 1):
         third.step()
     done = [second.correct()]
     g_last = third.solved
-    small = third.last()
-
-    steps = 4
-    part = cells // steps
-    whole = lambda x: pl.BlockSpec(x.shape, lambda i: (0,) * x.ndim)
-    by_cell = lambda x: pl.BlockSpec((part * V,) + x.shape[1:], lambda i: (i, 0, 0))
+    small = [mats[-1], *third.last()]
+
     out = run(
         functools.partial(finish, levels), [st.shape], [*small, g_last, blocks, near, *done],
-        grid=(steps,),
-        in_specs=[whole(x) for x in small]
-        + [by_cell(g_last), pl.BlockSpec((2, part * V, 16, LANES), lambda i: (0, i, 0, 0))]
-        + [by_cell(x) for x in (near, *done)],
-        out_specs=[pl.BlockSpec((part * V * NT * 2, LANES), lambda i: (i, 0))],
-        scratch=[pltpu.VMEM((2 * V, rows_of(CHUNKS[-1]), LANES), F32)], name="finish",
+        out_specs=[pl.BlockSpec(memory_space=pltpu.HBM)],
+        scratch=[
+            pltpu.VMEM((2 * V, rows_of(CHUNKS[-1]), LANES), F32),
+            pltpu.VMEM(st.shape, F32),
+            pltpu.SemaphoreType.DMA((4,)),
+        ],
+        name="finish",
     )[0]
     return out.reshape(cells, V, NT, 2, LANES).transpose(0, 3, 1, 2, 4)
 

time: 87.6 us -> 83.8 us (0.957)
  the two profiles are of different devices: /device:TPU:24 before, /device:TPU:0 now
where the time goes in v6:
time: 83.8 us; the launch traced here: 83.4 us
  Pallas kernels  33.6 us (40%)
  starting transfers between devices  23.5 us (28%)
  waiting for transfers between devices  18.9 us (23%)
  local copies, waits for them, and re-layouts  6.95 us (8%)
    pallas_call x16, Pallas kernels, __call__(): pl.pallas_call(body, out_shape=[jax.ShapeDtypeStruct(s, F32) for s in out...  32.2 us
    ppermute x9, waiting for transfers between devices, local(): lax.ppermute(x, 'seg', [(i, i ^ 1 << k) for i in range(segs)])  18.9 us
    ppermute x9, starting transfers between devices, local(): lax.ppermute(x, 'seg', [(i, i ^ 1 << k) for i in range(segs)])  14.3 us
    unnamed x28, local copies, waits for them, and re-layouts  6.79 us
    ppermute x3, starting transfers between devices, local(): to_far = lambda x: lax.ppermute(x, 'pitch', far_pairs)  4.12 us
    ppermute x1, starting transfers between devices, local(): lax.ppermute(last_cell, 'seg', [(i, i + 1) for i in range(segs - 1)])  3.4 us
  transfers between devices with their start and end apart: 15, of which 5 were waited for; matrix products, arithmetic and copies ran while one was open for 0% of the time, Pallas kernels for 35%

profile of v6, /device:TPU:0, one launch (start us, length us, event | category | flops | bytes accessed | tf_op | source)
XLA Modules:
  0.0 83.4 jit_solution(4241641113545707862)
XLA Ops:
  0.0 2.2 %copy-done.3 = f32[16,2,5,49,128]{4,1,3,2,0:T(2,128)S(1)} copy-done((f32[16,2,5,49,128]{4,1,3,2,0:T(2,128)S(1)}, f32[16,2,5,49,128]{4,1,3,2,0:T(2,128)}, u32[]{:S(2)}) %copy-start.3) | copy-done | bytes 4014104
  2.2 1.5 %split_cells.1 = (f32[980,128]{1,0:T(8,128)}, f32[496,128]{1,0:T(8,128)}, f32[496,128]{1,0:T(8,128)}, f32[80,56,128]{2,1,0:T(8,128)S(1)}, f32[80,56,128]{2,1,0:T(8,128)S(1)}) custom-call(f32[7840,128]{1,0:T(8,128)S(1)} %bitcast.27), custom_call_target="tpu_custom_call" | custom-call | tf_op jit(solution)/shard_map/split_cells/pallas_call | solution.py:630
  3.6 1.4 %copy-done = f32[80,56,128]{2,1,0:T(8,128)} copy-done((f32[80,56,128]{2,1,0:T(8,128)}, f32[80,56,128]{2,1,0:T(8,128)S(1)}, u32[]{:S(2)}) %copy-start) | copy-done | bytes 2293784
  5.0 0.5 collective-permute-start.1
  5.5 2.6 %collective-permute-start = (f32[980,128]{1,0:T(8,128)}, f32[980,128]{1,0:T(8,128)S(1)}, u32[]{:S(2)}, u32[]{:S(2)}) collective-permute-start(f32[980,128]{1,0:T(8,128)} %get-tuple-element.82), channel_id=1, source_target_pairs={{0,3},{1,2},{2,1},{3,0},{4,7},{5,6},{6,5},{7,4},{8,11},{9,10},{10,... | collective-permute-start | bytes 1505288 | tf_op jit(solution)/shard_map/ppermute | solution.py:611
  8.1 3.4 %collective-permute-start.2 = (f32[496,128]{1,0:T(8,128)}, f32[496,128]{1,0:T(8,128)S(1)}, u32[]{:S(2)}, u32[]{:S(2)}) collective-permute-start(f32[496,128]{1,0:T(8,128)} %get-tuple-element.86), channel_id=1, source_target_pairs={{0,4},{4,8},{8,12},{12,16},{16,20},{20,24},{24,28},{1,5},{5,9},{9,... | collective-permute-start | bytes 761864 | tf_op jit(solution)/shard_map/ppermute | solution.py:640
  11.5 1.3 %collective-permute-start.3 = (f32[496,128]{1,0:T(8,128)}, f32[496,128]{1,0:T(8,128)S(1)}, u32[]{:S(2)}, u32[]{:S(2)}) collective-permute-start(f32[496,128]{1,0:T(8,128)} %get-tuple-element.87), channel_id=1, source_target_pairs={{4,0},{8,4},{12,8},{16,12},{20,16},{24,20},{28,24},{5,1},{9,5},{13... | collective-permute-start | bytes 761864 | tf_op jit(solution)/shard_map/ppermute | solution.py:641
  12.8 0.0 copy-done.13
  12.9 0.1 stack.35.flags
  12.9 0.1 broadcast_in_dim.2.harmonic
  13.0 0.0 copy-done.11
  13.0 0.0 copy-done.6
  13.0 0.0 copy-start.1
  13.0 1.6 %copy-done.1 = f32[80,56,128]{2,1,0:T(8,128)S(1)} copy-done((f32[80,56,128]{2,1,0:T(8,128)S(1)}, f32[80,56,128]{2,1,0:T(8,128)}, u32[]{:S(2)}) %copy-start.1) | copy-done | bytes 2293784
  14.7 0.8 copy-done.9
  15.5 0.7 copy-done.10
  16.3 4.2 %prepare.1 = (f32[56,128]{1,0:T(8,128)S(1)}, f32[80,56,128]{2,1,0:T(8,128)S(1)}, f32[1984,128]{1,0:T(8,128)S(1)}, f32[960,128]{1,0:T(8,128)S(1)}) custom-call(s32[6]{0:T(128)S(1)} %stack.35.flags, s32[2]{0:T(128)S(1)} %copy-done.11, f32[80,56,128]{2,1,0:T(8,128)S(1)} %get-tuple-element.73.xn, f32[80,56,128]{2,1,0:T(8,128)S(1)} %copy-done.1, ...), custom_call_target="tpu_custom_call" | custom-call | flops 1000 | bytes 1000 | tf_op jit(solution)/shard_map/prepare/pallas_call | solution.py:49
  20.5 0.1 collective-permute-start.5
  20.6 0.0 copy-start.4
  20.6 0.0 copy-start.5
  20.6 0.0 copy-start.12
  20.6 3.5 %near_base.1.base = f32[80,56,128]{2,1,0:T(8,128)S(1)} custom-call(s32[6]{0:T(128)S(1)} %stack.35.flags, f32[80,56,128]{2,1,0:T(8,128)S(1)} %get-tuple-element.73.xn, f32[80,56,128]{2,1,0:T(8,128)S(1)} %copy-done.2, f32[160,128]{1,0:T(8,128)S(1)} %bitcast.40, f32[160,128]{1,0:T(8,128)S(1)} %bitcast.45, f32[56,192]{1,0:T(8,128)S(1)} %copy-done.9, ...), custom_call_target="tpu_custom_call" | custom-call | bytes 1000 | tf_op jit(solution)/shard_map/near_base/pallas_call | solution.py:49
  24.2 0.0 copy-done.4
  24.2 0.0 copy-done.5
  24.2 1.6 %transfer.1 = (f32[2,80,16,128]{3,2,1,0:T(8,128)S(1)}, f32[30,8,128]{2,1,0:T(8,128)S(1)}) custom-call(s32[6]{0:T(128)S(1)} %stack.35.flags, f32[800,128]{1,0:T(8,128)S(1)} %bitcast.28, f32[800,128]{1,0:T(8,128)S(1)} %bitcast.32), custom_call_target="tpu_custom_call" | custom-call | bytes 1000 | tf_op jit(solution)/shard_map/transfer/pallas_call | solution.py:49
  25.8 0.1 reshape.36
  25.9 0.0 collective-permute-done.slab
  25.9 1.2 %far_lead.1.lead = f32[20,56,128]{2,1,0:T(8,128)S(1)} custom-call(s32[6]{0:T(128)S(1)} %stack.35.flags, f32[980,128]{1,0:T(8,128)S(1)} %collective-permute-done.slab, f32[56,128]{1,0:T(8,128)S(1)} %get-tuple-element.77.trig, f32[56,56]{1,0:T(8,128)S(1)} %copy-done.10, f32[64,192]{1,0:T(8,128)S(1)} %copy-done.8), custom_call_target="tpu_custom_call" | custom-call | bytes 1000 | tf_op jit(solution)/shard_map/far_lead/pallas_call | solution.py:49
  27.1 0.0 collective-permute-done.2.from_left
  27.1 0.0 collective-permute-done.3.from_right
  27.1 0.0 collective-permute-done.1.halo
  27.1 4.8 %near_cell.1 = (f32[80,56,128]{2,1,0:T(8,128)S(1)}, f32[100,8,128]{2,1,0:T(8,128)S(1)}) custom-call(s32[6]{0:T(128)S(1)} %stack.35.flags, f32[80,56,128]{2,1,0:T(8,128)S(1)} %near_base.1.base, f32[80,56,128]{2,1,0:T(8,128)} %collective-permute-done.1.halo, f32[496,128]{1,0:T(8,128)S(1)} %collective-permute-done.2.from_left, ...), custom_call_target="tpu_custom_call" | custom-call | flops 6000000000 | bytes 1000 | tf_op jit(solution)/shard_map/near_cell/pallas_call | solution.py:49
  32.0 2.7 %collective-permute-start.4 = (f32[100,8,128]{2,1,0:T(8,128)S(1)}, f32[100,8,128]{2,1,0:T(8,128)S(1)}, u32[]{:S(2)}, u32[]{:S(2)}) collective-permute-start(f32[100,8,128]{2,1,0:T(8,128)S(1)} %get-tuple-element.91.flows), channel_id=1, source_target_pairs={{0,4},{4,0},{8,12},{12,8},{16,20},{20,16},{24,28},{28,24},{1,5},{5... | collective-permute-start | bytes 1228808 | tf_op jit(solution)/shard_map/ppermute | solution.py:612
  34.7 1.4 %collective-permute-start.8 = (f32[960,128]{1,0:T(8,128)S(1)}, f32[960,128]{1,0:T(8,128)S(1)}, u32[]{:S(2)}, u32[]{:S(2)}) collective-permute-start(f32[960,128]{1,0:T(8,128)S(1)} %get-tuple-element.108), channel_id=1, source_target_pairs={{0,3},{1,2},{2,1},{3,0},{4,7},{5,6},{6,5},{7,4},{8,11},{9,10},{10,... | collective-permute-start | bytes 1474568 | tf_op jit(solution)/shard_map/ppermute | solution.py:611
  36.1 8.8 %collective-permute-done.4.other = f32[100,8,128]{2,1,0:T(8,128)S(1)} collective-permute-done((f32[100,8,128]{2,1,0:T(8,128)S(1)}, f32[100,8,128]{2,1,0:T(8,128)S(1)}, u32[]{:S(2)}, u32[]{:S(2)}) %collective-permute-start.4) | collective-permute-done | bytes 409632 | tf_op jit(solution)/shard_map/ppermute | solution.py:612
  44.9 1.0 %merge_all.2 = (f32[2,30,8,128]{3,2,1,0:T(8,128)S(1)}, f32[100,8,128]{2,1,0:T(8,128)S(1)}, f32[2,15,8,128]{3,2,1,0:T(8,128)S(1)}, f32[70,8,128]{2,1,0:T(8,128)S(1)}) custom-call(s32[6]{0:T(128)S(1)} %stack.35.flags, f32[100,8,128]{2,1,0:T(8,128)S(1)} %get-tuple-element.91.flows, f32[100,8,128]{2,1,0:T(8,128)S(1)} %collective-permute-done.4.other), custom_call_target="tpu_custom_call" | custom-call | flops 1000 | bytes 1000 | tf_op jit(solution)/shard_map/merge_all/pallas_call | solution.py:49
  45.9 2.8 %collective-permute-start.7 = (f32[100,8,128]{2,1,0:T(8,128)S(1)}, f32[100,8,128]{2,1,0:T(8,128)S(1)}, u32[]{:S(2)}, u32[]{:S(2)}) collective-permute-start(f32[100,8,128]{2,1,0:T(8,128)S(1)} %get-tuple-element.103.flows), channel_id=1, source_target_pairs={{0,8},{4,12},{8,0},{12,4},{16,24},{20,28},{24,16},{28,20},{1,9},{5... | collective-permute-start | bytes 1228808 | tf_op jit(solution)/shard_map/ppermute | solution.py:612
  48.7 0.0 collective-permute-done.5.halo
  48.7 2.8 %far_chunk.2 = (f32[80,40,128]{2,1,0:T(8,128)S(1)}, f32[50,8,128]{2,1,0:T(8,128)S(1)}) custom-call(s32[6]{0:T(128)S(1)} %stack.35.flags, f32[80,56,128]{2,1,0:T(8,128)S(1)} %get-tuple-element.94.base, f32[20,56,128]{2,1,0:T(8,128)S(1)} %far_lead.1.lead, f32[1984,128]{1,0:T(8,128)S(1)} %collective-permute-done.5.halo, ...), custom_call_target="tpu_custom_call" | custom-call | flops 1000 | bytes 1000 | tf_op jit(solution)/shard_map/far_chunk/pallas_call | solution.py:49
  51.5 0.7 collective-permute-start.6
  52.1 5.9 %collective-permute-done.6.other = f32[50,8,128]{2,1,0:T(8,128)S(1)} collective-permute-done((f32[50,8,128]{2,1,0:T(8,128)S(1)}, f32[50,8,128]{2,1,0:T(8,128)S(1)}, u32[]{:S(2)}, u32[]{:S(2)}) %collective-permute-start.6) | collective-permute-done | bytes 204832 | tf_op jit(solution)/shard_map/ppermute | solution.py:612
  58.0 0.8 merge_flows.4
  58.8 0.4 collective-permute-start.9
  59.2 0.0 collective-permute-done.7.other
  59.2 1.0 %merge_all.3 = (f32[2,30,8,128]{3,2,1,0:T(8,128)S(1)}, f32[45,8,128]{2,1,0:T(8,128)S(1)}, f32[2,15,8,128]{3,2,1,0:T(8,128)S(1)}, f32[70,8,128]{2,1,0:T(8,128)S(1)}) custom-call(s32[6]{0:T(128)S(1)} %stack.35.flags, f32[100,8,128]{2,1,0:T(8,128)S(1)} %get-tuple-element.103.flows, f32[100,8,128]{2,1,0:T(8,128)S(1)} %collective-permute-done.7.other, ...), custom_call_target="tpu_custom_call" | custom-call | flops 1000 | bytes 1000 | tf_op jit(solution)/shard_map/merge_all/pallas_call | solution.py:49
  60.2 2.8 %collective-permute-start.11 = (f32[45,8,128]{2,1,0:T(8,128)S(1)}, f32[45,8,128]{2,1,0:T(8,128)S(1)}, u32[]{:S(2)}, u32[]{:S(2)}) collective-permute-start(f32[45,8,128]{2,1,0:T(8,128)S(1)} %get-tuple-element.119.ends), channel_id=1, source_target_pairs={{0,16},{4,20},{8,24},{12,28},{16,0},{20,4},{24,8},{28,12},{1,17},{... | collective-permute-start | bytes 552968 | tf_op jit(solution)/shard_map/ppermute | solution.py:612
  63.0 0.0 collective-permute-done.8.halo
  63.0 1.6 %far_chunk.3 = (f32[80,16,128]{2,1,0:T(8,128)S(1)}, f32[20,8,128]{2,1,0:T(8,128)S(1)}) custom-call(s32[6]{0:T(128)S(1)} %stack.35.flags, f32[80,56,128]{2,1,0:T(8,128)S(1)} %get-tuple-element.94.base, f32[20,56,128]{2,1,0:T(8,128)S(1)} %far_lead.1.lead, f32[960,128]{1,0:T(8,128)S(1)} %collective-permute-done.8.halo, ...), custom_call_target="tpu_custom_call" | custom-call | flops 1000 | bytes 1000 | tf_op jit(solution)/shard_map/far_chunk/pallas_call | solution.py:49
  64.6 0.7 collective-permute-start.10
  65.3 3.2 %collective-permute-done.9.other = f32[50,8,128]{2,1,0:T(8,128)S(1)} collective-permute-done((f32[50,8,128]{2,1,0:T(8,128)S(1)}, f32[50,8,128]{2,1,0:T(8,128)S(1)}, u32[]{:S(2)}, u32[]{:S(2)}) %collective-permute-start.9) | collective-permute-done | bytes 204832 | tf_op jit(solution)/shard_map/ppermute | solution.py:612
  68.4 0.8 merge_flows.5
  69.2 0.0 collective-permute-done.10.other
  69.3 0.6 merge_flows.6
  69.9 1.5 %collective-permute-start.12 = (f32[20,8,128]{2,1,0:T(8,128)S(1)}, f32[20,8,128]{2,1,0:T(8,128)S(1)}, u32[]{:S(2)}, u32[]{:S(2)}) collective-permute-start(f32[20,8,128]{2,1,0:T(8,128)S(1)} %get-tuple-element.126.flows), channel_id=1, source_target_pairs={{0,8},{4,12},{8,0},{12,4},{16,24},{20,28},{24,16},{28,20},{1,9},{5... | collective-permute-start | bytes 245768 | tf_op jit(solution)/shard_map/ppermute | solution.py:612
  71.4 0.3 collective-permute-start.13
  71.7 0.0 collective-permute-done.11.other
  71.7 2.6 %correct_all.1 = (f32[80,56,128]{2,1,0:T(8,128)S(1)}, f32[2,30,8,128]{3,2,1,0:T(8,128)S(1)}) custom-call(s32[6]{0:T(128)S(1)} %stack.35.flags, f32[45,8,128]{2,1,0:T(8,128)S(1)} %get-tuple-element.119.ends, f32[45,8,128]{2,1,0:T(8,128)S(1)} %collective-permute-done.11.other, f32[2,15,8,128]{3,2,1,0:T(8,128)S(1)} %get-tuple-element.120.share, ...), custom_call_target="tpu_custom_call" | custom-call | flops 1000 | bytes 1000 | tf_op jit(solution)/shard_map/correct_all/pallas_call | solution.py:49
  74.4 0.2 collective-permute-done.12.other
  74.6 0.7 merge_flows.7
  75.2 2.5 %collective-permute-start.14 = (f32[10,8,128]{2,1,0:T(8,128)S(1)}, f32[10,8,128]{2,1,0:T(8,128)S(1)}, u32[]{:S(2)}, u32[]{:S(2)}) collective-permute-start(f32[10,8,128]{2,1,0:T(8,128)S(1)} %get-tuple-element.135.ends), channel_id=1, source_target_pairs={{0,16},{4,20},{8,24},{12,28},{16,0},{20,4},{24,8},{28,12},{1,17},{... | collective-permute-start | bytes 122888 | tf_op jit(solution)/shard_map/ppermute | solution.py:612
  77.7 0.8 collective-permute-done.13.other
  78.5 2.1 %correct.1.refs_0_ = f32[80,40,128]{2,1,0:T(8,128)S(1)} custom-call(s32[6]{0:T(128)S(1)} %stack.35.flags, f32[2,30,8,128]{3,2,1,0:T(8,128)S(1)} %get-tuple-element.130.mats, f32[25,8,128]{2,1,0:T(8,128)S(1)} %get-tuple-element.131.ends, f32[25,8,128]{2,1,0:T(8,128)S(1)} %collective-permute-done.13.other, f32[50,8,128]{2,1,0:T(8,128)S(1)} %get-tuple-element.132.known, ...), custom_call_target="tpu_custom_call" | custom-call | flops 1000 | bytes 1000 | tf_op jit(solution)/shard_map/correct/pallas_call | solution.py:49
  80.6 0.0 collective-permute-done.14.other
  80.6 2.8 %finish.1 = f32[7840,128]{1,0:T(8,128)} custom-call(s32[6]{0:T(128)S(1)} %stack.35.flags, f32[2,30,8,128]{3,2,1,0:T(8,128)S(1)} %get-tuple-element.130.mats, f32[10,8,128]{2,1,0:T(8,128)S(1)} %get-tuple-element.135.ends, f32[10,8,128]{2,1,0:T(8,128)S(1)} %collective-permute-done.14.other, f32[20,8,128]{2,1,0:T(8,128)S(1)} %get-tuple-element.136.known, ...), custom_call_target="tpu_custom_call" | custom-call | flops 1000 | bytes 1000 | tf_op jit(solution)/shard_map/finish/pallas_call | solution.py:49
  (15 shorter events, 0.0 us)
Async XLA Ops:
  0.0 12.8 %copy-start.13 = (s32[24]{0:T(128)S(1)}, s32[24]{0:T(128)}, u32[]{:S(2)}) copy-start(s32[24]{0:T(128)} %param.18) | copy-start | bytes 292
  0.0 13.0 %copy-start.11 = (s32[2]{0:T(128)S(1)}, s32[2]{0:T(128)}, u32[]{:S(2)}) copy-start(s32[2]{0:T(128)} %blades.1) | copy-start | bytes 28
  0.0 2.2 %copy-start.3 = (f32[16,2,5,49,128]{4,1,3,2,0:T(2,128)S(1)}, f32[16,2,5,49,128]{4,1,3,2,0:T(2,128)}, u32[]{:S(2)}) copy-start(f32[16,2,5,49,128]{4,1,3,2,0:T(2,128)} %param.11) | copy-start | bytes 12042244
  2.2 10.8 %copy-start.6 = (f32[16,2,5,128]{3,1,2,0:T(2,128)S(1)}, f32[16,2,5,128]{3,1,2,0:T(2,128)}, u32[]{:S(2)}) copy-start(f32[16,2,5,128]{3,1,2,0:T(2,128)} %param.12) | copy-start | bytes 245764
  2.2 10.8 %copy-start.7 = (f32[16,2,5,128]{3,1,2,0:T(2,128)S(1)}, f32[16,2,5,128]{3,1,2,0:T(2,128)}, u32[]{:S(2)}) copy-start(f32[16,2,5,128]{3,1,2,0:T(2,128)} %param.13) | copy-start | bytes 245764
  2.2 10.9 %copy-start.8 = (f32[64,192]{1,0:T(8,128)S(1)}, f32[64,192]{1,0:T(8,128)}, u32[]{:S(2)}) copy-start(f32[64,192]{1,0:T(8,128)} %constant.33.clone.turned) | copy-start | bytes 147460
  3.6 1.4 %copy-start = (f32[80,56,128]{2,1,0:T(8,128)}, f32[80,56,128]{2,1,0:T(8,128)S(1)}, u32[]{:S(2)}) copy-start(f32[80,56,128]{2,1,0:T(8,128)S(1)} %get-tuple-element.74.xf) | copy-start | bytes 6881284
  5.0 22.1 %collective-permute-start.1 = (f32[80,56,128]{2,1,0:T(8,128)S(1)}, f32[80,56,128]{2,1,0:T(8,128)}, u32[]{:S(2)}, u32[]{:S(2)}) collective-permute-start(f32[80,56,128]{2,1,0:T(8,128)S(1)} %get-tuple-element.73.xn), channel_id=1, source_target_pairs={{0,1},{1,0},{2,3},{3,2},{4,5},{5,4},{6,7},{7,6},{8,9},{9,8},{10,11... | collective-permute-start | bytes 6881288 | tf_op jit(solution)/shard_map/ppermute | solution.py:638
  5.5 20.5 %collective-permute-start = (f32[980,128]{1,0:T(8,128)}, f32[980,128]{1,0:T(8,128)S(1)}, u32[]{:S(2)}, u32[]{:S(2)}) collective-permute-start(f32[980,128]{1,0:T(8,128)} %get-tuple-element.82), channel_id=1, source_target_pairs={{0,3},{1,2},{2,1},{3,0},{4,7},{5,6},{6,5},{7,4},{8,11},{9,10},{10,... | collective-permute-start | bytes 1505288 | tf_op jit(solution)/shard_map/ppermute | solution.py:611
  8.1 19.0 %collective-permute-start.2 = (f32[496,128]{1,0:T(8,128)}, f32[496,128]{1,0:T(8,128)S(1)}, u32[]{:S(2)}, u32[]{:S(2)}) collective-permute-start(f32[496,128]{1,0:T(8,128)} %get-tuple-element.86), channel_id=1, source_target_pairs={{0,4},{4,8},{8,12},{12,16},{16,20},{20,24},{24,28},{1,5},{5,9},{9,... | collective-permute-start | bytes 761864 | tf_op jit(solution)/shard_map/ppermute | solution.py:640
  11.5 15.6 %collective-permute-start.3 = (f32[496,128]{1,0:T(8,128)}, f32[496,128]{1,0:T(8,128)S(1)}, u32[]{:S(2)}, u32[]{:S(2)}) collective-permute-start(f32[496,128]{1,0:T(8,128)} %get-tuple-element.87), channel_id=1, source_target_pairs={{4,0},{8,4},{12,8},{16,12},{20,16},{24,20},{28,24},{5,1},{9,5},{13... | collective-permute-start | bytes 761864 | tf_op jit(solution)/shard_map/ppermute | solution.py:641
  13.0 1.6 %copy-start.1 = (f32[80,56,128]{2,1,0:T(8,128)S(1)}, f32[80,56,128]{2,1,0:T(8,128)}, u32[]{:S(2)}) copy-start(f32[80,56,128]{2,1,0:T(8,128)} %copy-done) | copy-start | bytes 6881284
  14.7 0.8 copy-start.9
  15.5 0.7 copy-start.10
  16.3 4.3 %copy-start.2 = (f32[80,56,128]{2,1,0:T(8,128)S(1)}, f32[80,56,128]{2,1,0:T(8,128)}, u32[]{:S(2)}) copy-start(f32[80,56,128]{2,1,0:T(8,128)} %copy-done) | copy-start | bytes 6881284
  20.5 28.2 %collective-permute-start.5 = (f32[1984,128]{1,0:T(8,128)S(1)}, f32[1984,128]{1,0:T(8,128)S(1)}, u32[]{:S(2)}, u32[]{:S(2)}) collective-permute-start(f32[1984,128]{1,0:T(8,128)S(1)} %get-tuple-element.96), channel_id=1, source_target_pairs={{0,3},{1,2},{2,1},{3,0},{4,7},{5,6},{6,5},{7,4},{8,11},{9,10},{10,... | collective-permute-start | bytes 3047432 | tf_op jit(solution)/shard_map/ppermute | solution.py:611
  20.6 3.6 %copy-start.4 = (f32[16,2,5,5,128]{4,1,3,2,0:T(2,128)S(1)}, f32[16,2,5,5,128]{4,1,3,2,0:T(2,128)}, u32[]{:S(2)}) copy-start(f32[16,2,5,5,128]{4,1,3,2,0:T(2,128)} %param.15) | copy-start | bytes 1228804
  20.6 3.6 %copy-start.5 = (f32[16,2,5,5,128]{4,1,3,2,0:T(2,128)S(1)}, f32[16,2,5,5,128]{4,1,3,2,0:T(2,128)}, u32[]{:S(2)}) copy-start(f32[16,2,5,5,128]{4,1,3,2,0:T(2,128)} %param.16) | copy-start | bytes 1228804
  20.6 5.2 %copy-start.12 = (bf16[16,2,5,5,128]{4,1,3,2,0:T(2,128)(2,1)S(1)}, bf16[16,2,5,5,128]{4,1,3,2,0:T(2,128)(2,1)}, u32[]{:S(2)}) copy-start(bf16[16,2,5,5,128]{4,1,3,2,0:T(2,128)(2,1)} %param.14) | copy-start | bytes 614404
  32.0 12.9 %collective-permute-start.4 = (f32[100,8,128]{2,1,0:T(8,128)S(1)}, f32[100,8,128]{2,1,0:T(8,128)S(1)}, u32[]{:S(2)}, u32[]{:S(2)}) collective-permute-start(f32[100,8,128]{2,1,0:T(8,128)S(1)} %get-tuple-element.91.flows), channel_id=1, source_target_pairs={{0,4},{4,0},{8,12},{12,8},{16,20},{20,16},{24,28},{28,24},{1,5},{5... | collective-permute-start | bytes 1228808 | tf_op jit(solution)/shard_map/ppermute | solution.py:612
  34.7 28.4 %collective-permute-start.8 = (f32[960,128]{1,0:T(8,128)S(1)}, f32[960,128]{1,0:T(8,128)S(1)}, u32[]{:S(2)}, u32[]{:S(2)}) collective-permute-start(f32[960,128]{1,0:T(8,128)S(1)} %get-tuple-element.108), channel_id=1, source_target_pairs={{0,3},{1,2},{2,1},{3,0},{4,7},{5,6},{6,5},{7,4},{8,11},{9,10},{10,... | collective-permute-start | bytes 1474568 | tf_op jit(solution)/shard_map/ppermute | solution.py:611
  45.9 13.3 %collective-permute-start.7 = (f32[100,8,128]{2,1,0:T(8,128)S(1)}, f32[100,8,128]{2,1,0:T(8,128)S(1)}, u32[]{:S(2)}, u32[]{:S(2)}) collective-permute-start(f32[100,8,128]{2,1,0:T(8,128)S(1)} %get-tuple-element.103.flows), channel_id=1, source_target_pairs={{0,8},{4,12},{8,0},{12,4},{16,24},{20,28},{24,16},{28,20},{1,9},{5... | collective-permute-start | bytes 1228808 | tf_op jit(solution)/shard_map/ppermute | solution.py:612
  51.5 6.6 %collective-permute-start.6 = (f32[50,8,128]{2,1,0:T(8,128)S(1)}, f32[50,8,128]{2,1,0:T(8,128)S(1)}, u32[]{:S(2)}, u32[]{:S(2)}) collective-permute-start(f32[50,8,128]{2,1,0:T(8,128)S(1)} %get-tuple-element.100.flows), channel_id=1, source_target_pairs={{0,4},{4,0},{8,12},{12,8},{16,20},{20,16},{24,28},{28,24},{1,5},{5... | collective-permute-start | bytes 614408 | tf_op jit(solution)/shard_map/ppermute | solution.py:612
  58.8 9.6 %collective-permute-start.9 = (f32[50,8,128]{2,1,0:T(8,128)S(1)}, f32[50,8,128]{2,1,0:T(8,128)S(1)}, u32[]{:S(2)}, u32[]{:S(2)}) collective-permute-start(f32[50,8,128]{2,1,0:T(8,128)S(1)} %get-tuple-element.112.flows), channel_id=1, source_target_pairs={{0,8},{4,12},{8,0},{12,4},{16,24},{20,28},{24,16},{28,20},{1,9},{5... | collective-permute-start | bytes 614408 | tf_op jit(solution)/shard_map/ppermute | solution.py:612
  60.2 11.5 %collective-permute-start.11 = (f32[45,8,128]{2,1,0:T(8,128)S(1)}, f32[45,8,128]{2,1,0:T(8,128)S(1)}, u32[]{:S(2)}, u32[]{:S(2)}) collective-permute-start(f32[45,8,128]{2,1,0:T(8,128)S(1)} %get-tuple-element.119.ends), channel_id=1, source_target_pairs={{0,16},{4,20},{8,24},{12,28},{16,0},{20,4},{24,8},{28,12},{1,17},{... | collective-permute-start | bytes 552968 | tf_op jit(solution)/shard_map/ppermute | solution.py:612
  64.6 4.7 %collective-permute-start.10 = (f32[20,8,128]{2,1,0:T(8,128)S(1)}, f32[20,8,128]{2,1,0:T(8,128)S(1)}, u32[]{:S(2)}, u32[]{:S(2)}) collective-permute-start(f32[20,8,128]{2,1,0:T(8,128)S(1)} %get-tuple-element.116.flows), channel_id=1, source_target_pairs={{0,4},{4,0},{8,12},{12,8},{16,20},{20,16},{24,28},{28,24},{1,5},{5... | collective-permute-start | bytes 245768 | tf_op jit(solution)/shard_map/ppermute | solution.py:612
  69.9 4.7 %collective-permute-start.12 = (f32[20,8,128]{2,1,0:T(8,128)S(1)}, f32[20,8,128]{2,1,0:T(8,128)S(1)}, u32[]{:S(2)}, u32[]{:S(2)}) collective-permute-start(f32[20,8,128]{2,1,0:T(8,128)S(1)} %get-tuple-element.126.flows), channel_id=1, source_target_pairs={{0,8},{4,12},{8,0},{12,4},{16,24},{20,28},{24,16},{28,20},{1,9},{5... | collective-permute-start | bytes 245768 | tf_op jit(solution)/shard_map/ppermute | solution.py:612
  71.4 7.1 %collective-permute-start.13 = (f32[25,8,128]{2,1,0:T(8,128)S(1)}, f32[25,8,128]{2,1,0:T(8,128)S(1)}, u32[]{:S(2)}, u32[]{:S(2)}) collective-permute-start(f32[25,8,128]{2,1,0:T(8,128)S(1)} %get-tuple-element.131.ends), channel_id=1, source_target_pairs={{0,16},{4,20},{8,24},{12,28},{16,0},{20,4},{24,8},{28,12},{1,17},{... | collective-permute-start | bytes 307208 | tf_op jit(solution)/shard_map/ppermute | solution.py:612
  75.2 5.4 %collective-permute-start.14 = (f32[10,8,128]{2,1,0:T(8,128)S(1)}, f32[10,8,128]{2,1,0:T(8,128)S(1)}, u32[]{:S(2)}, u32[]{:S(2)}) collective-permute-start(f32[10,8,128]{2,1,0:T(8,128)S(1)} %get-tuple-element.135.ends), channel_id=1, source_target_pairs={{0,16},{4,20},{8,24},{12,28},{16,0},{20,4},{24,8},{28,12},{1,17},{... | collective-permute-start | bytes 122888 | tf_op jit(solution)/shard_map/ppermute | solution.py:612

commit v7 on v6

--- a/solution.py
+++ b/solution.py
@@ -634,7 +634,7 @@
         out_specs=[held] * 5,
         compiler_params=pltpu.CompilerParams(vmem_limit_bytes=16 * MB),
         name="split_cells",
-    )(st)
+    )(run.before(st))
     halo_near = lax.ppermute(xn, "pitch", near_pairs)
     slab_in = to_far(slab_out)
     from_left = lax.ppermute(last_cell, "seg", [(i, i + 1) for i in range(segs - 1)])

time: 83.8 us -> 77.4 us (0.924)
  local copies, waits for them, and re-layouts: 6.95 us -> 2.34 us
  Pallas kernels: 33.6 us -> 31.5 us
    unnamed x28 -> x22, local copies, waits for them, and re-layouts: 6.79 us -> 2.18 us
    pallas_call x16, Pallas kernels: 32.2 us -> 31 us  [__call__(): pl.pallas_call(body, out_shape=[jax.ShapeDtypeStruct(s, F32) for s in out...]
    pallas_call x1, Pallas kernels: 1.46 us -> 0.51 us  [local(): pl.pallas_call(split_cells, out_shape=[jax.ShapeDtypeStruct(x, F32) for x...]
  transfers between devices with their start and end apart: 15 -> 15, of which waited for: 5 -> 6; matrix products, arithmetic and copies ran while one was open for 0% -> 0% of each run, Pallas kernels for 35% -> 37%
where the time goes in v7:
time: 77.4 us; the launch traced here: 77.2 us
  Pallas kernels  31.5 us (41%)
  starting transfers between devices  23.6 us (30%)
  waiting for transfers between devices  19.3 us (25%)
  local copies, waits for them, and re-layouts  2.34 us (3%)
    pallas_call x16, Pallas kernels, __call__(): pl.pallas_call(body, out_shape=[jax.ShapeDtypeStruct(s, F32) for s in out...  31 us
    ppermute x9, waiting for transfers between devices, local(): lax.ppermute(x, 'seg', [(i, i ^ 1 << k) for i in range(segs)])  19.3 us
    ppermute x9, starting transfers between devices, local(): lax.ppermute(x, 'seg', [(i, i ^ 1 << k) for i in range(segs)])  14.3 us
    ppermute x3, starting transfers between devices, local(): to_far = lambda x: lax.ppermute(x, 'pitch', far_pairs)  4.13 us
    ppermute x1, starting transfers between devices, local(): lax.ppermute(last_cell, 'seg', [(i, i + 1) for i in range(segs - 1)])  3.4 us
    unnamed x22, local copies, waits for them, and re-layouts  2.18 us
  transfers between devices with their start and end apart: 15, of which 6 were waited for; matrix products, arithmetic and copies ran while one was open for 0% of the time, Pallas kernels for 37%

profile of v7, /device:TPU:0, one launch (start us, length us, event | category | flops | bytes accessed | tf_op | source)
XLA Modules:
  0.0 77.2 jit_solution(18119896761130724472)
XLA Ops:
  0.0 0.1 stack.35.flags
  0.1 2.1 %copy-done = f32[16,2,5,49,128]{4,1,3,2,0:T(2,128)S(1)} copy-done((f32[16,2,5,49,128]{4,1,3,2,0:T(2,128)S(1)}, f32[16,2,5,49,128]{4,1,3,2,0:T(2,128)}, u32[]{:S(2)}) %copy-start) | copy-done | bytes 4014104
  2.2 0.5 split_cells.1
  2.8 0.5 collective-permute-start.1
  3.3 2.6 %collective-permute-start = (f32[980,128]{1,0:T(8,128)S(1)}, f32[980,128]{1,0:T(8,128)S(1)}, u32[]{:S(2)}, u32[]{:S(2)}) collective-permute-start(f32[980,128]{1,0:T(8,128)S(1)} %get-tuple-element.84), channel_id=1, source_target_pairs={{0,3},{1,2},{2,1},{3,0},{4,7},{5,6},{6,5},{7,4},{8,11},{9,10},{10,... | collective-permute-start | bytes 1505288 | tf_op jit(solution)/shard_map/ppermute | solution.py:611
  5.9 3.4 %collective-permute-start.2 = (f32[496,128]{1,0:T(8,128)S(1)}, f32[496,128]{1,0:T(8,128)S(1)}, u32[]{:S(2)}, u32[]{:S(2)}) collective-permute-start(f32[496,128]{1,0:T(8,128)S(1)} %get-tuple-element.88), channel_id=1, source_target_pairs={{0,4},{4,8},{8,12},{12,16},{16,20},{20,24},{24,28},{1,5},{5,9},{9,... | collective-permute-start | bytes 761864 | tf_op jit(solution)/shard_map/ppermute | solution.py:640
  9.3 1.3 %collective-permute-start.3 = (f32[496,128]{1,0:T(8,128)S(1)}, f32[496,128]{1,0:T(8,128)S(1)}, u32[]{:S(2)}, u32[]{:S(2)}) collective-permute-start(f32[496,128]{1,0:T(8,128)S(1)} %get-tuple-element.89), channel_id=1, source_target_pairs={{4,0},{8,4},{12,8},{16,12},{20,16},{24,20},{28,24},{5,1},{9,5},{13... | collective-permute-start | bytes 761864 | tf_op jit(solution)/shard_map/ppermute | solution.py:641
  10.6 0.0 copy-done.10
  10.7 0.1 broadcast_in_dim.2.harmonic
  10.7 0.0 copy-done.5
  10.7 0.0 copy-done.8
  10.7 0.0 copy-done.3
  10.8 0.0 copy-done.4
  10.8 0.0 copy-done.6
  10.8 0.0 copy-done.7
  10.8 4.2 %prepare.1 = (f32[56,128]{1,0:T(8,128)S(1)}, f32[80,56,128]{2,1,0:T(8,128)S(1)}, f32[1984,128]{1,0:T(8,128)S(1)}, f32[960,128]{1,0:T(8,128)S(1)}) custom-call(s32[6]{0:T(128)S(1)} %stack.35.flags, s32[2]{0:T(128)S(1)} %copy-done.8, f32[80,56,128]{2,1,0:T(8,128)S(1)} %get-tuple-element.75.xn, f32[80,56,128]{2,1,0:T(8,128)S(1)} %get-tuple-element.76.xf, ...), custom_call_target="tpu_custom_call" | custom-call | flops 1000 | bytes 1000 | tf_op jit(solution)/shard_map/prepare/pallas_call | solution.py:49
  15.0 0.1 collective-permute-start.5
  15.1 0.0 copy-start.1
  15.1 0.0 copy-start.2
  15.1 0.0 copy-start.9
  15.1 3.5 %near_base.1.base = f32[80,56,128]{2,1,0:T(8,128)S(1)} custom-call(s32[6]{0:T(128)S(1)} %stack.35.flags, f32[80,56,128]{2,1,0:T(8,128)S(1)} %get-tuple-element.75.xn, f32[80,56,128]{2,1,0:T(8,128)S(1)} %get-tuple-element.76.xf, f32[160,128]{1,0:T(8,128)S(1)} %bitcast.40, f32[160,128]{1,0:T(8,128)S(1)} %bitcast.45, f32[56,192]{1,0:T(8,128)S(1)} %copy-done.6, ...), custom_call_target="tpu_custom_call" | custom-call | bytes 1000 | tf_op jit(solution)/shard_map/near_base/pallas_call | solution.py:49
  18.7 0.0 copy-done.1
  18.7 0.0 copy-done.2
  18.7 1.6 %transfer.1 = (f32[2,80,16,128]{3,2,1,0:T(8,128)S(1)}, f32[30,8,128]{2,1,0:T(8,128)S(1)}) custom-call(s32[6]{0:T(128)S(1)} %stack.35.flags, f32[800,128]{1,0:T(8,128)S(1)} %bitcast.28, f32[800,128]{1,0:T(8,128)S(1)} %bitcast.32), custom_call_target="tpu_custom_call" | custom-call | bytes 1000 | tf_op jit(solution)/shard_map/transfer/pallas_call | solution.py:49
  20.3 0.0 copy-done.9
  20.3 0.1 reshape.36
  20.4 0.0 collective-permute-done.slab
  20.4 1.2 %far_lead.1.lead = f32[20,56,128]{2,1,0:T(8,128)S(1)} custom-call(s32[6]{0:T(128)S(1)} %stack.35.flags, f32[980,128]{1,0:T(8,128)S(1)} %collective-permute-done.slab, f32[56,128]{1,0:T(8,128)S(1)} %get-tuple-element.79.trig, f32[56,56]{1,0:T(8,128)S(1)} %copy-done.7, f32[64,192]{1,0:T(8,128)S(1)} %copy-done.5), custom_call_target="tpu_custom_call" | custom-call | bytes 1000 | tf_op jit(solution)/shard_map/far_lead/pallas_call | solution.py:49
  21.6 0.0 collective-permute-done.2.from_left
  21.6 0.0 collective-permute-done.3.from_right
  21.6 0.0 collective-permute-done.1.halo
  21.7 3.7 %near_cell.1 = (f32[80,56,128]{2,1,0:T(8,128)S(1)}, f32[100,8,128]{2,1,0:T(8,128)S(1)}) custom-call(s32[6]{0:T(128)S(1)} %stack.35.flags, f32[80,56,128]{2,1,0:T(8,128)S(1)} %near_base.1.base, f32[80,56,128]{2,1,0:T(8,128)S(1)} %collective-permute-done.1.halo, f32[496,128]{1,0:T(8,128)S(1)} %collective-permute-done.2.from_left, ...), custom_call_target="tpu_custom_call" | custom-call | flops 6000000000 | bytes 1000 | tf_op jit(solution)/shard_map/near_cell/pallas_call | solution.py:49
  25.3 2.7 %collective-permute-start.4 = (f32[100,8,128]{2,1,0:T(8,128)S(1)}, f32[100,8,128]{2,1,0:T(8,128)S(1)}, u32[]{:S(2)}, u32[]{:S(2)}) collective-permute-start(f32[100,8,128]{2,1,0:T(8,128)S(1)} %get-tuple-element.93.flows), channel_id=1, source_target_pairs={{0,4},{4,0},{8,12},{12,8},{16,20},{20,16},{24,28},{28,24},{1,5},{5... | collective-permute-start | bytes 1228808 | tf_op jit(solution)/shard_map/ppermute | solution.py:612
  28.0 1.4 %collective-permute-start.8 = (f32[960,128]{1,0:T(8,128)S(1)}, f32[960,128]{1,0:T(8,128)S(1)}, u32[]{:S(2)}, u32[]{:S(2)}) collective-permute-start(f32[960,128]{1,0:T(8,128)S(1)} %get-tuple-element.110), channel_id=1, source_target_pairs={{0,3},{1,2},{2,1},{3,0},{4,7},{5,6},{6,5},{7,4},{8,11},{9,10},{10,... | collective-permute-start | bytes 1474568 | tf_op jit(solution)/shard_map/ppermute | solution.py:611
  29.5 8.8 %collective-permute-done.4.other = f32[100,8,128]{2,1,0:T(8,128)S(1)} collective-permute-done((f32[100,8,128]{2,1,0:T(8,128)S(1)}, f32[100,8,128]{2,1,0:T(8,128)S(1)}, u32[]{:S(2)}, u32[]{:S(2)}) %collective-permute-start.4) | collective-permute-done | bytes 409632 | tf_op jit(solution)/shard_map/ppermute | solution.py:612
  38.2 1.0 %merge_all.2 = (f32[2,30,8,128]{3,2,1,0:T(8,128)S(1)}, f32[100,8,128]{2,1,0:T(8,128)S(1)}, f32[2,15,8,128]{3,2,1,0:T(8,128)S(1)}, f32[70,8,128]{2,1,0:T(8,128)S(1)}) custom-call(s32[6]{0:T(128)S(1)} %stack.35.flags, f32[100,8,128]{2,1,0:T(8,128)S(1)} %get-tuple-element.93.flows, f32[100,8,128]{2,1,0:T(8,128)S(1)} %collective-permute-done.4.other), custom_call_target="tpu_custom_call" | custom-call | flops 1000 | bytes 1000 | tf_op jit(solution)/shard_map/merge_all/pallas_call | solution.py:49
  39.3 2.8 %collective-permute-start.7 = (f32[100,8,128]{2,1,0:T(8,128)S(1)}, f32[100,8,128]{2,1,0:T(8,128)S(1)}, u32[]{:S(2)}, u32[]{:S(2)}) collective-permute-start(f32[100,8,128]{2,1,0:T(8,128)S(1)} %get-tuple-element.105.flows), channel_id=1, source_target_pairs={{0,8},{4,12},{8,0},{12,4},{16,24},{20,28},{24,16},{28,20},{1,9},{5... | collective-permute-start | bytes 1228808 | tf_op jit(solution)/shard_map/ppermute | solution.py:612
  42.1 0.0 collective-permute-done.5.halo
  42.1 2.8 %far_chunk.2 = (f32[80,40,128]{2,1,0:T(8,128)S(1)}, f32[50,8,128]{2,1,0:T(8,128)S(1)}) custom-call(s32[6]{0:T(128)S(1)} %stack.35.flags, f32[80,56,128]{2,1,0:T(8,128)S(1)} %get-tuple-element.96.base, f32[20,56,128]{2,1,0:T(8,128)S(1)} %far_lead.1.lead, f32[1984,128]{1,0:T(8,128)S(1)} %collective-permute-done.5.halo, ...), custom_call_target="tpu_custom_call" | custom-call | flops 1000 | bytes 1000 | tf_op jit(solution)/shard_map/far_chunk/pallas_call | solution.py:49
  44.8 0.7 collective-permute-start.6
  45.5 5.9 %collective-permute-done.6.other = f32[50,8,128]{2,1,0:T(8,128)S(1)} collective-permute-done((f32[50,8,128]{2,1,0:T(8,128)S(1)}, f32[50,8,128]{2,1,0:T(8,128)S(1)}, u32[]{:S(2)}, u32[]{:S(2)}) %collective-permute-start.6) | collective-permute-done | bytes 204832 | tf_op jit(solution)/shard_map/ppermute | solution.py:612
  51.4 0.8 %merge_flows.4 = (f32[50,8,128]{2,1,0:T(8,128)S(1)}, f32[50,8,128]{2,1,0:T(8,128)S(1)}) custom-call(s32[6]{0:T(128)S(1)} %stack.35.flags, f32[2,30,8,128]{3,2,1,0:T(8,128)S(1)} %get-tuple-element.101.mats, f32[50,8,128]{2,1,0:T(8,128)S(1)} %get-tuple-element.102.flows, f32[50,8,128]{2,1,0:T(8,128)S(1)} %collective-permute-done.6.other), custom_call_target="tpu_custom_call" | custom-call | flops 1000 | bytes 1000 | tf_op jit(solution)/shard_map/merge_flows/pallas_call | solution.py:49
  52.2 1.4 %collective-permute-start.9 = (f32[50,8,128]{2,1,0:T(8,128)S(1)}, f32[50,8,128]{2,1,0:T(8,128)S(1)}, u32[]{:S(2)}, u32[]{:S(2)}) collective-permute-start(f32[50,8,128]{2,1,0:T(8,128)S(1)} %get-tuple-element.114.flows), channel_id=1, source_target_pairs={{0,8},{4,12},{8,0},{12,4},{16,24},{20,28},{24,16},{28,20},{1,9},{5... | collective-permute-start | bytes 614408 | tf_op jit(solution)/shard_map/ppermute | solution.py:612
  53.6 0.0 collective-permute-done.7.other
  53.6 1.0 %merge_all.3 = (f32[2,30,8,128]{3,2,1,0:T(8,128)S(1)}, f32[45,8,128]{2,1,0:T(8,128)S(1)}, f32[2,15,8,128]{3,2,1,0:T(8,128)S(1)}, f32[70,8,128]{2,1,0:T(8,128)S(1)}) custom-call(s32[6]{0:T(128)S(1)} %stack.35.flags, f32[100,8,128]{2,1,0:T(8,128)S(1)} %get-tuple-element.105.flows, f32[100,8,128]{2,1,0:T(8,128)S(1)} %collective-permute-done.7.other, ...), custom_call_target="tpu_custom_call" | custom-call | flops 1000 | bytes 1000 | tf_op jit(solution)/shard_map/merge_all/pallas_call | solution.py:49
  54.6 2.7 %collective-permute-start.11 = (f32[45,8,128]{2,1,0:T(8,128)S(1)}, f32[45,8,128]{2,1,0:T(8,128)S(1)}, u32[]{:S(2)}, u32[]{:S(2)}) collective-permute-start(f32[45,8,128]{2,1,0:T(8,128)S(1)} %get-tuple-element.121.ends), channel_id=1, source_target_pairs={{0,16},{4,20},{8,24},{12,28},{16,0},{20,4},{24,8},{28,12},{1,17},{... | collective-permute-start | bytes 552968 | tf_op jit(solution)/shard_map/ppermute | solution.py:612
  57.3 0.0 collective-permute-done.8.halo
  57.3 1.6 %far_chunk.3 = (f32[80,16,128]{2,1,0:T(8,128)S(1)}, f32[20,8,128]{2,1,0:T(8,128)S(1)}) custom-call(s32[6]{0:T(128)S(1)} %stack.35.flags, f32[80,56,128]{2,1,0:T(8,128)S(1)} %get-tuple-element.96.base, f32[20,56,128]{2,1,0:T(8,128)S(1)} %far_lead.1.lead, f32[960,128]{1,0:T(8,128)S(1)} %collective-permute-done.8.halo, ...), custom_call_target="tpu_custom_call" | custom-call | flops 1000 | bytes 1000 | tf_op jit(solution)/shard_map/far_chunk/pallas_call | solution.py:49
  58.9 0.7 collective-permute-start.10
  59.5 0.9 %collective-permute-done.9.other = f32[50,8,128]{2,1,0:T(8,128)S(1)} collective-permute-done((f32[50,8,128]{2,1,0:T(8,128)S(1)}, f32[50,8,128]{2,1,0:T(8,128)S(1)}, u32[]{:S(2)}, u32[]{:S(2)}) %collective-permute-start.9) | collective-permute-done | bytes 204832 | tf_op jit(solution)/shard_map/ppermute | solution.py:612
  60.5 0.8 %merge_flows.5 = (f32[25,8,128]{2,1,0:T(8,128)S(1)}, f32[50,8,128]{2,1,0:T(8,128)S(1)}) custom-call(s32[6]{0:T(128)S(1)} %stack.35.flags, f32[2,30,8,128]{3,2,1,0:T(8,128)S(1)} %get-tuple-element.113.mats, f32[50,8,128]{2,1,0:T(8,128)S(1)} %get-tuple-element.114.flows, f32[50,8,128]{2,1,0:T(8,128)S(1)} %collective-permute-done.9.other, ...), custom_call_target="tpu_custom_call" | custom-call | flops 1000 | bytes 1000 | tf_op jit(solution)/shard_map/merge_flows/pallas_call | solution.py:49
  61.3 2.1 %collective-permute-done.10.other = f32[20,8,128]{2,1,0:T(8,128)S(1)} collective-permute-done((f32[20,8,128]{2,1,0:T(8,128)S(1)}, f32[20,8,128]{2,1,0:T(8,128)S(1)}, u32[]{:S(2)}, u32[]{:S(2)}) %collective-permute-start.10) | collective-permute-done | bytes 81952 | tf_op jit(solution)/shard_map/ppermute | solution.py:612
  63.4 0.6 merge_flows.6
  64.0 0.8 collective-permute-start.12
  64.8 0.8 collective-permute-start.13
  65.5 0.0 collective-permute-done.11.other
  65.5 2.6 %correct_all.1 = (f32[80,56,128]{2,1,0:T(8,128)S(1)}, f32[2,30,8,128]{3,2,1,0:T(8,128)S(1)}) custom-call(s32[6]{0:T(128)S(1)} %stack.35.flags, f32[45,8,128]{2,1,0:T(8,128)S(1)} %get-tuple-element.121.ends, f32[45,8,128]{2,1,0:T(8,128)S(1)} %collective-permute-done.11.other, f32[2,15,8,128]{3,2,1,0:T(8,128)S(1)} %get-tuple-element.122.share, ...), custom_call_target="tpu_custom_call" | custom-call | flops 1000 | bytes 1000 | tf_op jit(solution)/shard_map/correct_all/pallas_call | solution.py:49
  68.2 0.3 collective-permute-done.12.other
  68.5 0.7 merge_flows.7
  69.2 1.9 %collective-permute-start.14 = (f32[10,8,128]{2,1,0:T(8,128)S(1)}, f32[10,8,128]{2,1,0:T(8,128)S(1)}, u32[]{:S(2)}, u32[]{:S(2)}) collective-permute-start(f32[10,8,128]{2,1,0:T(8,128)S(1)} %get-tuple-element.137.ends), channel_id=1, source_target_pairs={{0,16},{4,20},{8,24},{12,28},{16,0},{20,4},{24,8},{28,12},{1,17},{... | collective-permute-start | bytes 122888 | tf_op jit(solution)/shard_map/ppermute | solution.py:612
  71.1 1.2 %collective-permute-done.13.other = f32[25,8,128]{2,1,0:T(8,128)S(1)} collective-permute-done((f32[25,8,128]{2,1,0:T(8,128)S(1)}, f32[25,8,128]{2,1,0:T(8,128)S(1)}, u32[]{:S(2)}, u32[]{:S(2)}) %collective-permute-start.13) | collective-permute-done | bytes 102432 | tf_op jit(solution)/shard_map/ppermute | solution.py:612
  72.3 2.1 %correct.1.refs_0_ = f32[80,40,128]{2,1,0:T(8,128)S(1)} custom-call(s32[6]{0:T(128)S(1)} %stack.35.flags, f32[2,30,8,128]{3,2,1,0:T(8,128)S(1)} %get-tuple-element.132.mats, f32[25,8,128]{2,1,0:T(8,128)S(1)} %get-tuple-element.133.ends, f32[25,8,128]{2,1,0:T(8,128)S(1)} %collective-permute-done.13.other, f32[50,8,128]{2,1,0:T(8,128)S(1)} %get-tuple-element.134.known, ...), custom_call_target="tpu_custom_call" | custom-call | flops 1000 | bytes 1000 | tf_op jit(solution)/shard_map/correct/pallas_call | solution.py:49
  74.4 0.0 collective-permute-done.14.other
  74.4 2.8 %finish.1 = f32[7840,128]{1,0:T(8,128)} custom-call(s32[6]{0:T(128)S(1)} %stack.35.flags, f32[2,30,8,128]{3,2,1,0:T(8,128)S(1)} %get-tuple-element.132.mats, f32[10,8,128]{2,1,0:T(8,128)S(1)} %get-tuple-element.137.ends, f32[10,8,128]{2,1,0:T(8,128)S(1)} %collective-permute-done.14.other, f32[20,8,128]{2,1,0:T(8,128)S(1)} %get-tuple-element.138.known, ...), custom_call_target="tpu_custom_call" | custom-call | flops 1000 | bytes 1000 | tf_op jit(solution)/shard_map/finish/pallas_call | solution.py:49
  (9 shorter events, 0.0 us)
Async XLA Ops:
  0.0 10.7 %copy-start.5 = (f32[64,192]{1,0:T(8,128)S(1)}, f32[64,192]{1,0:T(8,128)}, u32[]{:S(2)}) copy-start(f32[64,192]{1,0:T(8,128)} %constant.33.clone.turned) | copy-start | bytes 147460
  0.0 10.6 %copy-start.10 = (s32[24]{0:T(128)S(1)}, s32[24]{0:T(128)}, u32[]{:S(2)}) copy-start(s32[24]{0:T(128)} %param.18) | copy-start | bytes 292
  0.0 10.7 %copy-start.8 = (s32[2]{0:T(128)S(1)}, s32[2]{0:T(128)}, u32[]{:S(2)}) copy-start(s32[2]{0:T(128)} %blades.1) | copy-start | bytes 28
  0.1 2.1 %copy-start = (f32[16,2,5,49,128]{4,1,3,2,0:T(2,128)S(1)}, f32[16,2,5,49,128]{4,1,3,2,0:T(2,128)}, u32[]{:S(2)}) copy-start(f32[16,2,5,49,128]{4,1,3,2,0:T(2,128)} %param.11) | copy-start | bytes 12042244
  2.2 8.5 %copy-start.3 = (f32[16,2,5,128]{3,1,2,0:T(2,128)S(1)}, f32[16,2,5,128]{3,1,2,0:T(2,128)}, u32[]{:S(2)}) copy-start(f32[16,2,5,128]{3,1,2,0:T(2,128)} %param.12) | copy-start | bytes 245764
  2.2 8.5 %copy-start.4 = (f32[16,2,5,128]{3,1,2,0:T(2,128)S(1)}, f32[16,2,5,128]{3,1,2,0:T(2,128)}, u32[]{:S(2)}) copy-start(f32[16,2,5,128]{3,1,2,0:T(2,128)} %param.13) | copy-start | bytes 245764
  2.2 8.5 %copy-start.6 = (f32[56,192]{1,0:T(8,128)S(1)}, f32[56,192]{1,0:T(8,128)}, u32[]{:S(2)}) copy-start(f32[56,192]{1,0:T(8,128)} %constant.34.clone.table) | copy-start | bytes 129028
  2.2 8.5 %copy-start.7 = (f32[56,56]{1,0:T(8,128)S(1)}, f32[56,56]{1,0:T(8,128)}, u32[]{:S(2)}) copy-start(f32[56,56]{1,0:T(8,128)} %constant.32.clone.basis) | copy-start | bytes 37636
  2.8 18.9 %collective-permute-start.1 = (f32[80,56,128]{2,1,0:T(8,128)S(1)}, f32[80,56,128]{2,1,0:T(8,128)S(1)}, u32[]{:S(2)}, u32[]{:S(2)}) collective-permute-start(f32[80,56,128]{2,1,0:T(8,128)S(1)} %get-tuple-element.75.xn), channel_id=1, source_target_pairs={{0,1},{1,0},{2,3},{3,2},{4,5},{5,4},{6,7},{7,6},{8,9},{9,8},{10,11... | collective-permute-start | bytes 6881288 | tf_op jit(solution)/shard_map/ppermute | solution.py:638
  3.3 17.1 %collective-permute-start = (f32[980,128]{1,0:T(8,128)S(1)}, f32[980,128]{1,0:T(8,128)S(1)}, u32[]{:S(2)}, u32[]{:S(2)}) collective-permute-start(f32[980,128]{1,0:T(8,128)S(1)} %get-tuple-element.84), channel_id=1, source_target_pairs={{0,3},{1,2},{2,1},{3,0},{4,7},{5,6},{6,5},{7,4},{8,11},{9,10},{10,... | collective-permute-start | bytes 1505288 | tf_op jit(solution)/shard_map/ppermute | solution.py:611
  5.9 15.7 %collective-permute-start.2 = (f32[496,128]{1,0:T(8,128)S(1)}, f32[496,128]{1,0:T(8,128)S(1)}, u32[]{:S(2)}, u32[]{:S(2)}) collective-permute-start(f32[496,128]{1,0:T(8,128)S(1)} %get-tuple-element.88), channel_id=1, source_target_pairs={{0,4},{4,8},{8,12},{12,16},{16,20},{20,24},{24,28},{1,5},{5,9},{9,... | collective-permute-start | bytes 761864 | tf_op jit(solution)/shard_map/ppermute | solution.py:640
  9.3 12.3 %collective-permute-start.3 = (f32[496,128]{1,0:T(8,128)S(1)}, f32[496,128]{1,0:T(8,128)S(1)}, u32[]{:S(2)}, u32[]{:S(2)}) collective-permute-start(f32[496,128]{1,0:T(8,128)S(1)} %get-tuple-element.89), channel_id=1, source_target_pairs={{4,0},{8,4},{12,8},{16,12},{20,16},{24,20},{28,24},{5,1},{9,5},{13... | collective-permute-start | bytes 761864 | tf_op jit(solution)/shard_map/ppermute | solution.py:641
  15.0 27.1 %collective-permute-start.5 = (f32[1984,128]{1,0:T(8,128)S(1)}, f32[1984,128]{1,0:T(8,128)S(1)}, u32[]{:S(2)}, u32[]{:S(2)}) collective-permute-start(f32[1984,128]{1,0:T(8,128)S(1)} %get-tuple-element.98), channel_id=1, source_target_pairs={{0,3},{1,2},{2,1},{3,0},{4,7},{5,6},{6,5},{7,4},{8,11},{9,10},{10,... | collective-permute-start | bytes 3047432 | tf_op jit(solution)/shard_map/ppermute | solution.py:611
  15.1 3.6 %copy-start.1 = (f32[16,2,5,5,128]{4,1,3,2,0:T(2,128)S(1)}, f32[16,2,5,5,128]{4,1,3,2,0:T(2,128)}, u32[]{:S(2)}) copy-start(f32[16,2,5,5,128]{4,1,3,2,0:T(2,128)} %param.15) | copy-start | bytes 1228804
  15.1 3.6 %copy-start.2 = (f32[16,2,5,5,128]{4,1,3,2,0:T(2,128)S(1)}, f32[16,2,5,5,128]{4,1,3,2,0:T(2,128)}, u32[]{:S(2)}) copy-start(f32[16,2,5,5,128]{4,1,3,2,0:T(2,128)} %param.16) | copy-start | bytes 1228804
  15.1 5.2 %copy-start.9 = (bf16[16,2,5,5,128]{4,1,3,2,0:T(2,128)(2,1)S(1)}, bf16[16,2,5,5,128]{4,1,3,2,0:T(2,128)(2,1)}, u32[]{:S(2)}) copy-start(bf16[16,2,5,5,128]{4,1,3,2,0:T(2,128)(2,1)} %param.14) | copy-start | bytes 614404
  25.3 12.9 %collective-permute-start.4 = (f32[100,8,128]{2,1,0:T(8,128)S(1)}, f32[100,8,128]{2,1,0:T(8,128)S(1)}, u32[]{:S(2)}, u32[]{:S(2)}) collective-permute-start(f32[100,8,128]{2,1,0:T(8,128)S(1)} %get-tuple-element.93.flows), channel_id=1, source_target_pairs={{0,4},{4,0},{8,12},{12,8},{16,20},{20,16},{24,28},{28,24},{1,5},{5... | collective-permute-start | bytes 1228808 | tf_op jit(solution)/shard_map/ppermute | solution.py:612
  28.0 29.3 %collective-permute-start.8 = (f32[960,128]{1,0:T(8,128)S(1)}, f32[960,128]{1,0:T(8,128)S(1)}, u32[]{:S(2)}, u32[]{:S(2)}) collective-permute-start(f32[960,128]{1,0:T(8,128)S(1)} %get-tuple-element.110), channel_id=1, source_target_pairs={{0,3},{1,2},{2,1},{3,0},{4,7},{5,6},{6,5},{7,4},{8,11},{9,10},{10,... | collective-permute-start | bytes 1474568 | tf_op jit(solution)/shard_map/ppermute | solution.py:611
  39.3 14.3 %collective-permute-start.7 = (f32[100,8,128]{2,1,0:T(8,128)S(1)}, f32[100,8,128]{2,1,0:T(8,128)S(1)}, u32[]{:S(2)}, u32[]{:S(2)}) collective-permute-start(f32[100,8,128]{2,1,0:T(8,128)S(1)} %get-tuple-element.105.flows), channel_id=1, source_target_pairs={{0,8},{4,12},{8,0},{12,4},{16,24},{20,28},{24,16},{28,20},{1,9},{5... | collective-permute-start | bytes 1228808 | tf_op jit(solution)/shard_map/ppermute | solution.py:612
  44.8 6.6 %collective-permute-start.6 = (f32[50,8,128]{2,1,0:T(8,128)S(1)}, f32[50,8,128]{2,1,0:T(8,128)S(1)}, u32[]{:S(2)}, u32[]{:S(2)}) collective-permute-start(f32[50,8,128]{2,1,0:T(8,128)S(1)} %get-tuple-element.102.flows), channel_id=1, source_target_pairs={{0,4},{4,0},{8,12},{12,8},{16,20},{20,16},{24,28},{28,24},{1,5},{5... | collective-permute-start | bytes 614408 | tf_op jit(solution)/shard_map/ppermute | solution.py:612
  52.2 8.3 %collective-permute-start.9 = (f32[50,8,128]{2,1,0:T(8,128)S(1)}, f32[50,8,128]{2,1,0:T(8,128)S(1)}, u32[]{:S(2)}, u32[]{:S(2)}) collective-permute-start(f32[50,8,128]{2,1,0:T(8,128)S(1)} %get-tuple-element.114.flows), channel_id=1, source_target_pairs={{0,8},{4,12},{8,0},{12,4},{16,24},{20,28},{24,16},{28,20},{1,9},{5... | collective-permute-start | bytes 614408 | tf_op jit(solution)/shard_map/ppermute | solution.py:612
  54.6 10.9 %collective-permute-start.11 = (f32[45,8,128]{2,1,0:T(8,128)S(1)}, f32[45,8,128]{2,1,0:T(8,128)S(1)}, u32[]{:S(2)}, u32[]{:S(2)}) collective-permute-start(f32[45,8,128]{2,1,0:T(8,128)S(1)} %get-tuple-element.121.ends), channel_id=1, source_target_pairs={{0,16},{4,20},{8,24},{12,28},{16,0},{20,4},{24,8},{28,12},{1,17},{... | collective-permute-start | bytes 552968 | tf_op jit(solution)/shard_map/ppermute | solution.py:612
  58.9 4.5 %collective-permute-start.10 = (f32[20,8,128]{2,1,0:T(8,128)S(1)}, f32[20,8,128]{2,1,0:T(8,128)S(1)}, u32[]{:S(2)}, u32[]{:S(2)}) collective-permute-start(f32[20,8,128]{2,1,0:T(8,128)S(1)} %get-tuple-element.118.flows), channel_id=1, source_target_pairs={{0,4},{4,0},{8,12},{12,8},{16,20},{20,16},{24,28},{28,24},{1,5},{5... | collective-permute-start | bytes 245768 | tf_op jit(solution)/shard_map/ppermute | solution.py:612
  64.0 4.5 %collective-permute-start.12 = (f32[20,8,128]{2,1,0:T(8,128)S(1)}, f32[20,8,128]{2,1,0:T(8,128)S(1)}, u32[]{:S(2)}, u32[]{:S(2)}) collective-permute-start(f32[20,8,128]{2,1,0:T(8,128)S(1)} %get-tuple-element.128.flows), channel_id=1, source_target_pairs={{0,8},{4,12},{8,0},{12,4},{16,24},{20,28},{24,16},{28,20},{1,9},{5... | collective-permute-start | bytes 245768 | tf_op jit(solution)/shard_map/ppermute | solution.py:612
  64.8 7.5 %collective-permute-start.13 = (f32[25,8,128]{2,1,0:T(8,128)S(1)}, f32[25,8,128]{2,1,0:T(8,128)S(1)}, u32[]{:S(2)}, u32[]{:S(2)}) collective-permute-start(f32[25,8,128]{2,1,0:T(8,128)S(1)} %get-tuple-element.133.ends), channel_id=1, source_target_pairs={{0,16},{4,20},{8,24},{12,28},{16,0},{20,4},{24,8},{28,12},{1,17},{... | collective-permute-start | bytes 307208 | tf_op jit(solution)/shard_map/ppermute | solution.py:612
  69.2 5.3 %collective-permute-start.14 = (f32[10,8,128]{2,1,0:T(8,128)S(1)}, f32[10,8,128]{2,1,0:T(8,128)S(1)}, u32[]{:S(2)}, u32[]{:S(2)}) collective-permute-start(f32[10,8,128]{2,1,0:T(8,128)S(1)} %get-tuple-element.137.ends), channel_id=1, source_target_pairs={{0,16},{4,20},{8,24},{12,28},{16,0},{20,4},{24,8},{28,12},{1,17},{... | collective-permute-start | bytes 122888 | tf_op jit(solution)/shard_map/ppermute | solution.py:612

commit v8 on v7

--- a/solution.py
+++ b/solution.py
@@ -208,14 +208,35 @@
     one(cells - 1, below=False)
 
 
-def keep_tiles(ref, offset, values, first, last, height):
+def split_height(rows_high, extra):
+    return rows_high // 8 - (1 if extra else 0)
+
+
+def packed_rows(count, height, extra):
+    return count * height * 8 + (padded_even(count) if extra else 0)
+
+
+def vector_rows(count, i, t, height):
+    if isinstance(t, int) and t == height:
+        return pl.ds(count * height * 8 + i, 1)
+    return pl.ds(pl.multiple_of((i * height + t) * 8, 8), 8)
+
+
+def over_tiles(height, extra, tile):
+    lax.fori_loop(0, height, lambda t, carry: (tile(t), carry)[1], 0)
+    if extra:
+        tile(height)
+
+
+def keep_tiles(ref, kind, values, first, last, height, extra):
     for a in range(V):
         for t in range(first // 8, last // 8):
-            ref[offset + a * height + t] = values[a][t * 8 - first : t * 8 - first + 8]
-
-
-def sweeps(source, g, fg, offset, spans, p, inverse, lower, upper, cells):
-    height = g.shape[1] // 8
+            place = vector_rows(2 * V, kind + a, t, height)
+            ref[place, :] = values[a][t * 8 - first : t * 8 - first + (1 if t == height else 8)]
+
+
+def sweeps(source, g, fg, extra, spans, p, inverse, lower, upper, cells):
+    height = split_height(g.shape[1], extra)
     for first, last in spans:
         nothing = tuple(jnp.zeros((last - first, LANES), F32) for _ in range(V))
 
@@ -234,7 +255,7 @@
 
         out = lax.fori_loop(1, cells - 1, ahead, ahead(0, nothing))
         out = ahead(cells - 1, out)
-        keep_tiles(fg, offset, out, first, last, height)
+        keep_tiles(fg, 0, out, first, last, height, extra)
 
         def back(i, current, first=first, last=last):
             z = cells - 1 - i
@@ -248,7 +269,7 @@
             return tuple(result)
 
         out = lax.fori_loop(0, cells, back, nothing)
-        keep_tiles(fg, offset + V * height, out, first, last, height)
+        keep_tiles(fg, V, out, first, last, height, extra)
 
 
 def take_edges(edges, from_left, from_right, p):
@@ -287,8 +308,8 @@
             values.append(base[j, first:last, :] + viscous[pl.ds(j * 2 + p, 1), :] * halo[j, first:last, :])
         return edge_terms(z, cells, values, edges, advect, p, first, last)
 
-    sweeps(source, g, flows, 0, ((0, 32), (32, PAD)), p, inverse, lower, upper, cells)
-    flows[2 * V * PAD // 8 :] = group[...]
+    sweeps(source, g, flows, True, ((0, 32), (32, PAD)), p, inverse, lower, upper, cells)
+    flows[flows.shape[0] - group.shape[0] :, :] = group[...]
 
 
 def far_lead(flags, slab, trig, basis, turned, lead, halo):
@@ -337,7 +358,7 @@
         return result
 
     height = rows_of(chunk)
-    sweeps(source, g, fg, 0, ((0, height),), p, inverse, lower, upper, cells)
+    sweeps(source, g, fg, extra, ((0, height),), p, inverse, lower, upper, cells)
 
 
 def times(matrix, vector):
@@ -355,7 +376,7 @@
 
 
 def tiles(ref, c, kind):
-    return [ref[c, kind * V + a] for a in range(V)]
+    return [ref[c, kind * V + a, 0:V, :] for a in range(V)]
 
 
 def rows(ref, c, kind):
@@ -395,22 +416,23 @@
         )
         ends = lax.fori_loop(0, cells, back, start)
         for a in range(V):
-            group[c * 3 * V + a] = ends[a][:8]
-            group[(c * 3 + 1) * V + a] = ends[a][8:]
-            group[(c * 3 + 2) * V + a] = through[a]
+            for kind, value in enumerate((ends[a][:V], ends[a][8 : 8 + V], through[a][:V])):
+                group[pl.ds(((c * 3 + kind) * V + a) * V, V), :] = value
+    group[6 * V * V :, :] = jnp.zeros((group.shape[0] - 6 * V * V, LANES), F32)
 
 
 def merge_matrices(bit, levels, flags, mine, other, share, mats, merged, share_out, offset, new_offset):
     start, last = bit == 0, bit == levels - 1
     right = flags[3 + bit] == 1
     left = jnp.logical_not(right)
-    nothing = jnp.zeros((8, LANES), F32)
+    nothing = jnp.zeros((V, LANES), F32)
+    one = [unit(a)[:V] for a in range(V)]
     for c in range(2):
         kinds = 1 if last else 3
-        at = lambda ref, kind: [ref[offset + (c * kinds + kind) * V + a] for a in range(V)]
+        at = lambda ref, kind: [ref[pl.ds(offset + ((c * kinds + kind) * V + a) * V, V), :] for a in range(V)]
         pick = lambda kind, own: [jnp.where(own, m, t) for m, t in zip(at(mine, kind), at(other, kind))]
         if start:
-            own = [[unit(a) for a in range(V)], [nothing] * V, [unit(a) for a in range(V)]]
+            own = [one, [nothing] * V, one]
         else:
             own = [tiles(share, c, kind) for kind in range(3)]
         found = [
@@ -423,7 +445,7 @@
             found += [(0, pick(2, right)), (2, pick(1, left))]
         for kind, values in found:
             for a in range(V):
-                mats[c, kind * V + a] = values[a]
+                mats[c, kind * V + a, 0:V, :] = values[a]
         if last:
             continue
         p_left, g_left, h_right = pick(2, left), pick(0, left), pick(1, right)
@@ -433,15 +455,15 @@
             new += [times(rows(mats, c, 2), h_right), times(rows(mats, c, 0), p_left)]
         for kind, values in enumerate(new):
             for a in range(V):
-                merged[new_offset + (c * len(new) + kind) * V + a] = values[a]
+                merged[pl.ds(new_offset + ((c * len(new) + kind) * V + a) * V, V), :] = values[a]
         s0 = times(rows(mats, c, 3), p_left)
         s1 = times(rows(mats, c, 4), p_left)
         s1b = times(rows(mats, c, 5), turned)
         s2 = times(rows(mats, c, 5), h_right)
         for a in range(V):
-            share_out[c, a] = jnp.where(right, s0[a], own[0][a])
-            share_out[c, V + a] = jnp.where(right, s1[a], own[1][a] + s1b[a])
-            share_out[c, 2 * V + a] = jnp.where(right, own[2][a], s2[a])
+            share_out[c, a, 0:V, :] = jnp.where(right, s0[a], own[0][a])
+            share_out[c, V + a, 0:V, :] = jnp.where(right, s1[a], own[1][a] + s1b[a])
+            share_out[c, 2 * V + a, 0:V, :] = jnp.where(right, own[2][a], s2[a])
 
 
 def inflow_of(c, mats, f_left, g_right, known):
@@ -452,58 +474,58 @@
     return back, total if known is None else plus(known, total)
 
 
-def merge_all(parts, bit, levels, flags, flows, other, *refs):
+def merge_all(part, bit, levels, flags, flows, other, *refs):
     share, known, mats, merged, share_out, inflow = (None, None, *refs) if bit == 0 else refs
-    tall = sum(height for _, height in parts) * V
-    new_offset = tall * (1 if bit == levels - 2 else 2)
-    merge_matrices(bit, levels, flags, flows, other, share, mats, merged, share_out, 2 * tall, new_offset)
-    merge_flows(parts, bit, levels, flags, mats, flows, other, *([] if known is None else [known]), merged, inflow)
-
-
-def merge_flows(parts, bit, levels, flags, mats, flows, other, *refs):
+    _, height, extra = part
+    offset = packed_rows(2 * V, height, extra)
+    new_offset = packed_rows(V, height, extra) if bit == levels - 2 else offset
+    merge_matrices(bit, levels, flags, flows, other, share, mats, merged, share_out, offset, new_offset)
+    merge_flows(part, bit, levels, flags, mats, flows, other, *([] if known is None else [known]), merged, inflow)
+
+
+def merge_flows(part, bit, levels, flags, mats, flows, other, *refs):
     known, merged, inflow = (None, *refs) if bit == 0 else refs
     right, last_right = flags[3 + bit] == 1, flags[2 + levels] == 1
     last = bit == levels - 2
-    start = 0
-    for c, height in parts:
-
-        def tile(t, carry, c=c, height=height, start=start):
-            at = lambda i: start * 2 * V + i * height + t
-            mine = [flows[at(i)] for i in range(2 * V)]
-            theirs = [other[at(i)] for i in range(2 * V)]
-            f_left = [jnp.where(right, y, x) for x, y in zip(mine[:V], theirs[:V])]
-            f_right = [jnp.where(right, x, y) for x, y in zip(mine[:V], theirs[:V])]
-            g_left = [jnp.where(right, y, x) for x, y in zip(mine[V:], theirs[V:])]
-            g_right = [jnp.where(right, x, y) for x, y in zip(mine[V:], theirs[V:])]
-            before = None if known is None else [known[at(i)] for i in range(2 * V)]
-            back, total = inflow_of(c, mats, f_left, g_right, before)
-            new_f = plus(f_right, times(rows(mats, c, 0), f_left))
-            new_g = plus(g_left, times(rows(mats, c, 2), back))
-            if last:
-                for i in range(V):
-                    end = jnp.where(last_right, new_g[i], new_f[i])
-                    merged[start * V + i * height + t] = end
-            else:
-                for i, value in enumerate(new_f + new_g):
-                    merged[at(i)] = value
-            for i, value in enumerate(total):
-                inflow[at(i)] = value
-            return carry
-
-        lax.fori_loop(0, height, tile, 0)
-        start += height
-
-
-def last_inflow(right, c, mats, ends, other, known, start, height, inflow):
-    for t in range(height):
-        mine = [ends[start * V + a * height + t] for a in range(V)]
-        theirs = [other[start * V + a * height + t] for a in range(V)]
+    c, height, extra = part
+
+    def tile(t):
+        at = lambda i: vector_rows(2 * V, i, t, height)
+        mine = [flows[at(i), :] for i in range(2 * V)]
+        theirs = [other[at(i), :] for i in range(2 * V)]
+        f_left = [jnp.where(right, y, x) for x, y in zip(mine[:V], theirs[:V])]
+        f_right = [jnp.where(right, x, y) for x, y in zip(mine[:V], theirs[:V])]
+        g_left = [jnp.where(right, y, x) for x, y in zip(mine[V:], theirs[V:])]
+        g_right = [jnp.where(right, x, y) for x, y in zip(mine[V:], theirs[V:])]
+        before = None if known is None else [known[at(i), :] for i in range(2 * V)]
+        back, total = inflow_of(c, mats, f_left, g_right, before)
+        new_f = plus(f_right, times(rows(mats, c, 0), f_left))
+        new_g = plus(g_left, times(rows(mats, c, 2), back))
+        if last:
+            for i in range(V):
+                end = jnp.where(last_right, new_g[i], new_f[i])
+                merged[vector_rows(V, i, t, height), :] = end
+        else:
+            for i, value in enumerate(new_f + new_g):
+                merged[at(i), :] = value
+        for i, value in enumerate(total):
+            inflow[at(i), :] = value
+
+    over_tiles(height, extra, tile)
+
+
+def last_inflow(right, part, mats, ends, other, known, inflow):
+    c, height, extra = part
+    for t in range(height + (1 if extra else 0)):
+        place = lambda i: vector_rows(V, i, t, height)
+        mine = [ends[place(a), :] for a in range(V)]
+        theirs = [other[place(a), :] for a in range(V)]
         f_left = [jnp.where(right, y, x) for x, y in zip(mine, theirs)]
         g_right = [jnp.where(right, x, y) for x, y in zip(mine, theirs)]
-        before = [known[start * 2 * V + i * height + t] for i in range(2 * V)]
+        before = [known[vector_rows(2 * V, i, t, height), :] for i in range(2 * V)]
         _, total = inflow_of(c, mats, f_left, g_right, before)
         for i, value in enumerate(total):
-            inflow[i, t * 8 : t * 8 + 8, :] = value
+            inflow[i, t * 8 : t * 8 + 8, :] = jnp.broadcast_to(value, (8, LANES))
 
 
 def corrected(c, z, a, first, last, g, blocks, inflow):
@@ -514,31 +536,25 @@
     return total
 
 
-def correct(parts, levels, flags, mats, ends, other, known, blocks, *refs):
-    solved, results, inflow = refs[: len(parts)], refs[len(parts) : -1], refs[-1]
-    right = flags[2 + levels] == 1
-    start = 0
-    for (c, tall), g, result in zip(parts, solved, results):
-        last_inflow(right, c, mats, ends, other, known, start, tall, inflow)
-        start += tall
-        height = tall * 8
-        for first, last in ((0, 32), (32, height)) if height > 32 else ((0, height),):
-            flow = tuple(inflow[i, first:last, :] for i in range(2 * V))
-
-            def step(z, flow, c=c, first=first, last=last, g=g, result=result):
-                for a in range(V):
-                    result[z * V + a, first:last, :] = corrected(c, z, a, first, last, g, blocks, flow)
-                return flow
-
-            lax.fori_loop(0, g.shape[0] // V, step, flow)
-
-
-def correct_all(parts, levels, flags, ends, other, share, known, blocks, *refs):
-    count = len(parts)
-    solved, results, mats, inflow = refs[:count], refs[count : 2 * count], refs[-2], refs[-1]
-    tall = sum(height for _, height in parts) * V
-    merge_matrices(levels - 1, levels, flags, ends, other, share, mats, None, None, tall, 0)
-    correct(parts, levels, flags, mats, ends, other, known, blocks, *solved, *results, inflow)
+def correct(part, levels, flags, mats, ends, other, known, blocks, g, result, inflow):
+    c = part[0]
+    last_inflow(flags[2 + levels] == 1, part, mats, ends, other, known, inflow)
+    height = g.shape[1]
+    for first, last in ((0, 32), (32, height)) if height > 32 else ((0, height),):
+        flow = tuple(inflow[i, first:last, :] for i in range(2 * V))
+
+        def step(z, flow, first=first, last=last):
+            for a in range(V):
+                result[z * V + a, first:last, :] = corrected(c, z, a, first, last, g, blocks, flow)
+            return flow
+
+        lax.fori_loop(0, g.shape[0] // V, step, flow)
+
+
+def correct_all(part, levels, flags, ends, other, share, known, blocks, g, result, mats, inflow):
+    offset = packed_rows(V, *part[1:])
+    merge_matrices(levels - 1, levels, flags, ends, other, share, mats, None, None, offset, 0)
+    correct(part, levels, flags, mats, ends, other, known, blocks, g, result, inflow)
 
 
 def finish(levels, flags, mats, ends, other, known, g, blocks, near, *refs):
@@ -547,7 +563,8 @@
     p = flags[0]
     (first_row, last_row), last_extra = CHUNKS[-1]
     width, height = last_row - first_row, rows_of(CHUNKS[-1])
-    last_inflow(right, 1, mats, ends, other, known, 0, height // 8, inflow)
+    part = (1, split_height(height, last_extra), last_extra)
+    last_inflow(right, part, mats, ends, other, known, inflow)
     flow = tuple(inflow[i] for i in range(2 * V))
 
     def step(z, carry):
@@ -668,55 +685,63 @@
     mats_shape = (2, 6 * V, 8, LANES)
 
     def solve_chunk(i):
-        height = rows_of(CHUNKS[i])
+        height, extra = rows_of(CHUNKS[i]), CHUNKS[i][1]
+        tall = packed_rows(2 * V, split_height(height, extra), extra)
         return run(
             functools.partial(far_chunk, CHUNKS[i]),
-            [(cells * V, height, LANES), (2 * V * height // 8, 8, LANES)],
+            [(cells * V, height, LANES), (tall, LANES)],
             [base, lead, arrived[i], from_left, from_right, adv, vis, inv, low, upp],
             scratch=[edges], name="far_chunk",
         )
 
     class Exchange:
-        def __init__(self, c, g, flows, leads=False):
-            self.parts, self.leads = [(c, g.shape[1] // 8)], leads
+        def __init__(self, c, extra, g, flows, leads=False):
+            self.part, self.leads = (c, split_height(g.shape[1], extra), extra), leads
             self.flows, self.known, self.solved, self.level = flows, [], g, 0
             self.scratch = [pltpu.VMEM((2 * V, g.shape[1], LANES), F32)]
 
         def step(self):
-            tall, k = self.parts[0][1], self.level
-            shape = ((2 if k < levels - 2 else 1) * V * tall, 8, LANES)
-            inflow = (2 * V * tall, 8, LANES)
+            k = self.level
+            behind = k == levels - 2
+            inflow = (packed_rows(2 * V, *self.part[1:]), LANES)
+            tall = packed_rows(V if behind else 2 * V, *self.part[1:])
             other = to_level(self.flows, k)
             if self.leads:
-                shape = (shape[0] + (6 * V if k < levels - 2 else 2 * V),) + shape[1:]
+                tall += padded_even((2 if behind else 6) * V * V)
                 out = run(
-                    functools.partial(merge_all, self.parts, k, levels),
-                    [mats_shape, shape, (2, 3 * V, 8, LANES), inflow],
+                    functools.partial(merge_all, self.part, k, levels),
+                    [mats_shape, (tall, LANES), (2, 3 * V, 8, LANES), inflow],
                     [self.flows, other, *self.known], name="merge_all",
                 )
                 mats.append(out[0])
                 self.flows, self.known = out[1], out[2:]
             else:
                 out = run(
-                    functools.partial(merge_flows, self.parts, k, levels), [shape, inflow],
+                    functools.partial(merge_flows, self.part, k, levels), [(tall, LANES), inflow],
                     [mats[k], self.flows, other, *self.known], name="merge_flows",
                 )
                 self.flows, self.known = out[0], out[1:]
             self.level = k + 1
 
+        def send(self):
+            self.other = to_level(self.flows, levels - 1)
+
+        def ahead_of(self, later):
+            later.flows, self.other = lax.optimization_barrier((later.flows, self.other))
+
         def last(self):
-            return [self.flows, to_level(self.flows, levels - 1), *self.known]
+            return [self.flows, self.other, *self.known]
 
         def correct(self):
             if self.leads:
                 result, last = run(
-                    functools.partial(correct_all, self.parts, levels), [self.solved.shape, mats_shape],
+                    functools.partial(correct_all, self.part, levels), [self.solved.shape, mats_shape],
                     [*self.last(), blocks, self.solved], scratch=self.scratch, name="correct_all",
                 )
                 mats.append(last)
                 return result
             return run(
-                functools.partial(correct, self.parts, levels), [self.solved.shape],
+                functools.partial(correct, self.part, levels), [self.solved.shape],
                 [mats[-1], *self.last(), blocks, self.solved], scratch=self.scratch, name="correct",
             )[0]
 
@@ -724,36 +749,42 @@
         near_base, [x_shape], [xn, xf, adv, vis, table, trig], name="near_base", flops=COSTS[0]
     )[0]
     blocks, group = run(
-        transfer, [(2, cells * V, 16, LANES), (6 * V, 8, LANES)], [low, upp],
+        transfer, [(2, cells * V, 16, LANES), (padded_even(6 * V * V), LANES)], [low, upp],
         scratch=[pltpu.VMEM((cells * V, 8, LANES), F32)], name="transfer", flops=COSTS[1],
     )
     lead = run(
         far_lead, [(LEAD * V, PAD, LANES)], [slab_in, trig, basis, turned],
         scratch=[pltpu.VMEM((V, PAD, LANES), F32)], name="far_lead", flops=COSTS[3],
     )[0]
+    tall = packed_rows(2 * V, PAD // 8 - 1, True) + group.shape[0]
     first = Exchange(
         0,
+        True,
         *run(
-            near_cell, [x_shape, (2 * V * PAD // 8 + 6 * V, 8, LANES)],
+            near_cell, [x_shape, (tall, LANES)],
             [base_near, halo_near, from_left, from_right, adv, vis, inv, low, upp, group],
             scratch=[edges], name="near_cell", flops=COSTS[2],
         ),
         leads=True,
     )
     first.step()
-    second = Exchange(1, *solve_chunk(0))
-    second.step()
+    second = Exchange(1, CHUNKS[0][1], *solve_chunk(0))
     for k in range(1, levels - 1):
         first.step()
-    third = Exchange(1, *solve_chunk(1))
+    first.send()
+    second.step()
+    third = Exchange(1, CHUNKS[1][1], *solve_chunk(1))
+    third.step()
     for k in range(1, levels - 1):
         second.step()
-    third.step()
-    near = first.correct()
+    second.send()
+    first.ahead_of(third)
     for k in range(1, levels - 1):
         third.step()
+    near = first.correct()
     done = [second.correct()]
     g_last = third.solved
+    third.send()
     small = [mats[-1], *third.last()]
 
     out = run(

time: 77.4 us -> 75.2 us (0.972)
  waiting for transfers between devices: 19.3 us -> 15.8 us
  starting transfers between devices: 23.6 us -> 25 us
    ppermute x9, waiting for transfers between devices: 19.3 us -> 15.8 us  [local(): lax.ppermute(x, 'seg', [(i, i ^ 1 << k) for i in range(segs)])]
    ppermute x9, starting transfers between devices: 14.3 us -> 15.6 us  [local(): lax.ppermute(x, 'seg', [(i, i ^ 1 << k) for i in range(segs)])]
  transfers between devices with their start and end apart: 15 -> 15, of which waited for: 6 -> 4; matrix products, arithmetic and copies ran while one was open for 0% -> 0% of each run, Pallas kernels for 37% -> 38%
where the time goes in v8:
time: 75.2 us; the launch traced here: 75.1 us
  Pallas kernels  31.6 us (42%)
  starting transfers between devices  25 us (33%)
  waiting for transfers between devices  15.8 us (21%)
  local copies, waits for them, and re-layouts  2.34 us (3%)
    pallas_call x16, Pallas kernels, __call__(): pl.pallas_call(body, out_shape=[jax.ShapeDtypeStruct(s, F32) for s in out...  31 us
    ppermute x9, waiting for transfers between devices, local(): lax.ppermute(x, 'seg', [(i, i ^ 1 << k) for i in range(segs)])  15.8 us
    ppermute x9, starting transfers between devices, local(): lax.ppermute(x, 'seg', [(i, i ^ 1 << k) for i in range(segs)])  15.6 us
    ppermute x3, starting transfers between devices, local(): to_far = lambda x: lax.ppermute(x, 'pitch', far_pairs)  4.13 us
    ppermute x1, starting transfers between devices, local(): lax.ppermute(last_cell, 'seg', [(i, i + 1) for i in range(segs - 1)])  3.4 us
    unnamed x22, local copies, waits for them, and re-layouts  2.18 us
  transfers between devices with their start and end apart: 15, of which 4 were waited for; matrix products, arithmetic and copies ran while one was open for 0% of the time, Pallas kernels for 38%

profile of v8, /device:TPU:0, one launch (start us, length us, event | category | flops | bytes accessed | tf_op | source)
XLA Modules:
  0.0 75.1 jit_solution(15494648340211534033)
XLA Ops:
  0.0 0.1 stack.35.flags
  0.1 2.1 %copy-done = f32[16,2,5,49,128]{4,1,3,2,0:T(2,128)S(1)} copy-done((f32[16,2,5,49,128]{4,1,3,2,0:T(2,128)S(1)}, f32[16,2,5,49,128]{4,1,3,2,0:T(2,128)}, u32[]{:S(2)}) %copy-start) | copy-done | bytes 4014104
  2.2 0.5 split_cells.1
  2.8 0.5 collective-permute-start.1
  3.3 2.6 %collective-permute-start = (f32[980,128]{1,0:T(8,128)S(1)}, f32[980,128]{1,0:T(8,128)S(1)}, u32[]{:S(2)}, u32[]{:S(2)}) collective-permute-start(f32[980,128]{1,0:T(8,128)S(1)} %get-tuple-element.86), channel_id=1, source_target_pairs={{0,3},{1,2},{2,1},{3,0},{4,7},{5,6},{6,5},{7,4},{8,11},{9,10},{10,... | collective-permute-start | bytes 1505288 | tf_op jit(solution)/shard_map/ppermute | solution.py:628
  5.9 3.4 %collective-permute-start.2 = (f32[496,128]{1,0:T(8,128)S(1)}, f32[496,128]{1,0:T(8,128)S(1)}, u32[]{:S(2)}, u32[]{:S(2)}) collective-permute-start(f32[496,128]{1,0:T(8,128)S(1)} %get-tuple-element.90), channel_id=1, source_target_pairs={{0,4},{4,8},{8,12},{12,16},{16,20},{20,24},{24,28},{1,5},{5,9},{9,... | collective-permute-start | bytes 761864 | tf_op jit(solution)/shard_map/ppermute | solution.py:657
  9.3 1.3 %collective-permute-start.3 = (f32[496,128]{1,0:T(8,128)S(1)}, f32[496,128]{1,0:T(8,128)S(1)}, u32[]{:S(2)}, u32[]{:S(2)}) collective-permute-start(f32[496,128]{1,0:T(8,128)S(1)} %get-tuple-element.91), channel_id=1, source_target_pairs={{4,0},{8,4},{12,8},{16,12},{20,16},{24,20},{28,24},{5,1},{9,5},{13... | collective-permute-start | bytes 761864 | tf_op jit(solution)/shard_map/ppermute | solution.py:658
  10.6 0.0 copy-done.10
  10.7 0.1 broadcast_in_dim.2.harmonic
  10.7 0.0 copy-done.5
  10.7 0.0 copy-done.8
  10.7 0.0 copy-done.3
  10.8 0.0 copy-done.4
  10.8 0.0 copy-done.6
  10.8 0.0 copy-done.7
  10.8 4.2 %prepare.1 = (f32[56,128]{1,0:T(8,128)S(1)}, f32[80,56,128]{2,1,0:T(8,128)S(1)}, f32[1984,128]{1,0:T(8,128)S(1)}, f32[960,128]{1,0:T(8,128)S(1)}) custom-call(s32[6]{0:T(128)S(1)} %stack.35.flags, s32[2]{0:T(128)S(1)} %copy-done.8, f32[80,56,128]{2,1,0:T(8,128)S(1)} %get-tuple-element.77.xn, f32[80,56,128]{2,1,0:T(8,128)S(1)} %get-tuple-element.78.xf, ...), custom_call_target="tpu_custom_call" | custom-call | flops 1000 | bytes 1000 | tf_op jit(solution)/shard_map/prepare/pallas_call | solution.py:49
  15.0 0.1 collective-permute-start.5
  15.1 0.0 copy-start.1
  15.1 0.0 copy-start.2
  15.1 0.0 copy-start.9
  15.1 3.5 %near_base.1.base = f32[80,56,128]{2,1,0:T(8,128)S(1)} custom-call(s32[6]{0:T(128)S(1)} %stack.35.flags, f32[80,56,128]{2,1,0:T(8,128)S(1)} %get-tuple-element.77.xn, f32[80,56,128]{2,1,0:T(8,128)S(1)} %get-tuple-element.78.xf, f32[160,128]{1,0:T(8,128)S(1)} %bitcast.40, f32[160,128]{1,0:T(8,128)S(1)} %bitcast.45, f32[56,192]{1,0:T(8,128)S(1)} %copy-done.6, ...), custom_call_target="tpu_custom_call" | custom-call | bytes 1000 | tf_op jit(solution)/shard_map/near_base/pallas_call | solution.py:49
  18.7 0.0 copy-done.1
  18.7 0.0 copy-done.2
  18.7 1.6 %transfer.1 = (f32[2,80,16,128]{3,2,1,0:T(8,128)S(1)}, f32[152,128]{1,0:T(8,128)S(1)}) custom-call(s32[6]{0:T(128)S(1)} %stack.35.flags, f32[800,128]{1,0:T(8,128)S(1)} %bitcast.28, f32[800,128]{1,0:T(8,128)S(1)} %bitcast.32), custom_call_target="tpu_custom_call" | custom-call | bytes 1000 | tf_op jit(solution)/shard_map/transfer/pallas_call | solution.py:49
  20.3 0.0 copy-done.9
  20.3 0.1 reshape.36
  20.4 0.0 collective-permute-done.slab
  20.4 1.2 %far_lead.1.lead = f32[20,56,128]{2,1,0:T(8,128)S(1)} custom-call(s32[6]{0:T(128)S(1)} %stack.35.flags, f32[980,128]{1,0:T(8,128)S(1)} %collective-permute-done.slab, f32[56,128]{1,0:T(8,128)S(1)} %get-tuple-element.81.trig, f32[56,56]{1,0:T(8,128)S(1)} %copy-done.7, f32[64,192]{1,0:T(8,128)S(1)} %copy-done.5), custom_call_target="tpu_custom_call" | custom-call | bytes 1000 | tf_op jit(solution)/shard_map/far_lead/pallas_call | solution.py:49
  21.6 0.0 collective-permute-done.2.from_left
  21.6 0.0 collective-permute-done.3.from_right
  21.6 0.0 collective-permute-done.1.halo
  21.6 3.7 %near_cell.1 = (f32[80,56,128]{2,1,0:T(8,128)S(1)}, f32[648,128]{1,0:T(8,128)S(1)}) custom-call(s32[6]{0:T(128)S(1)} %stack.35.flags, f32[80,56,128]{2,1,0:T(8,128)S(1)} %near_base.1.base, f32[80,56,128]{2,1,0:T(8,128)S(1)} %collective-permute-done.1.halo, f32[496,128]{1,0:T(8,128)S(1)} %collective-permute-done.2.from_left, ...), custom_call_target="tpu_custom_call" | custom-call | flops 6000000000 | bytes 1000 | tf_op jit(solution)/shard_map/near_cell/pallas_call | solution.py:49
  25.3 2.7 %collective-permute-start.4 = (f32[648,128]{1,0:T(8,128)S(1)}, f32[648,128]{1,0:T(8,128)S(1)}, u32[]{:S(2)}, u32[]{:S(2)}) collective-permute-start(f32[648,128]{1,0:T(8,128)S(1)} %get-tuple-element.95.flows), channel_id=1, source_target_pairs={{0,4},{4,0},{8,12},{12,8},{16,20},{20,16},{24,28},{28,24},{1,5},{5... | collective-permute-start | bytes 995336 | tf_op jit(solution)/shard_map/ppermute | solution.py:629
  28.0 1.4 %collective-permute-start.8 = (f32[960,128]{1,0:T(8,128)S(1)}, f32[960,128]{1,0:T(8,128)S(1)}, u32[]{:S(2)}, u32[]{:S(2)}) collective-permute-start(f32[960,128]{1,0:T(8,128)S(1)} %get-tuple-element.112), channel_id=1, source_target_pairs={{0,3},{1,2},{2,1},{3,0},{4,7},{5,6},{6,5},{7,4},{8,11},{9,10},{10,... | collective-permute-start | bytes 1474568 | tf_op jit(solution)/shard_map/ppermute | solution.py:628
  29.5 7.1 %collective-permute-done.4.other = f32[648,128]{1,0:T(8,128)S(1)} collective-permute-done((f32[648,128]{1,0:T(8,128)S(1)}, f32[648,128]{1,0:T(8,128)S(1)}, u32[]{:S(2)}, u32[]{:S(2)}) %collective-permute-start.4) | collective-permute-done | bytes 331808 | tf_op jit(solution)/shard_map/ppermute | solution.py:629
  36.6 1.0 %merge_all.2 = (f32[2,30,8,128]{3,2,1,0:T(8,128)S(1)}, f32[648,128]{1,0:T(8,128)S(1)}, f32[2,15,8,128]{3,2,1,0:T(8,128)S(1)}, f32[496,128]{1,0:T(8,128)S(1)}) custom-call(s32[6]{0:T(128)S(1)} %stack.35.flags, f32[648,128]{1,0:T(8,128)S(1)} %get-tuple-element.95.flows, f32[648,128]{1,0:T(8,128)S(1)} %collective-permute-done.4.other), custom_call_target="tpu_custom_call" | custom-call | flops 1000 | bytes 1000 | tf_op jit(solution)/shard_map/merge_all/pallas_call | solution.py:49
  37.6 2.8 %collective-permute-start.6 = (f32[648,128]{1,0:T(8,128)S(1)}, f32[648,128]{1,0:T(8,128)S(1)}, u32[]{:S(2)}, u32[]{:S(2)}) collective-permute-start(f32[648,128]{1,0:T(8,128)S(1)} %get-tuple-element.103.flows), channel_id=1, source_target_pairs={{0,8},{4,12},{8,0},{12,4},{16,24},{20,28},{24,16},{28,20},{1,9},{5... | collective-permute-start | bytes 995336 | tf_op jit(solution)/shard_map/ppermute | solution.py:629
  40.4 0.0 collective-permute-done.5.halo
  40.4 2.8 %far_chunk.2 = (f32[80,40,128]{2,1,0:T(8,128)S(1)}, f32[336,128]{1,0:T(8,128)S(1)}) custom-call(s32[6]{0:T(128)S(1)} %stack.35.flags, f32[80,56,128]{2,1,0:T(8,128)S(1)} %get-tuple-element.98.base, f32[20,56,128]{2,1,0:T(8,128)S(1)} %far_lead.1.lead, f32[1984,128]{1,0:T(8,128)S(1)} %collective-permute-done.5.halo, ...), custom_call_target="tpu_custom_call" | custom-call | flops 1000 | bytes 1000 | tf_op jit(solution)/shard_map/far_chunk/pallas_call | solution.py:49
  43.2 2.1 %collective-permute-start.7 = (f32[336,128]{1,0:T(8,128)S(1)}, f32[336,128]{1,0:T(8,128)S(1)}, u32[]{:S(2)}, u32[]{:S(2)}) collective-permute-start(f32[336,128]{1,0:T(8,128)S(1)} %get-tuple-element.109.flows), channel_id=1, source_target_pairs={{0,4},{4,0},{8,12},{12,8},{16,20},{20,16},{24,28},{28,24},{1,5},{5... | collective-permute-start | bytes 516104 | tf_op jit(solution)/shard_map/ppermute | solution.py:629
  45.3 2.8 %collective-permute-done.6.other = f32[648,128]{1,0:T(8,128)S(1)} collective-permute-done((f32[648,128]{1,0:T(8,128)S(1)}, f32[648,128]{1,0:T(8,128)S(1)}, u32[]{:S(2)}, u32[]{:S(2)}) %collective-permute-start.6) | collective-permute-done | bytes 331808 | tf_op jit(solution)/shard_map/ppermute | solution.py:629
  48.2 1.0 %merge_all.3 = (f32[2,30,8,128]{3,2,1,0:T(8,128)S(1)}, f32[304,128]{1,0:T(8,128)S(1)}, f32[2,15,8,128]{3,2,1,0:T(8,128)S(1)}, f32[496,128]{1,0:T(8,128)S(1)}) custom-call(s32[6]{0:T(128)S(1)} %stack.35.flags, f32[648,128]{1,0:T(8,128)S(1)} %get-tuple-element.103.flows, f32[648,128]{1,0:T(8,128)S(1)} %collective-permute-done.6.other, ...), custom_call_target="tpu_custom_call" | custom-call | flops 1000 | bytes 1000 | tf_op jit(solution)/shard_map/merge_all/pallas_call | solution.py:49
  49.2 2.8 %collective-permute-start.11 = (f32[304,128]{1,0:T(8,128)S(1)}, f32[304,128]{1,0:T(8,128)S(1)}, u32[]{:S(2)}, u32[]{:S(2)}) collective-permute-start(f32[304,128]{1,0:T(8,128)S(1)} %get-tuple-element.124.ends), channel_id=1, source_target_pairs={{0,16},{4,20},{8,24},{12,28},{16,0},{20,4},{24,8},{28,12},{1,17},{... | collective-permute-start | bytes 466952 | tf_op jit(solution)/shard_map/ppermute | solution.py:629
  52.0 0.0 collective-permute-done.7.other
  52.0 0.8 %merge_flows.4 = (f32[336,128]{1,0:T(8,128)S(1)}, f32[336,128]{1,0:T(8,128)S(1)}) custom-call(s32[6]{0:T(128)S(1)} %stack.35.flags, f32[2,30,8,128]{3,2,1,0:T(8,128)S(1)} %get-tuple-element.108.mats, f32[336,128]{1,0:T(8,128)S(1)} %get-tuple-element.109.flows, f32[336,128]{1,0:T(8,128)S(1)} %collective-permute-done.7.other), custom_call_target="tpu_custom_call" | custom-call | flops 1000 | bytes 1000 | tf_op jit(solution)/shard_map/merge_flows/pallas_call | solution.py:49
  52.8 1.6 %collective-permute-start.10 = (f32[336,128]{1,0:T(8,128)S(1)}, f32[336,128]{1,0:T(8,128)S(1)}, u32[]{:S(2)}, u32[]{:S(2)}) collective-permute-start(f32[336,128]{1,0:T(8,128)S(1)} %get-tuple-element.119.flows), channel_id=1, source_target_pairs={{0,8},{4,12},{8,0},{12,4},{16,24},{20,28},{24,16},{28,20},{1,9},{5... | collective-permute-start | bytes 516104 | tf_op jit(solution)/shard_map/ppermute | solution.py:629
  54.4 0.0 collective-permute-done.8.halo
  54.4 1.6 %far_chunk.3 = (f32[80,16,128]{2,1,0:T(8,128)S(1)}, f32[160,128]{1,0:T(8,128)S(1)}) custom-call(s32[6]{0:T(128)S(1)} %stack.35.flags, f32[80,56,128]{2,1,0:T(8,128)S(1)} %get-tuple-element.98.base, f32[20,56,128]{2,1,0:T(8,128)S(1)} %far_lead.1.lead, f32[960,128]{1,0:T(8,128)S(1)} %collective-permute-done.8.halo, ...), custom_call_target="tpu_custom_call" | custom-call | flops 1000 | bytes 1000 | tf_op jit(solution)/shard_map/far_chunk/pallas_call | solution.py:49
  56.0 0.7 collective-permute-start.9
  56.7 3.8 %collective-permute-done.9.other = f32[160,128]{1,0:T(8,128)S(1)} collective-permute-done((f32[160,128]{1,0:T(8,128)S(1)}, f32[160,128]{1,0:T(8,128)S(1)}, u32[]{:S(2)}, u32[]{:S(2)}) %collective-permute-start.9) | collective-permute-done | bytes 81952 | tf_op jit(solution)/shard_map/ppermute | solution.py:629
  60.5 0.6 merge_flows.5
  61.2 0.0 collective-permute-done.11.other
  61.2 0.5 collective-permute-start.12
  61.7 0.0 collective-permute-done.10.other
  61.7 0.8 %merge_flows.6 = (f32[168,128]{1,0:T(8,128)S(1)}, f32[336,128]{1,0:T(8,128)S(1)}) custom-call(s32[6]{0:T(128)S(1)} %stack.35.flags, f32[2,30,8,128]{3,2,1,0:T(8,128)S(1)} %get-tuple-element.118.mats, f32[336,128]{1,0:T(8,128)S(1)} %get-tuple-element.119.flows, f32[336,128]{1,0:T(8,128)S(1)} %collective-permute-done.10.other, ...), custom_call_target="tpu_custom_call" | custom-call | flops 1000 | bytes 1000 | tf_op jit(solution)/shard_map/merge_flows/pallas_call | solution.py:49
  62.5 1.4 %collective-permute-start.13 = (f32[168,128]{1,0:T(8,128)S(1)}, f32[168,128]{1,0:T(8,128)S(1)}, u32[]{:S(2)}, u32[]{:S(2)}) collective-permute-start(f32[168,128]{1,0:T(8,128)S(1)} %get-tuple-element.137.ends), channel_id=1, source_target_pairs={{0,16},{4,20},{8,24},{12,28},{16,0},{20,4},{24,8},{28,12},{1,17},{... | collective-permute-start | bytes 258056 | tf_op jit(solution)/shard_map/ppermute | solution.py:629
  63.9 2.0 %collective-permute-done.12.other = f32[160,128]{1,0:T(8,128)S(1)} collective-permute-done((f32[160,128]{1,0:T(8,128)S(1)}, f32[160,128]{1,0:T(8,128)S(1)}, u32[]{:S(2)}, u32[]{:S(2)}) %collective-permute-start.12) | collective-permute-done | bytes 81952 | tf_op jit(solution)/shard_map/ppermute | solution.py:629
  65.9 0.7 merge_flows.7
  66.5 0.9 %collective-permute-start.14 = (f32[80,128]{1,0:T(8,128)S(1)}, f32[80,128]{1,0:T(8,128)S(1)}, u32[]{:S(2)}, u32[]{:S(2)}) collective-permute-start(f32[80,128]{1,0:T(8,128)S(1)} %get-tuple-element.141.ends), channel_id=1, source_target_pairs={{0,16},{4,20},{8,24},{12,28},{16,0},{20,4},{24,8},{28,12},{1,17},{... | collective-permute-start | bytes 122888 | tf_op jit(solution)/shard_map/ppermute | solution.py:629
  67.5 2.7 %correct_all.1 = (f32[80,56,128]{2,1,0:T(8,128)S(1)}, f32[2,30,8,128]{3,2,1,0:T(8,128)S(1)}) custom-call(s32[6]{0:T(128)S(1)} %stack.35.flags, f32[304,128]{1,0:T(8,128)S(1)} %get-tuple-element.124.ends, f32[304,128]{1,0:T(8,128)S(1)} %collective-permute-done.11.other, f32[2,15,8,128]{3,2,1,0:T(8,128)S(1)} %get-tuple-element.130.share, ...), custom_call_target="tpu_custom_call" | custom-call | flops 1000 | bytes 1000 | tf_op jit(solution)/shard_map/correct_all/pallas_call | solution.py:49
  70.1 0.0 collective-permute-done.13.other
  70.1 2.1 %correct.1.refs_0_ = f32[80,40,128]{2,1,0:T(8,128)S(1)} custom-call(s32[6]{0:T(128)S(1)} %stack.35.flags, f32[2,30,8,128]{3,2,1,0:T(8,128)S(1)} %get-tuple-element.136.mats, f32[168,128]{1,0:T(8,128)S(1)} %get-tuple-element.137.ends, f32[168,128]{1,0:T(8,128)S(1)} %collective-permute-done.13.other, f32[336,128]{1,0:T(8,128)S(1)} %get-tuple-element.138.known, ...), custom_call_target="tpu_custom_call" | custom-call | flops 1000 | bytes 1000 | tf_op jit(solution)/shard_map/correct/pallas_call | solution.py:49
  72.3 0.0 collective-permute-done.14.other
  72.3 2.8 %finish.1 = f32[7840,128]{1,0:T(8,128)} custom-call(s32[6]{0:T(128)S(1)} %stack.35.flags, f32[2,30,8,128]{3,2,1,0:T(8,128)S(1)} %get-tuple-element.136.mats, f32[80,128]{1,0:T(8,128)S(1)} %get-tuple-element.141.ends, f32[80,128]{1,0:T(8,128)S(1)} %collective-permute-done.14.other, f32[160,128]{1,0:T(8,128)S(1)} %get-tuple-element.142.known, ...), custom_call_target="tpu_custom_call" | custom-call | flops 1000 | bytes 1000 | tf_op jit(solution)/shard_map/finish/pallas_call | solution.py:49
  (9 shorter events, 0.0 us)
Async XLA Ops:
  0.0 10.7 %copy-start.5 = (f32[64,192]{1,0:T(8,128)S(1)}, f32[64,192]{1,0:T(8,128)}, u32[]{:S(2)}) copy-start(f32[64,192]{1,0:T(8,128)} %constant.33.clone.turned) | copy-start | bytes 147460
  0.0 10.6 %copy-start.10 = (s32[24]{0:T(128)S(1)}, s32[24]{0:T(128)}, u32[]{:S(2)}) copy-start(s32[24]{0:T(128)} %param.18) | copy-start | bytes 292
  0.0 10.7 %copy-start.8 = (s32[2]{0:T(128)S(1)}, s32[2]{0:T(128)}, u32[]{:S(2)}) copy-start(s32[2]{0:T(128)} %blades.1) | copy-start | bytes 28
  0.1 2.1 %copy-start = (f32[16,2,5,49,128]{4,1,3,2,0:T(2,128)S(1)}, f32[16,2,5,49,128]{4,1,3,2,0:T(2,128)}, u32[]{:S(2)}) copy-start(f32[16,2,5,49,128]{4,1,3,2,0:T(2,128)} %param.11) | copy-start | bytes 12042244
  2.2 8.5 %copy-start.3 = (f32[16,2,5,128]{3,1,2,0:T(2,128)S(1)}, f32[16,2,5,128]{3,1,2,0:T(2,128)}, u32[]{:S(2)}) copy-start(f32[16,2,5,128]{3,1,2,0:T(2,128)} %param.12) | copy-start | bytes 245764
  2.2 8.5 %copy-start.4 = (f32[16,2,5,128]{3,1,2,0:T(2,128)S(1)}, f32[16,2,5,128]{3,1,2,0:T(2,128)}, u32[]{:S(2)}) copy-start(f32[16,2,5,128]{3,1,2,0:T(2,128)} %param.13) | copy-start | bytes 245764
  2.2 8.5 %copy-start.6 = (f32[56,192]{1,0:T(8,128)S(1)}, f32[56,192]{1,0:T(8,128)}, u32[]{:S(2)}) copy-start(f32[56,192]{1,0:T(8,128)} %constant.34.clone.table) | copy-start | bytes 129028
  2.2 8.5 %copy-start.7 = (f32[56,56]{1,0:T(8,128)S(1)}, f32[56,56]{1,0:T(8,128)}, u32[]{:S(2)}) copy-start(f32[56,56]{1,0:T(8,128)} %constant.32.clone.basis) | copy-start | bytes 37636
  2.8 18.9 %collective-permute-start.1 = (f32[80,56,128]{2,1,0:T(8,128)S(1)}, f32[80,56,128]{2,1,0:T(8,128)S(1)}, u32[]{:S(2)}, u32[]{:S(2)}) collective-permute-start(f32[80,56,128]{2,1,0:T(8,128)S(1)} %get-tuple-element.77.xn), channel_id=1, source_target_pairs={{0,1},{1,0},{2,3},{3,2},{4,5},{5,4},{6,7},{7,6},{8,9},{9,8},{10,11... | collective-permute-start | bytes 6881288 | tf_op jit(solution)/shard_map/ppermute | solution.py:655
  3.3 17.1 %collective-permute-start = (f32[980,128]{1,0:T(8,128)S(1)}, f32[980,128]{1,0:T(8,128)S(1)}, u32[]{:S(2)}, u32[]{:S(2)}) collective-permute-start(f32[980,128]{1,0:T(8,128)S(1)} %get-tuple-element.86), channel_id=1, source_target_pairs={{0,3},{1,2},{2,1},{3,0},{4,7},{5,6},{6,5},{7,4},{8,11},{9,10},{10,... | collective-permute-start | bytes 1505288 | tf_op jit(solution)/shard_map/ppermute | solution.py:628
  5.9 15.7 %collective-permute-start.2 = (f32[496,128]{1,0:T(8,128)S(1)}, f32[496,128]{1,0:T(8,128)S(1)}, u32[]{:S(2)}, u32[]{:S(2)}) collective-permute-start(f32[496,128]{1,0:T(8,128)S(1)} %get-tuple-element.90), channel_id=1, source_target_pairs={{0,4},{4,8},{8,12},{12,16},{16,20},{20,24},{24,28},{1,5},{5,9},{9,... | collective-permute-start | bytes 761864 | tf_op jit(solution)/shard_map/ppermute | solution.py:657
  9.3 12.3 %collective-permute-start.3 = (f32[496,128]{1,0:T(8,128)S(1)}, f32[496,128]{1,0:T(8,128)S(1)}, u32[]{:S(2)}, u32[]{:S(2)}) collective-permute-start(f32[496,128]{1,0:T(8,128)S(1)} %get-tuple-element.91), channel_id=1, source_target_pairs={{4,0},{8,4},{12,8},{16,12},{20,16},{24,20},{28,24},{5,1},{9,5},{13... | collective-permute-start | bytes 761864 | tf_op jit(solution)/shard_map/ppermute | solution.py:658
  15.0 25.4 %collective-permute-start.5 = (f32[1984,128]{1,0:T(8,128)S(1)}, f32[1984,128]{1,0:T(8,128)S(1)}, u32[]{:S(2)}, u32[]{:S(2)}) collective-permute-start(f32[1984,128]{1,0:T(8,128)S(1)} %get-tuple-element.100), channel_id=1, source_target_pairs={{0,3},{1,2},{2,1},{3,0},{4,7},{5,6},{6,5},{7,4},{8,11},{9,10},{10,... | collective-permute-start | bytes 3047432 | tf_op jit(solution)/shard_map/ppermute | solution.py:628
  15.1 3.6 %copy-start.1 = (f32[16,2,5,5,128]{4,1,3,2,0:T(2,128)S(1)}, f32[16,2,5,5,128]{4,1,3,2,0:T(2,128)}, u32[]{:S(2)}) copy-start(f32[16,2,5,5,128]{4,1,3,2,0:T(2,128)} %param.15) | copy-start | bytes 1228804
  15.1 3.6 %copy-start.2 = (f32[16,2,5,5,128]{4,1,3,2,0:T(2,128)S(1)}, f32[16,2,5,5,128]{4,1,3,2,0:T(2,128)}, u32[]{:S(2)}) copy-start(f32[16,2,5,5,128]{4,1,3,2,0:T(2,128)} %param.16) | copy-start | bytes 1228804
  15.1 5.2 %copy-start.9 = (bf16[16,2,5,5,128]{4,1,3,2,0:T(2,128)(2,1)S(1)}, bf16[16,2,5,5,128]{4,1,3,2,0:T(2,128)(2,1)}, u32[]{:S(2)}) copy-start(bf16[16,2,5,5,128]{4,1,3,2,0:T(2,128)(2,1)} %param.14) | copy-start | bytes 614404
  25.3 11.2 %collective-permute-start.4 = (f32[648,128]{1,0:T(8,128)S(1)}, f32[648,128]{1,0:T(8,128)S(1)}, u32[]{:S(2)}, u32[]{:S(2)}) collective-permute-start(f32[648,128]{1,0:T(8,128)S(1)} %get-tuple-element.95.flows), channel_id=1, source_target_pairs={{0,4},{4,0},{8,12},{12,8},{16,20},{20,16},{24,28},{28,24},{1,5},{5... | collective-permute-start | bytes 995336 | tf_op jit(solution)/shard_map/ppermute | solution.py:629
  28.0 26.4 %collective-permute-start.8 = (f32[960,128]{1,0:T(8,128)S(1)}, f32[960,128]{1,0:T(8,128)S(1)}, u32[]{:S(2)}, u32[]{:S(2)}) collective-permute-start(f32[960,128]{1,0:T(8,128)S(1)} %get-tuple-element.112), channel_id=1, source_target_pairs={{0,3},{1,2},{2,1},{3,0},{4,7},{5,6},{6,5},{7,4},{8,11},{9,10},{10,... | collective-permute-start | bytes 1474568 | tf_op jit(solution)/shard_map/ppermute | solution.py:628
  37.6 10.6 %collective-permute-start.6 = (f32[648,128]{1,0:T(8,128)S(1)}, f32[648,128]{1,0:T(8,128)S(1)}, u32[]{:S(2)}, u32[]{:S(2)}) collective-permute-start(f32[648,128]{1,0:T(8,128)S(1)} %get-tuple-element.103.flows), channel_id=1, source_target_pairs={{0,8},{4,12},{8,0},{12,4},{16,24},{20,28},{24,16},{28,20},{1,9},{5... | collective-permute-start | bytes 995336 | tf_op jit(solution)/shard_map/ppermute | solution.py:629
  43.2 8.8 %collective-permute-start.7 = (f32[336,128]{1,0:T(8,128)S(1)}, f32[336,128]{1,0:T(8,128)S(1)}, u32[]{:S(2)}, u32[]{:S(2)}) collective-permute-start(f32[336,128]{1,0:T(8,128)S(1)} %get-tuple-element.109.flows), channel_id=1, source_target_pairs={{0,4},{4,0},{8,12},{12,8},{16,20},{20,16},{24,28},{28,24},{1,5},{5... | collective-permute-start | bytes 516104 | tf_op jit(solution)/shard_map/ppermute | solution.py:629
  49.2 12.0 %collective-permute-start.11 = (f32[304,128]{1,0:T(8,128)S(1)}, f32[304,128]{1,0:T(8,128)S(1)}, u32[]{:S(2)}, u32[]{:S(2)}) collective-permute-start(f32[304,128]{1,0:T(8,128)S(1)} %get-tuple-element.124.ends), channel_id=1, source_target_pairs={{0,16},{4,20},{8,24},{12,28},{16,0},{20,4},{24,8},{28,12},{1,17},{... | collective-permute-start | bytes 466952 | tf_op jit(solution)/shard_map/ppermute | solution.py:629
  52.8 8.9 %collective-permute-start.10 = (f32[336,128]{1,0:T(8,128)S(1)}, f32[336,128]{1,0:T(8,128)S(1)}, u32[]{:S(2)}, u32[]{:S(2)}) collective-permute-start(f32[336,128]{1,0:T(8,128)S(1)} %get-tuple-element.119.flows), channel_id=1, source_target_pairs={{0,8},{4,12},{8,0},{12,4},{16,24},{20,28},{24,16},{28,20},{1,9},{5... | collective-permute-start | bytes 516104 | tf_op jit(solution)/shard_map/ppermute | solution.py:629
  56.0 4.5 %collective-permute-start.9 = (f32[160,128]{1,0:T(8,128)S(1)}, f32[160,128]{1,0:T(8,128)S(1)}, u32[]{:S(2)}, u32[]{:S(2)}) collective-permute-start(f32[160,128]{1,0:T(8,128)S(1)} %get-tuple-element.115.flows), channel_id=1, source_target_pairs={{0,4},{4,0},{8,12},{12,8},{16,20},{20,16},{24,28},{28,24},{1,5},{5... | collective-permute-start | bytes 245768 | tf_op jit(solution)/shard_map/ppermute | solution.py:629
  61.2 4.7 %collective-permute-start.12 = (f32[160,128]{1,0:T(8,128)S(1)}, f32[160,128]{1,0:T(8,128)S(1)}, u32[]{:S(2)}, u32[]{:S(2)}) collective-permute-start(f32[160,128]{1,0:T(8,128)S(1)} %get-tuple-element.125.flows), channel_id=1, source_target_pairs={{0,8},{4,12},{8,0},{12,4},{16,24},{20,28},{24,16},{28,20},{1,9},{5... | collective-permute-start | bytes 245768 | tf_op jit(solution)/shard_map/ppermute | solution.py:629
  62.5 7.6 %collective-permute-start.13 = (f32[168,128]{1,0:T(8,128)S(1)}, f32[168,128]{1,0:T(8,128)S(1)}, u32[]{:S(2)}, u32[]{:S(2)}) collective-permute-start(f32[168,128]{1,0:T(8,128)S(1)} %get-tuple-element.137.ends), channel_id=1, source_target_pairs={{0,16},{4,20},{8,24},{12,28},{16,0},{20,4},{24,8},{28,12},{1,17},{... | collective-permute-start | bytes 258056 | tf_op jit(solution)/shard_map/ppermute | solution.py:629
  66.5 5.7 %collective-permute-start.14 = (f32[80,128]{1,0:T(8,128)S(1)}, f32[80,128]{1,0:T(8,128)S(1)}, u32[]{:S(2)}, u32[]{:S(2)}) collective-permute-start(f32[80,128]{1,0:T(8,128)S(1)} %get-tuple-element.141.ends), channel_id=1, source_target_pairs={{0,16},{4,20},{8,24},{12,28},{16,0},{20,4},{24,8},{28,12},{1,17},{... | collective-permute-start | bytes 122888 | tf_op jit(solution)/shard_map/ppermute | solution.py:629

commit v9 on v8

--- a/solution.py
+++ b/solution.py
@@ -19,7 +19,7 @@
 LEAD = 4
 MB = 1 << 20
 
-CHUNKS = (((0, 32), True), ((32, 48), False))
+CHUNKS = (((0, 32), False), ((32, 48), True))
 
 
 def rows_of(chunk):
@@ -186,7 +186,8 @@
 
     one(0, above=False, sends=False)
     lax.fori_loop(1, LEAD, early, 0)
-    lax.fori_loop(LEAD, cells - 1, late, 0)
+    one(LEAD)
+    lax.fori_loop(LEAD + 1, cells - 1, late, 0, unroll=5)
     one(cells - 1, below=False)
 
 
@@ -204,7 +205,7 @@
         return carry
 
     one(0, above=False)
-    lax.fori_loop(1, cells - 1, inner, 0)
+    lax.fori_loop(1, cells - 1, inner, 0, unroll=7)
     one(cells - 1, below=False)
 
 
@@ -253,7 +254,7 @@
                 result.append(total)
             return tuple(result)
 
-        out = lax.fori_loop(1, cells - 1, ahead, ahead(0, nothing))
+        out = lax.fori_loop(1, cells - 1, ahead, ahead(0, nothing), unroll=2)
         out = ahead(cells - 1, out)
         keep_tiles(fg, 0, out, first, last, height, extra)
 
@@ -268,7 +269,7 @@
                 result.append(total)
             return tuple(result)
 
-        out = lax.fori_loop(0, cells, back, nothing)
+        out = lax.fori_loop(0, cells, back, nothing, unroll=2)
         keep_tiles(fg, V, out, first, last, height, extra)
 
 
@@ -399,7 +400,7 @@
                 forward[z * V + a] = result[a]
             return tuple(result)
 
-        through = lax.fori_loop(0, cells, ahead, tuple(unit(a) for a in range(V)))
+        through = lax.fori_loop(0, cells, ahead, tuple(unit(a) for a in range(V)), unroll=4)
 
         def back(i, current):
             z = cells - 1 - i
@@ -414,7 +415,7 @@
         start = tuple(
             jnp.concatenate([jnp.zeros((8, LANES), F32), unit(a)], axis=0) for a in range(V)
         )
-        ends = lax.fori_loop(0, cells, back, start)
+        ends = lax.fori_loop(0, cells, back, start, unroll=4)
         for a in range(V):
             for kind, value in enumerate((ends[a][:V], ends[a][8 : 8 + V], through[a][:V])):
                 group[pl.ds(((c * 3 + kind) * V + a) * V, V), :] = value
@@ -548,7 +549,7 @@
                 result[z * V + a, first:last, :] = corrected(c, z, a, first, last, g, blocks, flow)
             return flow
 
-        lax.fori_loop(0, g.shape[0] // V, step, flow)
+        lax.fori_loop(0, g.shape[0] // V, step, flow, unroll=2)
 
 
 def correct_all(part, levels, flags, ends, other, share, known, blocks, g, result, mats, inflow):
@@ -587,7 +588,7 @@
     size = held.shape[0] // parts
     copies = []
     for i in range(parts):
-        lax.fori_loop(i * cells, (i + 1) * cells, step, 0)
+        lax.fori_loop(i * cells, (i + 1) * cells, step, 0, unroll=2)
         span = pl.ds(i * size, size)
         copies.append(pltpu.make_async_copy(held.at[span, :], out.at[span, :], sems.at[i]))
         copies[-1].start()

time: 75.2 us -> 73.6 us (0.979)
  Pallas kernels: 31.6 us -> 28 us
  starting transfers between devices: 25 us -> 27.6 us
    ppermute x9, starting transfers between devices: 15.6 us -> 19.4 us  [local(): lax.ppermute(x, 'seg', [(i, i ^ 1 << k) for i in range(segs)])]
    pallas_call x16, Pallas kernels: 31 us -> 27.5 us  [__call__(): pl.pallas_call(body, out_shape=[jax.ShapeDtypeStruct(s, F32) for s in out...]
    ppermute x9, waiting for transfers between devices: 15.8 us -> 13 us  [local(): lax.ppermute(x, 'seg', [(i, i ^ 1 << k) for i in range(segs)])]
    ppermute x1, waiting for transfers between devices: 0.01 us -> 1.37 us  [local(): lax.ppermute(last_cell, 'seg', [(i, i + 1) for i in range(segs - 1)])]
    ppermute x3, starting transfers between devices: 4.13 us -> 2.97 us  [local(): to_far = lambda x: lax.ppermute(x, 'pitch', far_pairs)]
  transfers between devices with their start and end apart: 15 -> 15, of which waited for: 4 -> 5; matrix products, arithmetic and copies ran while one was open for 0% -> 0% of each run, Pallas kernels for 38% -> 33%
where the time goes in v9:
time: 73.6 us; the launch traced here: 73.4 us
  Pallas kernels  28 us (38%)
  starting transfers between devices  27.6 us (38%)
  waiting for transfers between devices  15.1 us (21%)
  local copies, waits for them, and re-layouts  2.34 us (3%)
    pallas_call x16, Pallas kernels, __call__(): pl.pallas_call(body, out_shape=[jax.ShapeDtypeStruct(s, F32) for s in out...  27.5 us
    ppermute x9, starting transfers between devices, local(): lax.ppermute(x, 'seg', [(i, i ^ 1 << k) for i in range(segs)])  19.4 us
    ppermute x9, waiting for transfers between devices, local(): lax.ppermute(x, 'seg', [(i, i ^ 1 << k) for i in range(segs)])  13 us
    ppermute x1, starting transfers between devices, local(): lax.ppermute(last_cell, 'seg', [(i, i + 1) for i in range(segs - 1)])  3.4 us
    ppermute x3, starting transfers between devices, local(): to_far = lambda x: lax.ppermute(x, 'pitch', far_pairs)  2.97 us
    unnamed x22, local copies, waits for them, and re-layouts  2.18 us
  transfers between devices with their start and end apart: 15, of which 5 were waited for; matrix products, arithmetic and copies ran while one was open for 0% of the time, Pallas kernels for 33%

profile of v9, /device:TPU:0, one launch (start us, length us, event | category | flops | bytes accessed | tf_op | source)
XLA Modules:
  0.0 73.4 jit_solution(14970793853819489476)
XLA Ops:
  0.0 0.1 stack.35.flags
  0.1 2.1 %copy-done = f32[16,2,5,49,128]{4,1,3,2,0:T(2,128)S(1)} copy-done((f32[16,2,5,49,128]{4,1,3,2,0:T(2,128)S(1)}, f32[16,2,5,49,128]{4,1,3,2,0:T(2,128)}, u32[]{:S(2)}) %copy-start) | copy-done | bytes 4014104
  2.2 0.5 split_cells.1
  2.8 0.5 collective-permute-start.1
  3.3 2.6 %collective-permute-start = (f32[980,128]{1,0:T(8,128)S(1)}, f32[980,128]{1,0:T(8,128)S(1)}, u32[]{:S(2)}, u32[]{:S(2)}) collective-permute-start(f32[980,128]{1,0:T(8,128)S(1)} %get-tuple-element.86), channel_id=1, source_target_pairs={{0,3},{1,2},{2,1},{3,0},{4,7},{5,6},{6,5},{7,4},{8,11},{9,10},{10,... | collective-permute-start | bytes 1505288 | tf_op jit(solution)/shard_map/ppermute | solution.py:629
  5.9 3.4 %collective-permute-start.2 = (f32[496,128]{1,0:T(8,128)S(1)}, f32[496,128]{1,0:T(8,128)S(1)}, u32[]{:S(2)}, u32[]{:S(2)}) collective-permute-start(f32[496,128]{1,0:T(8,128)S(1)} %get-tuple-element.90), channel_id=1, source_target_pairs={{0,4},{4,8},{8,12},{12,16},{16,20},{20,24},{24,28},{1,5},{5,9},{9,... | collective-permute-start | bytes 761864 | tf_op jit(solution)/shard_map/ppermute | solution.py:658
  9.3 1.3 %collective-permute-start.3 = (f32[496,128]{1,0:T(8,128)S(1)}, f32[496,128]{1,0:T(8,128)S(1)}, u32[]{:S(2)}, u32[]{:S(2)}) collective-permute-start(f32[496,128]{1,0:T(8,128)S(1)} %get-tuple-element.91), channel_id=1, source_target_pairs={{4,0},{8,4},{12,8},{16,12},{20,16},{24,20},{28,24},{5,1},{9,5},{13... | collective-permute-start | bytes 761864 | tf_op jit(solution)/shard_map/ppermute | solution.py:659
  10.6 0.0 copy-done.10
  10.7 0.1 broadcast_in_dim.2.harmonic
  10.7 0.0 copy-done.5
  10.7 0.0 copy-done.8
  10.7 0.0 copy-done.3
  10.8 0.0 copy-done.4
  10.8 0.0 copy-done.6
  10.8 0.0 copy-done.7
  10.8 3.3 %prepare.1 = (f32[56,128]{1,0:T(8,128)S(1)}, f32[80,56,128]{2,1,0:T(8,128)S(1)}, f32[1920,128]{1,0:T(8,128)S(1)}, f32[1024,128]{1,0:T(8,128)S(1)}) custom-call(s32[6]{0:T(128)S(1)} %stack.35.flags, s32[2]{0:T(128)S(1)} %copy-done.8, f32[80,56,128]{2,1,0:T(8,128)S(1)} %get-tuple-element.77.xn, f32[80,56,128]{2,1,0:T(8,128)S(1)} %get-tuple-element.78.xf, ...), custom_call_target="tpu_custom_call" | custom-call | flops 1000 | bytes 1000 | tf_op jit(solution)/shard_map/prepare/pallas_call | solution.py:49
  14.1 0.1 collective-permute-start.5
  14.2 0.0 copy-start.1
  14.2 0.0 copy-start.2
  14.2 0.0 copy-start.9
  14.2 2.1 %near_base.1.base = f32[80,56,128]{2,1,0:T(8,128)S(1)} custom-call(s32[6]{0:T(128)S(1)} %stack.35.flags, f32[80,56,128]{2,1,0:T(8,128)S(1)} %get-tuple-element.77.xn, f32[80,56,128]{2,1,0:T(8,128)S(1)} %get-tuple-element.78.xf, f32[160,128]{1,0:T(8,128)S(1)} %bitcast.40, f32[160,128]{1,0:T(8,128)S(1)} %bitcast.45, f32[56,192]{1,0:T(8,128)S(1)} %copy-done.6, ...), custom_call_target="tpu_custom_call" | custom-call | bytes 1000 | tf_op jit(solution)/shard_map/near_base/pallas_call | solution.py:49
  16.4 0.0 copy-done.1
  16.4 0.0 copy-done.2
  16.4 1.3 %transfer.1 = (f32[2,80,16,128]{3,2,1,0:T(8,128)S(1)}, f32[152,128]{1,0:T(8,128)S(1)}) custom-call(s32[6]{0:T(128)S(1)} %stack.35.flags, f32[800,128]{1,0:T(8,128)S(1)} %bitcast.28, f32[800,128]{1,0:T(8,128)S(1)} %bitcast.32), custom_call_target="tpu_custom_call" | custom-call | bytes 1000 | tf_op jit(solution)/shard_map/transfer/pallas_call | solution.py:49
  17.6 0.0 copy-done.9
  17.7 0.1 reshape.36
  17.8 0.0 collective-permute-done.slab
  17.8 1.2 %far_lead.1.lead = f32[20,56,128]{2,1,0:T(8,128)S(1)} custom-call(s32[6]{0:T(128)S(1)} %stack.35.flags, f32[980,128]{1,0:T(8,128)S(1)} %collective-permute-done.slab, f32[56,128]{1,0:T(8,128)S(1)} %get-tuple-element.81.trig, f32[56,56]{1,0:T(8,128)S(1)} %copy-done.7, f32[64,192]{1,0:T(8,128)S(1)} %copy-done.5), custom_call_target="tpu_custom_call" | custom-call | bytes 1000 | tf_op jit(solution)/shard_map/far_lead/pallas_call | solution.py:49
  19.0 1.4 %collective-permute-done.2.from_left = f32[496,128]{1,0:T(8,128)S(1)} collective-permute-done((f32[496,128]{1,0:T(8,128)S(1)}, f32[496,128]{1,0:T(8,128)S(1)}, u32[]{:S(2)}, u32[]{:S(2)}) %collective-permute-start.2) | collective-permute-done | bytes 253984 | tf_op jit(solution)/shard_map/ppermute | solution.py:658
  20.4 0.0 collective-permute-done.3.from_right
  20.4 0.0 collective-permute-done.1.halo
  20.4 3.4 %near_cell.1 = (f32[80,56,128]{2,1,0:T(8,128)S(1)}, f32[648,128]{1,0:T(8,128)S(1)}) custom-call(s32[6]{0:T(128)S(1)} %stack.35.flags, f32[80,56,128]{2,1,0:T(8,128)S(1)} %near_base.1.base, f32[80,56,128]{2,1,0:T(8,128)S(1)} %collective-permute-done.1.halo, f32[496,128]{1,0:T(8,128)S(1)} %collective-permute-done.2.from_left, ...), custom_call_target="tpu_custom_call" | custom-call | flops 6000000000 | bytes 1000 | tf_op jit(solution)/shard_map/near_cell/pallas_call | solution.py:49
  23.8 2.5 %collective-permute-start.4 = (f32[648,128]{1,0:T(8,128)S(1)}, f32[648,128]{1,0:T(8,128)S(1)}, u32[]{:S(2)}, u32[]{:S(2)}) collective-permute-start(f32[648,128]{1,0:T(8,128)S(1)} %get-tuple-element.95.flows), channel_id=1, source_target_pairs={{0,4},{4,0},{8,12},{12,8},{16,20},{20,16},{24,28},{28,24},{1,5},{5... | collective-permute-start | bytes 995336 | tf_op jit(solution)/shard_map/ppermute | solution.py:630
  26.3 0.3 collective-permute-start.8
  26.6 7.1 %collective-permute-done.4.other = f32[648,128]{1,0:T(8,128)S(1)} collective-permute-done((f32[648,128]{1,0:T(8,128)S(1)}, f32[648,128]{1,0:T(8,128)S(1)}, u32[]{:S(2)}, u32[]{:S(2)}) %collective-permute-start.4) | collective-permute-done | bytes 331808 | tf_op jit(solution)/shard_map/ppermute | solution.py:630
  33.7 1.0 %merge_all.2 = (f32[2,30,8,128]{3,2,1,0:T(8,128)S(1)}, f32[648,128]{1,0:T(8,128)S(1)}, f32[2,15,8,128]{3,2,1,0:T(8,128)S(1)}, f32[496,128]{1,0:T(8,128)S(1)}) custom-call(s32[6]{0:T(128)S(1)} %stack.35.flags, f32[648,128]{1,0:T(8,128)S(1)} %get-tuple-element.95.flows, f32[648,128]{1,0:T(8,128)S(1)} %collective-permute-done.4.other), custom_call_target="tpu_custom_call" | custom-call | flops 1000 | bytes 1000 | tf_op jit(solution)/shard_map/merge_all/pallas_call | solution.py:49
  34.7 3.4 %collective-permute-start.6 = (f32[648,128]{1,0:T(8,128)S(1)}, f32[648,128]{1,0:T(8,128)S(1)}, u32[]{:S(2)}, u32[]{:S(2)}) collective-permute-start(f32[648,128]{1,0:T(8,128)S(1)} %get-tuple-element.103.flows), channel_id=1, source_target_pairs={{0,8},{4,12},{8,0},{12,4},{16,24},{20,28},{24,16},{28,20},{1,9},{5... | collective-permute-start | bytes 995336 | tf_op jit(solution)/shard_map/ppermute | solution.py:630
  38.1 0.7 collective-permute-done.5.halo
  38.8 2.2 %far_chunk.2 = (f32[80,32,128]{2,1,0:T(8,128)S(1)}, f32[320,128]{1,0:T(8,128)S(1)}) custom-call(s32[6]{0:T(128)S(1)} %stack.35.flags, f32[80,56,128]{2,1,0:T(8,128)S(1)} %get-tuple-element.98.base, f32[20,56,128]{2,1,0:T(8,128)S(1)} %far_lead.1.lead, f32[1920,128]{1,0:T(8,128)S(1)} %collective-permute-done.5.halo, ...), custom_call_target="tpu_custom_call" | custom-call | flops 1000 | bytes 1000 | tf_op jit(solution)/shard_map/far_chunk/pallas_call | solution.py:49
  41.1 2.2 %collective-permute-start.7 = (f32[320,128]{1,0:T(8,128)S(1)}, f32[320,128]{1,0:T(8,128)S(1)}, u32[]{:S(2)}, u32[]{:S(2)}) collective-permute-start(f32[320,128]{1,0:T(8,128)S(1)} %get-tuple-element.109.flows), channel_id=1, source_target_pairs={{0,4},{4,0},{8,12},{12,8},{16,20},{20,16},{24,28},{28,24},{1,5},{5... | collective-permute-start | bytes 491528 | tf_op jit(solution)/shard_map/ppermute | solution.py:630
  43.3 2.0 %collective-permute-done.6.other = f32[648,128]{1,0:T(8,128)S(1)} collective-permute-done((f32[648,128]{1,0:T(8,128)S(1)}, f32[648,128]{1,0:T(8,128)S(1)}, u32[]{:S(2)}, u32[]{:S(2)}) %collective-permute-start.6) | collective-permute-done | bytes 331808 | tf_op jit(solution)/shard_map/ppermute | solution.py:630
  45.3 1.0 %merge_all.3 = (f32[2,30,8,128]{3,2,1,0:T(8,128)S(1)}, f32[304,128]{1,0:T(8,128)S(1)}, f32[2,15,8,128]{3,2,1,0:T(8,128)S(1)}, f32[496,128]{1,0:T(8,128)S(1)}) custom-call(s32[6]{0:T(128)S(1)} %stack.35.flags, f32[648,128]{1,0:T(8,128)S(1)} %get-tuple-element.103.flows, f32[648,128]{1,0:T(8,128)S(1)} %collective-permute-done.6.other, ...), custom_call_target="tpu_custom_call" | custom-call | flops 1000 | bytes 1000 | tf_op jit(solution)/shard_map/merge_all/pallas_call | solution.py:49
  46.3 2.8 %collective-permute-start.11 = (f32[304,128]{1,0:T(8,128)S(1)}, f32[304,128]{1,0:T(8,128)S(1)}, u32[]{:S(2)}, u32[]{:S(2)}) collective-permute-start(f32[304,128]{1,0:T(8,128)S(1)} %get-tuple-element.124.ends), channel_id=1, source_target_pairs={{0,16},{4,20},{8,24},{12,28},{16,0},{20,4},{24,8},{28,12},{1,17},{... | collective-permute-start | bytes 466952 | tf_op jit(solution)/shard_map/ppermute | solution.py:630
  49.1 0.0 collective-permute-done.7.other
  49.1 0.8 %merge_flows.4 = (f32[320,128]{1,0:T(8,128)S(1)}, f32[320,128]{1,0:T(8,128)S(1)}) custom-call(s32[6]{0:T(128)S(1)} %stack.35.flags, f32[2,30,8,128]{3,2,1,0:T(8,128)S(1)} %get-tuple-element.108.mats, f32[320,128]{1,0:T(8,128)S(1)} %get-tuple-element.109.flows, f32[320,128]{1,0:T(8,128)S(1)} %collective-permute-done.7.other), custom_call_target="tpu_custom_call" | custom-call | flops 1000 | bytes 1000 | tf_op jit(solution)/shard_map/merge_flows/pallas_call | solution.py:49
  49.9 1.6 %collective-permute-start.10 = (f32[320,128]{1,0:T(8,128)S(1)}, f32[320,128]{1,0:T(8,128)S(1)}, u32[]{:S(2)}, u32[]{:S(2)}) collective-permute-start(f32[320,128]{1,0:T(8,128)S(1)} %get-tuple-element.119.flows), channel_id=1, source_target_pairs={{0,8},{4,12},{8,0},{12,4},{16,24},{20,28},{24,16},{28,20},{1,9},{5... | collective-permute-start | bytes 491528 | tf_op jit(solution)/shard_map/ppermute | solution.py:630
  51.5 0.0 collective-permute-done.8.halo
  51.5 1.9 %far_chunk.3 = (f32[80,24,128]{2,1,0:T(8,128)S(1)}, f32[176,128]{1,0:T(8,128)S(1)}) custom-call(s32[6]{0:T(128)S(1)} %stack.35.flags, f32[80,56,128]{2,1,0:T(8,128)S(1)} %get-tuple-element.98.base, f32[20,56,128]{2,1,0:T(8,128)S(1)} %far_lead.1.lead, f32[1024,128]{1,0:T(8,128)S(1)} %collective-permute-done.8.halo, ...), custom_call_target="tpu_custom_call" | custom-call | flops 1000 | bytes 1000 | tf_op jit(solution)/shard_map/far_chunk/pallas_call | solution.py:49
  53.4 0.7 collective-permute-start.9
  54.1 3.9 %collective-permute-done.9.other = f32[176,128]{1,0:T(8,128)S(1)} collective-permute-done((f32[176,128]{1,0:T(8,128)S(1)}, f32[176,128]{1,0:T(8,128)S(1)}, u32[]{:S(2)}, u32[]{:S(2)}) %collective-permute-start.9) | collective-permute-done | bytes 90144 | tf_op jit(solution)/shard_map/ppermute | solution.py:630
  58.0 0.7 merge_flows.5
  58.7 0.0 collective-permute-done.11.other
  58.7 1.3 %collective-permute-start.12 = (f32[176,128]{1,0:T(8,128)S(1)}, f32[176,128]{1,0:T(8,128)S(1)}, u32[]{:S(2)}, u32[]{:S(2)}) collective-permute-start(f32[176,128]{1,0:T(8,128)S(1)} %get-tuple-element.125.flows), channel_id=1, source_target_pairs={{0,8},{4,12},{8,0},{12,4},{16,24},{20,28},{24,16},{28,20},{1,9},{5... | collective-permute-start | bytes 270344 | tf_op jit(solution)/shard_map/ppermute | solution.py:630
  60.0 0.0 collective-permute-done.10.other
  60.0 0.8 %merge_flows.6 = (f32[160,128]{1,0:T(8,128)S(1)}, f32[320,128]{1,0:T(8,128)S(1)}) custom-call(s32[6]{0:T(128)S(1)} %stack.35.flags, f32[2,30,8,128]{3,2,1,0:T(8,128)S(1)} %get-tuple-element.118.mats, f32[320,128]{1,0:T(8,128)S(1)} %get-tuple-element.119.flows, f32[320,128]{1,0:T(8,128)S(1)} %collective-permute-done.10.other, ...), custom_call_target="tpu_custom_call" | custom-call | flops 1000 | bytes 1000 | tf_op jit(solution)/shard_map/merge_flows/pallas_call | solution.py:49
  60.8 2.7 %collective-permute-start.13 = (f32[160,128]{1,0:T(8,128)S(1)}, f32[160,128]{1,0:T(8,128)S(1)}, u32[]{:S(2)}, u32[]{:S(2)}) collective-permute-start(f32[160,128]{1,0:T(8,128)S(1)} %get-tuple-element.137.ends), channel_id=1, source_target_pairs={{0,16},{4,20},{8,24},{12,28},{16,0},{20,4},{24,8},{28,12},{1,17},{... | collective-permute-start | bytes 245768 | tf_op jit(solution)/shard_map/ppermute | solution.py:630
  63.4 0.0 collective-permute-done.12.other
  63.4 0.7 merge_flows.7
  64.1 2.2 %collective-permute-start.14 = (f32[88,128]{1,0:T(8,128)S(1)}, f32[88,128]{1,0:T(8,128)S(1)}, u32[]{:S(2)}, u32[]{:S(2)}) collective-permute-start(f32[88,128]{1,0:T(8,128)S(1)} %get-tuple-element.141.ends), channel_id=1, source_target_pairs={{0,16},{4,20},{8,24},{12,28},{16,0},{20,4},{24,8},{28,12},{1,17},{... | collective-permute-start | bytes 135176 | tf_op jit(solution)/shard_map/ppermute | solution.py:630
  66.3 2.5 %correct_all.1 = (f32[80,56,128]{2,1,0:T(8,128)S(1)}, f32[2,30,8,128]{3,2,1,0:T(8,128)S(1)}) custom-call(s32[6]{0:T(128)S(1)} %stack.35.flags, f32[304,128]{1,0:T(8,128)S(1)} %get-tuple-element.124.ends, f32[304,128]{1,0:T(8,128)S(1)} %collective-permute-done.11.other, f32[2,15,8,128]{3,2,1,0:T(8,128)S(1)} %get-tuple-element.130.share, ...), custom_call_target="tpu_custom_call" | custom-call | flops 1000 | bytes 1000 | tf_op jit(solution)/shard_map/correct_all/pallas_call | solution.py:49
  68.8 0.0 collective-permute-done.13.other
  68.8 1.7 %correct.1.refs_0_ = f32[80,32,128]{2,1,0:T(8,128)S(1)} custom-call(s32[6]{0:T(128)S(1)} %stack.35.flags, f32[2,30,8,128]{3,2,1,0:T(8,128)S(1)} %get-tuple-element.136.mats, f32[160,128]{1,0:T(8,128)S(1)} %get-tuple-element.137.ends, f32[160,128]{1,0:T(8,128)S(1)} %collective-permute-done.13.other, f32[320,128]{1,0:T(8,128)S(1)} %get-tuple-element.138.known, ...), custom_call_target="tpu_custom_call" | custom-call | flops 1000 | bytes 1000 | tf_op jit(solution)/shard_map/correct/pallas_call | solution.py:49
  70.5 0.0 collective-permute-done.14.other
  70.5 2.9 %finish.1 = f32[7840,128]{1,0:T(8,128)} custom-call(s32[6]{0:T(128)S(1)} %stack.35.flags, f32[2,30,8,128]{3,2,1,0:T(8,128)S(1)} %get-tuple-element.136.mats, f32[88,128]{1,0:T(8,128)S(1)} %get-tuple-element.141.ends, f32[88,128]{1,0:T(8,128)S(1)} %collective-permute-done.14.other, f32[176,128]{1,0:T(8,128)S(1)} %get-tuple-element.142.known, ...), custom_call_target="tpu_custom_call" | custom-call | flops 1000 | bytes 1000 | tf_op jit(solution)/shard_map/finish/pallas_call | solution.py:49
  (9 shorter events, 0.0 us)
Async XLA Ops:
  0.0 10.7 %copy-start.5 = (f32[64,192]{1,0:T(8,128)S(1)}, f32[64,192]{1,0:T(8,128)}, u32[]{:S(2)}) copy-start(f32[64,192]{1,0:T(8,128)} %constant.33.clone.turned) | copy-start | bytes 147460
  0.0 10.6 %copy-start.10 = (s32[24]{0:T(128)S(1)}, s32[24]{0:T(128)}, u32[]{:S(2)}) copy-start(s32[24]{0:T(128)} %param.18) | copy-start | bytes 292
  0.0 10.7 %copy-start.8 = (s32[2]{0:T(128)S(1)}, s32[2]{0:T(128)}, u32[]{:S(2)}) copy-start(s32[2]{0:T(128)} %blades.1) | copy-start | bytes 28
  0.1 2.1 %copy-start = (f32[16,2,5,49,128]{4,1,3,2,0:T(2,128)S(1)}, f32[16,2,5,49,128]{4,1,3,2,0:T(2,128)}, u32[]{:S(2)}) copy-start(f32[16,2,5,49,128]{4,1,3,2,0:T(2,128)} %param.11) | copy-start | bytes 12042244
  2.2 8.5 %copy-start.3 = (f32[16,2,5,128]{3,1,2,0:T(2,128)S(1)}, f32[16,2,5,128]{3,1,2,0:T(2,128)}, u32[]{:S(2)}) copy-start(f32[16,2,5,128]{3,1,2,0:T(2,128)} %param.12) | copy-start | bytes 245764
  2.2 8.5 %copy-start.4 = (f32[16,2,5,128]{3,1,2,0:T(2,128)S(1)}, f32[16,2,5,128]{3,1,2,0:T(2,128)}, u32[]{:S(2)}) copy-start(f32[16,2,5,128]{3,1,2,0:T(2,128)} %param.13) | copy-start | bytes 245764
  2.2 8.5 %copy-start.6 = (f32[56,192]{1,0:T(8,128)S(1)}, f32[56,192]{1,0:T(8,128)}, u32[]{:S(2)}) copy-start(f32[56,192]{1,0:T(8,128)} %constant.34.clone.table) | copy-start | bytes 129028
  2.2 8.5 %copy-start.7 = (f32[56,56]{1,0:T(8,128)S(1)}, f32[56,56]{1,0:T(8,128)}, u32[]{:S(2)}) copy-start(f32[56,56]{1,0:T(8,128)} %constant.32.clone.basis) | copy-start | bytes 37636
  2.8 17.6 %collective-permute-start.1 = (f32[80,56,128]{2,1,0:T(8,128)S(1)}, f32[80,56,128]{2,1,0:T(8,128)S(1)}, u32[]{:S(2)}, u32[]{:S(2)}) collective-permute-start(f32[80,56,128]{2,1,0:T(8,128)S(1)} %get-tuple-element.77.xn), channel_id=1, source_target_pairs={{0,1},{1,0},{2,3},{3,2},{4,5},{5,4},{6,7},{7,6},{8,9},{9,8},{10,11... | collective-permute-start | bytes 6881288 | tf_op jit(solution)/shard_map/ppermute | solution.py:656
  3.3 14.5 %collective-permute-start = (f32[980,128]{1,0:T(8,128)S(1)}, f32[980,128]{1,0:T(8,128)S(1)}, u32[]{:S(2)}, u32[]{:S(2)}) collective-permute-start(f32[980,128]{1,0:T(8,128)S(1)} %get-tuple-element.86), channel_id=1, source_target_pairs={{0,3},{1,2},{2,1},{3,0},{4,7},{5,6},{6,5},{7,4},{8,11},{9,10},{10,... | collective-permute-start | bytes 1505288 | tf_op jit(solution)/shard_map/ppermute | solution.py:629
  5.9 14.4 %collective-permute-start.2 = (f32[496,128]{1,0:T(8,128)S(1)}, f32[496,128]{1,0:T(8,128)S(1)}, u32[]{:S(2)}, u32[]{:S(2)}) collective-permute-start(f32[496,128]{1,0:T(8,128)S(1)} %get-tuple-element.90), channel_id=1, source_target_pairs={{0,4},{4,8},{8,12},{12,16},{16,20},{20,24},{24,28},{1,5},{5,9},{9,... | collective-permute-start | bytes 761864 | tf_op jit(solution)/shard_map/ppermute | solution.py:658
  9.3 11.0 %collective-permute-start.3 = (f32[496,128]{1,0:T(8,128)S(1)}, f32[496,128]{1,0:T(8,128)S(1)}, u32[]{:S(2)}, u32[]{:S(2)}) collective-permute-start(f32[496,128]{1,0:T(8,128)S(1)} %get-tuple-element.91), channel_id=1, source_target_pairs={{4,0},{8,4},{12,8},{16,12},{20,16},{24,20},{28,24},{5,1},{9,5},{13... | collective-permute-start | bytes 761864 | tf_op jit(solution)/shard_map/ppermute | solution.py:659
  14.1 24.7 %collective-permute-start.5 = (f32[1920,128]{1,0:T(8,128)S(1)}, f32[1920,128]{1,0:T(8,128)S(1)}, u32[]{:S(2)}, u32[]{:S(2)}) collective-permute-start(f32[1920,128]{1,0:T(8,128)S(1)} %get-tuple-element.100), channel_id=1, source_target_pairs={{0,3},{1,2},{2,1},{3,0},{4,7},{5,6},{6,5},{7,4},{8,11},{9,10},{10,... | collective-permute-start | bytes 2949128 | tf_op jit(solution)/shard_map/ppermute | solution.py:629
  14.2 2.2 %copy-start.1 = (f32[16,2,5,5,128]{4,1,3,2,0:T(2,128)S(1)}, f32[16,2,5,5,128]{4,1,3,2,0:T(2,128)}, u32[]{:S(2)}) copy-start(f32[16,2,5,5,128]{4,1,3,2,0:T(2,128)} %param.15) | copy-start | bytes 1228804
  14.2 2.2 %copy-start.2 = (f32[16,2,5,5,128]{4,1,3,2,0:T(2,128)S(1)}, f32[16,2,5,5,128]{4,1,3,2,0:T(2,128)}, u32[]{:S(2)}) copy-start(f32[16,2,5,5,128]{4,1,3,2,0:T(2,128)} %param.16) | copy-start | bytes 1228804
  14.2 3.4 %copy-start.9 = (bf16[16,2,5,5,128]{4,1,3,2,0:T(2,128)(2,1)S(1)}, bf16[16,2,5,5,128]{4,1,3,2,0:T(2,128)(2,1)}, u32[]{:S(2)}) copy-start(bf16[16,2,5,5,128]{4,1,3,2,0:T(2,128)(2,1)} %param.14) | copy-start | bytes 614404
  23.8 9.9 %collective-permute-start.4 = (f32[648,128]{1,0:T(8,128)S(1)}, f32[648,128]{1,0:T(8,128)S(1)}, u32[]{:S(2)}, u32[]{:S(2)}) collective-permute-start(f32[648,128]{1,0:T(8,128)S(1)} %get-tuple-element.95.flows), channel_id=1, source_target_pairs={{0,4},{4,0},{8,12},{12,8},{16,20},{20,16},{24,28},{28,24},{1,5},{5... | collective-permute-start | bytes 995336 | tf_op jit(solution)/shard_map/ppermute | solution.py:630
  26.3 25.2 %collective-permute-start.8 = (f32[1024,128]{1,0:T(8,128)S(1)}, f32[1024,128]{1,0:T(8,128)S(1)}, u32[]{:S(2)}, u32[]{:S(2)}) collective-permute-start(f32[1024,128]{1,0:T(8,128)S(1)} %get-tuple-element.112), channel_id=1, source_target_pairs={{0,3},{1,2},{2,1},{3,0},{4,7},{5,6},{6,5},{7,4},{8,11},{9,10},{10,... | collective-permute-start | bytes 1572872 | tf_op jit(solution)/shard_map/ppermute | solution.py:629
  34.7 10.5 %collective-permute-start.6 = (f32[648,128]{1,0:T(8,128)S(1)}, f32[648,128]{1,0:T(8,128)S(1)}, u32[]{:S(2)}, u32[]{:S(2)}) collective-permute-start(f32[648,128]{1,0:T(8,128)S(1)} %get-tuple-element.103.flows), channel_id=1, source_target_pairs={{0,8},{4,12},{8,0},{12,4},{16,24},{20,28},{24,16},{28,20},{1,9},{5... | collective-permute-start | bytes 995336 | tf_op jit(solution)/shard_map/ppermute | solution.py:630
  41.1 8.0 %collective-permute-start.7 = (f32[320,128]{1,0:T(8,128)S(1)}, f32[320,128]{1,0:T(8,128)S(1)}, u32[]{:S(2)}, u32[]{:S(2)}) collective-permute-start(f32[320,128]{1,0:T(8,128)S(1)} %get-tuple-element.109.flows), channel_id=1, source_target_pairs={{0,4},{4,0},{8,12},{12,8},{16,20},{20,16},{24,28},{28,24},{1,5},{5... | collective-permute-start | bytes 491528 | tf_op jit(solution)/shard_map/ppermute | solution.py:630
  46.3 12.4 %collective-permute-start.11 = (f32[304,128]{1,0:T(8,128)S(1)}, f32[304,128]{1,0:T(8,128)S(1)}, u32[]{:S(2)}, u32[]{:S(2)}) collective-permute-start(f32[304,128]{1,0:T(8,128)S(1)} %get-tuple-element.124.ends), channel_id=1, source_target_pairs={{0,16},{4,20},{8,24},{12,28},{16,0},{20,4},{24,8},{28,12},{1,17},{... | collective-permute-start | bytes 466952 | tf_op jit(solution)/shard_map/ppermute | solution.py:630
  49.9 10.1 %collective-permute-start.10 = (f32[320,128]{1,0:T(8,128)S(1)}, f32[320,128]{1,0:T(8,128)S(1)}, u32[]{:S(2)}, u32[]{:S(2)}) collective-permute-start(f32[320,128]{1,0:T(8,128)S(1)} %get-tuple-element.119.flows), channel_id=1, source_target_pairs={{0,8},{4,12},{8,0},{12,4},{16,24},{20,28},{24,16},{28,20},{1,9},{5... | collective-permute-start | bytes 491528 | tf_op jit(solution)/shard_map/ppermute | solution.py:630
  53.4 4.6 %collective-permute-start.9 = (f32[176,128]{1,0:T(8,128)S(1)}, f32[176,128]{1,0:T(8,128)S(1)}, u32[]{:S(2)}, u32[]{:S(2)}) collective-permute-start(f32[176,128]{1,0:T(8,128)S(1)} %get-tuple-element.115.flows), channel_id=1, source_target_pairs={{0,4},{4,0},{8,12},{12,8},{16,20},{20,16},{24,28},{28,24},{1,5},{5... | collective-permute-start | bytes 270344 | tf_op jit(solution)/shard_map/ppermute | solution.py:630
  58.7 4.7 %collective-permute-start.12 = (f32[176,128]{1,0:T(8,128)S(1)}, f32[176,128]{1,0:T(8,128)S(1)}, u32[]{:S(2)}, u32[]{:S(2)}) collective-permute-start(f32[176,128]{1,0:T(8,128)S(1)} %get-tuple-element.125.flows), channel_id=1, source_target_pairs={{0,8},{4,12},{8,0},{12,4},{16,24},{20,28},{24,16},{28,20},{1,9},{5... | collective-permute-start | bytes 270344 | tf_op jit(solution)/shard_map/ppermute | solution.py:630
  60.8 8.1 %collective-permute-start.13 = (f32[160,128]{1,0:T(8,128)S(1)}, f32[160,128]{1,0:T(8,128)S(1)}, u32[]{:S(2)}, u32[]{:S(2)}) collective-permute-start(f32[160,128]{1,0:T(8,128)S(1)} %get-tuple-element.137.ends), channel_id=1, source_target_pairs={{0,16},{4,20},{8,24},{12,28},{16,0},{20,4},{24,8},{28,12},{1,17},{... | collective-permute-start | bytes 245768 | tf_op jit(solution)/shard_map/ppermute | solution.py:630
  64.1 6.4 %collective-permute-start.14 = (f32[88,128]{1,0:T(8,128)S(1)}, f32[88,128]{1,0:T(8,128)S(1)}, u32[]{:S(2)}, u32[]{:S(2)}) collective-permute-start(f32[88,128]{1,0:T(8,128)S(1)} %get-tuple-element.141.ends), channel_id=1, source_target_pairs={{0,16},{4,20},{8,24},{12,28},{16,0},{20,4},{24,8},{28,12},{1,17},{... | collective-permute-start | bytes 135176 | tf_op jit(solution)/shard_map/ppermute | solution.py:630

commit v10 on v9

--- a/solution.py
+++ b/solution.py
@@ -558,40 +558,42 @@
     correct(part, levels, flags, mats, ends, other, known, blocks, g, result, inflow)
 
 
-def finish(levels, flags, mats, ends, other, known, g, blocks, near, *refs):
-    done, (out, inflow, held, sems) = refs[:-4], refs[-4:]
+def finish(levels, flags, mats, blocks, near, *refs):
+    count = len(CHUNKS)
+    (out, held, sems), inflows = refs[4 * count : 4 * count + 3], refs[4 * count + 3 :]
     right = flags[2 + levels] == 1
     p = flags[0]
-    (first_row, last_row), last_extra = CHUNKS[-1]
-    width, height = last_row - first_row, rows_of(CHUNKS[-1])
-    part = (1, split_height(height, last_extra), last_extra)
-    last_inflow(right, part, mats, ends, other, known, inflow)
-    flow = tuple(inflow[i] for i in range(2 * V))
+    chunks = []
+    for i, ((first, last), extra) in enumerate(CHUNKS):
+        ends, other, known, g = refs[4 * i : 4 * i + 4]
+        height = g.shape[1]
+        part = (1, split_height(height, extra), extra)
+        last_inflow(right, part, mats, ends, other, known, inflows[i])
+        chunks.append((first, last - first, height, extra, g, inflows[i]))
+    flows = [tuple(inflow[i] for i in range(2 * V)) for *_, inflow in chunks]
 
     def step(z, carry):
         for a in range(V):
             j = z * V + a
             row = j * 2 * NT
             held[pl.ds(row + 1 - p, NT, stride=2), :] = near[j, 0:NT, :]
-            for ref, ((first, last), extra) in zip(done, CHUNKS):
-                held[pl.ds(row + p + 2 * first, last - first, stride=2), :] = ref[j, 0 : last - first, :]
+            for (first, width, height, extra, g, _), flow in zip(chunks, flows):
+                value = corrected(1, z, a, 0, height, g, blocks, flow)
+                held[pl.ds(row + p + 2 * first, width, stride=2), :] = value[:width]
                 if extra:
-                    held[pl.ds(row + p + 2 * (NT - 1), 1), :] = ref[j, last - first : last - first + 1, :]
-            value = corrected(1, z, a, 0, height, g, blocks, flow)
-            held[pl.ds(row + p + 2 * first_row, width, stride=2), :] = value[:width]
-            if last_extra:
-                held[pl.ds(row + p + 2 * (NT - 1), 1), :] = value[width : width + 1]
+                    held[pl.ds(row + p + 2 * (NT - 1), 1), :] = value[width : width + 1]
         return carry
 
-    parts = sems.shape[0]
-    cells = g.shape[0] // V // parts
-    size = held.shape[0] // parts
-    copies = []
-    for i in range(parts):
-        lax.fori_loop(i * cells, (i + 1) * cells, step, 0, unroll=2)
-        span = pl.ds(i * size, size)
+    cells = near.shape[0] // V
+    stops = [cells // 4, cells // 2, cells * 3 // 4, cells - 1, cells]
+    copies, cell, row = [], 0, 0
+    for i, stop in enumerate(stops):
+        lax.fori_loop(cell, stop, step, 0, unroll=2 if (stop - cell) % 2 == 0 else 1)
+        size = stop * V * NT * 2 // 8 * 8 - row
+        span = pl.ds(row, size)
         copies.append(pltpu.make_async_copy(held.at[span, :], out.at[span, :], sems.at[i]))
         copies[-1].start()
+        cell, row = stop, row + size
     for copy in copies:
         copy.wait()
 
@@ -783,19 +785,15 @@
     for k in range(1, levels - 1):
         third.step()
     near = first.correct()
-    done = [second.correct()]
-    g_last = third.solved
     third.send()
-    small = [mats[-1], *third.last()]
-
+    operands = [mats[-1], blocks, near]
+    for item in (second, third):
+        operands += [*item.last(), item.solved]
     out = run(
-        functools.partial(finish, levels), [st.shape], [*small, g_last, blocks, near, *done],
+        functools.partial(finish, levels), [st.shape], operands,
         out_specs=[pl.BlockSpec(memory_space=pltpu.HBM)],
-        scratch=[
-            pltpu.VMEM((2 * V, rows_of(CHUNKS[-1]), LANES), F32),
-            pltpu.VMEM(st.shape, F32),
-            pltpu.SemaphoreType.DMA((4,)),
-        ],
+        scratch=[pltpu.VMEM(st.shape, F32), pltpu.SemaphoreType.DMA((5,))]
+        + [pltpu.VMEM((2 * V, rows_of(chunk), LANES), F32) for chunk in CHUNKS],
         name="finish",
     )[0]
     return out.reshape(cells, V, NT, 2, LANES).transpose(0, 3, 1, 2, 4)

time: 73.6 us -> 72.9 us (level)
  Pallas kernels: 28 us -> 27 us
    pallas_call x16 -> x15, Pallas kernels: 27.5 us -> 26.5 us  [__call__(): pl.pallas_call(body, out_shape=[jax.ShapeDtypeStruct(s, F32) for s in out...]
  transfers between devices with their start and end apart: 15 -> 15, of which waited for: 5 -> 6; matrix products, arithmetic and copies ran while one was open for 0% -> 0% of each run, Pallas kernels for 33% -> 31%
where the time goes in v10:
time: 72.9 us; the launch traced here: 72.7 us
  starting transfers between devices  27.6 us (38%)
  Pallas kernels  27 us (37%)
  waiting for transfers between devices  15.4 us (21%)
  local copies, waits for them, and re-layouts  2.34 us (3%)
    pallas_call x15, Pallas kernels, __call__(): pl.pallas_call(body, out_shape=[jax.ShapeDtypeStruct(s, F32) for s in out...  26.5 us
    ppermute x9, starting transfers between devices, local(): lax.ppermute(x, 'seg', [(i, i ^ 1 << k) for i in range(segs)])  19.4 us
    ppermute x9, waiting for transfers between devices, local(): lax.ppermute(x, 'seg', [(i, i ^ 1 << k) for i in range(segs)])  13.3 us
    ppermute x1, starting transfers between devices, local(): lax.ppermute(last_cell, 'seg', [(i, i + 1) for i in range(segs - 1)])  3.4 us
    ppermute x3, starting transfers between devices, local(): to_far = lambda x: lax.ppermute(x, 'pitch', far_pairs)  2.97 us
    unnamed x22, local copies, waits for them, and re-layouts  2.18 us
  transfers between devices with their start and end apart: 15, of which 6 were waited for; matrix products, arithmetic and copies ran while one was open for 0% of the time, Pallas kernels for 31%

profile of v10, /device:TPU:0, one launch (start us, length us, event | category | flops | bytes accessed | tf_op | source)
XLA Modules:
  0.0 72.7 jit_solution(5682289515202314372)
XLA Ops:
  0.0 0.0 copy-start.5
  0.0 0.1 stack.35.flags
  0.1 2.1 %copy-done = f32[16,2,5,49,128]{4,1,3,2,0:T(2,128)S(1)} copy-done((f32[16,2,5,49,128]{4,1,3,2,0:T(2,128)S(1)}, f32[16,2,5,49,128]{4,1,3,2,0:T(2,128)}, u32[]{:S(2)}) %copy-start) | copy-done | bytes 4014104
  2.2 0.5 split_cells.1
  2.8 0.5 collective-permute-start.1
  3.3 2.6 %collective-permute-start = (f32[980,128]{1,0:T(8,128)S(1)}, f32[980,128]{1,0:T(8,128)S(1)}, u32[]{:S(2)}, u32[]{:S(2)}) collective-permute-start(f32[980,128]{1,0:T(8,128)S(1)} %get-tuple-element.84), channel_id=1, source_target_pairs={{0,3},{1,2},{2,1},{3,0},{4,7},{5,6},{6,5},{7,4},{8,11},{9,10},{10,... | collective-permute-start | bytes 1505288 | tf_op jit(solution)/shard_map/ppermute | solution.py:631
  5.9 3.4 %collective-permute-start.2 = (f32[496,128]{1,0:T(8,128)S(1)}, f32[496,128]{1,0:T(8,128)S(1)}, u32[]{:S(2)}, u32[]{:S(2)}) collective-permute-start(f32[496,128]{1,0:T(8,128)S(1)} %get-tuple-element.88), channel_id=1, source_target_pairs={{0,4},{4,8},{8,12},{12,16},{16,20},{20,24},{24,28},{1,5},{5,9},{9,... | collective-permute-start | bytes 761864 | tf_op jit(solution)/shard_map/ppermute | solution.py:660
  9.3 1.3 %collective-permute-start.3 = (f32[496,128]{1,0:T(8,128)S(1)}, f32[496,128]{1,0:T(8,128)S(1)}, u32[]{:S(2)}, u32[]{:S(2)}) collective-permute-start(f32[496,128]{1,0:T(8,128)S(1)} %get-tuple-element.89), channel_id=1, source_target_pairs={{4,0},{8,4},{12,8},{16,12},{20,16},{24,20},{28,24},{5,1},{9,5},{13... | collective-permute-start | bytes 761864 | tf_op jit(solution)/shard_map/ppermute | solution.py:661
  10.6 0.0 copy-done.10
  10.7 0.1 broadcast_in_dim.2.harmonic
  10.7 0.0 copy-done.5
  10.7 0.0 copy-done.8
  10.7 0.0 copy-done.3
  10.8 0.0 copy-done.4
  10.8 0.0 copy-done.6
  10.8 0.0 copy-done.7
  10.8 3.3 %prepare.1 = (f32[56,128]{1,0:T(8,128)S(1)}, f32[80,56,128]{2,1,0:T(8,128)S(1)}, f32[1920,128]{1,0:T(8,128)S(1)}, f32[1024,128]{1,0:T(8,128)S(1)}) custom-call(s32[6]{0:T(128)S(1)} %stack.35.flags, s32[2]{0:T(128)S(1)} %copy-done.8, f32[80,56,128]{2,1,0:T(8,128)S(1)} %get-tuple-element.75.xn, f32[80,56,128]{2,1,0:T(8,128)S(1)} %get-tuple-element.76.xf, ...), custom_call_target="tpu_custom_call" | custom-call | flops 1000 | bytes 1000 | tf_op jit(solution)/shard_map/prepare/pallas_call | solution.py:49
  14.1 0.1 collective-permute-start.5
  14.2 0.0 copy-start.1
  14.2 0.0 copy-start.2
  14.2 0.0 copy-start.9
  14.2 2.1 %near_base.1.base = f32[80,56,128]{2,1,0:T(8,128)S(1)} custom-call(s32[6]{0:T(128)S(1)} %stack.35.flags, f32[80,56,128]{2,1,0:T(8,128)S(1)} %get-tuple-element.75.xn, f32[80,56,128]{2,1,0:T(8,128)S(1)} %get-tuple-element.76.xf, f32[160,128]{1,0:T(8,128)S(1)} %bitcast.40, f32[160,128]{1,0:T(8,128)S(1)} %bitcast.45, f32[56,192]{1,0:T(8,128)S(1)} %copy-done.6, ...), custom_call_target="tpu_custom_call" | custom-call | bytes 1000 | tf_op jit(solution)/shard_map/near_base/pallas_call | solution.py:49
  16.4 0.0 copy-done.1
  16.4 0.0 copy-done.2
  16.4 1.3 %transfer.1 = (f32[2,80,16,128]{3,2,1,0:T(8,128)S(1)}, f32[152,128]{1,0:T(8,128)S(1)}) custom-call(s32[6]{0:T(128)S(1)} %stack.35.flags, f32[800,128]{1,0:T(8,128)S(1)} %bitcast.28, f32[800,128]{1,0:T(8,128)S(1)} %bitcast.32), custom_call_target="tpu_custom_call" | custom-call | bytes 1000 | tf_op jit(solution)/shard_map/transfer/pallas_call | solution.py:49
  17.6 0.0 copy-done.9
  17.7 0.1 reshape.36
  17.8 0.0 collective-permute-done.slab
  17.8 1.2 %far_lead.1.lead = f32[20,56,128]{2,1,0:T(8,128)S(1)} custom-call(s32[6]{0:T(128)S(1)} %stack.35.flags, f32[980,128]{1,0:T(8,128)S(1)} %collective-permute-done.slab, f32[56,128]{1,0:T(8,128)S(1)} %get-tuple-element.79.trig, f32[56,56]{1,0:T(8,128)S(1)} %copy-done.7, f32[64,192]{1,0:T(8,128)S(1)} %copy-done.5), custom_call_target="tpu_custom_call" | custom-call | bytes 1000 | tf_op jit(solution)/shard_map/far_lead/pallas_call | solution.py:49
  19.0 1.4 %collective-permute-done.2.from_left = f32[496,128]{1,0:T(8,128)S(1)} collective-permute-done((f32[496,128]{1,0:T(8,128)S(1)}, f32[496,128]{1,0:T(8,128)S(1)}, u32[]{:S(2)}, u32[]{:S(2)}) %collective-permute-start.2) | collective-permute-done | bytes 253984 | tf_op jit(solution)/shard_map/ppermute | solution.py:660
  20.4 0.0 collective-permute-done.3.from_right
  20.4 0.0 collective-permute-done.1.halo
  20.4 3.4 %near_cell.1 = (f32[80,56,128]{2,1,0:T(8,128)S(1)}, f32[648,128]{1,0:T(8,128)S(1)}) custom-call(s32[6]{0:T(128)S(1)} %stack.35.flags, f32[80,56,128]{2,1,0:T(8,128)S(1)} %near_base.1.base, f32[80,56,128]{2,1,0:T(8,128)S(1)} %collective-permute-done.1.halo, f32[496,128]{1,0:T(8,128)S(1)} %collective-permute-done.2.from_left, ...), custom_call_target="tpu_custom_call" | custom-call | flops 6000000000 | bytes 1000 | tf_op jit(solution)/shard_map/near_cell/pallas_call | solution.py:49
  23.8 2.5 %collective-permute-start.4 = (f32[648,128]{1,0:T(8,128)S(1)}, f32[648,128]{1,0:T(8,128)S(1)}, u32[]{:S(2)}, u32[]{:S(2)}) collective-permute-start(f32[648,128]{1,0:T(8,128)S(1)} %get-tuple-element.93.flows), channel_id=1, source_target_pairs={{0,4},{4,0},{8,12},{12,8},{16,20},{20,16},{24,28},{28,24},{1,5},{5... | collective-permute-start | bytes 995336 | tf_op jit(solution)/shard_map/ppermute | solution.py:632
  26.3 0.3 collective-permute-start.8
  26.6 7.1 %collective-permute-done.4.other = f32[648,128]{1,0:T(8,128)S(1)} collective-permute-done((f32[648,128]{1,0:T(8,128)S(1)}, f32[648,128]{1,0:T(8,128)S(1)}, u32[]{:S(2)}, u32[]{:S(2)}) %collective-permute-start.4) | collective-permute-done | bytes 331808 | tf_op jit(solution)/shard_map/ppermute | solution.py:632
  33.7 1.0 %merge_all.2 = (f32[2,30,8,128]{3,2,1,0:T(8,128)S(1)}, f32[648,128]{1,0:T(8,128)S(1)}, f32[2,15,8,128]{3,2,1,0:T(8,128)S(1)}, f32[496,128]{1,0:T(8,128)S(1)}) custom-call(s32[6]{0:T(128)S(1)} %stack.35.flags, f32[648,128]{1,0:T(8,128)S(1)} %get-tuple-element.93.flows, f32[648,128]{1,0:T(8,128)S(1)} %collective-permute-done.4.other), custom_call_target="tpu_custom_call" | custom-call | flops 1000 | bytes 1000 | tf_op jit(solution)/shard_map/merge_all/pallas_call | solution.py:49
  34.7 3.4 %collective-permute-start.6 = (f32[648,128]{1,0:T(8,128)S(1)}, f32[648,128]{1,0:T(8,128)S(1)}, u32[]{:S(2)}, u32[]{:S(2)}) collective-permute-start(f32[648,128]{1,0:T(8,128)S(1)} %get-tuple-element.101.flows), channel_id=1, source_target_pairs={{0,8},{4,12},{8,0},{12,4},{16,24},{20,28},{24,16},{28,20},{1,9},{5... | collective-permute-start | bytes 995336 | tf_op jit(solution)/shard_map/ppermute | solution.py:632
  38.1 0.7 collective-permute-done.5.halo
  38.8 2.2 %far_chunk.2 = (f32[80,32,128]{2,1,0:T(8,128)S(1)}, f32[320,128]{1,0:T(8,128)S(1)}) custom-call(s32[6]{0:T(128)S(1)} %stack.35.flags, f32[80,56,128]{2,1,0:T(8,128)S(1)} %get-tuple-element.96.base, f32[20,56,128]{2,1,0:T(8,128)S(1)} %far_lead.1.lead, f32[1920,128]{1,0:T(8,128)S(1)} %collective-permute-done.5.halo, ...), custom_call_target="tpu_custom_call" | custom-call | flops 1000 | bytes 1000 | tf_op jit(solution)/shard_map/far_chunk/pallas_call | solution.py:49
  41.1 2.2 %collective-permute-start.7 = (f32[320,128]{1,0:T(8,128)S(1)}, f32[320,128]{1,0:T(8,128)S(1)}, u32[]{:S(2)}, u32[]{:S(2)}) collective-permute-start(f32[320,128]{1,0:T(8,128)S(1)} %get-tuple-element.107.flows), channel_id=1, source_target_pairs={{0,4},{4,0},{8,12},{12,8},{16,20},{20,16},{24,28},{28,24},{1,5},{5... | collective-permute-start | bytes 491528 | tf_op jit(solution)/shard_map/ppermute | solution.py:632
  43.3 2.0 %collective-permute-done.6.other = f32[648,128]{1,0:T(8,128)S(1)} collective-permute-done((f32[648,128]{1,0:T(8,128)S(1)}, f32[648,128]{1,0:T(8,128)S(1)}, u32[]{:S(2)}, u32[]{:S(2)}) %collective-permute-start.6) | collective-permute-done | bytes 331808 | tf_op jit(solution)/shard_map/ppermute | solution.py:632
  45.3 1.0 %merge_all.3 = (f32[2,30,8,128]{3,2,1,0:T(8,128)S(1)}, f32[304,128]{1,0:T(8,128)S(1)}, f32[2,15,8,128]{3,2,1,0:T(8,128)S(1)}, f32[496,128]{1,0:T(8,128)S(1)}) custom-call(s32[6]{0:T(128)S(1)} %stack.35.flags, f32[648,128]{1,0:T(8,128)S(1)} %get-tuple-element.101.flows, f32[648,128]{1,0:T(8,128)S(1)} %collective-permute-done.6.other, ...), custom_call_target="tpu_custom_call" | custom-call | flops 1000 | bytes 1000 | tf_op jit(solution)/shard_map/merge_all/pallas_call | solution.py:49
  46.3 2.8 %collective-permute-start.11 = (f32[304,128]{1,0:T(8,128)S(1)}, f32[304,128]{1,0:T(8,128)S(1)}, u32[]{:S(2)}, u32[]{:S(2)}) collective-permute-start(f32[304,128]{1,0:T(8,128)S(1)} %get-tuple-element.122.ends), channel_id=1, source_target_pairs={{0,16},{4,20},{8,24},{12,28},{16,0},{20,4},{24,8},{28,12},{1,17},{... | collective-permute-start | bytes 466952 | tf_op jit(solution)/shard_map/ppermute | solution.py:632
  49.1 0.0 collective-permute-done.7.other
  49.1 0.8 %merge_flows.4 = (f32[320,128]{1,0:T(8,128)S(1)}, f32[320,128]{1,0:T(8,128)S(1)}) custom-call(s32[6]{0:T(128)S(1)} %stack.35.flags, f32[2,30,8,128]{3,2,1,0:T(8,128)S(1)} %get-tuple-element.106.mats, f32[320,128]{1,0:T(8,128)S(1)} %get-tuple-element.107.flows, f32[320,128]{1,0:T(8,128)S(1)} %collective-permute-done.7.other), custom_call_target="tpu_custom_call" | custom-call | flops 1000 | bytes 1000 | tf_op jit(solution)/shard_map/merge_flows/pallas_call | solution.py:49
  49.9 1.6 %collective-permute-start.10 = (f32[320,128]{1,0:T(8,128)S(1)}, f32[320,128]{1,0:T(8,128)S(1)}, u32[]{:S(2)}, u32[]{:S(2)}) collective-permute-start(f32[320,128]{1,0:T(8,128)S(1)} %get-tuple-element.117.flows), channel_id=1, source_target_pairs={{0,8},{4,12},{8,0},{12,4},{16,24},{20,28},{24,16},{28,20},{1,9},{5... | collective-permute-start | bytes 491528 | tf_op jit(solution)/shard_map/ppermute | solution.py:632
  51.5 0.0 collective-permute-done.8.halo
  51.5 1.9 %far_chunk.3 = (f32[80,24,128]{2,1,0:T(8,128)S(1)}, f32[176,128]{1,0:T(8,128)S(1)}) custom-call(s32[6]{0:T(128)S(1)} %stack.35.flags, f32[80,56,128]{2,1,0:T(8,128)S(1)} %get-tuple-element.96.base, f32[20,56,128]{2,1,0:T(8,128)S(1)} %far_lead.1.lead, f32[1024,128]{1,0:T(8,128)S(1)} %collective-permute-done.8.halo, ...), custom_call_target="tpu_custom_call" | custom-call | flops 1000 | bytes 1000 | tf_op jit(solution)/shard_map/far_chunk/pallas_call | solution.py:49
  53.4 0.7 collective-permute-start.9
  54.1 3.9 %collective-permute-done.9.other = f32[176,128]{1,0:T(8,128)S(1)} collective-permute-done((f32[176,128]{1,0:T(8,128)S(1)}, f32[176,128]{1,0:T(8,128)S(1)}, u32[]{:S(2)}, u32[]{:S(2)}) %collective-permute-start.9) | collective-permute-done | bytes 90144 | tf_op jit(solution)/shard_map/ppermute | solution.py:632
  58.0 0.7 merge_flows.5
  58.7 0.0 collective-permute-done.11.other
  58.7 1.3 %collective-permute-start.12 = (f32[176,128]{1,0:T(8,128)S(1)}, f32[176,128]{1,0:T(8,128)S(1)}, u32[]{:S(2)}, u32[]{:S(2)}) collective-permute-start(f32[176,128]{1,0:T(8,128)S(1)} %get-tuple-element.123.flows), channel_id=1, source_target_pairs={{0,8},{4,12},{8,0},{12,4},{16,24},{20,28},{24,16},{28,20},{1,9},{5... | collective-permute-start | bytes 270344 | tf_op jit(solution)/shard_map/ppermute | solution.py:632
  60.0 0.0 collective-permute-done.10.other
  60.0 0.8 %merge_flows.6 = (f32[160,128]{1,0:T(8,128)S(1)}, f32[320,128]{1,0:T(8,128)S(1)}) custom-call(s32[6]{0:T(128)S(1)} %stack.35.flags, f32[2,30,8,128]{3,2,1,0:T(8,128)S(1)} %get-tuple-element.116.mats, f32[320,128]{1,0:T(8,128)S(1)} %get-tuple-element.117.flows, f32[320,128]{1,0:T(8,128)S(1)} %collective-permute-done.10.other, ...), custom_call_target="tpu_custom_call" | custom-call | flops 1000 | bytes 1000 | tf_op jit(solution)/shard_map/merge_flows/pallas_call | solution.py:49
  60.8 2.7 %collective-permute-start.13 = (f32[160,128]{1,0:T(8,128)S(1)}, f32[160,128]{1,0:T(8,128)S(1)}, u32[]{:S(2)}, u32[]{:S(2)}) collective-permute-start(f32[160,128]{1,0:T(8,128)S(1)} %get-tuple-element.136.refs_0_), channel_id=1, source_target_pairs={{0,16},{4,20},{8,24},{12,28},{16,0},{20,4},{24,8},{28,12},{1,17},{... | collective-permute-start | bytes 245768 | tf_op jit(solution)/shard_map/ppermute | solution.py:632
  63.4 0.0 collective-permute-done.12.other
  63.4 0.7 merge_flows.7
  64.1 2.2 %collective-permute-start.14 = (f32[88,128]{1,0:T(8,128)S(1)}, f32[88,128]{1,0:T(8,128)S(1)}, u32[]{:S(2)}, u32[]{:S(2)}) collective-permute-start(f32[88,128]{1,0:T(8,128)S(1)} %get-tuple-element.139.refs_4_), channel_id=1, source_target_pairs={{0,16},{4,20},{8,24},{12,28},{16,0},{20,4},{24,8},{28,12},{1,17},{... | collective-permute-start | bytes 135176 | tf_op jit(solution)/shard_map/ppermute | solution.py:632
  66.3 2.5 %correct_all.1 = (f32[80,56,128]{2,1,0:T(8,128)S(1)}, f32[2,30,8,128]{3,2,1,0:T(8,128)S(1)}) custom-call(s32[6]{0:T(128)S(1)} %stack.35.flags, f32[304,128]{1,0:T(8,128)S(1)} %get-tuple-element.122.ends, f32[304,128]{1,0:T(8,128)S(1)} %collective-permute-done.11.other, f32[2,15,8,128]{3,2,1,0:T(8,128)S(1)} %get-tuple-element.128.share, ...), custom_call_target="tpu_custom_call" | custom-call | flops 1000 | bytes 1000 | tf_op jit(solution)/shard_map/correct_all/pallas_call | solution.py:49
  68.8 0.0 collective-permute-done.13.refs_1_
  68.8 0.3 collective-permute-done.14.refs_5_
  69.1 3.6 %finish.1 = f32[7840,128]{1,0:T(8,128)} custom-call(s32[6]{0:T(128)S(1)} %stack.35.flags, f32[2,30,8,128]{3,2,1,0:T(8,128)S(1)} %get-tuple-element.134.mats, f32[2,80,16,128]{3,2,1,0:T(8,128)S(1)} %get-tuple-element.130.blocks, f32[80,56,128]{2,1,0:T(8,128)S(1)} %get-tuple-element.135.near, f32[160,128]{1,0:T(8,128)S(1)} %get-tuple-element.136.refs_0_, ...), custom_call_target="tpu_custom_call" | custom-call | flops 1000 | bytes 1000 | tf_op jit(solution)/shard_map/finish/pallas_call | solution.py:49
  (8 shorter events, 0.0 us)
Async XLA Ops:
  0.0 10.7 %copy-start.5 = (f32[64,192]{1,0:T(8,128)S(1)}, f32[64,192]{1,0:T(8,128)}, u32[]{:S(2)}) copy-start(f32[64,192]{1,0:T(8,128)} %constant.33.clone.turned) | copy-start | bytes 147460
  0.0 10.6 %copy-start.10 = (s32[24]{0:T(128)S(1)}, s32[24]{0:T(128)}, u32[]{:S(2)}) copy-start(s32[24]{0:T(128)} %param.18) | copy-start | bytes 292
  0.0 10.7 %copy-start.8 = (s32[2]{0:T(128)S(1)}, s32[2]{0:T(128)}, u32[]{:S(2)}) copy-start(s32[2]{0:T(128)} %blades.1) | copy-start | bytes 28
  0.1 2.1 %copy-start = (f32[16,2,5,49,128]{4,1,3,2,0:T(2,128)S(1)}, f32[16,2,5,49,128]{4,1,3,2,0:T(2,128)}, u32[]{:S(2)}) copy-start(f32[16,2,5,49,128]{4,1,3,2,0:T(2,128)} %param.11) | copy-start | bytes 12042244
  2.2 8.5 %copy-start.3 = (f32[16,2,5,128]{3,1,2,0:T(2,128)S(1)}, f32[16,2,5,128]{3,1,2,0:T(2,128)}, u32[]{:S(2)}) copy-start(f32[16,2,5,128]{3,1,2,0:T(2,128)} %param.12) | copy-start | bytes 245764
  2.2 8.5 %copy-start.4 = (f32[16,2,5,128]{3,1,2,0:T(2,128)S(1)}, f32[16,2,5,128]{3,1,2,0:T(2,128)}, u32[]{:S(2)}) copy-start(f32[16,2,5,128]{3,1,2,0:T(2,128)} %param.13) | copy-start | bytes 245764
  2.2 8.5 %copy-start.6 = (f32[56,192]{1,0:T(8,128)S(1)}, f32[56,192]{1,0:T(8,128)}, u32[]{:S(2)}) copy-start(f32[56,192]{1,0:T(8,128)} %constant.34.clone.table) | copy-start | bytes 129028
  2.2 8.5 %copy-start.7 = (f32[56,56]{1,0:T(8,128)S(1)}, f32[56,56]{1,0:T(8,128)}, u32[]{:S(2)}) copy-start(f32[56,56]{1,0:T(8,128)} %constant.32.clone.basis) | copy-start | bytes 37636
  2.8 17.6 %collective-permute-start.1 = (f32[80,56,128]{2,1,0:T(8,128)S(1)}, f32[80,56,128]{2,1,0:T(8,128)S(1)}, u32[]{:S(2)}, u32[]{:S(2)}) collective-permute-start(f32[80,56,128]{2,1,0:T(8,128)S(1)} %get-tuple-element.75.xn), channel_id=1, source_target_pairs={{0,1},{1,0},{2,3},{3,2},{4,5},{5,4},{6,7},{7,6},{8,9},{9,8},{10,11... | collective-permute-start | bytes 6881288 | tf_op jit(solution)/shard_map/ppermute | solution.py:658
  3.3 14.5 %collective-permute-start = (f32[980,128]{1,0:T(8,128)S(1)}, f32[980,128]{1,0:T(8,128)S(1)}, u32[]{:S(2)}, u32[]{:S(2)}) collective-permute-start(f32[980,128]{1,0:T(8,128)S(1)} %get-tuple-element.84), channel_id=1, source_target_pairs={{0,3},{1,2},{2,1},{3,0},{4,7},{5,6},{6,5},{7,4},{8,11},{9,10},{10,... | collective-permute-start | bytes 1505288 | tf_op jit(solution)/shard_map/ppermute | solution.py:631
  5.9 14.4 %collective-permute-start.2 = (f32[496,128]{1,0:T(8,128)S(1)}, f32[496,128]{1,0:T(8,128)S(1)}, u32[]{:S(2)}, u32[]{:S(2)}) collective-permute-start(f32[496,128]{1,0:T(8,128)S(1)} %get-tuple-element.88), channel_id=1, source_target_pairs={{0,4},{4,8},{8,12},{12,16},{16,20},{20,24},{24,28},{1,5},{5,9},{9,... | collective-permute-start | bytes 761864 | tf_op jit(solution)/shard_map/ppermute | solution.py:660
  9.3 11.0 %collective-permute-start.3 = (f32[496,128]{1,0:T(8,128)S(1)}, f32[496,128]{1,0:T(8,128)S(1)}, u32[]{:S(2)}, u32[]{:S(2)}) collective-permute-start(f32[496,128]{1,0:T(8,128)S(1)} %get-tuple-element.89), channel_id=1, source_target_pairs={{4,0},{8,4},{12,8},{16,12},{20,16},{24,20},{28,24},{5,1},{9,5},{13... | collective-permute-start | bytes 761864 | tf_op jit(solution)/shard_map/ppermute | solution.py:661
  14.1 24.7 %collective-permute-start.5 = (f32[1920,128]{1,0:T(8,128)S(1)}, f32[1920,128]{1,0:T(8,128)S(1)}, u32[]{:S(2)}, u32[]{:S(2)}) collective-permute-start(f32[1920,128]{1,0:T(8,128)S(1)} %get-tuple-element.98), channel_id=1, source_target_pairs={{0,3},{1,2},{2,1},{3,0},{4,7},{5,6},{6,5},{7,4},{8,11},{9,10},{10,... | collective-permute-start | bytes 2949128 | tf_op jit(solution)/shard_map/ppermute | solution.py:631
  14.2 2.2 %copy-start.1 = (f32[16,2,5,5,128]{4,1,3,2,0:T(2,128)S(1)}, f32[16,2,5,5,128]{4,1,3,2,0:T(2,128)}, u32[]{:S(2)}) copy-start(f32[16,2,5,5,128]{4,1,3,2,0:T(2,128)} %param.15) | copy-start | bytes 1228804
  14.2 2.2 %copy-start.2 = (f32[16,2,5,5,128]{4,1,3,2,0:T(2,128)S(1)}, f32[16,2,5,5,128]{4,1,3,2,0:T(2,128)}, u32[]{:S(2)}) copy-start(f32[16,2,5,5,128]{4,1,3,2,0:T(2,128)} %param.16) | copy-start | bytes 1228804
  14.2 3.4 %copy-start.9 = (bf16[16,2,5,5,128]{4,1,3,2,0:T(2,128)(2,1)S(1)}, bf16[16,2,5,5,128]{4,1,3,2,0:T(2,128)(2,1)}, u32[]{:S(2)}) copy-start(bf16[16,2,5,5,128]{4,1,3,2,0:T(2,128)(2,1)} %param.14) | copy-start | bytes 614404
  23.8 9.9 %collective-permute-start.4 = (f32[648,128]{1,0:T(8,128)S(1)}, f32[648,128]{1,0:T(8,128)S(1)}, u32[]{:S(2)}, u32[]{:S(2)}) collective-permute-start(f32[648,128]{1,0:T(8,128)S(1)} %get-tuple-element.93.flows), channel_id=1, source_target_pairs={{0,4},{4,0},{8,12},{12,8},{16,20},{20,16},{24,28},{28,24},{1,5},{5... | collective-permute-start | bytes 995336 | tf_op jit(solution)/shard_map/ppermute | solution.py:632
  26.3 25.2 %collective-permute-start.8 = (f32[1024,128]{1,0:T(8,128)S(1)}, f32[1024,128]{1,0:T(8,128)S(1)}, u32[]{:S(2)}, u32[]{:S(2)}) collective-permute-start(f32[1024,128]{1,0:T(8,128)S(1)} %get-tuple-element.110), channel_id=1, source_target_pairs={{0,3},{1,2},{2,1},{3,0},{4,7},{5,6},{6,5},{7,4},{8,11},{9,10},{10,... | collective-permute-start | bytes 1572872 | tf_op jit(solution)/shard_map/ppermute | solution.py:631
  34.7 10.5 %collective-permute-start.6 = (f32[648,128]{1,0:T(8,128)S(1)}, f32[648,128]{1,0:T(8,128)S(1)}, u32[]{:S(2)}, u32[]{:S(2)}) collective-permute-start(f32[648,128]{1,0:T(8,128)S(1)} %get-tuple-element.101.flows), channel_id=1, source_target_pairs={{0,8},{4,12},{8,0},{12,4},{16,24},{20,28},{24,16},{28,20},{1,9},{5... | collective-permute-start | bytes 995336 | tf_op jit(solution)/shard_map/ppermute | solution.py:632
  41.1 8.0 %collective-permute-start.7 = (f32[320,128]{1,0:T(8,128)S(1)}, f32[320,128]{1,0:T(8,128)S(1)}, u32[]{:S(2)}, u32[]{:S(2)}) collective-permute-start(f32[320,128]{1,0:T(8,128)S(1)} %get-tuple-element.107.flows), channel_id=1, source_target_pairs={{0,4},{4,0},{8,12},{12,8},{16,20},{20,16},{24,28},{28,24},{1,5},{5... | collective-permute-start | bytes 491528 | tf_op jit(solution)/shard_map/ppermute | solution.py:632
  46.3 12.4 %collective-permute-start.11 = (f32[304,128]{1,0:T(8,128)S(1)}, f32[304,128]{1,0:T(8,128)S(1)}, u32[]{:S(2)}, u32[]{:S(2)}) collective-permute-start(f32[304,128]{1,0:T(8,128)S(1)} %get-tuple-element.122.ends), channel_id=1, source_target_pairs={{0,16},{4,20},{8,24},{12,28},{16,0},{20,4},{24,8},{28,12},{1,17},{... | collective-permute-start | bytes 466952 | tf_op jit(solution)/shard_map/ppermute | solution.py:632
  49.9 10.1 %collective-permute-start.10 = (f32[320,128]{1,0:T(8,128)S(1)}, f32[320,128]{1,0:T(8,128)S(1)}, u32[]{:S(2)}, u32[]{:S(2)}) collective-permute-start(f32[320,128]{1,0:T(8,128)S(1)} %get-tuple-element.117.flows), channel_id=1, source_target_pairs={{0,8},{4,12},{8,0},{12,4},{16,24},{20,28},{24,16},{28,20},{1,9},{5... | collective-permute-start | bytes 491528 | tf_op jit(solution)/shard_map/ppermute | solution.py:632
  53.4 4.6 %collective-permute-start.9 = (f32[176,128]{1,0:T(8,128)S(1)}, f32[176,128]{1,0:T(8,128)S(1)}, u32[]{:S(2)}, u32[]{:S(2)}) collective-permute-start(f32[176,128]{1,0:T(8,128)S(1)} %get-tuple-element.113.flows), channel_id=1, source_target_pairs={{0,4},{4,0},{8,12},{12,8},{16,20},{20,16},{24,28},{28,24},{1,5},{5... | collective-permute-start | bytes 270344 | tf_op jit(solution)/shard_map/ppermute | solution.py:632
  58.7 4.7 %collective-permute-start.12 = (f32[176,128]{1,0:T(8,128)S(1)}, f32[176,128]{1,0:T(8,128)S(1)}, u32[]{:S(2)}, u32[]{:S(2)}) collective-permute-start(f32[176,128]{1,0:T(8,128)S(1)} %get-tuple-element.123.flows), channel_id=1, source_target_pairs={{0,8},{4,12},{8,0},{12,4},{16,24},{20,28},{24,16},{28,20},{1,9},{5... | collective-permute-start | bytes 270344 | tf_op jit(solution)/shard_map/ppermute | solution.py:632
  60.8 8.1 %collective-permute-start.13 = (f32[160,128]{1,0:T(8,128)S(1)}, f32[160,128]{1,0:T(8,128)S(1)}, u32[]{:S(2)}, u32[]{:S(2)}) collective-permute-start(f32[160,128]{1,0:T(8,128)S(1)} %get-tuple-element.136.refs_0_), channel_id=1, source_target_pairs={{0,16},{4,20},{8,24},{12,28},{16,0},{20,4},{24,8},{28,12},{1,17},{... | collective-permute-start | bytes 245768 | tf_op jit(solution)/shard_map/ppermute | solution.py:632
  64.1 5.0 %collective-permute-start.14 = (f32[88,128]{1,0:T(8,128)S(1)}, f32[88,128]{1,0:T(8,128)S(1)}, u32[]{:S(2)}, u32[]{:S(2)}) collective-permute-start(f32[88,128]{1,0:T(8,128)S(1)} %get-tuple-element.139.refs_4_), channel_id=1, source_target_pairs={{0,16},{4,20},{8,24},{12,28},{16,0},{20,4},{24,8},{28,12},{1,17},{... | collective-permute-start | bytes 135176 | tf_op jit(solution)/shard_map/ppermute | solution.py:632

commit v11 on v10

--- a/solution.py
+++ b/solution.py
@@ -101,6 +101,11 @@
     return [[x[:, i * LANES : (i + 1) * LANES] for i in range(len(cells))] for x in products]
 
 
+def take_rows(ref, start, store):
+    store(0, NT - 1, ref[pl.ds(start, NT - 1, stride=2), :])
+    store(NT - 1, NT, ref[pl.ds(start + 2 * (NT - 1), 1), :])
+
+
 def split_cells(st, slab, first_cell, last_cell, xn, xf):
     p = lax.axis_index("pitch") % 2
     edge = first_cell.shape[0]
@@ -120,7 +125,11 @@
             j = z * V + v
             for out, q in ((xn, 1 - p), (xf, p)):
                 out[j, PAD - 8 : PAD, :] = zeros
-                out[j, 0:NT, :] = st[pl.ds(j * 2 * NT + q, NT, stride=2), :]
+
+                def store(first, last, value, out=out, j=j):
+                    out[j, first:last, :] = value
+
+                take_rows(st, j * 2 * NT + q, store)
         return carry
 
     lax.fori_loop(0, xn.shape[0] // V, separate, 0)
@@ -275,11 +284,14 @@
 
 def take_edges(edges, from_left, from_right, p):
     skip = from_left.shape[0] - V * NT * 2
-    for v in range(V):
-        edges[v, PAD - 8 : PAD, :] = jnp.zeros((8, LANES), F32)
-        edges[v, 0:NT, :] = from_left[pl.ds(skip + v * 2 * NT + p, NT, stride=2), :]
-        edges[V + v, PAD - 8 : PAD, :] = jnp.zeros((8, LANES), F32)
-        edges[V + v, 0:NT, :] = from_right[pl.ds(v * 2 * NT + p, NT, stride=2), :]
+    for ref, offset, kind in ((from_left, skip, 0), (from_right, 0, V)):
+        for v in range(V):
+            edges[kind + v, PAD - 8 : PAD, :] = jnp.zeros((8, LANES), F32)
+
+            def store(first, last, value, i=kind + v):
+                edges[i, first:last, :] = value
+
+            take_rows(ref, offset + v * 2 * NT + p, store)
 
 
 def edge_terms(z, cells, values, edges, advect, p, first, last):
@@ -576,7 +588,8 @@
         for a in range(V):
             j = z * V + a
             row = j * 2 * NT
-            held[pl.ds(row + 1 - p, NT, stride=2), :] = near[j, 0:NT, :]
+            held[pl.ds(row + 1 - p, NT - 1, stride=2), :] = near[j, 0 : NT - 1, :]
+            held[pl.ds(row + 1 - p + 2 * (NT - 1), 1), :] = near[j, NT - 1 : NT, :]
             for (first, width, height, extra, g, _), flow in zip(chunks, flows):
                 value = corrected(1, z, a, 0, height, g, blocks, flow)
                 held[pl.ds(row + p + 2 * first, width, stride=2), :] = value[:width]
@@ -792,7 +805,7 @@
     out = run(
         functools.partial(finish, levels), [st.shape], operands,
         out_specs=[pl.BlockSpec(memory_space=pltpu.HBM)],
-        scratch=[pltpu.VMEM(st.shape, F32), pltpu.SemaphoreType.DMA((5,))]
+        scratch=[pltpu.VMEM((st.shape[0] + 8, LANES), F32), pltpu.SemaphoreType.DMA((5,))]
         + [pltpu.VMEM((2 * V, rows_of(chunk), LANES), F32) for chunk in CHUNKS],
         name="finish",
     )[0]

time: 72.9 us -> 72.9 us (level)
  no operation moved by 1% of the time
where the time goes in v11:
time: 72.9 us; the launch traced here: 72.7 us
  starting transfers between devices  27.6 us (38%)
  Pallas kernels  27 us (37%)
  waiting for transfers between devices  15.4 us (21%)
  local copies, waits for them, and re-layouts  2.34 us (3%)
    pallas_call x15, Pallas kernels, __call__(): pl.pallas_call(body, out_shape=[jax.ShapeDtypeStruct(s, F32) for s in out...  26.5 us
    ppermute x9, starting transfers between devices, local(): lax.ppermute(x, 'seg', [(i, i ^ 1 << k) for i in range(segs)])  19.4 us
    ppermute x9, waiting for transfers between devices, local(): lax.ppermute(x, 'seg', [(i, i ^ 1 << k) for i in range(segs)])  13.4 us
    ppermute x1, starting transfers between devices, local(): lax.ppermute(last_cell, 'seg', [(i, i + 1) for i in range(segs - 1)])  3.4 us
    ppermute x3, starting transfers between devices, local(): to_far = lambda x: lax.ppermute(x, 'pitch', far_pairs)  2.97 us
    unnamed x22, local copies, waits for them, and re-layouts  2.18 us
  transfers between devices with their start and end apart: 15, of which 6 were waited for; matrix products, arithmetic and copies ran while one was open for 0% of the time, Pallas kernels for 31%

profile of v11, /device:TPU:0, one launch (start us, length us, event | category | flops | bytes accessed | tf_op | source)
XLA Modules:
  0.0 72.7 jit_solution(10593620633350597096)
XLA Ops:
  0.0 0.0 copy-start.5
  0.0 0.1 stack.35.flags
  0.1 2.1 %copy-done = f32[16,2,5,49,128]{4,1,3,2,0:T(2,128)S(1)} copy-done((f32[16,2,5,49,128]{4,1,3,2,0:T(2,128)S(1)}, f32[16,2,5,49,128]{4,1,3,2,0:T(2,128)}, u32[]{:S(2)}) %copy-start) | copy-done | bytes 4014104
  2.2 0.5 split_cells.1
  2.7 0.5 collective-permute-start.1
  3.3 2.6 %collective-permute-start = (f32[980,128]{1,0:T(8,128)S(1)}, f32[980,128]{1,0:T(8,128)S(1)}, u32[]{:S(2)}, u32[]{:S(2)}) collective-permute-start(f32[980,128]{1,0:T(8,128)S(1)} %get-tuple-element.84), channel_id=1, source_target_pairs={{0,3},{1,2},{2,1},{3,0},{4,7},{5,6},{6,5},{7,4},{8,11},{9,10},{10,... | collective-permute-start | bytes 1505288 | tf_op jit(solution)/shard_map/ppermute | solution.py:644
  5.9 3.4 %collective-permute-start.2 = (f32[496,128]{1,0:T(8,128)S(1)}, f32[496,128]{1,0:T(8,128)S(1)}, u32[]{:S(2)}, u32[]{:S(2)}) collective-permute-start(f32[496,128]{1,0:T(8,128)S(1)} %get-tuple-element.88), channel_id=1, source_target_pairs={{0,4},{4,8},{8,12},{12,16},{16,20},{20,24},{24,28},{1,5},{5,9},{9,... | collective-permute-start | bytes 761864 | tf_op jit(solution)/shard_map/ppermute | solution.py:673
  9.3 1.3 %collective-permute-start.3 = (f32[496,128]{1,0:T(8,128)S(1)}, f32[496,128]{1,0:T(8,128)S(1)}, u32[]{:S(2)}, u32[]{:S(2)}) collective-permute-start(f32[496,128]{1,0:T(8,128)S(1)} %get-tuple-element.89), channel_id=1, source_target_pairs={{4,0},{8,4},{12,8},{16,12},{20,16},{24,20},{28,24},{5,1},{9,5},{13... | collective-permute-start | bytes 761864 | tf_op jit(solution)/shard_map/ppermute | solution.py:674
  10.6 0.0 copy-done.10
  10.7 0.1 broadcast_in_dim.2.harmonic
  10.7 0.0 copy-done.5
  10.7 0.0 copy-done.8
  10.7 0.0 copy-done.3
  10.7 0.0 copy-done.4
  10.8 0.0 copy-done.6
  10.8 0.0 copy-done.7
  10.8 3.3 %prepare.1 = (f32[56,128]{1,0:T(8,128)S(1)}, f32[80,56,128]{2,1,0:T(8,128)S(1)}, f32[1920,128]{1,0:T(8,128)S(1)}, f32[1024,128]{1,0:T(8,128)S(1)}) custom-call(s32[6]{0:T(128)S(1)} %stack.35.flags, s32[2]{0:T(128)S(1)} %copy-done.8, f32[80,56,128]{2,1,0:T(8,128)S(1)} %get-tuple-element.75.xn, f32[80,56,128]{2,1,0:T(8,128)S(1)} %get-tuple-element.76.xf, ...), custom_call_target="tpu_custom_call" | custom-call | flops 1000 | bytes 1000 | tf_op jit(solution)/shard_map/prepare/pallas_call | solution.py:49
  14.1 0.1 collective-permute-start.5
  14.2 0.0 copy-start.1
  14.2 0.0 copy-start.2
  14.2 0.0 copy-start.9
  14.2 2.1 %near_base.1.base = f32[80,56,128]{2,1,0:T(8,128)S(1)} custom-call(s32[6]{0:T(128)S(1)} %stack.35.flags, f32[80,56,128]{2,1,0:T(8,128)S(1)} %get-tuple-element.75.xn, f32[80,56,128]{2,1,0:T(8,128)S(1)} %get-tuple-element.76.xf, f32[160,128]{1,0:T(8,128)S(1)} %bitcast.40, f32[160,128]{1,0:T(8,128)S(1)} %bitcast.45, f32[56,192]{1,0:T(8,128)S(1)} %copy-done.6, ...), custom_call_target="tpu_custom_call" | custom-call | bytes 1000 | tf_op jit(solution)/shard_map/near_base/pallas_call | solution.py:49
  16.3 0.0 copy-done.1
  16.4 0.0 copy-done.2
  16.4 1.3 %transfer.1 = (f32[2,80,16,128]{3,2,1,0:T(8,128)S(1)}, f32[152,128]{1,0:T(8,128)S(1)}) custom-call(s32[6]{0:T(128)S(1)} %stack.35.flags, f32[800,128]{1,0:T(8,128)S(1)} %bitcast.28, f32[800,128]{1,0:T(8,128)S(1)} %bitcast.32), custom_call_target="tpu_custom_call" | custom-call | bytes 1000 | tf_op jit(solution)/shard_map/transfer/pallas_call | solution.py:49
  17.6 0.0 copy-done.9
  17.6 0.1 reshape.36
  17.8 0.0 collective-permute-done.slab
  17.8 1.2 %far_lead.1.lead = f32[20,56,128]{2,1,0:T(8,128)S(1)} custom-call(s32[6]{0:T(128)S(1)} %stack.35.flags, f32[980,128]{1,0:T(8,128)S(1)} %collective-permute-done.slab, f32[56,128]{1,0:T(8,128)S(1)} %get-tuple-element.79.trig, f32[56,56]{1,0:T(8,128)S(1)} %copy-done.7, f32[64,192]{1,0:T(8,128)S(1)} %copy-done.5), custom_call_target="tpu_custom_call" | custom-call | bytes 1000 | tf_op jit(solution)/shard_map/far_lead/pallas_call | solution.py:49
  19.0 1.4 %collective-permute-done.2.from_left = f32[496,128]{1,0:T(8,128)S(1)} collective-permute-done((f32[496,128]{1,0:T(8,128)S(1)}, f32[496,128]{1,0:T(8,128)S(1)}, u32[]{:S(2)}, u32[]{:S(2)}) %collective-permute-start.2) | collective-permute-done | bytes 253984 | tf_op jit(solution)/shard_map/ppermute | solution.py:673
  20.4 0.0 collective-permute-done.3.from_right
  20.4 0.0 collective-permute-done.1.halo
  20.4 3.4 %near_cell.1 = (f32[80,56,128]{2,1,0:T(8,128)S(1)}, f32[648,128]{1,0:T(8,128)S(1)}) custom-call(s32[6]{0:T(128)S(1)} %stack.35.flags, f32[80,56,128]{2,1,0:T(8,128)S(1)} %near_base.1.base, f32[80,56,128]{2,1,0:T(8,128)S(1)} %collective-permute-done.1.halo, f32[496,128]{1,0:T(8,128)S(1)} %collective-permute-done.2.from_left, ...), custom_call_target="tpu_custom_call" | custom-call | flops 6000000000 | bytes 1000 | tf_op jit(solution)/shard_map/near_cell/pallas_call | solution.py:49
  23.8 2.5 %collective-permute-start.4 = (f32[648,128]{1,0:T(8,128)S(1)}, f32[648,128]{1,0:T(8,128)S(1)}, u32[]{:S(2)}, u32[]{:S(2)}) collective-permute-start(f32[648,128]{1,0:T(8,128)S(1)} %get-tuple-element.93.flows), channel_id=1, source_target_pairs={{0,4},{4,0},{8,12},{12,8},{16,20},{20,16},{24,28},{28,24},{1,5},{5... | collective-permute-start | bytes 995336 | tf_op jit(solution)/shard_map/ppermute | solution.py:645
  26.3 0.3 collective-permute-start.8
  26.6 7.1 %collective-permute-done.4.other = f32[648,128]{1,0:T(8,128)S(1)} collective-permute-done((f32[648,128]{1,0:T(8,128)S(1)}, f32[648,128]{1,0:T(8,128)S(1)}, u32[]{:S(2)}, u32[]{:S(2)}) %collective-permute-start.4) | collective-permute-done | bytes 331808 | tf_op jit(solution)/shard_map/ppermute | solution.py:645
  33.7 1.0 %merge_all.2 = (f32[2,30,8,128]{3,2,1,0:T(8,128)S(1)}, f32[648,128]{1,0:T(8,128)S(1)}, f32[2,15,8,128]{3,2,1,0:T(8,128)S(1)}, f32[496,128]{1,0:T(8,128)S(1)}) custom-call(s32[6]{0:T(128)S(1)} %stack.35.flags, f32[648,128]{1,0:T(8,128)S(1)} %get-tuple-element.93.flows, f32[648,128]{1,0:T(8,128)S(1)} %collective-permute-done.4.other), custom_call_target="tpu_custom_call" | custom-call | flops 1000 | bytes 1000 | tf_op jit(solution)/shard_map/merge_all/pallas_call | solution.py:49
  34.7 3.4 %collective-permute-start.6 = (f32[648,128]{1,0:T(8,128)S(1)}, f32[648,128]{1,0:T(8,128)S(1)}, u32[]{:S(2)}, u32[]{:S(2)}) collective-permute-start(f32[648,128]{1,0:T(8,128)S(1)} %get-tuple-element.101.flows), channel_id=1, source_target_pairs={{0,8},{4,12},{8,0},{12,4},{16,24},{20,28},{24,16},{28,20},{1,9},{5... | collective-permute-start | bytes 995336 | tf_op jit(solution)/shard_map/ppermute | solution.py:645
  38.1 0.7 collective-permute-done.5.halo
  38.8 2.2 %far_chunk.2 = (f32[80,32,128]{2,1,0:T(8,128)S(1)}, f32[320,128]{1,0:T(8,128)S(1)}) custom-call(s32[6]{0:T(128)S(1)} %stack.35.flags, f32[80,56,128]{2,1,0:T(8,128)S(1)} %get-tuple-element.96.base, f32[20,56,128]{2,1,0:T(8,128)S(1)} %far_lead.1.lead, f32[1920,128]{1,0:T(8,128)S(1)} %collective-permute-done.5.halo, ...), custom_call_target="tpu_custom_call" | custom-call | flops 1000 | bytes 1000 | tf_op jit(solution)/shard_map/far_chunk/pallas_call | solution.py:49
  41.1 2.2 %collective-permute-start.7 = (f32[320,128]{1,0:T(8,128)S(1)}, f32[320,128]{1,0:T(8,128)S(1)}, u32[]{:S(2)}, u32[]{:S(2)}) collective-permute-start(f32[320,128]{1,0:T(8,128)S(1)} %get-tuple-element.107.flows), channel_id=1, source_target_pairs={{0,4},{4,0},{8,12},{12,8},{16,20},{20,16},{24,28},{28,24},{1,5},{5... | collective-permute-start | bytes 491528 | tf_op jit(solution)/shard_map/ppermute | solution.py:645
  43.3 2.0 %collective-permute-done.6.other = f32[648,128]{1,0:T(8,128)S(1)} collective-permute-done((f32[648,128]{1,0:T(8,128)S(1)}, f32[648,128]{1,0:T(8,128)S(1)}, u32[]{:S(2)}, u32[]{:S(2)}) %collective-permute-start.6) | collective-permute-done | bytes 331808 | tf_op jit(solution)/shard_map/ppermute | solution.py:645
  45.3 1.0 %merge_all.3 = (f32[2,30,8,128]{3,2,1,0:T(8,128)S(1)}, f32[304,128]{1,0:T(8,128)S(1)}, f32[2,15,8,128]{3,2,1,0:T(8,128)S(1)}, f32[496,128]{1,0:T(8,128)S(1)}) custom-call(s32[6]{0:T(128)S(1)} %stack.35.flags, f32[648,128]{1,0:T(8,128)S(1)} %get-tuple-element.101.flows, f32[648,128]{1,0:T(8,128)S(1)} %collective-permute-done.6.other, ...), custom_call_target="tpu_custom_call" | custom-call | flops 1000 | bytes 1000 | tf_op jit(solution)/shard_map/merge_all/pallas_call | solution.py:49
  46.3 2.8 %collective-permute-start.11 = (f32[304,128]{1,0:T(8,128)S(1)}, f32[304,128]{1,0:T(8,128)S(1)}, u32[]{:S(2)}, u32[]{:S(2)}) collective-permute-start(f32[304,128]{1,0:T(8,128)S(1)} %get-tuple-element.122.ends), channel_id=1, source_target_pairs={{0,16},{4,20},{8,24},{12,28},{16,0},{20,4},{24,8},{28,12},{1,17},{... | collective-permute-start | bytes 466952 | tf_op jit(solution)/shard_map/ppermute | solution.py:645
  49.1 0.0 collective-permute-done.7.other
  49.1 0.8 %merge_flows.4 = (f32[320,128]{1,0:T(8,128)S(1)}, f32[320,128]{1,0:T(8,128)S(1)}) custom-call(s32[6]{0:T(128)S(1)} %stack.35.flags, f32[2,30,8,128]{3,2,1,0:T(8,128)S(1)} %get-tuple-element.106.mats, f32[320,128]{1,0:T(8,128)S(1)} %get-tuple-element.107.flows, f32[320,128]{1,0:T(8,128)S(1)} %collective-permute-done.7.other), custom_call_target="tpu_custom_call" | custom-call | flops 1000 | bytes 1000 | tf_op jit(solution)/shard_map/merge_flows/pallas_call | solution.py:49
  49.9 1.6 %collective-permute-start.10 = (f32[320,128]{1,0:T(8,128)S(1)}, f32[320,128]{1,0:T(8,128)S(1)}, u32[]{:S(2)}, u32[]{:S(2)}) collective-permute-start(f32[320,128]{1,0:T(8,128)S(1)} %get-tuple-element.117.flows), channel_id=1, source_target_pairs={{0,8},{4,12},{8,0},{12,4},{16,24},{20,28},{24,16},{28,20},{1,9},{5... | collective-permute-start | bytes 491528 | tf_op jit(solution)/shard_map/ppermute | solution.py:645
  51.5 0.0 collective-permute-done.8.halo
  51.5 1.9 %far_chunk.3 = (f32[80,24,128]{2,1,0:T(8,128)S(1)}, f32[176,128]{1,0:T(8,128)S(1)}) custom-call(s32[6]{0:T(128)S(1)} %stack.35.flags, f32[80,56,128]{2,1,0:T(8,128)S(1)} %get-tuple-element.96.base, f32[20,56,128]{2,1,0:T(8,128)S(1)} %far_lead.1.lead, f32[1024,128]{1,0:T(8,128)S(1)} %collective-permute-done.8.halo, ...), custom_call_target="tpu_custom_call" | custom-call | flops 1000 | bytes 1000 | tf_op jit(solution)/shard_map/far_chunk/pallas_call | solution.py:49
  53.4 0.7 collective-permute-start.9
  54.0 3.9 %collective-permute-done.9.other = f32[176,128]{1,0:T(8,128)S(1)} collective-permute-done((f32[176,128]{1,0:T(8,128)S(1)}, f32[176,128]{1,0:T(8,128)S(1)}, u32[]{:S(2)}, u32[]{:S(2)}) %collective-permute-start.9) | collective-permute-done | bytes 90144 | tf_op jit(solution)/shard_map/ppermute | solution.py:645
  58.0 0.7 merge_flows.5
  58.7 0.0 collective-permute-done.11.other
  58.7 1.3 %collective-permute-start.12 = (f32[176,128]{1,0:T(8,128)S(1)}, f32[176,128]{1,0:T(8,128)S(1)}, u32[]{:S(2)}, u32[]{:S(2)}) collective-permute-start(f32[176,128]{1,0:T(8,128)S(1)} %get-tuple-element.123.flows), channel_id=1, source_target_pairs={{0,8},{4,12},{8,0},{12,4},{16,24},{20,28},{24,16},{28,20},{1,9},{5... | collective-permute-start | bytes 270344 | tf_op jit(solution)/shard_map/ppermute | solution.py:645
  60.0 0.0 collective-permute-done.10.other
  60.0 0.8 %merge_flows.6 = (f32[160,128]{1,0:T(8,128)S(1)}, f32[320,128]{1,0:T(8,128)S(1)}) custom-call(s32[6]{0:T(128)S(1)} %stack.35.flags, f32[2,30,8,128]{3,2,1,0:T(8,128)S(1)} %get-tuple-element.116.mats, f32[320,128]{1,0:T(8,128)S(1)} %get-tuple-element.117.flows, f32[320,128]{1,0:T(8,128)S(1)} %collective-permute-done.10.other, ...), custom_call_target="tpu_custom_call" | custom-call | flops 1000 | bytes 1000 | tf_op jit(solution)/shard_map/merge_flows/pallas_call | solution.py:49
  60.8 2.7 %collective-permute-start.13 = (f32[160,128]{1,0:T(8,128)S(1)}, f32[160,128]{1,0:T(8,128)S(1)}, u32[]{:S(2)}, u32[]{:S(2)}) collective-permute-start(f32[160,128]{1,0:T(8,128)S(1)} %get-tuple-element.136.refs_0_), channel_id=1, source_target_pairs={{0,16},{4,20},{8,24},{12,28},{16,0},{20,4},{24,8},{28,12},{1,17},{... | collective-permute-start | bytes 245768 | tf_op jit(solution)/shard_map/ppermute | solution.py:645
  63.4 0.0 collective-permute-done.12.other
  63.4 0.7 merge_flows.7
  64.1 2.2 %collective-permute-start.14 = (f32[88,128]{1,0:T(8,128)S(1)}, f32[88,128]{1,0:T(8,128)S(1)}, u32[]{:S(2)}, u32[]{:S(2)}) collective-permute-start(f32[88,128]{1,0:T(8,128)S(1)} %get-tuple-element.139.refs_4_), channel_id=1, source_target_pairs={{0,16},{4,20},{8,24},{12,28},{16,0},{20,4},{24,8},{28,12},{1,17},{... | collective-permute-start | bytes 135176 | tf_op jit(solution)/shard_map/ppermute | solution.py:645
  66.3 2.5 %correct_all.1 = (f32[80,56,128]{2,1,0:T(8,128)S(1)}, f32[2,30,8,128]{3,2,1,0:T(8,128)S(1)}) custom-call(s32[6]{0:T(128)S(1)} %stack.35.flags, f32[304,128]{1,0:T(8,128)S(1)} %get-tuple-element.122.ends, f32[304,128]{1,0:T(8,128)S(1)} %collective-permute-done.11.other, f32[2,15,8,128]{3,2,1,0:T(8,128)S(1)} %get-tuple-element.128.share, ...), custom_call_target="tpu_custom_call" | custom-call | flops 1000 | bytes 1000 | tf_op jit(solution)/shard_map/correct_all/pallas_call | solution.py:49
  68.8 0.0 collective-permute-done.13.refs_1_
  68.8 0.3 collective-permute-done.14.refs_5_
  69.1 3.6 %finish.1 = f32[7840,128]{1,0:T(8,128)} custom-call(s32[6]{0:T(128)S(1)} %stack.35.flags, f32[2,30,8,128]{3,2,1,0:T(8,128)S(1)} %get-tuple-element.134.mats, f32[2,80,16,128]{3,2,1,0:T(8,128)S(1)} %get-tuple-element.130.blocks, f32[80,56,128]{2,1,0:T(8,128)S(1)} %get-tuple-element.135.near, f32[160,128]{1,0:T(8,128)S(1)} %get-tuple-element.136.refs_0_, ...), custom_call_target="tpu_custom_call" | custom-call | flops 1000 | bytes 1000 | tf_op jit(solution)/shard_map/finish/pallas_call | solution.py:49
  (8 shorter events, 0.0 us)
Async XLA Ops:
  0.0 10.7 %copy-start.5 = (f32[64,192]{1,0:T(8,128)S(1)}, f32[64,192]{1,0:T(8,128)}, u32[]{:S(2)}) copy-start(f32[64,192]{1,0:T(8,128)} %constant.33.clone.turned) | copy-start | bytes 147460
  0.0 10.6 %copy-start.10 = (s32[24]{0:T(128)S(1)}, s32[24]{0:T(128)}, u32[]{:S(2)}) copy-start(s32[24]{0:T(128)} %param.18) | copy-start | bytes 292
  0.0 10.7 %copy-start.8 = (s32[2]{0:T(128)S(1)}, s32[2]{0:T(128)}, u32[]{:S(2)}) copy-start(s32[2]{0:T(128)} %blades.1) | copy-start | bytes 28
  0.1 2.1 %copy-start = (f32[16,2,5,49,128]{4,1,3,2,0:T(2,128)S(1)}, f32[16,2,5,49,128]{4,1,3,2,0:T(2,128)}, u32[]{:S(2)}) copy-start(f32[16,2,5,49,128]{4,1,3,2,0:T(2,128)} %param.11) | copy-start | bytes 12042244
  2.2 8.5 %copy-start.3 = (f32[16,2,5,128]{3,1,2,0:T(2,128)S(1)}, f32[16,2,5,128]{3,1,2,0:T(2,128)}, u32[]{:S(2)}) copy-start(f32[16,2,5,128]{3,1,2,0:T(2,128)} %param.12) | copy-start | bytes 245764
  2.2 8.5 %copy-start.4 = (f32[16,2,5,128]{3,1,2,0:T(2,128)S(1)}, f32[16,2,5,128]{3,1,2,0:T(2,128)}, u32[]{:S(2)}) copy-start(f32[16,2,5,128]{3,1,2,0:T(2,128)} %param.13) | copy-start | bytes 245764
  2.2 8.5 %copy-start.6 = (f32[56,192]{1,0:T(8,128)S(1)}, f32[56,192]{1,0:T(8,128)}, u32[]{:S(2)}) copy-start(f32[56,192]{1,0:T(8,128)} %constant.34.clone.table) | copy-start | bytes 129028
  2.2 8.5 %copy-start.7 = (f32[56,56]{1,0:T(8,128)S(1)}, f32[56,56]{1,0:T(8,128)}, u32[]{:S(2)}) copy-start(f32[56,56]{1,0:T(8,128)} %constant.32.clone.basis) | copy-start | bytes 37636
  2.7 17.6 %collective-permute-start.1 = (f32[80,56,128]{2,1,0:T(8,128)S(1)}, f32[80,56,128]{2,1,0:T(8,128)S(1)}, u32[]{:S(2)}, u32[]{:S(2)}) collective-permute-start(f32[80,56,128]{2,1,0:T(8,128)S(1)} %get-tuple-element.75.xn), channel_id=1, source_target_pairs={{0,1},{1,0},{2,3},{3,2},{4,5},{5,4},{6,7},{7,6},{8,9},{9,8},{10,11... | collective-permute-start | bytes 6881288 | tf_op jit(solution)/shard_map/ppermute | solution.py:671
  3.3 14.5 %collective-permute-start = (f32[980,128]{1,0:T(8,128)S(1)}, f32[980,128]{1,0:T(8,128)S(1)}, u32[]{:S(2)}, u32[]{:S(2)}) collective-permute-start(f32[980,128]{1,0:T(8,128)S(1)} %get-tuple-element.84), channel_id=1, source_target_pairs={{0,3},{1,2},{2,1},{3,0},{4,7},{5,6},{6,5},{7,4},{8,11},{9,10},{10,... | collective-permute-start | bytes 1505288 | tf_op jit(solution)/shard_map/ppermute | solution.py:644
  5.9 14.4 %collective-permute-start.2 = (f32[496,128]{1,0:T(8,128)S(1)}, f32[496,128]{1,0:T(8,128)S(1)}, u32[]{:S(2)}, u32[]{:S(2)}) collective-permute-start(f32[496,128]{1,0:T(8,128)S(1)} %get-tuple-element.88), channel_id=1, source_target_pairs={{0,4},{4,8},{8,12},{12,16},{16,20},{20,24},{24,28},{1,5},{5,9},{9,... | collective-permute-start | bytes 761864 | tf_op jit(solution)/shard_map/ppermute | solution.py:673
  9.3 11.0 %collective-permute-start.3 = (f32[496,128]{1,0:T(8,128)S(1)}, f32[496,128]{1,0:T(8,128)S(1)}, u32[]{:S(2)}, u32[]{:S(2)}) collective-permute-start(f32[496,128]{1,0:T(8,128)S(1)} %get-tuple-element.89), channel_id=1, source_target_pairs={{4,0},{8,4},{12,8},{16,12},{20,16},{24,20},{28,24},{5,1},{9,5},{13... | collective-permute-start | bytes 761864 | tf_op jit(solution)/shard_map/ppermute | solution.py:674
  14.1 24.7 %collective-permute-start.5 = (f32[1920,128]{1,0:T(8,128)S(1)}, f32[1920,128]{1,0:T(8,128)S(1)}, u32[]{:S(2)}, u32[]{:S(2)}) collective-permute-start(f32[1920,128]{1,0:T(8,128)S(1)} %get-tuple-element.98), channel_id=1, source_target_pairs={{0,3},{1,2},{2,1},{3,0},{4,7},{5,6},{6,5},{7,4},{8,11},{9,10},{10,... | collective-permute-start | bytes 2949128 | tf_op jit(solution)/shard_map/ppermute | solution.py:644
  14.2 2.2 %copy-start.1 = (f32[16,2,5,5,128]{4,1,3,2,0:T(2,128)S(1)}, f32[16,2,5,5,128]{4,1,3,2,0:T(2,128)}, u32[]{:S(2)}) copy-start(f32[16,2,5,5,128]{4,1,3,2,0:T(2,128)} %param.15) | copy-start | bytes 1228804
  14.2 2.2 %copy-start.2 = (f32[16,2,5,5,128]{4,1,3,2,0:T(2,128)S(1)}, f32[16,2,5,5,128]{4,1,3,2,0:T(2,128)}, u32[]{:S(2)}) copy-start(f32[16,2,5,5,128]{4,1,3,2,0:T(2,128)} %param.16) | copy-start | bytes 1228804
  14.2 3.4 %copy-start.9 = (bf16[16,2,5,5,128]{4,1,3,2,0:T(2,128)(2,1)S(1)}, bf16[16,2,5,5,128]{4,1,3,2,0:T(2,128)(2,1)}, u32[]{:S(2)}) copy-start(bf16[16,2,5,5,128]{4,1,3,2,0:T(2,128)(2,1)} %param.14) | copy-start | bytes 614404
  23.8 9.9 %collective-permute-start.4 = (f32[648,128]{1,0:T(8,128)S(1)}, f32[648,128]{1,0:T(8,128)S(1)}, u32[]{:S(2)}, u32[]{:S(2)}) collective-permute-start(f32[648,128]{1,0:T(8,128)S(1)} %get-tuple-element.93.flows), channel_id=1, source_target_pairs={{0,4},{4,0},{8,12},{12,8},{16,20},{20,16},{24,28},{28,24},{1,5},{5... | collective-permute-start | bytes 995336 | tf_op jit(solution)/shard_map/ppermute | solution.py:645
  26.3 25.2 %collective-permute-start.8 = (f32[1024,128]{1,0:T(8,128)S(1)}, f32[1024,128]{1,0:T(8,128)S(1)}, u32[]{:S(2)}, u32[]{:S(2)}) collective-permute-start(f32[1024,128]{1,0:T(8,128)S(1)} %get-tuple-element.110), channel_id=1, source_target_pairs={{0,3},{1,2},{2,1},{3,0},{4,7},{5,6},{6,5},{7,4},{8,11},{9,10},{10,... | collective-permute-start | bytes 1572872 | tf_op jit(solution)/shard_map/ppermute | solution.py:644
  34.7 10.5 %collective-permute-start.6 = (f32[648,128]{1,0:T(8,128)S(1)}, f32[648,128]{1,0:T(8,128)S(1)}, u32[]{:S(2)}, u32[]{:S(2)}) collective-permute-start(f32[648,128]{1,0:T(8,128)S(1)} %get-tuple-element.101.flows), channel_id=1, source_target_pairs={{0,8},{4,12},{8,0},{12,4},{16,24},{20,28},{24,16},{28,20},{1,9},{5... | collective-permute-start | bytes 995336 | tf_op jit(solution)/shard_map/ppermute | solution.py:645
  41.1 8.0 %collective-permute-start.7 = (f32[320,128]{1,0:T(8,128)S(1)}, f32[320,128]{1,0:T(8,128)S(1)}, u32[]{:S(2)}, u32[]{:S(2)}) collective-permute-start(f32[320,128]{1,0:T(8,128)S(1)} %get-tuple-element.107.flows), channel_id=1, source_target_pairs={{0,4},{4,0},{8,12},{12,8},{16,20},{20,16},{24,28},{28,24},{1,5},{5... | collective-permute-start | bytes 491528 | tf_op jit(solution)/shard_map/ppermute | solution.py:645
  46.3 12.4 %collective-permute-start.11 = (f32[304,128]{1,0:T(8,128)S(1)}, f32[304,128]{1,0:T(8,128)S(1)}, u32[]{:S(2)}, u32[]{:S(2)}) collective-permute-start(f32[304,128]{1,0:T(8,128)S(1)} %get-tuple-element.122.ends), channel_id=1, source_target_pairs={{0,16},{4,20},{8,24},{12,28},{16,0},{20,4},{24,8},{28,12},{1,17},{... | collective-permute-start | bytes 466952 | tf_op jit(solution)/shard_map/ppermute | solution.py:645
  49.9 10.1 %collective-permute-start.10 = (f32[320,128]{1,0:T(8,128)S(1)}, f32[320,128]{1,0:T(8,128)S(1)}, u32[]{:S(2)}, u32[]{:S(2)}) collective-permute-start(f32[320,128]{1,0:T(8,128)S(1)} %get-tuple-element.117.flows), channel_id=1, source_target_pairs={{0,8},{4,12},{8,0},{12,4},{16,24},{20,28},{24,16},{28,20},{1,9},{5... | collective-permute-start | bytes 491528 | tf_op jit(solution)/shard_map/ppermute | solution.py:645
  53.4 4.6 %collective-permute-start.9 = (f32[176,128]{1,0:T(8,128)S(1)}, f32[176,128]{1,0:T(8,128)S(1)}, u32[]{:S(2)}, u32[]{:S(2)}) collective-permute-start(f32[176,128]{1,0:T(8,128)S(1)} %get-tuple-element.113.flows), channel_id=1, source_target_pairs={{0,4},{4,0},{8,12},{12,8},{16,20},{20,16},{24,28},{28,24},{1,5},{5... | collective-permute-start | bytes 270344 | tf_op jit(solution)/shard_map/ppermute | solution.py:645
  58.7 4.7 %collective-permute-start.12 = (f32[176,128]{1,0:T(8,128)S(1)}, f32[176,128]{1,0:T(8,128)S(1)}, u32[]{:S(2)}, u32[]{:S(2)}) collective-permute-start(f32[176,128]{1,0:T(8,128)S(1)} %get-tuple-element.123.flows), channel_id=1, source_target_pairs={{0,8},{4,12},{8,0},{12,4},{16,24},{20,28},{24,16},{28,20},{1,9},{5... | collective-permute-start | bytes 270344 | tf_op jit(solution)/shard_map/ppermute | solution.py:645
  60.8 8.1 %collective-permute-start.13 = (f32[160,128]{1,0:T(8,128)S(1)}, f32[160,128]{1,0:T(8,128)S(1)}, u32[]{:S(2)}, u32[]{:S(2)}) collective-permute-start(f32[160,128]{1,0:T(8,128)S(1)} %get-tuple-element.136.refs_0_), channel_id=1, source_target_pairs={{0,16},{4,20},{8,24},{12,28},{16,0},{20,4},{24,8},{28,12},{1,17},{... | collective-permute-start | bytes 245768 | tf_op jit(solution)/shard_map/ppermute | solution.py:645
  64.1 5.0 %collective-permute-start.14 = (f32[88,128]{1,0:T(8,128)S(1)}, f32[88,128]{1,0:T(8,128)S(1)}, u32[]{:S(2)}, u32[]{:S(2)}) collective-permute-start(f32[88,128]{1,0:T(8,128)S(1)} %get-tuple-element.139.refs_4_), channel_id=1, source_target_pairs={{0,16},{4,20},{8,24},{12,28},{16,0},{20,4},{24,8},{28,12},{1,17},{... | collective-permute-start | bytes 135176 | tf_op jit(solution)/shard_map/ppermute | solution.py:645

commit v12 on v11

--- a/solution.py
+++ b/solution.py
@@ -263,7 +263,7 @@
                 result.append(total)
             return tuple(result)
 
-        out = lax.fori_loop(1, cells - 1, ahead, ahead(0, nothing), unroll=2)
+        out = lax.fori_loop(1, cells - 1, ahead, ahead(0, nothing), unroll=7)
         out = ahead(cells - 1, out)
         keep_tiles(fg, 0, out, first, last, height, extra)
 
@@ -278,7 +278,7 @@
                 result.append(total)
             return tuple(result)
 
-        out = lax.fori_loop(0, cells, back, nothing, unroll=2)
+        out = lax.fori_loop(0, cells, back, nothing, unroll=4)
         keep_tiles(fg, V, out, first, last, height, extra)
 
 
@@ -561,7 +561,7 @@
                 result[z * V + a, first:last, :] = corrected(c, z, a, first, last, g, blocks, flow)
             return flow
 
-        lax.fori_loop(0, g.shape[0] // V, step, flow, unroll=2)
+        lax.fori_loop(0, g.shape[0] // V, step, flow, unroll=4)
 
 
 def correct_all(part, levels, flags, ends, other, share, known, blocks, g, result, mats, inflow):
@@ -601,7 +601,7 @@
     stops = [cells // 4, cells // 2, cells * 3 // 4, cells - 1, cells]
     copies, cell, row = [], 0, 0
     for i, stop in enumerate(stops):
-        lax.fori_loop(cell, stop, step, 0, unroll=2 if (stop - cell) % 2 == 0 else 1)
+        lax.fori_loop(cell, stop, step, 0, unroll=4 if (stop - cell) % 4 == 0 else 1)
         size = stop * V * NT * 2 // 8 * 8 - row
         span = pl.ds(row, size)
         copies.append(pltpu.make_async_copy(held.at[span, :], out.at[span, :], sems.at[i]))

time: 72.9 us -> 72.8 us (level)
  no operation moved by 1% of the time
where the time goes in v12:
time: 72.8 us; the launch traced here: 72.6 us
  starting transfers between devices  27.7 us (38%)
  Pallas kernels  26.5 us (36%)
  waiting for transfers between devices  15.6 us (21%)
  local copies, waits for them, and re-layouts  2.34 us (3%)
    pallas_call x15, Pallas kernels, __call__(): pl.pallas_call(body, out_shape=[jax.ShapeDtypeStruct(s, F32) for s in out...  26 us
    ppermute x9, starting transfers between devices, local(): lax.ppermute(x, 'seg', [(i, i ^ 1 << k) for i in range(segs)])  19.5 us
    ppermute x9, waiting for transfers between devices, local(): lax.ppermute(x, 'seg', [(i, i ^ 1 << k) for i in range(segs)])  13.4 us
    ppermute x1, starting transfers between devices, local(): lax.ppermute(last_cell, 'seg', [(i, i + 1) for i in range(segs - 1)])  3.4 us
    ppermute x3, starting transfers between devices, local(): to_far = lambda x: lax.ppermute(x, 'pitch', far_pairs)  2.97 us
    unnamed x22, local copies, waits for them, and re-layouts  2.18 us
  transfers between devices with their start and end apart: 15, of which 6 were waited for; matrix products, arithmetic and copies ran while one was open for 0% of the time, Pallas kernels for 31%

profile of v12, /device:TPU:0, one launch (start us, length us, event | category | flops | bytes accessed | tf_op | source)
XLA Modules:
  0.0 72.6 jit_solution(9473096133462600067)
XLA Ops:
  0.0 0.0 copy-start.5
  0.0 0.1 stack.35.flags
  0.1 2.1 %copy-done = f32[16,2,5,49,128]{4,1,3,2,0:T(2,128)S(1)} copy-done((f32[16,2,5,49,128]{4,1,3,2,0:T(2,128)S(1)}, f32[16,2,5,49,128]{4,1,3,2,0:T(2,128)}, u32[]{:S(2)}) %copy-start) | copy-done | bytes 4014104
  2.2 0.5 split_cells.1
  2.7 0.5 collective-permute-start.1
  3.3 2.6 %collective-permute-start = (f32[980,128]{1,0:T(8,128)S(1)}, f32[980,128]{1,0:T(8,128)S(1)}, u32[]{:S(2)}, u32[]{:S(2)}) collective-permute-start(f32[980,128]{1,0:T(8,128)S(1)} %get-tuple-element.84), channel_id=1, source_target_pairs={{0,3},{1,2},{2,1},{3,0},{4,7},{5,6},{6,5},{7,4},{8,11},{9,10},{10,... | collective-permute-start | bytes 1505288 | tf_op jit(solution)/shard_map/ppermute | solution.py:644
  5.9 3.4 %collective-permute-start.2 = (f32[496,128]{1,0:T(8,128)S(1)}, f32[496,128]{1,0:T(8,128)S(1)}, u32[]{:S(2)}, u32[]{:S(2)}) collective-permute-start(f32[496,128]{1,0:T(8,128)S(1)} %get-tuple-element.88), channel_id=1, source_target_pairs={{0,4},{4,8},{8,12},{12,16},{16,20},{20,24},{24,28},{1,5},{5,9},{9,... | collective-permute-start | bytes 761864 | tf_op jit(solution)/shard_map/ppermute | solution.py:673
  9.3 1.3 %collective-permute-start.3 = (f32[496,128]{1,0:T(8,128)S(1)}, f32[496,128]{1,0:T(8,128)S(1)}, u32[]{:S(2)}, u32[]{:S(2)}) collective-permute-start(f32[496,128]{1,0:T(8,128)S(1)} %get-tuple-element.89), channel_id=1, source_target_pairs={{4,0},{8,4},{12,8},{16,12},{20,16},{24,20},{28,24},{5,1},{9,5},{13... | collective-permute-start | bytes 761864 | tf_op jit(solution)/shard_map/ppermute | solution.py:674
  10.6 0.0 copy-done.10
  10.7 0.1 broadcast_in_dim.2.harmonic
  10.7 0.0 copy-done.5
  10.7 0.0 copy-done.8
  10.7 0.0 copy-done.3
  10.7 0.0 copy-done.4
  10.8 0.0 copy-done.6
  10.8 0.0 copy-done.7
  10.8 3.3 %prepare.1 = (f32[56,128]{1,0:T(8,128)S(1)}, f32[80,56,128]{2,1,0:T(8,128)S(1)}, f32[1920,128]{1,0:T(8,128)S(1)}, f32[1024,128]{1,0:T(8,128)S(1)}) custom-call(s32[6]{0:T(128)S(1)} %stack.35.flags, s32[2]{0:T(128)S(1)} %copy-done.8, f32[80,56,128]{2,1,0:T(8,128)S(1)} %get-tuple-element.75.xn, f32[80,56,128]{2,1,0:T(8,128)S(1)} %get-tuple-element.76.xf, ...), custom_call_target="tpu_custom_call" | custom-call | flops 1000 | bytes 1000 | tf_op jit(solution)/shard_map/prepare/pallas_call | solution.py:49
  14.1 0.1 collective-permute-start.5
  14.2 0.0 copy-start.1
  14.2 0.0 copy-start.2
  14.2 0.0 copy-start.9
  14.2 2.1 %near_base.1.base = f32[80,56,128]{2,1,0:T(8,128)S(1)} custom-call(s32[6]{0:T(128)S(1)} %stack.35.flags, f32[80,56,128]{2,1,0:T(8,128)S(1)} %get-tuple-element.75.xn, f32[80,56,128]{2,1,0:T(8,128)S(1)} %get-tuple-element.76.xf, f32[160,128]{1,0:T(8,128)S(1)} %bitcast.40, f32[160,128]{1,0:T(8,128)S(1)} %bitcast.45, f32[56,192]{1,0:T(8,128)S(1)} %copy-done.6, ...), custom_call_target="tpu_custom_call" | custom-call | bytes 1000 | tf_op jit(solution)/shard_map/near_base/pallas_call | solution.py:49
  16.3 0.0 copy-done.1
  16.4 0.0 copy-done.2
  16.4 1.3 %transfer.1 = (f32[2,80,16,128]{3,2,1,0:T(8,128)S(1)}, f32[152,128]{1,0:T(8,128)S(1)}) custom-call(s32[6]{0:T(128)S(1)} %stack.35.flags, f32[800,128]{1,0:T(8,128)S(1)} %bitcast.28, f32[800,128]{1,0:T(8,128)S(1)} %bitcast.32), custom_call_target="tpu_custom_call" | custom-call | bytes 1000 | tf_op jit(solution)/shard_map/transfer/pallas_call | solution.py:49
  17.6 0.0 copy-done.9
  17.6 0.1 reshape.36
  17.8 0.0 collective-permute-done.slab
  17.8 1.2 %far_lead.1.lead = f32[20,56,128]{2,1,0:T(8,128)S(1)} custom-call(s32[6]{0:T(128)S(1)} %stack.35.flags, f32[980,128]{1,0:T(8,128)S(1)} %collective-permute-done.slab, f32[56,128]{1,0:T(8,128)S(1)} %get-tuple-element.79.trig, f32[56,56]{1,0:T(8,128)S(1)} %copy-done.7, f32[64,192]{1,0:T(8,128)S(1)} %copy-done.5), custom_call_target="tpu_custom_call" | custom-call | bytes 1000 | tf_op jit(solution)/shard_map/far_lead/pallas_call | solution.py:49
  19.0 1.4 %collective-permute-done.2.from_left = f32[496,128]{1,0:T(8,128)S(1)} collective-permute-done((f32[496,128]{1,0:T(8,128)S(1)}, f32[496,128]{1,0:T(8,128)S(1)}, u32[]{:S(2)}, u32[]{:S(2)}) %collective-permute-start.2) | collective-permute-done | bytes 253984 | tf_op jit(solution)/shard_map/ppermute | solution.py:673
  20.4 0.0 collective-permute-done.3.from_right
  20.4 0.0 collective-permute-done.1.halo
  20.4 3.3 %near_cell.1 = (f32[80,56,128]{2,1,0:T(8,128)S(1)}, f32[648,128]{1,0:T(8,128)S(1)}) custom-call(s32[6]{0:T(128)S(1)} %stack.35.flags, f32[80,56,128]{2,1,0:T(8,128)S(1)} %near_base.1.base, f32[80,56,128]{2,1,0:T(8,128)S(1)} %collective-permute-done.1.halo, f32[496,128]{1,0:T(8,128)S(1)} %collective-permute-done.2.from_left, ...), custom_call_target="tpu_custom_call" | custom-call | flops 6000000000 | bytes 1000 | tf_op jit(solution)/shard_map/near_cell/pallas_call | solution.py:49
  23.6 2.5 %collective-permute-start.4 = (f32[648,128]{1,0:T(8,128)S(1)}, f32[648,128]{1,0:T(8,128)S(1)}, u32[]{:S(2)}, u32[]{:S(2)}) collective-permute-start(f32[648,128]{1,0:T(8,128)S(1)} %get-tuple-element.93.flows), channel_id=1, source_target_pairs={{0,4},{4,0},{8,12},{12,8},{16,20},{20,16},{24,28},{28,24},{1,5},{5... | collective-permute-start | bytes 995336 | tf_op jit(solution)/shard_map/ppermute | solution.py:645
  26.2 0.3 collective-permute-start.8
  26.5 7.1 %collective-permute-done.4.other = f32[648,128]{1,0:T(8,128)S(1)} collective-permute-done((f32[648,128]{1,0:T(8,128)S(1)}, f32[648,128]{1,0:T(8,128)S(1)}, u32[]{:S(2)}, u32[]{:S(2)}) %collective-permute-start.4) | collective-permute-done | bytes 331808 | tf_op jit(solution)/shard_map/ppermute | solution.py:645
  33.5 1.0 %merge_all.2 = (f32[2,30,8,128]{3,2,1,0:T(8,128)S(1)}, f32[648,128]{1,0:T(8,128)S(1)}, f32[2,15,8,128]{3,2,1,0:T(8,128)S(1)}, f32[496,128]{1,0:T(8,128)S(1)}) custom-call(s32[6]{0:T(128)S(1)} %stack.35.flags, f32[648,128]{1,0:T(8,128)S(1)} %get-tuple-element.93.flows, f32[648,128]{1,0:T(8,128)S(1)} %collective-permute-done.4.other), custom_call_target="tpu_custom_call" | custom-call | flops 1000 | bytes 1000 | tf_op jit(solution)/shard_map/merge_all/pallas_call | solution.py:49
  34.6 3.4 %collective-permute-start.6 = (f32[648,128]{1,0:T(8,128)S(1)}, f32[648,128]{1,0:T(8,128)S(1)}, u32[]{:S(2)}, u32[]{:S(2)}) collective-permute-start(f32[648,128]{1,0:T(8,128)S(1)} %get-tuple-element.101.flows), channel_id=1, source_target_pairs={{0,8},{4,12},{8,0},{12,4},{16,24},{20,28},{24,16},{28,20},{1,9},{5... | collective-permute-start | bytes 995336 | tf_op jit(solution)/shard_map/ppermute | solution.py:645
  38.0 0.8 %collective-permute-done.5.halo = f32[1920,128]{1,0:T(8,128)S(1)} collective-permute-done((f32[1920,128]{1,0:T(8,128)S(1)}, f32[1920,128]{1,0:T(8,128)S(1)}, u32[]{:S(2)}, u32[]{:S(2)}) %collective-permute-start.5) | collective-permute-done | bytes 983072 | tf_op jit(solution)/shard_map/ppermute | solution.py:644
  38.8 2.2 %far_chunk.2 = (f32[80,32,128]{2,1,0:T(8,128)S(1)}, f32[320,128]{1,0:T(8,128)S(1)}) custom-call(s32[6]{0:T(128)S(1)} %stack.35.flags, f32[80,56,128]{2,1,0:T(8,128)S(1)} %get-tuple-element.96.base, f32[20,56,128]{2,1,0:T(8,128)S(1)} %far_lead.1.lead, f32[1920,128]{1,0:T(8,128)S(1)} %collective-permute-done.5.halo, ...), custom_call_target="tpu_custom_call" | custom-call | flops 1000 | bytes 1000 | tf_op jit(solution)/shard_map/far_chunk/pallas_call | solution.py:49
  41.0 2.2 %collective-permute-start.7 = (f32[320,128]{1,0:T(8,128)S(1)}, f32[320,128]{1,0:T(8,128)S(1)}, u32[]{:S(2)}, u32[]{:S(2)}) collective-permute-start(f32[320,128]{1,0:T(8,128)S(1)} %get-tuple-element.107.flows), channel_id=1, source_target_pairs={{0,4},{4,0},{8,12},{12,8},{16,20},{20,16},{24,28},{28,24},{1,5},{5... | collective-permute-start | bytes 491528 | tf_op jit(solution)/shard_map/ppermute | solution.py:645
  43.2 1.9 %collective-permute-done.6.other = f32[648,128]{1,0:T(8,128)S(1)} collective-permute-done((f32[648,128]{1,0:T(8,128)S(1)}, f32[648,128]{1,0:T(8,128)S(1)}, u32[]{:S(2)}, u32[]{:S(2)}) %collective-permute-start.6) | collective-permute-done | bytes 331808 | tf_op jit(solution)/shard_map/ppermute | solution.py:645
  45.1 1.0 %merge_all.3 = (f32[2,30,8,128]{3,2,1,0:T(8,128)S(1)}, f32[304,128]{1,0:T(8,128)S(1)}, f32[2,15,8,128]{3,2,1,0:T(8,128)S(1)}, f32[496,128]{1,0:T(8,128)S(1)}) custom-call(s32[6]{0:T(128)S(1)} %stack.35.flags, f32[648,128]{1,0:T(8,128)S(1)} %get-tuple-element.101.flows, f32[648,128]{1,0:T(8,128)S(1)} %collective-permute-done.6.other, ...), custom_call_target="tpu_custom_call" | custom-call | flops 1000 | bytes 1000 | tf_op jit(solution)/shard_map/merge_all/pallas_call | solution.py:49
  46.1 2.8 %collective-permute-start.11 = (f32[304,128]{1,0:T(8,128)S(1)}, f32[304,128]{1,0:T(8,128)S(1)}, u32[]{:S(2)}, u32[]{:S(2)}) collective-permute-start(f32[304,128]{1,0:T(8,128)S(1)} %get-tuple-element.122.ends), channel_id=1, source_target_pairs={{0,16},{4,20},{8,24},{12,28},{16,0},{20,4},{24,8},{28,12},{1,17},{... | collective-permute-start | bytes 466952 | tf_op jit(solution)/shard_map/ppermute | solution.py:645
  49.0 0.0 collective-permute-done.7.other
  49.0 0.8 %merge_flows.4 = (f32[320,128]{1,0:T(8,128)S(1)}, f32[320,128]{1,0:T(8,128)S(1)}) custom-call(s32[6]{0:T(128)S(1)} %stack.35.flags, f32[2,30,8,128]{3,2,1,0:T(8,128)S(1)} %get-tuple-element.106.mats, f32[320,128]{1,0:T(8,128)S(1)} %get-tuple-element.107.flows, f32[320,128]{1,0:T(8,128)S(1)} %collective-permute-done.7.other), custom_call_target="tpu_custom_call" | custom-call | flops 1000 | bytes 1000 | tf_op jit(solution)/shard_map/merge_flows/pallas_call | solution.py:49
  49.7 1.6 %collective-permute-start.10 = (f32[320,128]{1,0:T(8,128)S(1)}, f32[320,128]{1,0:T(8,128)S(1)}, u32[]{:S(2)}, u32[]{:S(2)}) collective-permute-start(f32[320,128]{1,0:T(8,128)S(1)} %get-tuple-element.117.flows), channel_id=1, source_target_pairs={{0,8},{4,12},{8,0},{12,4},{16,24},{20,28},{24,16},{28,20},{1,9},{5... | collective-permute-start | bytes 491528 | tf_op jit(solution)/shard_map/ppermute | solution.py:645
  51.4 0.0 collective-permute-done.8.halo
  51.4 1.8 %far_chunk.3 = (f32[80,24,128]{2,1,0:T(8,128)S(1)}, f32[176,128]{1,0:T(8,128)S(1)}) custom-call(s32[6]{0:T(128)S(1)} %stack.35.flags, f32[80,56,128]{2,1,0:T(8,128)S(1)} %get-tuple-element.96.base, f32[20,56,128]{2,1,0:T(8,128)S(1)} %far_lead.1.lead, f32[1024,128]{1,0:T(8,128)S(1)} %collective-permute-done.8.halo, ...), custom_call_target="tpu_custom_call" | custom-call | flops 1000 | bytes 1000 | tf_op jit(solution)/shard_map/far_chunk/pallas_call | solution.py:49
  53.2 0.7 collective-permute-start.9
  53.8 3.9 %collective-permute-done.9.other = f32[176,128]{1,0:T(8,128)S(1)} collective-permute-done((f32[176,128]{1,0:T(8,128)S(1)}, f32[176,128]{1,0:T(8,128)S(1)}, u32[]{:S(2)}, u32[]{:S(2)}) %collective-permute-start.9) | collective-permute-done | bytes 90144 | tf_op jit(solution)/shard_map/ppermute | solution.py:645
  57.8 0.7 merge_flows.5
  58.5 0.0 collective-permute-done.11.other
  58.5 1.5 %collective-permute-start.12 = (f32[176,128]{1,0:T(8,128)S(1)}, f32[176,128]{1,0:T(8,128)S(1)}, u32[]{:S(2)}, u32[]{:S(2)}) collective-permute-start(f32[176,128]{1,0:T(8,128)S(1)} %get-tuple-element.123.flows), channel_id=1, source_target_pairs={{0,8},{4,12},{8,0},{12,4},{16,24},{20,28},{24,16},{28,20},{1,9},{5... | collective-permute-start | bytes 270344 | tf_op jit(solution)/shard_map/ppermute | solution.py:645
  59.9 0.0 collective-permute-done.10.other
  59.9 0.8 %merge_flows.6 = (f32[160,128]{1,0:T(8,128)S(1)}, f32[320,128]{1,0:T(8,128)S(1)}) custom-call(s32[6]{0:T(128)S(1)} %stack.35.flags, f32[2,30,8,128]{3,2,1,0:T(8,128)S(1)} %get-tuple-element.116.mats, f32[320,128]{1,0:T(8,128)S(1)} %get-tuple-element.117.flows, f32[320,128]{1,0:T(8,128)S(1)} %collective-permute-done.10.other, ...), custom_call_target="tpu_custom_call" | custom-call | flops 1000 | bytes 1000 | tf_op jit(solution)/shard_map/merge_flows/pallas_call | solution.py:49
  60.7 2.7 %collective-permute-start.13 = (f32[160,128]{1,0:T(8,128)S(1)}, f32[160,128]{1,0:T(8,128)S(1)}, u32[]{:S(2)}, u32[]{:S(2)}) collective-permute-start(f32[160,128]{1,0:T(8,128)S(1)} %get-tuple-element.136.refs_0_), channel_id=1, source_target_pairs={{0,16},{4,20},{8,24},{12,28},{16,0},{20,4},{24,8},{28,12},{1,17},{... | collective-permute-start | bytes 245768 | tf_op jit(solution)/shard_map/ppermute | solution.py:645
  63.3 0.0 collective-permute-done.12.other
  63.3 0.7 merge_flows.7
  64.1 2.2 %collective-permute-start.14 = (f32[88,128]{1,0:T(8,128)S(1)}, f32[88,128]{1,0:T(8,128)S(1)}, u32[]{:S(2)}, u32[]{:S(2)}) collective-permute-start(f32[88,128]{1,0:T(8,128)S(1)} %get-tuple-element.139.refs_4_), channel_id=1, source_target_pairs={{0,16},{4,20},{8,24},{12,28},{16,0},{20,4},{24,8},{28,12},{1,17},{... | collective-permute-start | bytes 135176 | tf_op jit(solution)/shard_map/ppermute | solution.py:645
  66.2 2.4 %correct_all.1 = (f32[80,56,128]{2,1,0:T(8,128)S(1)}, f32[2,30,8,128]{3,2,1,0:T(8,128)S(1)}) custom-call(s32[6]{0:T(128)S(1)} %stack.35.flags, f32[304,128]{1,0:T(8,128)S(1)} %get-tuple-element.122.ends, f32[304,128]{1,0:T(8,128)S(1)} %collective-permute-done.11.other, f32[2,15,8,128]{3,2,1,0:T(8,128)S(1)} %get-tuple-element.128.share, ...), custom_call_target="tpu_custom_call" | custom-call | flops 1000 | bytes 1000 | tf_op jit(solution)/shard_map/correct_all/pallas_call | solution.py:49
  68.6 0.0 collective-permute-done.13.refs_1_
  68.7 0.4 collective-permute-done.14.refs_5_
  69.1 3.5 %finish.1 = f32[7840,128]{1,0:T(8,128)} custom-call(s32[6]{0:T(128)S(1)} %stack.35.flags, f32[2,30,8,128]{3,2,1,0:T(8,128)S(1)} %get-tuple-element.134.mats, f32[2,80,16,128]{3,2,1,0:T(8,128)S(1)} %get-tuple-element.130.blocks, f32[80,56,128]{2,1,0:T(8,128)S(1)} %get-tuple-element.135.near, f32[160,128]{1,0:T(8,128)S(1)} %get-tuple-element.136.refs_0_, ...), custom_call_target="tpu_custom_call" | custom-call | flops 1000 | bytes 1000 | tf_op jit(solution)/shard_map/finish/pallas_call | solution.py:49
  (8 shorter events, 0.0 us)
Async XLA Ops:
  0.0 10.7 %copy-start.5 = (f32[64,192]{1,0:T(8,128)S(1)}, f32[64,192]{1,0:T(8,128)}, u32[]{:S(2)}) copy-start(f32[64,192]{1,0:T(8,128)} %constant.33.clone.turned) | copy-start | bytes 147460
  0.0 10.6 %copy-start.10 = (s32[24]{0:T(128)S(1)}, s32[24]{0:T(128)}, u32[]{:S(2)}) copy-start(s32[24]{0:T(128)} %param.18) | copy-start | bytes 292
  0.0 10.7 %copy-start.8 = (s32[2]{0:T(128)S(1)}, s32[2]{0:T(128)}, u32[]{:S(2)}) copy-start(s32[2]{0:T(128)} %blades.1) | copy-start | bytes 28
  0.1 2.1 %copy-start = (f32[16,2,5,49,128]{4,1,3,2,0:T(2,128)S(1)}, f32[16,2,5,49,128]{4,1,3,2,0:T(2,128)}, u32[]{:S(2)}) copy-start(f32[16,2,5,49,128]{4,1,3,2,0:T(2,128)} %param.11) | copy-start | bytes 12042244
  2.2 8.5 %copy-start.3 = (f32[16,2,5,128]{3,1,2,0:T(2,128)S(1)}, f32[16,2,5,128]{3,1,2,0:T(2,128)}, u32[]{:S(2)}) copy-start(f32[16,2,5,128]{3,1,2,0:T(2,128)} %param.12) | copy-start | bytes 245764
  2.2 8.5 %copy-start.4 = (f32[16,2,5,128]{3,1,2,0:T(2,128)S(1)}, f32[16,2,5,128]{3,1,2,0:T(2,128)}, u32[]{:S(2)}) copy-start(f32[16,2,5,128]{3,1,2,0:T(2,128)} %param.13) | copy-start | bytes 245764
  2.2 8.5 %copy-start.6 = (f32[56,192]{1,0:T(8,128)S(1)}, f32[56,192]{1,0:T(8,128)}, u32[]{:S(2)}) copy-start(f32[56,192]{1,0:T(8,128)} %constant.34.clone.table) | copy-start | bytes 129028
  2.2 8.5 %copy-start.7 = (f32[56,56]{1,0:T(8,128)S(1)}, f32[56,56]{1,0:T(8,128)}, u32[]{:S(2)}) copy-start(f32[56,56]{1,0:T(8,128)} %constant.32.clone.basis) | copy-start | bytes 37636
  2.7 17.6 %collective-permute-start.1 = (f32[80,56,128]{2,1,0:T(8,128)S(1)}, f32[80,56,128]{2,1,0:T(8,128)S(1)}, u32[]{:S(2)}, u32[]{:S(2)}) collective-permute-start(f32[80,56,128]{2,1,0:T(8,128)S(1)} %get-tuple-element.75.xn), channel_id=1, source_target_pairs={{0,1},{1,0},{2,3},{3,2},{4,5},{5,4},{6,7},{7,6},{8,9},{9,8},{10,11... | collective-permute-start | bytes 6881288 | tf_op jit(solution)/shard_map/ppermute | solution.py:671
  3.3 14.5 %collective-permute-start = (f32[980,128]{1,0:T(8,128)S(1)}, f32[980,128]{1,0:T(8,128)S(1)}, u32[]{:S(2)}, u32[]{:S(2)}) collective-permute-start(f32[980,128]{1,0:T(8,128)S(1)} %get-tuple-element.84), channel_id=1, source_target_pairs={{0,3},{1,2},{2,1},{3,0},{4,7},{5,6},{6,5},{7,4},{8,11},{9,10},{10,... | collective-permute-start | bytes 1505288 | tf_op jit(solution)/shard_map/ppermute | solution.py:644
  5.9 14.4 %collective-permute-start.2 = (f32[496,128]{1,0:T(8,128)S(1)}, f32[496,128]{1,0:T(8,128)S(1)}, u32[]{:S(2)}, u32[]{:S(2)}) collective-permute-start(f32[496,128]{1,0:T(8,128)S(1)} %get-tuple-element.88), channel_id=1, source_target_pairs={{0,4},{4,8},{8,12},{12,16},{16,20},{20,24},{24,28},{1,5},{5,9},{9,... | collective-permute-start | bytes 761864 | tf_op jit(solution)/shard_map/ppermute | solution.py:673
  9.3 11.0 %collective-permute-start.3 = (f32[496,128]{1,0:T(8,128)S(1)}, f32[496,128]{1,0:T(8,128)S(1)}, u32[]{:S(2)}, u32[]{:S(2)}) collective-permute-start(f32[496,128]{1,0:T(8,128)S(1)} %get-tuple-element.89), channel_id=1, source_target_pairs={{4,0},{8,4},{12,8},{16,12},{20,16},{24,20},{28,24},{5,1},{9,5},{13... | collective-permute-start | bytes 761864 | tf_op jit(solution)/shard_map/ppermute | solution.py:674
  14.1 24.7 %collective-permute-start.5 = (f32[1920,128]{1,0:T(8,128)S(1)}, f32[1920,128]{1,0:T(8,128)S(1)}, u32[]{:S(2)}, u32[]{:S(2)}) collective-permute-start(f32[1920,128]{1,0:T(8,128)S(1)} %get-tuple-element.98), channel_id=1, source_target_pairs={{0,3},{1,2},{2,1},{3,0},{4,7},{5,6},{6,5},{7,4},{8,11},{9,10},{10,... | collective-permute-start | bytes 2949128 | tf_op jit(solution)/shard_map/ppermute | solution.py:644
  14.2 2.2 %copy-start.1 = (f32[16,2,5,5,128]{4,1,3,2,0:T(2,128)S(1)}, f32[16,2,5,5,128]{4,1,3,2,0:T(2,128)}, u32[]{:S(2)}) copy-start(f32[16,2,5,5,128]{4,1,3,2,0:T(2,128)} %param.15) | copy-start | bytes 1228804
  14.2 2.2 %copy-start.2 = (f32[16,2,5,5,128]{4,1,3,2,0:T(2,128)S(1)}, f32[16,2,5,5,128]{4,1,3,2,0:T(2,128)}, u32[]{:S(2)}) copy-start(f32[16,2,5,5,128]{4,1,3,2,0:T(2,128)} %param.16) | copy-start | bytes 1228804
  14.2 3.4 %copy-start.9 = (bf16[16,2,5,5,128]{4,1,3,2,0:T(2,128)(2,1)S(1)}, bf16[16,2,5,5,128]{4,1,3,2,0:T(2,128)(2,1)}, u32[]{:S(2)}) copy-start(bf16[16,2,5,5,128]{4,1,3,2,0:T(2,128)(2,1)} %param.14) | copy-start | bytes 614404
  23.6 9.9 %collective-permute-start.4 = (f32[648,128]{1,0:T(8,128)S(1)}, f32[648,128]{1,0:T(8,128)S(1)}, u32[]{:S(2)}, u32[]{:S(2)}) collective-permute-start(f32[648,128]{1,0:T(8,128)S(1)} %get-tuple-element.93.flows), channel_id=1, source_target_pairs={{0,4},{4,0},{8,12},{12,8},{16,20},{20,16},{24,28},{28,24},{1,5},{5... | collective-permute-start | bytes 995336 | tf_op jit(solution)/shard_map/ppermute | solution.py:645
  26.2 25.2 %collective-permute-start.8 = (f32[1024,128]{1,0:T(8,128)S(1)}, f32[1024,128]{1,0:T(8,128)S(1)}, u32[]{:S(2)}, u32[]{:S(2)}) collective-permute-start(f32[1024,128]{1,0:T(8,128)S(1)} %get-tuple-element.110), channel_id=1, source_target_pairs={{0,3},{1,2},{2,1},{3,0},{4,7},{5,6},{6,5},{7,4},{8,11},{9,10},{10,... | collective-permute-start | bytes 1572872 | tf_op jit(solution)/shard_map/ppermute | solution.py:644
  34.6 10.5 %collective-permute-start.6 = (f32[648,128]{1,0:T(8,128)S(1)}, f32[648,128]{1,0:T(8,128)S(1)}, u32[]{:S(2)}, u32[]{:S(2)}) collective-permute-start(f32[648,128]{1,0:T(8,128)S(1)} %get-tuple-element.101.flows), channel_id=1, source_target_pairs={{0,8},{4,12},{8,0},{12,4},{16,24},{20,28},{24,16},{28,20},{1,9},{5... | collective-permute-start | bytes 995336 | tf_op jit(solution)/shard_map/ppermute | solution.py:645
  41.0 8.0 %collective-permute-start.7 = (f32[320,128]{1,0:T(8,128)S(1)}, f32[320,128]{1,0:T(8,128)S(1)}, u32[]{:S(2)}, u32[]{:S(2)}) collective-permute-start(f32[320,128]{1,0:T(8,128)S(1)} %get-tuple-element.107.flows), channel_id=1, source_target_pairs={{0,4},{4,0},{8,12},{12,8},{16,20},{20,16},{24,28},{28,24},{1,5},{5... | collective-permute-start | bytes 491528 | tf_op jit(solution)/shard_map/ppermute | solution.py:645
  46.1 12.3 %collective-permute-start.11 = (f32[304,128]{1,0:T(8,128)S(1)}, f32[304,128]{1,0:T(8,128)S(1)}, u32[]{:S(2)}, u32[]{:S(2)}) collective-permute-start(f32[304,128]{1,0:T(8,128)S(1)} %get-tuple-element.122.ends), channel_id=1, source_target_pairs={{0,16},{4,20},{8,24},{12,28},{16,0},{20,4},{24,8},{28,12},{1,17},{... | collective-permute-start | bytes 466952 | tf_op jit(solution)/shard_map/ppermute | solution.py:645
  49.7 10.2 %collective-permute-start.10 = (f32[320,128]{1,0:T(8,128)S(1)}, f32[320,128]{1,0:T(8,128)S(1)}, u32[]{:S(2)}, u32[]{:S(2)}) collective-permute-start(f32[320,128]{1,0:T(8,128)S(1)} %get-tuple-element.117.flows), channel_id=1, source_target_pairs={{0,8},{4,12},{8,0},{12,4},{16,24},{20,28},{24,16},{28,20},{1,9},{5... | collective-permute-start | bytes 491528 | tf_op jit(solution)/shard_map/ppermute | solution.py:645
  53.2 4.6 %collective-permute-start.9 = (f32[176,128]{1,0:T(8,128)S(1)}, f32[176,128]{1,0:T(8,128)S(1)}, u32[]{:S(2)}, u32[]{:S(2)}) collective-permute-start(f32[176,128]{1,0:T(8,128)S(1)} %get-tuple-element.113.flows), channel_id=1, source_target_pairs={{0,4},{4,0},{8,12},{12,8},{16,20},{20,16},{24,28},{28,24},{1,5},{5... | collective-permute-start | bytes 270344 | tf_op jit(solution)/shard_map/ppermute | solution.py:645
  58.5 4.9 %collective-permute-start.12 = (f32[176,128]{1,0:T(8,128)S(1)}, f32[176,128]{1,0:T(8,128)S(1)}, u32[]{:S(2)}, u32[]{:S(2)}) collective-permute-start(f32[176,128]{1,0:T(8,128)S(1)} %get-tuple-element.123.flows), channel_id=1, source_target_pairs={{0,8},{4,12},{8,0},{12,4},{16,24},{20,28},{24,16},{28,20},{1,9},{5... | collective-permute-start | bytes 270344 | tf_op jit(solution)/shard_map/ppermute | solution.py:645
  60.7 8.0 %collective-permute-start.13 = (f32[160,128]{1,0:T(8,128)S(1)}, f32[160,128]{1,0:T(8,128)S(1)}, u32[]{:S(2)}, u32[]{:S(2)}) collective-permute-start(f32[160,128]{1,0:T(8,128)S(1)} %get-tuple-element.136.refs_0_), channel_id=1, source_target_pairs={{0,16},{4,20},{8,24},{12,28},{16,0},{20,4},{24,8},{28,12},{1,17},{... | collective-permute-start | bytes 245768 | tf_op jit(solution)/shard_map/ppermute | solution.py:645
  64.1 5.0 %collective-permute-start.14 = (f32[88,128]{1,0:T(8,128)S(1)}, f32[88,128]{1,0:T(8,128)S(1)}, u32[]{:S(2)}, u32[]{:S(2)}) collective-permute-start(f32[88,128]{1,0:T(8,128)S(1)} %get-tuple-element.139.refs_4_), channel_id=1, source_target_pairs={{0,16},{4,20},{8,24},{12,28},{16,0},{20,4},{24,8},{28,12},{1,17},{... | collective-permute-start | bytes 135176 | tf_op jit(solution)/shard_map/ppermute | solution.py:645
